TPU v7x, 32 devices: a whole 2x2x4 slice. The times are simulated.
32 devices in a mesh: sample: 4 (over y, core), turb: 8 (over z, x).
Axes of the slice: x: 2, y: 2, z: 4, core: 2. Of those that a mesh axis runs over, the one named last changes fastest.
Arguments:
- inflow: bfloat16 [32, 1024, 512], P('sample', 'turb'), may hold values from -6 to 6
- cotangent: bfloat16 [32, 1024, 512], P('sample', 'turb'), may hold values from -6 to 6
- norm_gain: float32 [512], replicated, may hold values from 0.25 to 1.75
- query_weight: bfloat16 [512, 512], replicated, may hold values from -2 to 2, as said below
- key_weight: bfloat16 [512, 512], replicated, may hold values from -2 to 2, as said below
- value_weight: bfloat16 [512, 512], replicated, may hold values from -0.25 to 0.25
- out_weight: bfloat16 [512, 512], replicated, may hold values from -0.25 to 0.25
- adjacency: int32 [8, 8, 3], replicated, may hold values from -1 to 7, as said below
- sectors: int32 [32], P('sample'), may hold values from 0 to 7, as said below
Outputs:
- layer_output: bfloat16 [32, 1024, 512], P('sample', 'turb')
- grad_inflow: bfloat16 [32, 1024, 512], P('sample', 'turb')
- grad_query_weight: float32 [512, 512], replicated
- grad_key_weight: float32 [512, 512], replicated
- grad_value_weight: float32 [512, 512], replicated
- grad_out_weight: float32 [512, 512], replicated
- grad_norm_gain: float32 [512], replicated
Inputs may be any that keep to these rules, and one draw needn't show every extreme that they name: `adjacency`: row [s, b] lists distinct blocks other than b, the used entries first and -1 after them. For every block and every group of 8 consecutive samples, another block is listed upstream of it for at most 4 of the group's samples, and some pair of blocks reaches 4. `sectors`: every group of 8 consecutive samples holds each sector exactly 1 times. `query_weight`: A projection of rows of 512 features. `key_weight`: A projection of rows of 512 features.
All inputs are finite; a program needn't handle non-finite values.
Results may differ from a plain program's by a relative error of at most 0.004.
The roundings to bfloat16 on the way count: a program that leaves them out, or rounds other values in their place, can miss the bound.
Values may be sent and summed in bfloat16 or wider, within the bound.
No kernel may reach another device: no remote copies, remote signals or barrier semaphores. Data moves between devices by JAX's collectives and lax.ppermute only.
A program may use at most 192 MiB of HBM per device.

v0:
```python
import jax
import jax.numpy as jnp
from jax import lax
from jax.sharding import PartitionSpec as P

HEADS = 8
UPSTREAM = 3
SECTORS = 8
REPEAT = 1


epsilon = 1e-05


def normalize(row_block, norm_gain):
    widened = row_block.astype(jnp.float32)
    centred = widened - jnp.mean(widened, axis=-1, keepdims=True)
    inverse = lax.rsqrt(jnp.mean(centred * centred, axis=-1, keepdims=True) + epsilon)
    scaled = centred * inverse
    return (scaled, inverse, (scaled * norm_gain).astype(jnp.bfloat16))


def attend(pieces):
    queries, key_rows, value_rows, key_usable, grad_attended = pieces
    batch_count, query_count, model_width = queries.shape
    key_count = key_rows.shape[1]
    head_dim = model_width // HEADS
    score_scale = head_dim ** (-0.5)
    query_heads = queries.reshape(batch_count, query_count, HEADS, head_dim)
    key_heads = key_rows.reshape(batch_count, key_count, HEADS, head_dim)
    value_heads = value_rows.reshape(batch_count, key_count, HEADS, head_dim)
    grad_heads = grad_attended.reshape(batch_count, query_count, HEADS, head_dim)
    scores = (
        jnp.einsum("nqhd,nkhd->nhqk", query_heads, key_heads, preferred_element_type=jnp.float32)
        * score_scale
    )
    scores = jnp.where(key_usable[:, None, None, :], scores, -1e30)
    highest = jnp.max(scores, axis=-1, keepdims=True)
    weights = jnp.exp(scores - highest)
    probabilities = weights / jnp.sum(weights, axis=-1, keepdims=True)
    rounded = probabilities.astype(jnp.bfloat16)
    attended = jnp.einsum(
        "nhqk,nkhd->nqhd", rounded, value_heads, preferred_element_type=jnp.float32
    ).astype(jnp.bfloat16)
    grad_probs = jnp.einsum(
        "nqhd,nkhd->nhqk", grad_heads, value_heads, preferred_element_type=jnp.float32
    )
    centred = grad_probs - jnp.sum(probabilities * grad_probs, axis=-1, keepdims=True)
    grad_scores = (probabilities * centred * score_scale).astype(jnp.bfloat16)
    grad_queries = jnp.einsum(
        "nhqk,nkhd->nqhd", grad_scores, key_heads, preferred_element_type=jnp.float32
    ).astype(jnp.bfloat16)
    grad_keys = jnp.einsum(
        "nhqk,nqhd->nkhd", grad_scores, query_heads, preferred_element_type=jnp.float32
    )
    grad_values = jnp.einsum(
        "nhqk,nqhd->nkhd", rounded, grad_heads, preferred_element_type=jnp.float32
    )
    pair_terms = jnp.concatenate(
        [
            grad_keys.reshape(batch_count, key_count, model_width),
            grad_values.reshape(batch_count, key_count, model_width),
        ],
        axis=-1,
    )
    return (
        attended.reshape(batch_count, query_count, model_width),
        grad_queries.reshape(batch_count, query_count, model_width),
        pair_terms,
    )


def on_device(
    inflow,
    cotangent,
    norm_gain,
    query_weight,
    key_weight,
    value_weight,
    out_weight,
    adjacency,
    sectors,
):
    sample_count, block_rows, model_width = inflow.shape
    block_count = lax.axis_size("turb")
    own_block = lax.axis_index("turb")
    slot_count = REPEAT * ((SECTORS * UPSTREAM + block_count - 2) // (block_count - 1))
    flat_rows = sample_count * block_rows
    pair_width = 2 * model_width
    input_rows = inflow.reshape(flat_rows, model_width)
    grad_rows = cotangent.reshape(flat_rows, model_width)
    scaled, inverse, normed = normalize(input_rows, norm_gain)
    queries = jnp.dot(normed, query_weight, preferred_element_type=jnp.float32).astype(jnp.bfloat16)
    key_rows = jnp.dot(normed, key_weight, preferred_element_type=jnp.float32).astype(jnp.bfloat16)
    value_rows = jnp.dot(normed, value_weight, preferred_element_type=jnp.float32).astype(
        jnp.bfloat16
    )
    upstream = adjacency[sectors]
    needed = jnp.any(upstream == own_block, axis=2).astype(jnp.int32)
    earlier_need = jnp.cumsum(needed, axis=0) - needed
    slot_index = lax.broadcasted_iota(jnp.int32, (block_count, slot_count, sample_count), 1)
    chosen = (needed.T[:, None, :] == 1) & (earlier_need.T[:, None, :] == slot_index)
    selector = chosen.astype(jnp.bfloat16).reshape(block_count * slot_count, sample_count)
    own_lists = lax.dynamic_index_in_dim(upstream, own_block, axis=1, keepdims=False)
    usable = own_lists >= 0
    matches = jnp.any(own_lists[:, :, None, None] == own_lists[None, None, :, :], axis=3)
    sample_ids = lax.broadcasted_iota(jnp.int32, (sample_count, sample_count), 0)
    earlier = lax.broadcasted_iota(jnp.int32, (sample_count, sample_count), 1) < sample_ids
    position = jnp.sum((matches & earlier[:, None, :]).astype(jnp.int32), axis=2)
    flat_slot = own_lists * slot_count + position
    fetch_at = jnp.where(usable, flat_slot, 0)
    payload = jnp.concatenate([key_rows, value_rows], axis=1).reshape(
        sample_count, block_rows * pair_width
    )
    packed = jnp.dot(selector, payload, preferred_element_type=jnp.float32).astype(jnp.bfloat16)
    arrived = lax.all_to_all(
        packed.reshape(block_count, slot_count, block_rows, pair_width),
        "turb",
        split_axis=0,
        concat_axis=0,
        tiled=True,
    )
    fetched = arrived.reshape(block_count * slot_count, block_rows, pair_width)[fetch_at]
    upstream_keys = fetched[..., :model_width]
    upstream_values = fetched[..., model_width:]
    key_count = (1 + UPSTREAM) * block_rows
    key_all = jnp.concatenate(
        [key_rows.reshape(sample_count, 1, block_rows, model_width), upstream_keys], axis=1
    ).reshape(sample_count, key_count, model_width)
    value_all = jnp.concatenate(
        [value_rows.reshape(sample_count, 1, block_rows, model_width), upstream_values], axis=1
    ).reshape(sample_count, key_count, model_width)
    block_usable = jnp.concatenate([jnp.ones((sample_count, 1), dtype=jnp.bool_), usable], axis=1)
    key_usable = jnp.repeat(block_usable, block_rows, axis=1)
    grad_attended = jnp.dot(grad_rows, out_weight.T, preferred_element_type=jnp.float32).astype(
        jnp.bfloat16
    )
    group_size = min(sample_count, max(1, 512 // block_rows))
    while sample_count % group_size != 0:
        group_size = group_size - 1
    group_count = sample_count // group_size

    def grouped(tensor):
        return tensor.reshape((group_count, group_size) + tensor.shape[1:])

    attended, grad_queries, pair_terms = lax.map(
        attend,
        (
            grouped(queries.reshape(sample_count, block_rows, model_width)),
            grouped(key_all),
            grouped(value_all),
            grouped(key_usable),
            grouped(grad_attended.reshape(sample_count, block_rows, model_width)),
        ),
    )
    attended = attended.reshape(flat_rows, model_width)
    grad_queries = grad_queries.reshape(flat_rows, model_width)
    pair_terms = pair_terms.reshape(sample_count, 1 + UPSTREAM, block_rows, pair_width)
    layer_output = (
        (
            input_rows.astype(jnp.float32)
            + jnp.dot(attended, out_weight, preferred_element_type=jnp.float32)
        )
        .astype(jnp.bfloat16)
        .reshape(inflow.shape)
    )
    outgoing = (
        pair_terms[:, 1:]
        .astype(jnp.bfloat16)
        .reshape(sample_count * UPSTREAM, block_rows, pair_width)
    )
    target = jnp.where(usable, flat_slot, block_count * slot_count).reshape(-1)
    outbound = (
        jnp.zeros((block_count * slot_count, block_rows, pair_width), jnp.bfloat16)
        .at[target]
        .set(outgoing, mode="drop")
    )
    sum_out = jnp.dot(attended.T, grad_rows, preferred_element_type=jnp.float32)
    sum_query = jnp.dot(normed.T, grad_queries, preferred_element_type=jnp.float32)
    returned = lax.all_to_all(
        outbound.reshape(block_count, slot_count, block_rows, pair_width),
        "turb",
        split_axis=0,
        concat_axis=0,
        tiled=True,
    )
    remote = jnp.dot(
        selector.T,
        returned.reshape(block_count * slot_count, block_rows * pair_width),
        preferred_element_type=jnp.float32,
    )
    combined = (
        (pair_terms[:, 0].reshape(sample_count, block_rows * pair_width) + remote)
        .astype(jnp.bfloat16)
        .reshape(flat_rows, pair_width)
    )
    grad_keys = combined[:, :model_width]
    grad_values = combined[:, model_width:]
    sum_key = jnp.dot(normed.T, grad_keys, preferred_element_type=jnp.float32)
    sum_value = jnp.dot(normed.T, grad_values, preferred_element_type=jnp.float32)
    grad_normed = jnp.dot(grad_queries, query_weight.T, preferred_element_type=jnp.float32)
    grad_normed = grad_normed + jnp.dot(grad_keys, key_weight.T, preferred_element_type=jnp.float32)
    grad_normed = grad_normed + jnp.dot(
        grad_values, value_weight.T, preferred_element_type=jnp.float32
    )
    sum_gain = jnp.sum(grad_normed * scaled, axis=0)
    grad_scaled = grad_normed * norm_gain
    grad_input = inverse * (
        grad_scaled
        - jnp.mean(grad_scaled, axis=-1, keepdims=True)
        - scaled * jnp.mean(grad_scaled * scaled, axis=-1, keepdims=True)
    )
    grad_inflow = (
        (grad_rows.astype(jnp.float32) + grad_input).astype(jnp.bfloat16).reshape(inflow.shape)
    )
    sum_query, sum_key, sum_value, sum_out, sum_gain = lax.psum(
        (sum_query, sum_key, sum_value, sum_out, sum_gain), ("sample", "turb")
    )
    return (layer_output, grad_inflow, sum_query, sum_key, sum_value, sum_out, sum_gain)


def solution(mesh):
    placed = (
        P("sample", "turb", None),
        P("sample", "turb", None),
        P(),
        P(),
        P(),
        P(),
        P(),
        P(),
        P("sample"),
    )
    return jax.shard_map(
        on_device,
        mesh=mesh,
        in_specs=placed,
        out_specs=(P("sample", "turb", None), P("sample", "turb", None), P(), P(), P(), P(), P()),
        check_vma=False,
    )
```

profile of v0, /device:TPU:0, one launch (start us, length us, event | category | flops | bytes accessed | tf_op | source)
XLA Modules:
  0.0 933.5 jit_solution(829343091033864475)
XLA Ops:
  20.0 2.5 reshape.315
  22.5 5.5 convolution_convert_fusion
  28.1 11.3 %copy.83 = bf16[4,8,128,1024]{3,2,1,0:T(8,128)(2,1)} copy(bf16[4,8,128,1024]{3,1,2,0:T(8,128)(2,1)} %bitcast.191) | data formatting | bytes 16777216
  39.4 20.5 %all-to-all-start = ((bf16[8,4,128,1024]{3,2,1,0:T(8,128)(2,1)}), bf16[8,4,128,1024]{3,2,1,0:T(8,128)(2,1)}, u32[]{:S(2)}, u32[]{:S(2)}) async-start(bf16[8,4,128,1024]{3,2,1,0:T(8,128)(2,1)} %bitcast.190), calls=%async_computation | async-start | bytes 16777216 | tf_op jit(solution)/shard_map/all_to_all | solution.py:116
  63.9 2.8 convolution_convert_fusion.1
  66.7 176.3 %all-to-all-done = bf16[8,4,128,1024]{3,2,1,0:T(8,128)(2,1)} async-done(((bf16[8,4,128,1024]{3,2,1,0:T(8,128)(2,1)}), bf16[8,4,128,1024]{3,2,1,0:T(8,128)(2,1)}, u32[]{:S(2)}, u32[]{:S(2)}) %all-to-all-start) | async-done | bytes 8388640 | tf_op jit(solution)/shard_map/all_to_all | solution.py:116
  243.0 7.9 gather_fusion.1
  250.9 3.5 fusion.67
  254.3 3.6 pad_maximum_fusion
  257.9 276.2 %while.14 = (s32[]{:T(128)}, bf16[2,4,128,512]{3,2,1,0:T(8,128)(2,1)}, bf16[2,4,128,512]{3,2,1,0:T(8,128)(2,1)}, f32[2,4,512,1024]{3,2,1,0:T(8,128)}, bf16[2,4,5...) while((s32[]{:T(128)}, ...), condition=%wide.region_10.11_spmd, body=%wide.region_6.10_spmd.sunk | while | flops 1659381248 | bytes 168908992 | solution.py:146
  257.9 1.7 constant_dynamic-slice_fusion.8
  259.7 2.4 copy.93
  263.4 3.1 constant_dynamic-slice_fusion.10
  266.5 2.8 copy.95
  269.3 4.5 fusion.136
  274.7 2.0 copy.96
  276.7 7.8 fusion.137
  284.5 34.5 %fusion.138 = bf16[4,8,64,128]{3,2,1,0:T(8,128)(2,1)} fusion(bf16[4,512,8,64]{1,3,2,0:T(8,128)(2,1)} %bitcast.186, f32[4,8,128,512]{3,2,1,0:T(8,128)} %fusion.136, f32[4,8,128,512]{3,2,1,0:T(8,128)} %get-tuple-element.190, f32[4,8,128]{2,1,0:T(8,128)S(1)} %get-tuple-element.191), kind=kOutput, calls=%fused_computation.23.clone.1 | convolution fusion | flops 283382272 | bytes 19415040 | tf_op jit(solution)/shard_map/while/body/eval_jaxpr/nhqk,nkhd->nqhd/dot_general | solution.py:50
  319.1 2.1 copy.97
  321.1 5.8 fusion.139
  328.2 2.1 constant_dynamic-update-slice_fusion.5
  330.3 6.2 fusion.140
  336.5 34.9 %fusion.141 = f32[4,8,64,512]{3,2,1,0:T(8,128)} fusion(bf16[4,128,8,64]{1,3,2,0:T(8,128)(2,1)S(1)} %bitcast.196, f32[4,8,128,512]{3,2,1,0:T(8,128)} %fusion.136, f32[4,8,128,512]{3,2,1,0:T(8,128)} %get-tuple-element.190, f32[4,8,128]{2,1,0:T(8,128)S(1)} %get-tuple-element.191), kind=kOutput, calls=%fused_computation.15.clone.1 | convolution fusion | flops 283120128 | bytes 21512192 | tf_op jit(solution)/shard_map/while/body/eval_jaxpr/nhqk,nqhd->nkhd/dot_general | solution.py:53
  371.4 7.7 maximum_bitcast_fusion.2
  379.1 8.7 copy.99
  387.8 8.3 constant_dynamic-update-slice_fusion.6
  396.1 1.7 constant_dynamic-slice_fusion.8
  397.8 2.4 copy.93
  401.5 3.1 constant_dynamic-slice_fusion.10
  404.6 2.8 copy.95
  407.4 4.5 fusion.136
  412.8 2.0 copy.96
  414.8 7.8 fusion.137
  422.6 34.5 %fusion.138 = bf16[4,8,64,128]{3,2,1,0:T(8,128)(2,1)} fusion(bf16[4,512,8,64]{1,3,2,0:T(8,128)(2,1)} %bitcast.186, f32[4,8,128,512]{3,2,1,0:T(8,128)} %fusion.136, f32[4,8,128,512]{3,2,1,0:T(8,128)} %get-tuple-element.190, f32[4,8,128]{2,1,0:T(8,128)S(1)} %get-tuple-element.191), kind=kOutput, calls=%fused_computation.23.clone.1 | convolution fusion | flops 283382272 | bytes 19415040 | tf_op jit(solution)/shard_map/while/body/eval_jaxpr/nhqk,nkhd->nqhd/dot_general | solution.py:50
  457.2 2.1 copy.97
  459.2 5.8 fusion.139
  466.3 2.1 constant_dynamic-update-slice_fusion.5
  468.5 6.2 fusion.140
  474.6 34.9 %fusion.141 = f32[4,8,64,512]{3,2,1,0:T(8,128)} fusion(bf16[4,128,8,64]{1,3,2,0:T(8,128)(2,1)S(1)} %bitcast.196, f32[4,8,128,512]{3,2,1,0:T(8,128)} %fusion.136, f32[4,8,128,512]{3,2,1,0:T(8,128)} %get-tuple-element.190, f32[4,8,128]{2,1,0:T(8,128)S(1)} %get-tuple-element.191), kind=kOutput, calls=%fused_computation.15.clone.1 | convolution fusion | flops 283120128 | bytes 21512192 | tf_op jit(solution)/shard_map/while/body/eval_jaxpr/nhqk,nqhd->nkhd/dot_general | solution.py:53
  509.5 7.7 maximum_bitcast_fusion.2
  517.2 8.7 copy.99
  525.9 8.3 constant_dynamic-update-slice_fusion.6
  534.2 8.2 slice.45
  542.4 4.3 broadcast_in_dim.60
  546.7 15.1 %scatter_fusion = bf16[32,128,1024]{2,1,0:T(8,128)(2,1)} fusion(bf16[32,128,1024]{2,1,0:T(8,128)(2,1)} %broadcast_in_dim.60, s32[24]{0:T(128)S(1)} %copy-done.32, bf16[24,128,1024]{2,1,0:T(8,128)(2,1)} %bitcast.193), kind=kCustom, calls=%fused_computation.2 | custom fusion | bytes 18874464 | tf_op jit(solution)/shard_map/scatter | solution.py:176
  561.8 5.1 all-to-all-start.1
  567.4 2.5 slice_bitcast_fusion
  569.9 4.4 copy.84
  574.4 1.7 fusion.71
  576.1 1.7 fusion.70
  577.8 171.5 %all-to-all-done.1 = bf16[8,4,128,1024]{3,2,1,0:T(8,128)(2,1)} async-done(((bf16[8,4,128,1024]{3,2,1,0:T(8,128)(2,1)}), bf16[8,4,128,1024]{3,2,1,0:T(8,128)(2,1)}, u32[]{:S(2)}, u32[]{:S(2)}) %all-to-all-start.1) | async-done | bytes 8388640 | tf_op jit(solution)/shard_map/all_to_all | solution.py:180
  749.3 11.4 %copy.85 = bf16[4,8,128,1024]{3,1,2,0:T(8,128)(2,1)} copy(bf16[4,8,128,1024]{3,2,1,0:T(8,128)(2,1)} %bitcast.59) | data formatting | bytes 16777216
  760.7 7.2 fusion.33
  767.9 3.9 reshape.327
  771.8 3.4 fusion.55
  775.2 1.9 fusion.52
  777.2 2.1 fusion.69
  779.3 3.0 fusion.51
  783.1 2.9 fusion.50
  786.1 38.1 %psum.39 = f32[512]{0:T(512)} all-reduce(f32[512]{0:T(512)S(1)} %get-tuple-element.86), channel_id=1, replica_groups=mesh['sample'=4,'turb'=8] {'sample','turb'}, use_global_device_ids=true, to_apply=%region_19.20 | all-reduce | flops 512 | bytes 4096 | tf_op jit(solution)/shard_map/psum | solution.py:216
  824.2 3.0 fusion.49
  827.1 92.7 %all-reduce.4.cloned.1.call-done = (f32[512,512]{1,0:T(8,128)}, f32[512,512]{1,0:T(8,128)}, f32[512,512]{1,0:T(8,128)}, f32[512,512]{1,0:T(8,128)}) async-done(((f32[512,512]{1,0:T(8,128)}, f32[512,512]{1,0:T(8,128)}, f32[512,512]{1,0:T(8,128)}, f32[512,512]{1,0:T(8,128)}), (f32[512,512]{1,0:T(8,128)}, f32[512,512]{1,0:T(8,128)}, f32[512,512]{1,0:T(8,128)}, ...) | async-done | bytes 4194320 | tf_op jit(solution)/shard_map/psum | solution.py:216
  919.8 2.4 copy.122
  922.3 2.3 copy.123
  (133 shorter events, 26.8 us)
Async XLA Ops:
  7.2 8.3 copy-start
  7.2 9.2 copy-start.20
  10.9 0.6 copy-start.26
  10.9 6.2 copy-start.22
  13.8 3.4 copy-start.24
  15.4 1.0 copy-start.13
  16.4 1.0 copy-start.6
  17.4 1.0 copy-start.8
  22.5 5.5 copy-start.28
  39.4 22.8 %copy-start.14 = (bf16[1024,512]{1,0:T(8,128)(2,1)S(1)}, bf16[1024,512]{1,0:T(8,128)(2,1)}, u32[]{:S(2)}) copy-start(bf16[1024,512]{1,0:T(8,128)(2,1)} %copy-done.13) | copy-start | bytes 3145732
  39.4 22.8 %copy-start.18 = (bf16[512,512]{1,0:T(8,128)(2,1)S(1)}, bf16[512,512]{1,0:T(8,128)(2,1)}, u32[]{:S(2)}) copy-start(bf16[512,512]{1,0:T(8,128)(2,1)} %param.14) | copy-start | bytes 1572868
  39.4 24.5 %copy-start.10 = (bf16[8,128,512]{2,1,0:T(8,128)(2,1)S(1)}, bf16[8,128,512]{2,1,0:T(8,128)(2,1)}, u32[]{:S(2)}) copy-start(bf16[8,128,512]{2,1,0:T(8,128)(2,1)} %param.12) | copy-start | bytes 3145732
  39.4 203.6 %all-to-all-start = ((bf16[8,4,128,1024]{3,2,1,0:T(8,128)(2,1)}), bf16[8,4,128,1024]{3,2,1,0:T(8,128)(2,1)}, u32[]{:S(2)}, u32[]{:S(2)}) async-start(bf16[8,4,128,1024]{3,2,1,0:T(8,128)(2,1)} %bitcast.190), calls=%async_computation | async-start | bytes 16777216 | tf_op jit(solution)/shard_map/all_to_all | solution.py:116
  250.9 3.5 copy-start.7
  250.9 3.5 copy-start.9
  269.3 4.5 copy-start.5
  330.3 6.2 copy-start.2
  407.4 4.5 copy-start.5
  468.4 6.2 copy-start.2
  542.4 4.3 copy-start.32
  561.8 5.2 copy-start.1
  561.8 5.2 copy-start.27
  561.8 5.2 copy-start.30
  561.8 5.2 copy-start.31
  561.8 187.5 %all-to-all-start.1 = ((bf16[8,4,128,1024]{3,2,1,0:T(8,128)(2,1)}), bf16[8,4,128,1024]{3,2,1,0:T(8,128)(2,1)}, u32[]{:S(2)}, u32[]{:S(2)}) async-start(bf16[8,4,128,1024]{3,2,1,0:T(8,128)(2,1)} %bitcast.184), calls=%async_computation.1 | async-start | bytes 16777216 | tf_op jit(solution)/shard_map/all_to_all | solution.py:180
  566.9 352.9 %all-reduce.4.cloned.1.call-start = ((), (), s32[]{:S(2)}) async-start(), calls=%async_computation.2 | async-start | bytes 8388608 | tf_op jit(solution)/shard_map/psum | solution.py:216
  569.9 4.4 copy-start.11
  569.9 4.4 copy-start.33
  574.4 1.7 copy-start.12
  749.3 11.4 %copy-start.29 = (pred[8,4,8]{2,1,0:T(4,128)(4,1)S(1)}, pred[8,4,8]{2,1,0:T(4,128)(4,1)}, u32[]{:S(2)}) copy-start(pred[8,4,8]{2,1,0:T(4,128)(4,1)} %copy-done.28) | copy-start | bytes 772
  771.8 3.4 copy-start.3
  771.8 3.4 copy-start.15
  775.2 2.0 copy-start.19
  777.2 5.2 copy-start.4
  777.2 5.2 copy-start.21
  779.3 3.8 copy-start.23
  779.3 3.8 copy-start.25
  919.8 4.7 copy-start.17
  919.8 5.7 copy-start.16
Sparse Core Ops, SparseCore 0:
  777.3 142.5 all-reduce.3
where the time goes:
time: 943 us; the launch traced here: 934 us
  waiting for transfers between devices  441 us (47%)
  matrix products  224 us (24%)
  local copies, waits for them, and re-layouts  160 us (17%)
  blocking collectives  38.1 us (4%)
  other arithmetic  31.3 us (3%)
  starting transfers between devices  25.6 us (3%)
  between operations  14.7 us (2%)
    all_to_all x1, waiting for transfers between devices, on_device(): lax.all_to_all(packed.reshape(block_count, slot_count, block_rows, pair_w...  176 us
    all_to_all x1, waiting for transfers between devices, on_device(): lax.all_to_all(outbound.reshape(block_count, slot_count, block_rows, pair...  171 us
    psum x1, waiting for transfers between devices, on_device(): lax.psum((sum_query, sum_key, sum_value, sum_out, sum_gain), ('sample', '...  92.7 us
    dot_general x2, matrix products, attend(): jnp.einsum('nhqk,nqhd->nkhd', grad_scores, query_heads, preferred_element...  69.8 us
    dot_general x2, matrix products, attend(): jnp.einsum('nhqk,nkhd->nqhd', grad_scores, key_heads, preferred_element_t...  69.1 us
    dynamic_update_slice x10, local copies, waits for them, and re-layouts, on_device(): lax.map(attend, (grouped(queries.reshape(sample_count, block_rows, model_...  44.8 us
    unnamed x73, local copies, waits for them, and re-layouts  38.5 us
    psum x1, blocking collectives, on_device(): lax.psum((sum_query, sum_key, sum_value, sum_out, sum_gain), ('sample', '...  38.1 us
  transfers between devices with their start and end apart: 3, of which 3 were waited for; matrix products, arithmetic and copies ran while one was open for 3% of the time, Pallas kernels for 0%

commit v1 on v0

--- a/solution.py
+++ b/solution.py
@@ -1,6 +1,8 @@
 import jax
 import jax.numpy as jnp
 from jax import lax
+from jax.experimental import pallas as pl
+from jax.experimental.pallas import tpu as pltpu
 from jax.sharding import PartitionSpec as P
 
 HEADS = 8
@@ -219,6 +221,256 @@
     return (layer_output, grad_inflow, sum_query, sum_key, sum_value, sum_out, sum_gain)
 
 
+HEAD_PAIR = 2
+LOG2_E = 1.4426950408889634
+
+
+def project_kernel(x_ref, gain_ref, wq_ref, wk_ref, wv_ref, wkt_ref, wvt_ref,
+                   normed_ref, q_ref, k_ref, v_ref, kt_ref, vt_ref):
+    _, _, normed = normalize(x_ref[...], gain_ref[...])
+    normed_ref[...] = normed
+
+    def straight(weight_ref):
+        return jnp.dot(normed, weight_ref[...], preferred_element_type=jnp.float32).astype(
+            jnp.bfloat16
+        )
+
+    def turned(weight_ref):
+        return lax.dot_general(
+            weight_ref[...], normed, (((1,), (1,)), ((), ())), preferred_element_type=jnp.float32
+        ).astype(jnp.bfloat16)
+
+    q_ref[...] = straight(wq_ref)
+    k_ref[...] = straight(wk_ref)
+    v_ref[...] = straight(wv_ref)
+    kt_ref[...] = turned(wkt_ref)
+    vt_ref[...] = turned(wvt_ref)
+
+
+def project(rows, norm_gain, query_weight, key_weight, value_weight):
+    row_count, width = rows.shape
+    step = min(row_count, 256)
+    whole = lambda shape: pl.BlockSpec(shape, lambda i: (0,) * len(shape))
+    by_row = pl.BlockSpec((step, width), lambda i: (i, 0))
+    by_column = pl.BlockSpec((width, step), lambda i: (0, i))
+    flat = jax.ShapeDtypeStruct((row_count, width), jnp.bfloat16)
+    turned = jax.ShapeDtypeStruct((width, row_count), jnp.bfloat16)
+    return pl.pallas_call(
+        project_kernel,
+        grid=(row_count // step,),
+        in_specs=[by_row, whole((1, width))] + [whole((width, width))] * 5,
+        out_specs=[by_row] * 4 + [by_column] * 2,
+        out_shape=[flat] * 4 + [turned] * 2,
+        compiler_params=pltpu.CompilerParams(vmem_limit_bytes=32 * 2**20),
+        cost_estimate=pl.CostEstimate(
+            flops=10 * row_count * width * width,
+            bytes_accessed=14 * row_count * width + 10 * width * width,
+            transcendentals=0,
+        ),
+        name="project",
+    )(rows, norm_gain.reshape(1, width), query_weight, key_weight, value_weight,
+      key_weight.T, value_weight.T)
+
+
+def pair_kernel(block_rows, block_count, head_dim, lists_ref, q_ref, k_ref, v_ref, kt_ref, vt_ref,
+                cot_ref, wo_ref, att_ref, gq_ref, gk_ref, gv_ref, ga_ref, gk_acc, gv_acc):
+    width = HEAD_PAIR * head_dim
+    ga_ref[...] = lax.dot_general(
+        cot_ref[...], wo_ref[...], (((1,), (1,)), ((), ())), preferred_element_type=jnp.float32
+    ).astype(jnp.bfloat16)
+    gk_acc[...] = jnp.zeros_like(gk_acc)
+    gv_acc[...] = jnp.zeros_like(gv_acc)
+    scale = head_dim ** (-0.5)
+
+    def split_heads(rows):
+        lane = lax.broadcasted_iota(jnp.int32, rows.shape, 1)
+        wide = rows.astype(jnp.float32)
+        return jnp.concatenate(
+            [jnp.where(lane < head_dim, wide, 0.0), jnp.where(lane >= head_dim, wide, 0.0)], axis=0
+        ).astype(jnp.bfloat16)
+
+    def join_heads(wide):
+        first = lax.broadcasted_iota(jnp.int32, (width, block_rows), 0) < head_dim
+        return jnp.where(first, wide[:, :block_rows], wide[:, block_rows:]).astype(jnp.bfloat16)
+
+    def attend_block(block, used):
+        starts = [pl.multiple_of(block * block_rows, block_rows)]
+        for slot in range(used):
+            starts.append(
+                pl.multiple_of(lists_ref[block * UPSTREAM + slot] * block_rows, block_rows)
+            )
+        own = pl.ds(starts[0], block_rows)
+
+        def stacked(ref):
+            return jnp.concatenate([ref[pl.ds(s, block_rows), :] for s in starts], axis=0)
+
+        def beside(ref):
+            return jnp.concatenate([ref[:, pl.ds(s, block_rows)] for s in starts], axis=1)
+
+        queries = split_heads(q_ref[own, :])
+        grads = split_heads(ga_ref[own, :])
+        scores = lax.dot_general(
+            stacked(k_ref), queries, (((1,), (1,)), ((), ())), preferred_element_type=jnp.float32
+        )
+        highest = jnp.max(scores, axis=0, keepdims=True)
+        weights = jnp.exp2((scores - highest) * (scale * LOG2_E))
+        probs = weights * (1.0 / jnp.sum(weights, axis=0, keepdims=True))
+        probs_b = probs.astype(jnp.bfloat16)
+        att_ref[:, own] = join_heads(
+            jnp.dot(beside(vt_ref), probs_b, preferred_element_type=jnp.float32)
+        )
+        grad_probs = lax.dot_general(
+            stacked(v_ref), grads * scale, (((1,), (1,)), ((), ())),
+            preferred_element_type=jnp.float32,
+        )
+        total = jnp.sum(probs * grad_probs, axis=0, keepdims=True)
+        grad_scores = (probs * (grad_probs - total)).astype(jnp.bfloat16)
+        gq_ref[:, own] = join_heads(
+            jnp.dot(beside(kt_ref), grad_scores, preferred_element_type=jnp.float32)
+        )
+        grad_keys = jnp.dot(grad_scores, queries, preferred_element_type=jnp.float32)
+        grad_values = jnp.dot(probs_b, grads, preferred_element_type=jnp.float32)
+        for slot, start in enumerate(starts):
+            rows = pl.ds(start, block_rows)
+            part = slice(slot * block_rows, (slot + 1) * block_rows)
+            for acc, terms in ((gk_acc, grad_keys), (gv_acc, grad_values)):
+                term = terms[part]
+                if slot > 0:
+                    term = term.astype(jnp.bfloat16).astype(jnp.float32)
+                acc[rows, :] += term
+
+    def step(block, carry):
+        used = jnp.int32(0)
+        for slot in range(UPSTREAM):
+            used = used + (lists_ref[block * UPSTREAM + slot] >= 0).astype(jnp.int32)
+        for count in range(UPSTREAM + 1):
+            @pl.when(used == count)
+            def _():
+                attend_block(block, count)
+        return carry
+
+    lax.fori_loop(0, block_count, step, 0)
+    gk_ref[...] = gk_acc[...].astype(jnp.bfloat16)
+    gv_ref[...] = gv_acc[...].astype(jnp.bfloat16)
+
+
+def attend_sample(lists, queries, keys, values, keys_t, values_t, cotangent, out_weight, block_rows):
+    row_count, width = queries.shape
+    head_dim = width // HEADS
+    pair = HEAD_PAIR * head_dim
+    block_count = row_count // block_rows
+    by_column = pl.BlockSpec((row_count, pair), lambda p, lists: (0, p))
+    by_row = pl.BlockSpec((pair, row_count), lambda p, lists: (p, 0))
+    flat = jax.ShapeDtypeStruct((row_count, width), jnp.bfloat16)
+    turned = jax.ShapeDtypeStruct((width, row_count), jnp.bfloat16)
+    return pl.pallas_call(
+        lambda *refs: pair_kernel(block_rows, block_count, head_dim, *refs),
+        grid_spec=pltpu.PrefetchScalarGridSpec(
+            num_scalar_prefetch=1,
+            grid=(width // pair,),
+            in_specs=[
+                by_column, by_column, by_column, by_row, by_row,
+                pl.BlockSpec((row_count, width), lambda p, lists: (0, 0)),
+                pl.BlockSpec((pair, width), lambda p, lists: (p, 0)),
+            ],
+            out_specs=[by_row, by_row, by_column, by_column],
+            scratch_shapes=[
+                pltpu.VMEM((row_count, pair), jnp.bfloat16),
+                pltpu.VMEM((row_count, pair), jnp.float32),
+                pltpu.VMEM((row_count, pair), jnp.float32),
+            ],
+        ),
+        out_shape=[turned, turned, flat, flat],
+        compiler_params=pltpu.CompilerParams(vmem_limit_bytes=40 * 2**20),
+        cost_estimate=pl.CostEstimate(
+            flops=2 * row_count * width * width + 48 * row_count * block_rows * width,
+            bytes_accessed=20 * row_count * width,
+            transcendentals=row_count * 4 * block_rows * HEADS,
+        ),
+        name="attend",
+    )(lists, queries, keys, values, keys_t, values_t, cotangent, out_weight)
+
+
+def by_sample(
+    inflow,
+    cotangent,
+    norm_gain,
+    query_weight,
+    key_weight,
+    value_weight,
+    out_weight,
+    adjacency,
+    sectors,
+):
+    sample_count, block_rows, width = inflow.shape
+    sample_axis = lax.axis_size("sample")
+    block_count = lax.axis_size("turb")
+    row_count = block_count * block_rows
+    sector = lax.dynamic_index_in_dim(sectors, lax.axis_index("turb"), keepdims=False)
+    lists = lax.dynamic_index_in_dim(adjacency, sector, keepdims=False).reshape(-1)
+
+    def exchange(tensor):
+        return lax.all_to_all(tensor, "turb", split_axis=0, concat_axis=0, tiled=True)
+
+    rows = exchange(inflow)
+    rows, cotangent = lax.optimization_barrier((rows, cotangent))
+    rows = rows.reshape(row_count, width)
+    grad_rows = exchange(cotangent).reshape(row_count, width)
+    normed, queries, keys, values, keys_t, values_t = project(
+        rows, norm_gain, query_weight, key_weight, value_weight
+    )
+    attended_t, grad_queries_t, grad_keys, grad_values = attend_sample(
+        lists, queries, keys, values, keys_t, values_t, grad_rows, out_weight, block_rows
+    )
+
+    def contract(left, right, left_dim, right_dim):
+        return lax.dot_general(
+            left, right, (((left_dim,), (right_dim,)), ((), ())), preferred_element_type=jnp.float32
+        )
+
+    layer_rows = (
+        rows.astype(jnp.float32) + contract(attended_t, out_weight, 0, 0)
+    ).astype(jnp.bfloat16)
+    layer_output = exchange(layer_rows.reshape(inflow.shape))
+
+    sums = jnp.concatenate(
+        [
+            contract(normed, grad_queries_t, 0, 1),
+            contract(normed, grad_keys, 0, 0),
+            contract(normed, grad_values, 0, 0),
+            contract(attended_t, grad_rows, 1, 0),
+        ],
+        axis=0,
+    ).astype(jnp.bfloat16)
+    share = 4 * width // (sample_axis * block_count)
+    sums = sums.reshape(sample_axis, block_count * share, width)
+    sums = lax.all_to_all(sums, "sample", split_axis=0, concat_axis=0, tiled=True)
+    sums = jnp.sum(sums.astype(jnp.float32), axis=0).astype(jnp.bfloat16)
+    sums = sums.reshape(block_count, share, width)
+    sums = lax.all_to_all(sums, "turb", split_axis=0, concat_axis=0, tiled=True)
+    sums = jnp.sum(sums.astype(jnp.float32), axis=0).astype(jnp.bfloat16)
+    sums = lax.all_gather(sums, ("sample", "turb"), axis=0, tiled=True).astype(jnp.float32)
+    sum_query, sum_key, sum_value, sum_out = (
+        sums[i * width : (i + 1) * width] for i in range(4)
+    )
+
+    grad_normed = contract(grad_queries_t, query_weight, 0, 1)
+    grad_normed = grad_normed + contract(grad_keys, key_weight, 1, 1)
+    grad_normed = grad_normed + contract(grad_values, value_weight, 1, 1)
+    scaled, inverse, _ = normalize(rows, norm_gain)
+    sum_gain = jnp.sum(grad_normed * scaled, axis=0)
+    grad_scaled = grad_normed * norm_gain
+    grad_input = inverse * (
+        grad_scaled
+        - jnp.mean(grad_scaled, axis=-1, keepdims=True)
+        - scaled * jnp.mean(grad_scaled * scaled, axis=-1, keepdims=True)
+    )
+    grad_inflow = (grad_rows.astype(jnp.float32) + grad_input).astype(jnp.bfloat16)
+    grad_inflow = exchange(grad_inflow.reshape(inflow.shape))
+    sum_gain = jnp.sum(lax.all_gather(sum_gain, ("sample", "turb")), axis=0)
+    return (layer_output, grad_inflow, sum_query, sum_key, sum_value, sum_out, sum_gain)
+
+
 def solution(mesh):
     placed = (
         P("sample", "turb", None),
@@ -231,8 +483,15 @@
         P(),
         P("sample"),
     )
+
+    def plan(*args):
+        sample_count = args[0].shape[0]
+        if sample_count == mesh.shape["turb"]:
+            return by_sample(*args)
+        return on_device(*args)
+
     return jax.shard_map(
-        on_device,
+        plan,
         mesh=mesh,
         in_specs=placed,
         out_specs=(P("sample", "turb", None), P("sample", "turb", None), P(), P(), P(), P(), P()),

time: 943 us -> 314 us (0.33)
  waiting for transfers between devices: 441 us -> 42 us
  matrix products: 224 us -> 10.3 us
  local copies, waits for them, and re-layouts: 160 us -> 27.7 us
  blocking collectives: 38.1 us -> 149 us
  Pallas kernels: 0 us -> 43.7 us
  other arithmetic: 31.3 us -> 8.05 us
  starting transfers between devices: 25.6 us -> 15.9 us
    all_to_all x2 -> x4, waiting for transfers between devices: 348 us -> 42 us  [the longest x3 28.4 us: exchange(): lax.all_to_all(tensor, 'turb', split_axis=0, concat_axis=0, tiled=True)]
    dot_general x24 -> x8, matrix products: 208 us -> 10.3 us  [contract(): lax.dot_general(left, right, (((left_dim,), (right_dim,)), ((), ())), pre...]
    psum x1 -> x0, waiting for transfers between devices: 92.7 us -> none  [on_device(): lax.psum((sum_query, sum_key, sum_value, sum_out, sum_gain), ('sample', '...]
    all_gather x0 -> x1, blocking collectives: none -> 87.1 us  [by_sample(): sum_gain = jnp.sum(lax.all_gather(sum_gain, ('sample', 'turb')), axis=0)]
    all_to_all x0 -> x2, blocking collectives: none -> 62.1 us  [the longest x1 33.2 us: exchange(): lax.all_to_all(tensor, 'turb', split_axis=0, concat_axis=0, tiled=True)]
    dynamic_update_slice x10 -> x0, local copies, waits for them, and re-layouts: 44.8 us -> none  [on_device(): lax.map(attend, (grouped(queries.reshape(sample_count, block_rows, model_...]
    pallas_call x0 -> x2, Pallas kernels: none -> 43.7 us  [the longest x1 39.3 us: attend_sample(): pl.pallas_call(lambda *refs: pair_kernel(block_rows, block_count, head_di...]
    psum x1 -> x0, blocking collectives: 38.1 us -> none  [on_device(): lax.psum((sum_query, sum_key, sum_value, sum_out, sum_gain), ('sample', '...]
  transfers between devices with their start and end apart: 3 -> 5, of which waited for: 3 -> 3; matrix products, arithmetic and copies ran while one was open for 3% -> 4% of each run, Pallas kernels for 0% -> 1%
where the time goes in v1:
time: 314 us; the launch traced here: 313 us
  blocking collectives  149 us (47%)
  Pallas kernels  43.7 us (14%)
  waiting for transfers between devices  42 us (13%)
  local copies, waits for them, and re-layouts  27.7 us (9%)
  between operations  16.3 us (5%)
  starting transfers between devices  15.9 us (5%)
  matrix products  10.3 us (3%)
  other arithmetic  8.05 us (3%)
    all_gather x1, blocking collectives, by_sample(): sum_gain = jnp.sum(lax.all_gather(sum_gain, ('sample', 'turb')), axis=0)  87.1 us
    pallas_call x1, Pallas kernels, attend_sample(): pl.pallas_call(lambda *refs: pair_kernel(block_rows, block_count, head_di...  39.3 us
    all_to_all x1, blocking collectives, exchange(): lax.all_to_all(tensor, 'turb', split_axis=0, concat_axis=0, tiled=True)  33.2 us
    all_to_all x1, blocking collectives, by_sample(): lax.all_to_all(sums, 'sample', split_axis=0, concat_axis=0, tiled=True)  28.9 us
    all_to_all x3, waiting for transfers between devices, exchange(): lax.all_to_all(tensor, 'turb', split_axis=0, concat_axis=0, tiled=True)  28.4 us
    unnamed x60, local copies, waits for them, and re-layouts  23.2 us
    all_to_all x1, waiting for transfers between devices, by_sample(): sums = lax.all_to_all(sums, 'turb', split_axis=0, concat_axis=0, tiled=True)  13.6 us
    all_to_all x3, starting transfers between devices, exchange(): lax.all_to_all(tensor, 'turb', split_axis=0, concat_axis=0, tiled=True)  11.7 us
  transfers between devices with their start and end apart: 5, of which 3 were waited for; matrix products, arithmetic and copies ran while one was open for 4% of the time, Pallas kernels for 1%

profile of v1, /device:TPU:0, one launch (start us, length us, event | category | flops | bytes accessed | tf_op | source)
XLA Modules:
  0.0 313.1 jit_solution(6629646495275527428)
XLA Ops:
  7.2 0.0 copy-start
  7.2 33.2 %all_to_all.30 = bf16[8,128,512]{2,1,0:T(8,128)(2,1)S(1)} all-to-all(bf16[8,128,512]{2,1,0:T(8,128)(2,1)} %param.9), channel_id=1, replica_groups=mesh['sample'=4,'turb'=8] {'turb'}, dimensions={0} | all-to-all | bytes 2097152 | tf_op jit(solution)/shard_map/all_to_all | solution.py:413
  40.4 3.7 %all-to-all-start.1 = ((bf16[8,128,512]{2,1,0:T(8,128)(2,1)}), bf16[8,128,512]{2,1,0:T(8,128)(2,1)S(1)}, u32[]{:S(2)}, u32[]{:S(2)}) async-start(bf16[8,128,512]{2,1,0:T(8,128)(2,1)} %param.10), calls=%async_computation.1 | async-start | bytes 2097152 | tf_op jit(solution)/shard_map/all_to_all | solution.py:413
  44.1 0.6 dynamic_slice.8
  46.7 0.1 copy.25
  46.7 0.1 reshape.81.refs_0_
  46.8 1.0 copy.26
  47.8 1.0 copy.27
  48.8 1.0 copy-done.8
  49.9 1.0 copy-done.10
  50.9 1.0 copy-done.11
  52.0 4.4 %project.1 = (bf16[1024,512]{1,0:T(8,128)(2,1)S(1)}, bf16[1024,512]{1,0:T(8,128)(2,1)S(1)}, bf16[1024,512]{1,0:T(8,128)(2,1)S(1)}, bf16[1024,512]{1,0:T(8,128)(2...) custom-call(bf16[1024,512]{1,0:T(8,128)(2,1)S(1)} %bitcast.35, f32[1,512]{1,0:T(1,128)S(1)} %bitcast.41, ...), custom_call_target="tpu_custom_call" | custom-call | flops 2684354560 | bytes 9961472 | tf_op jit(solution)/shard_map/project/pallas_call | solution.py:258
  56.4 0.0 copy-start.15
  56.4 1.0 copy-done.15
  57.4 1.0 copy-done.17
  58.4 1.0 copy-done.19
  59.3 1.0 copy-done.21
  60.3 1.0 copy-done.23
  61.3 1.0 copy-done.25
  62.2 7.4 %all-to-all-done.1 = bf16[8,128,512]{2,1,0:T(8,128)(2,1)S(1)} async-done(((bf16[8,128,512]{2,1,0:T(8,128)(2,1)}), bf16[8,128,512]{2,1,0:T(8,128)(2,1)S(1)}, u32[]{:S(2)}, u32[]{:S(2)}) %all-to-all-start.1) | async-done | bytes 1048608 | tf_op jit(solution)/shard_map/all_to_all | solution.py:413
  69.7 1.0 copy-done.13
  70.7 1.2 copy-done.18
  72.0 1.2 copy-done.20
  73.2 1.2 copy-done.22
  74.4 1.2 copy-done.24
  75.6 1.2 copy-done.26
  76.9 39.3 %attend.1 = (bf16[512,1024]{1,0:T(8,128)(2,1)S(1)}, bf16[512,1024]{1,0:T(8,128)(2,1)S(1)}, bf16[1024,512]{1,0:T(8,128)(2,1)S(1)}, bf16[1024,512]{1,0:T(8,128)(2,1)S(1)}) custom-call(s32[24]{0:T(128)S(1)} %reshape.81.refs_0_, bf16[1024,512]{1,0:T(8,128)(2,1)S(1)} %copy-done.18, bf16[1024,512]{1,0:T(8,128)(2,1)S(1)} %copy-done.20, ...), custom_call_target="tpu_custom_call" | custom-call | flops 3758096384 | bytes 10485760 | tf_op jit(solution)/shard_map/attend/pallas_call | solution.py:366
  116.1 0.0 copy-start.3
  116.2 0.0 copy-start.14
  116.2 0.0 copy-start.5
  116.2 0.0 copy-start.6
  116.2 0.0 copy-start.16
  116.2 0.7 convolution_convert_fusion
  116.9 1.3 copy-done.16
  118.2 0.7 convolution_convert_fusion.3
  119.0 0.7 convolution_convert_fusion.2
  119.8 0.7 convolution_convert_fusion.1
  120.5 0.1 pad_maximum_fusion
  120.6 28.9 %all_to_all.31 = bf16[4,512,512]{2,1,0:T(8,128)(2,1)} all-to-all(bf16[4,512,512]{2,1,0:T(8,128)(2,1)S(1)} %bitcast.42), channel_id=1, replica_groups=mesh['sample'=4,'turb'=8] {'sample'}, dimensions={0} | all-to-all | bytes 4194304 | tf_op jit(solution)/shard_map/all_to_all | solution.py:447
  149.6 2.9 reduce_sum.82
  152.4 4.1 %all-to-all-start.5 = ((bf16[8,64,512]{2,1,0:T(8,128)(2,1)}), bf16[8,64,512]{2,1,0:T(8,128)(2,1)}, u32[]{:S(2)}, u32[]{:S(2)}) async-start(bf16[8,64,512]{2,1,0:T(8,128)(2,1)} %bitcast.43), calls=%async_computation.5 | async-start | bytes 1048576 | tf_op jit(solution)/shard_map/all_to_all | solution.py:450
  156.6 0.0 all-gather.4.cloned.1.call-start
  156.6 0.2 convert_reduce_fusion
  156.9 0.5 fusion.12
  157.4 13.6 %all-to-all-done.5 = bf16[8,64,512]{2,1,0:T(8,128)(2,1)} async-done(((bf16[8,64,512]{2,1,0:T(8,128)(2,1)}), bf16[8,64,512]{2,1,0:T(8,128)(2,1)}, u32[]{:S(2)}, u32[]{:S(2)}) %all-to-all-start.5) | async-done | bytes 524320 | tf_op jit(solution)/shard_map/all_to_all | solution.py:450
  171.0 1.8 reduce_sum.83
  172.7 0.0 all-gather.4.cloned.1.call-update
  172.8 3.1 fusion
  175.8 4.4 %all-to-all-start.2 = ((bf16[8,128,512]{2,1,0:T(8,128)(2,1)}), bf16[8,128,512]{2,1,0:T(8,128)(2,1)}, u32[]{:S(2)}, u32[]{:S(2)}) async-start(bf16[8,128,512]{2,1,0:T(8,128)(2,1)} %bitcast.44), calls=%async_computation.2 | async-start | bytes 2097152 | tf_op jit(solution)/shard_map/all_to_all | solution.py:413
  180.3 0.0 copy-start.4
  180.3 0.0 copy-start.9
  180.3 2.1 fusion.16
  182.4 0.0 copy-start.7
  182.4 0.8 fusion.15
  183.2 0.5 copy-done.7
  183.6 1.5 fusion.10
  185.1 1.9 fusion.9
  187.0 20.9 %all-to-all-done.2 = bf16[8,128,512]{2,1,0:T(8,128)(2,1)} async-done(((bf16[8,128,512]{2,1,0:T(8,128)(2,1)}), bf16[8,128,512]{2,1,0:T(8,128)(2,1)}, u32[]{:S(2)}, u32[]{:S(2)}) %all-to-all-start.2) | async-done | bytes 1048608 | tf_op jit(solution)/shard_map/all_to_all | solution.py:413
  208.0 3.6 %all-to-all-start.3 = ((bf16[8,128,512]{2,1,0:T(8,128)(2,1)}), bf16[8,128,512]{2,1,0:T(8,128)(2,1)S(1)}, u32[]{:S(2)}, u32[]{:S(2)}) async-start(bf16[8,128,512]{2,1,0:T(8,128)(2,1)} %bitcast.9), calls=%async_computation.3 | async-start | bytes 2097152 | tf_op jit(solution)/shard_map/all_to_all | solution.py:413
  211.5 87.1 %all-gather.1 = f32[32,1,512]{2,1,0:T(1,128)S(1)} all-gather(f32[1,1,512]{2,1,0:T(1,128)S(1)} %bitcast.45), channel_id=2, replica_groups=mesh['sample'=4,'turb'=8] {'sample','turb'}, dimensions={0}, use_global_device_ids=true | all-gather | bytes 67584 | tf_op jit(solution)/shard_map/all_gather | solution.py:470
  298.7 0.6 reduce_sum.85
  299.3 3.8 %fusion.14 = (f32[512,512]{1,0:T(8,128)}, f32[512,512]{1,0:T(8,128)}, f32[512,512]{1,0:T(8,128)}, f32[512,512]{1,0:T(8,128)}) fusion(bf16[2048,512]{1,0:T(8,128)(2,1)} %all-gather.4.cloned.1.call-done), kind=kLoop, calls=%fused_computation.30 | loop fusion | bytes 8388608 | tf_op jit(solution)/shard_map/slice | solution.py:454
  303.1 2.3 copy.30
  305.3 1.0 copy.31
  (35 shorter events, 0.1 us)
Async XLA Ops:
  7.2 39.5 %copy-start = (s32[8,8,3]{1,0,2:T(8,128)S(1)}, s32[8,8,3]{1,0,2:T(8,128)}, u32[]{:S(2)}) copy-start(s32[8,8,3]{1,0,2:T(8,128)} %param.16) | copy-start | bytes 2308
  7.2 36.9 %copy-start.27 = (s32[8]{0:T(128)S(1)}, s32[8]{0:T(128)}, u32[]{:S(2)}) copy-start(s32[8]{0:T(128)} %param.17) | copy-start | bytes 100
  7.2 39.6 %copy-start.1 = (bf16[512,512]{1,0:T(8,128)(2,1)S(1)}, bf16[512,512]{1,0:T(8,128)(2,1)}, u32[]{:S(2)}) copy-start(bf16[512,512]{1,0:T(8,128)(2,1)} %wk_ref.1) | copy-start | bytes 1572868
  40.4 7.5 %copy-start.2 = (bf16[512,512]{1,0:T(8,128)(2,1)S(1)}, bf16[512,512]{1,0:T(8,128)(2,1)}, u32[]{:S(2)}) copy-start(bf16[512,512]{1,0:T(8,128)(2,1)} %wv_ref.1) | copy-start | bytes 1572868
  40.4 8.5 %copy-start.12 = (f32[512]{0:T(512)S(1)}, f32[512]{0:T(512)}, u32[]{:S(2)}) copy-start(f32[512]{0:T(512)} %param.11) | copy-start | bytes 6148
  40.4 29.3 %all-to-all-start.1 = ((bf16[8,128,512]{2,1,0:T(8,128)(2,1)}), bf16[8,128,512]{2,1,0:T(8,128)(2,1)S(1)}, u32[]{:S(2)}, u32[]{:S(2)}) async-start(bf16[8,128,512]{2,1,0:T(8,128)(2,1)} %param.10), calls=%async_computation.1 | async-start | bytes 2097152 | tf_op jit(solution)/shard_map/all_to_all | solution.py:413
  48.8 1.0 copy-start.8
  49.9 1.0 copy-start.10
  50.9 1.0 copy-start.11
  56.4 1.0 copy-start.15
  57.4 1.0 copy-start.17
  58.4 1.0 copy-start.19
  59.3 1.0 copy-start.21
  60.3 1.0 copy-start.23
  61.3 1.0 copy-start.25
  69.7 1.0 copy-start.13
  70.7 1.2 copy-start.18
  72.0 1.2 copy-start.20
  73.2 1.2 copy-start.22
  74.4 1.2 copy-start.24
  75.6 1.2 copy-start.26
  116.1 2.8 copy-start.3
  116.2 2.8 copy-start.14
  116.2 2.8 copy-start.5
  116.2 3.6 %copy-start.6 = (bf16[1024,512]{1,0:T(8,128)(2,1)}, bf16[1024,512]{1,0:T(8,128)(2,1)S(1)}, u32[]{:S(2)}) copy-start(bf16[1024,512]{1,0:T(8,128)(2,1)S(1)} %get-tuple-element.29) | copy-start | bytes 3145732
  116.2 2.0 copy-start.16
  152.4 18.6 %all-to-all-start.5 = ((bf16[8,64,512]{2,1,0:T(8,128)(2,1)}), bf16[8,64,512]{2,1,0:T(8,128)(2,1)}, u32[]{:S(2)}, u32[]{:S(2)}) async-start(bf16[8,64,512]{2,1,0:T(8,128)(2,1)} %bitcast.43), calls=%async_computation.5 | async-start | bytes 1048576 | tf_op jit(solution)/shard_map/all_to_all | solution.py:450
  156.6 142.7 %all-gather.4.cloned.1.call-start = ((), (), s32[]{:S(2)}) async-start(), calls=%async_computation.6 | async-start | bytes 2162688 | tf_op jit(solution)/shard_map/all_gather | solution.py:452
  175.8 32.1 %all-to-all-start.2 = ((bf16[8,128,512]{2,1,0:T(8,128)(2,1)}), bf16[8,128,512]{2,1,0:T(8,128)(2,1)}, u32[]{:S(2)}, u32[]{:S(2)}) async-start(bf16[8,128,512]{2,1,0:T(8,128)(2,1)} %bitcast.44), calls=%async_computation.2 | async-start | bytes 2097152 | tf_op jit(solution)/shard_map/all_to_all | solution.py:413
  180.3 2.1 copy-start.4
  180.3 2.1 copy-start.9
  182.4 1.2 copy-start.7
  208.0 91.3 %all-to-all-start.3 = ((bf16[8,128,512]{2,1,0:T(8,128)(2,1)}), bf16[8,128,512]{2,1,0:T(8,128)(2,1)S(1)}, u32[]{:S(2)}, u32[]{:S(2)}) async-start(bf16[8,128,512]{2,1,0:T(8,128)(2,1)} %bitcast.9), calls=%async_computation.3 | async-start | bytes 2097152 | tf_op jit(solution)/shard_map/all_to_all | solution.py:413
Sparse Core Ops, SparseCore 0:
  172.9 69.0 all-gather.3

commit v2 on v0

--- a/solution.py
+++ b/solution.py
@@ -1,6 +1,8 @@
 import jax
 import jax.numpy as jnp
 from jax import lax
+from jax.experimental import pallas as pl
+from jax.experimental.pallas import tpu as pltpu
 from jax.sharding import PartitionSpec as P
 
 HEADS = 8
@@ -219,6 +221,398 @@
     return (layer_output, grad_inflow, sum_query, sum_key, sum_value, sum_out, sum_gain)
 
 
+PAIR = 2
+QUAD = 4
+LOG2_E = 1.4426950408889634
+VMEM_LIMIT = 58 * 2**20
+
+
+def contract(left, right, left_dim, right_dim):
+    return lax.dot_general(
+        left, right, (((left_dim,), (right_dim,)), ((), ())), preferred_element_type=jnp.float32
+    )
+
+
+def split_heads(rows, head_dim):
+    lane = lax.broadcasted_iota(jnp.int32, rows.shape, 1)
+    wide = rows.astype(jnp.float32)
+    return jnp.concatenate(
+        [jnp.where(lane < head_dim, wide, 0.0), jnp.where(lane >= head_dim, wide, 0.0)], axis=0
+    ).astype(jnp.bfloat16)
+
+
+def join_heads(wide, head_dim):
+    block_rows = wide.shape[1] // PAIR
+    first = lax.broadcasted_iota(jnp.int32, (wide.shape[0], block_rows), 0) < head_dim
+    return jnp.where(first, wide[:, :block_rows], wide[:, block_rows:])
+
+
+def for_each_block(lists_ref, block_count, block_rows, work):
+    def step(block, carry):
+        used = jnp.int32(0)
+        for slot in range(UPSTREAM):
+            used = used + (lists_ref[block * UPSTREAM + slot] >= 0).astype(jnp.int32)
+        for count in range(UPSTREAM + 1):
+
+            @pl.when(used == count)
+            def _():
+                sources = [block] + [
+                    lists_ref[block * UPSTREAM + slot] for slot in range(count)
+                ]
+                work(block, [pl.multiple_of(s * block_rows, block_rows) for s in sources])
+
+        return carry
+
+    lax.fori_loop(0, block_count, step, 0)
+
+
+def stacked(ref, starts, block_rows, lanes):
+    return jnp.concatenate([ref[pl.ds(s, block_rows), lanes] for s in starts], axis=0)
+
+
+def beside(ref, starts, block_rows, rows):
+    return jnp.concatenate([ref[rows, pl.ds(s, block_rows)] for s in starts], axis=1)
+
+
+def forward_kernel(block_rows, head_dim, lists_ref, x_ref, gain_ref, wq_ref, wk_ref, wv_ref,
+                   wkt_ref, wvt_ref, wo_ref, normed_t_ref, q_ref, k_ref, v_ref, kt_ref, att_ref,
+                   top_ref, inverse_ref, out_ref, normed_ref, vt_ref, rows_ref, sum_ref):
+    row_count = x_ref.shape[0]
+    quad = pl.program_id(0)
+    pair = PAIR * head_dim
+    exponent = head_dim ** (-0.5) * LOG2_E
+    chunk = min(row_count, 256)
+
+    @pl.when(quad == 0)
+    def _():
+        for start in range(0, row_count, chunk):
+            part = slice(start, start + chunk)
+            scaled, _, normed = normalize(x_ref[part, :], gain_ref[...])
+            normed_ref[part, :] = normed
+            normed_t_ref[:, part] = (scaled * gain_ref[...]).T.astype(jnp.bfloat16)
+
+    normed = normed_ref[...]
+    q_ref[...] = contract(normed, wq_ref[...], 1, 0).astype(jnp.bfloat16)
+    k_ref[...] = contract(normed, wk_ref[...], 1, 0).astype(jnp.bfloat16)
+    v_ref[...] = contract(normed, wv_ref[...], 1, 0).astype(jnp.bfloat16)
+    kt_ref[...] = contract(wkt_ref[...], normed, 1, 1).astype(jnp.bfloat16)
+    vt_ref[...] = contract(wvt_ref[...], normed, 1, 1).astype(jnp.bfloat16)
+
+    def work(block, starts):
+        own = pl.ds(starts[0], block_rows)
+        lanes = [slice(p * pair, (p + 1) * pair) for p in range(QUAD // PAIR)]
+        scores = [
+            contract(
+                stacked(k_ref, starts, block_rows, lane), split_heads(q_ref[own, lane], head_dim), 1, 1
+            )
+            for lane in lanes
+        ]
+        for p, lane in enumerate(lanes):
+            highest = jnp.max(scores[p], axis=0, keepdims=True)
+            weights = jnp.exp2((scores[p] - highest) * exponent)
+            inverse = 1.0 / jnp.sum(weights, axis=0, keepdims=True)
+            probs = (weights * inverse).astype(jnp.bfloat16)
+            top_ref[0, pl.ds(block * (QUAD // PAIR) + p, 1), :] = highest
+            inverse_ref[0, pl.ds(block * (QUAD // PAIR) + p, 1), :] = inverse
+            joined = join_heads(
+                jnp.dot(
+                    beside(vt_ref, starts, block_rows, lane),
+                    probs,
+                    preferred_element_type=jnp.float32,
+                ),
+                head_dim,
+            )
+            att_ref[lane, own] = joined.astype(jnp.bfloat16)
+            rows_ref[own, lane] = joined.T.astype(jnp.bfloat16)
+
+    for_each_block(lists_ref, row_count // block_rows, block_rows, work)
+    part = contract(rows_ref[...], wo_ref[...], 1, 0)
+
+    @pl.when(quad == 0)
+    def _():
+        sum_ref[...] = x_ref[...].astype(jnp.float32) + part
+
+    @pl.when(quad > 0)
+    def _():
+        sum_ref[...] += part
+
+    @pl.when(quad == pl.num_programs(0) - 1)
+    def _():
+        out_ref[...] = sum_ref[...].astype(jnp.bfloat16)
+
+
+def forward(lists, rows, norm_gain, query_weight, key_weight, value_weight, out_weight, block_rows):
+    row_count, width = rows.shape
+    head_dim = width // HEADS
+    quad = QUAD * head_dim
+    quads = width // quad
+    stat_rows = row_count // block_rows * (QUAD // PAIR)
+    fixed = lambda *shape: pl.BlockSpec(shape, lambda p, lists: (0,) * len(shape))
+    across = lambda size: pl.BlockSpec((size, quad), lambda p, lists: (0, p))
+    down = lambda size: pl.BlockSpec((quad, size), lambda p, lists: (p, 0))
+    stat = pl.BlockSpec((1, stat_rows, PAIR * block_rows), lambda p, lists: (p, 0, 0))
+    flat = jax.ShapeDtypeStruct((row_count, width), jnp.bfloat16)
+    turned = jax.ShapeDtypeStruct((width, row_count), jnp.bfloat16)
+    stats = jax.ShapeDtypeStruct((quads, stat_rows, PAIR * block_rows), jnp.float32)
+    return pl.pallas_call(
+        lambda *refs: forward_kernel(block_rows, head_dim, *refs),
+        grid_spec=pltpu.PrefetchScalarGridSpec(
+            num_scalar_prefetch=1,
+            grid=(quads,),
+            in_specs=[fixed(row_count, width), fixed(1, width)]
+            + [across(width)] * 3
+            + [down(width)] * 3,
+            out_specs=[fixed(width, row_count)]
+            + [across(row_count)] * 3
+            + [down(row_count)] * 2
+            + [stat] * 2
+            + [fixed(row_count, width)],
+            scratch_shapes=[
+                pltpu.VMEM((row_count, width), jnp.bfloat16),
+                pltpu.VMEM((quad, row_count), jnp.bfloat16),
+                pltpu.VMEM((row_count, quad), jnp.bfloat16),
+                pltpu.VMEM((row_count, width), jnp.float32),
+            ],
+        ),
+        out_shape=[turned, flat, flat, flat, turned, turned, stats, stats, flat],
+        compiler_params=pltpu.CompilerParams(vmem_limit_bytes=VMEM_LIMIT),
+        cost_estimate=pl.CostEstimate(
+            flops=12 * row_count * width * width + 32 * row_count * block_rows * width,
+            bytes_accessed=20 * row_count * width,
+            transcendentals=row_count * 4 * block_rows * HEADS,
+        ),
+        name="forward",
+    )(lists, rows, norm_gain.reshape(1, width), query_weight, key_weight, value_weight,
+      key_weight.T, value_weight.T, out_weight)
+
+
+def backward_kernel(block_rows, head_dim, lists_ref, cot_ref, wo_ref, normed_t_ref, q_ref, k_ref,
+                    v_ref, kt_ref, att_ref, top_ref, inverse_ref, gq_ref, gk_ref, gv_ref, sums_ref,
+                    ga_ref, gk_acc, gv_acc):
+    row_count, width = cot_ref.shape
+    pair = PAIR * head_dim
+    quad = QUAD * head_dim
+    scale = head_dim ** (-0.5)
+    ga_ref[...] = contract(cot_ref[...], wo_ref[...], 1, 1).astype(jnp.bfloat16)
+    gk_acc[...] = jnp.zeros_like(gk_acc)
+    gv_acc[...] = jnp.zeros_like(gv_acc)
+
+    def work(block, starts):
+        own = pl.ds(starts[0], block_rows)
+        lanes = [slice(p * pair, (p + 1) * pair) for p in range(QUAD // PAIR)]
+        queries = [split_heads(q_ref[own, lane], head_dim) for lane in lanes]
+        grads = [split_heads(ga_ref[own, lane], head_dim) for lane in lanes]
+        scores = [
+            contract(stacked(k_ref, starts, block_rows, lane), queries[p], 1, 1)
+            for p, lane in enumerate(lanes)
+        ]
+        grad_probs = [
+            contract(stacked(v_ref, starts, block_rows, lane), grads[p] * scale, 1, 1)
+            for p, lane in enumerate(lanes)
+        ]
+        for p, lane in enumerate(lanes):
+            stat = pl.ds(block * (QUAD // PAIR) + p, 1)
+            probs = jnp.exp2((scores[p] - top_ref[0, stat, :]) * (scale * LOG2_E))
+            probs = probs * inverse_ref[0, stat, :]
+            total = jnp.sum(probs * grad_probs[p], axis=0, keepdims=True)
+            grad_scores = (probs * (grad_probs[p] - total)).astype(jnp.bfloat16)
+            probs_b = probs.astype(jnp.bfloat16)
+            grad_values = jnp.dot(probs_b, grads[p], preferred_element_type=jnp.float32)
+            grad_keys = jnp.dot(grad_scores, queries[p], preferred_element_type=jnp.float32)
+            joined = join_heads(
+                jnp.dot(
+                    beside(kt_ref, starts, block_rows, lane),
+                    grad_scores,
+                    preferred_element_type=jnp.float32,
+                ),
+                head_dim,
+            )
+            gq_ref[own, lane] = joined.T.astype(jnp.bfloat16)
+            for slot, start in enumerate(starts):
+                rows = pl.ds(start, block_rows)
+                part = slice(slot * block_rows, (slot + 1) * block_rows)
+                for acc, terms in ((gk_acc, grad_keys), (gv_acc, grad_values)):
+                    term = terms[part]
+                    if slot > 0:
+                        term = term.astype(jnp.bfloat16).astype(jnp.float32)
+                    acc[rows, lane] += term
+
+    for_each_block(lists_ref, row_count // block_rows, block_rows, work)
+    gk_ref[...] = gk_acc[...].astype(jnp.bfloat16)
+    gv_ref[...] = gv_acc[...].astype(jnp.bfloat16)
+    for i, ref in enumerate((gq_ref, gk_ref, gv_ref)):
+        sums_ref[i * width : (i + 1) * width, :] = contract(
+            normed_t_ref[...], ref[...], 1, 0
+        ).astype(jnp.bfloat16)
+    for i in range(width // quad):
+        start = 3 * width + i * quad
+        sums_ref[start : start + quad, :] = contract(
+            att_ref[...], cot_ref[:, i * quad : (i + 1) * quad], 1, 0
+        ).astype(jnp.bfloat16)
+
+
+def backward(lists, cotangent, out_weight, normed_t, queries, keys, values, keys_t, attended_t,
+             tops, inverses, block_rows, which):
+    row_count, width = cotangent.shape
+    head_dim = width // HEADS
+    quad = QUAD * head_dim
+    fixed = lambda *shape: pl.BlockSpec(shape, lambda i, lists: (0,) * len(shape))
+    across = pl.BlockSpec((row_count, quad), lambda i, lists: (0, which))
+    down = lambda size: pl.BlockSpec((quad, size), lambda i, lists: (which, 0))
+    stat = pl.BlockSpec((1,) + tops.shape[1:], lambda i, lists: (which, 0, 0))
+    part = jax.ShapeDtypeStruct((row_count, quad), jnp.bfloat16)
+    return pl.pallas_call(
+        lambda *refs: backward_kernel(block_rows, head_dim, *refs),
+        grid_spec=pltpu.PrefetchScalarGridSpec(
+            num_scalar_prefetch=1,
+            grid=(1,),
+            in_specs=[fixed(row_count, width), down(width), fixed(width, row_count)]
+            + [across] * 3
+            + [down(row_count)] * 2
+            + [stat] * 2,
+            out_specs=[fixed(row_count, quad)] * 3 + [fixed(4 * width, quad)],
+            scratch_shapes=[
+                pltpu.VMEM((row_count, quad), jnp.bfloat16),
+                pltpu.VMEM((row_count, quad), jnp.float32),
+                pltpu.VMEM((row_count, quad), jnp.float32),
+            ],
+        ),
+        out_shape=[part] * 3 + [jax.ShapeDtypeStruct((4 * width, quad), jnp.bfloat16)],
+        compiler_params=pltpu.CompilerParams(vmem_limit_bytes=VMEM_LIMIT),
+        cost_estimate=pl.CostEstimate(
+            flops=10 * row_count * width * quad + 80 * row_count * block_rows * quad,
+            bytes_accessed=14 * row_count * width,
+            transcendentals=row_count * 4 * block_rows * QUAD,
+        ),
+        name="backward",
+    )(lists, cotangent, out_weight, normed_t, queries, keys, values, keys_t, attended_t, tops,
+      inverses)
+
+
+def finish_kernel(quads, x_ref, cot_ref, gain_ref, wq_ref, wk_ref, wv_ref, *refs):
+    grad_refs, (out_ref, sum_ref) = refs[:-2], refs[-2:]
+    scaled, inverse, _ = normalize(x_ref[...], gain_ref[...])
+    quad = grad_refs[0].shape[1]
+    grad_normed = jnp.zeros(x_ref.shape, jnp.float32)
+    for i in range(quads):
+        lanes = slice(i * quad, (i + 1) * quad)
+        for j, weight_ref in enumerate((wq_ref, wk_ref, wv_ref)):
+            grad_normed += contract(grad_refs[3 * i + j][...], weight_ref[:, lanes], 1, 1)
+
+    @pl.when(pl.program_id(0) == 0)
+    def _():
+        sum_ref[...] = jnp.zeros_like(sum_ref)
+
+    sum_ref[...] += jnp.sum(grad_normed * scaled, axis=0, keepdims=True)
+    grad_scaled = grad_normed * gain_ref[...]
+    grad_input = inverse * (
+        grad_scaled
+        - jnp.mean(grad_scaled, axis=-1, keepdims=True)
+        - scaled * jnp.mean(grad_scaled * scaled, axis=-1, keepdims=True)
+    )
+    out_ref[...] = (cot_ref[...].astype(jnp.float32) + grad_input).astype(jnp.bfloat16)
+
+
+def finish(rows, cotangent, norm_gain, query_weight, key_weight, value_weight, grads):
+    row_count, width = rows.shape
+    quad = grads[0].shape[1]
+    step = min(row_count, 256)
+    fixed = lambda *shape: pl.BlockSpec(shape, lambda i: (0,) * len(shape))
+    by_row = lambda size: pl.BlockSpec((step, size), lambda i: (i, 0))
+    return pl.pallas_call(
+        lambda *refs: finish_kernel(width // quad, *refs),
+        grid=(row_count // step,),
+        in_specs=[by_row(width)] * 2
+        + [fixed(1, width)]
+        + [fixed(width, width)] * 3
+        + [by_row(quad)] * len(grads),
+        out_specs=[by_row(width), fixed(1, width)],
+        out_shape=[
+            jax.ShapeDtypeStruct((row_count, width), jnp.bfloat16),
+            jax.ShapeDtypeStruct((1, width), jnp.float32),
+        ],
+        compiler_params=pltpu.CompilerParams(vmem_limit_bytes=VMEM_LIMIT),
+        cost_estimate=pl.CostEstimate(
+            flops=6 * row_count * width * width,
+            bytes_accessed=16 * row_count * width,
+            transcendentals=0,
+        ),
+        name="finish",
+    )(rows, cotangent, norm_gain.reshape(1, width), query_weight, key_weight, value_weight, *grads)
+
+
+def swap(tensor, axis):
+    return lax.all_to_all(tensor, axis, split_axis=0, concat_axis=0, tiled=True)
+
+
+def reduce_sums(sums):
+    row_count, width = sums.shape
+    for axis in ("sample", "turb"):
+        size = lax.axis_size(axis)
+        sums = swap(sums.reshape(size, -1, width), axis)
+        sums = jnp.sum(sums.astype(jnp.float32), axis=0).astype(jnp.bfloat16)
+    for axis in ("turb", "sample"):
+        size = lax.axis_size(axis)
+        sums = swap(jnp.broadcast_to(sums, (size,) + sums.shape), axis).reshape(-1, width)
+    return sums.astype(jnp.float32)
+
+
+def by_sample(
+    inflow,
+    cotangent,
+    norm_gain,
+    query_weight,
+    key_weight,
+    value_weight,
+    out_weight,
+    adjacency,
+    sectors,
+):
+    sample_count, block_rows, width = inflow.shape
+    row_count = lax.axis_size("turb") * block_rows
+    quads = HEADS // QUAD
+    quad = width // quads
+    sector = lax.dynamic_index_in_dim(sectors, lax.axis_index("turb"), keepdims=False)
+    lists = lax.dynamic_index_in_dim(adjacency, sector, keepdims=False).reshape(-1)
+
+    rows = swap(inflow, "turb")
+    rows, cotangent = lax.optimization_barrier((rows, cotangent))
+    rows = rows.reshape(row_count, width)
+    grad_rows = swap(cotangent, "turb").reshape(row_count, width)
+    *saved, layer_rows = forward(
+        lists, rows, norm_gain, query_weight, key_weight, value_weight, out_weight, block_rows
+    )
+    layer_output = swap(layer_rows.reshape(inflow.shape), "turb")
+    grads, sums = [], []
+    for which in range(quads):
+        *part, terms = backward(lists, grad_rows, out_weight, *saved, block_rows, which)
+        grads += part
+        sums.append(reduce_sums(terms))
+    grad_rows, sum_gain = finish(
+        rows, grad_rows, norm_gain, query_weight, key_weight, value_weight, grads
+    )
+    grad_inflow = swap(grad_rows.reshape(inflow.shape), "turb")
+    sum_gain = jnp.sum(lax.all_gather(sum_gain.reshape(width), ("sample", "turb")), axis=0)
+    projections = [
+        jnp.concatenate([part[i * width : (i + 1) * width] for part in sums], axis=1)
+        for i in range(3)
+    ]
+    sum_out = jnp.concatenate(
+        [
+            jnp.concatenate(
+                [
+                    part[3 * width + i * quad : 3 * width + (i + 1) * quad]
+                    for i in range(quads)
+                ],
+                axis=1,
+            )
+            for part in sums
+        ],
+        axis=0,
+    )
+    return (layer_output, grad_inflow, *projections, sum_out, sum_gain)
+
+
 def solution(mesh):
     placed = (
         P("sample", "turb", None),
@@ -231,8 +625,15 @@
         P(),
         P("sample"),
     )
+
+    def plan(*args):
+        sample_count = args[0].shape[0]
+        if sample_count == mesh.shape["turb"]:
+            return by_sample(*args)
+        return on_device(*args)
+
     return jax.shard_map(
-        on_device,
+        plan,
         mesh=mesh,
         in_specs=placed,
         out_specs=(P("sample", "turb", None), P("sample", "turb", None), P(), P(), P(), P(), P()),

time: 943 us -> 313 us (0.33)
  waiting for transfers between devices: 441 us -> 51.3 us
  matrix products: 224 us -> 0 us
  local copies, waits for them, and re-layouts: 160 us -> 10.6 us
  blocking collectives: 38.1 us -> 147 us
  Pallas kernels: 0 us -> 57.1 us
  other arithmetic: 31.3 us -> 8 us
  between operations: 14.7 us -> 2.75 us
    all_to_all x2 -> x9, waiting for transfers between devices: 348 us -> 51.3 us  [swap(): return lax.all_to_all(tensor, axis, split_axis=0, concat_axis=0, tiled=True)]
    dot_general x24 -> x0, matrix products: 208 us -> none  [the longest x2 69.8 us: attend(): jnp.einsum('nhqk,nqhd->nkhd', grad_scores, query_heads, preferred_element...]
    psum x1 -> x0, waiting for transfers between devices: 92.7 us -> none  [on_device(): lax.psum((sum_query, sum_key, sum_value, sum_out, sum_gain), ('sample', '...]
    all_to_all x0 -> x3, blocking collectives: none -> 80 us  [swap(): return lax.all_to_all(tensor, axis, split_axis=0, concat_axis=0, tiled=True)]
    all_gather x0 -> x1, blocking collectives: none -> 67.2 us  [by_sample(): lax.all_gather(sum_gain.reshape(width), ('sample', 'turb'))]
    pallas_call x0 -> x4, Pallas kernels: none -> 57.1 us  [the longest x2 28 us: backward(): pl.pallas_call(lambda *refs: backward_kernel(block_rows, head_dim, *refs)...]
    dynamic_update_slice x10 -> x0, local copies, waits for them, and re-layouts: 44.8 us -> none  [on_device(): lax.map(attend, (grouped(queries.reshape(sample_count, block_rows, model_...]
    psum x1 -> x0, blocking collectives: 38.1 us -> none  [on_device(): lax.psum((sum_query, sum_key, sum_value, sum_out, sum_gain), ('sample', '...]
  transfers between devices with their start and end apart: 3 -> 9, of which waited for: 3 -> 7; matrix products, arithmetic and copies ran while one was open for 3% -> 3% of each run, Pallas kernels for 0% -> 18%
where the time goes in v2:
time: 313 us; the launch traced here: 311 us
  blocking collectives  147 us (47%)
  Pallas kernels  57.1 us (18%)
  waiting for transfers between devices  51.3 us (16%)
  starting transfers between devices  34.4 us (11%)
  local copies, waits for them, and re-layouts  10.6 us (3%)
  other arithmetic  8 us (3%)
    all_to_all x3, blocking collectives, swap(): return lax.all_to_all(tensor, axis, split_axis=0, concat_axis=0, tiled=True)  80 us
    all_gather x1, blocking collectives, by_sample(): lax.all_gather(sum_gain.reshape(width), ('sample', 'turb'))  67.2 us
    all_to_all x9, waiting for transfers between devices, swap(): return lax.all_to_all(tensor, axis, split_axis=0, concat_axis=0, tiled=True)  51.3 us
    all_to_all x9, starting transfers between devices, swap(): return lax.all_to_all(tensor, axis, split_axis=0, concat_axis=0, tiled=True)  34.4 us
    pallas_call x2, Pallas kernels, backward(): pl.pallas_call(lambda *refs: backward_kernel(block_rows, head_dim, *refs)...  28 us
    pallas_call x1, Pallas kernels, forward(): pl.pallas_call(lambda *refs: forward_kernel(block_rows, head_dim, *refs),...  22.4 us
    pallas_call x1, Pallas kernels, finish(): pl.pallas_call(lambda *refs: finish_kernel(width // quad, *refs), grid=(r...  6.74 us
  transfers between devices with their start and end apart: 9, of which 7 were waited for; matrix products, arithmetic and copies ran while one was open for 3% of the time, Pallas kernels for 18%

profile of v2, /device:TPU:0, one launch (start us, length us, event | category | flops | bytes accessed | tf_op | source)
XLA Modules:
  0.0 311.4 jit_solution(5092733759572046149)
XLA Ops:
  0.6 0.0 copy-start
  0.6 0.0 copy-start.11
  0.7 0.0 copy-start.5
  0.7 33.3 %all_to_all.60 = bf16[8,128,512]{2,1,0:T(8,128)(2,1)} all-to-all(bf16[8,128,512]{2,1,0:T(8,128)(2,1)} %param.9), channel_id=1, replica_groups=mesh['sample'=4,'turb'=8] {'turb'}, dimensions={0} | all-to-all | bytes 2097152 | tf_op jit(solution)/shard_map/all_to_all | solution.py:545
  33.9 3.7 %all-to-all-start.2 = ((bf16[8,128,512]{2,1,0:T(8,128)(2,1)}), bf16[8,128,512]{2,1,0:T(8,128)(2,1)S(1)}, u32[]{:S(2)}, u32[]{:S(2)}) async-start(bf16[8,128,512]{2,1,0:T(8,128)(2,1)} %param.10), calls=%async_computation.2 | async-start | bytes 2097152 | tf_op jit(solution)/shard_map/all_to_all | solution.py:545
  37.7 0.0 copy-done.11
  37.7 0.6 dynamic_slice.8
  40.2 0.0 copy-done
  40.2 0.1 copy.25
  40.3 0.6 reshape.62.refs_0_
  40.9 0.0 copy-done.5
  40.9 1.0 copy.26
  41.9 0.0 copy-done.6
  41.9 1.0 copy.27
  42.9 22.4 %forward.1 = (bf16[512,1024]{1,0:T(8,128)(2,1)}, bf16[1024,512]{1,0:T(8,128)(2,1)}, bf16[1024,512]{1,0:T(8,128)(2,1)}, bf16[1024,512]{1,0:T(8,128)(2,1)}, bf16[5...) custom-call(s32[24]{0:T(128)} %reshape.62.refs_0_, ...), custom_call_target="tpu_custom_call" | custom-call | flops 5368709120 | bytes 10485760 | tf_op jit(solution)/shard_map/forward/pallas_call | solution.py:357
  65.3 0.0 all-to-all-done.2
  65.3 0.0 copy-start.1
  65.3 5.9 %all-to-all-start.1 = ((bf16[8,128,512]{2,1,0:T(8,128)(2,1)}), bf16[8,128,512]{2,1,0:T(8,128)(2,1)S(1)}, u32[]{:S(2)}, u32[]{:S(2)}) async-start(bf16[8,128,512]{2,1,0:T(8,128)(2,1)} %bitcast.39), calls=%async_computation.1 | async-start | bytes 2097152 | tf_op jit(solution)/shard_map/all_to_all | solution.py:545
  71.2 0.0 copy-done.1
  71.2 14.0 %backward.2 = (bf16[1024,256]{1,0:T(8,128)(2,1)}, bf16[1024,256]{1,0:T(8,128)(2,1)}, bf16[1024,256]{1,0:T(8,128)(2,1)}, bf16[2048,256]{1,0:T(8,128)(2,1)}) custom-call(s32[24]{0:T(128)} %reshape.62.refs_0_, bf16[1024,512]{1,0:T(8,128)(2,1)} %bitcast.33, bf16[512,512]{1,0:T(8,128)(2,1)} %refs_2_.3, bf16[512,1024]{1,0:T(8,128)(2,1)} %get-tuple-element.31.refs_3_, ...), custom_call_target="tpu_custom_call" | custom-call | flops 4026531840 | bytes 7340032 | tf_op jit(solution)/shard_map/backward/pallas_call | solution.py:464
  85.2 10.6 %all-to-all-done.1 = bf16[8,128,512]{2,1,0:T(8,128)(2,1)S(1)} async-done(((bf16[8,128,512]{2,1,0:T(8,128)(2,1)}), bf16[8,128,512]{2,1,0:T(8,128)(2,1)S(1)}, u32[]{:S(2)}, u32[]{:S(2)}) %all-to-all-start.1) | async-done | bytes 1048608 | tf_op jit(solution)/shard_map/all_to_all | solution.py:545
  95.8 3.7 %all-to-all-start.4 = ((bf16[4,512,256]{2,1,0:T(8,128)(2,1)}), bf16[4,512,256]{2,1,0:T(8,128)(2,1)S(1)}, u32[]{:S(2)}, u32[]{:S(2)}) async-start(bf16[4,512,256]{2,1,0:T(8,128)(2,1)} %bitcast.38), calls=%async_computation.4 | async-start | bytes 2097152 | tf_op jit(solution)/shard_map/all_to_all | solution.py:545
  99.5 14.0 %backward.3 = (bf16[1024,256]{1,0:T(8,128)(2,1)}, bf16[1024,256]{1,0:T(8,128)(2,1)}, bf16[1024,256]{1,0:T(8,128)(2,1)}, bf16[2048,256]{1,0:T(8,128)(2,1)}) custom-call(s32[24]{0:T(128)} %reshape.62.refs_0_, bf16[1024,512]{1,0:T(8,128)(2,1)} %bitcast.34, bf16[512,512]{1,0:T(8,128)(2,1)} %refs_2_.3, bf16[512,1024]{1,0:T(8,128)(2,1)} %get-tuple-element.31.refs_3_, ...), custom_call_target="tpu_custom_call" | custom-call | flops 4026531840 | bytes 7340032 | tf_op jit(solution)/shard_map/backward/pallas_call | solution.py:464
  113.5 0.0 copy-done.2
  113.5 0.2 all-to-all-done.4
  113.8 3.5 %all-to-all-start.8 = ((bf16[4,512,256]{2,1,0:T(8,128)(2,1)}), bf16[4,512,256]{2,1,0:T(8,128)(2,1)S(1)}, u32[]{:S(2)}, u32[]{:S(2)}) async-start(bf16[4,512,256]{2,1,0:T(8,128)(2,1)} %bitcast.40), calls=%async_computation.8 | async-start | bytes 2097152 | tf_op jit(solution)/shard_map/all_to_all | solution.py:545
  117.3 0.9 reduce_sum.57
  118.2 13.5 %all-to-all-done.8 = bf16[4,512,256]{2,1,0:T(8,128)(2,1)S(1)} async-done(((bf16[4,512,256]{2,1,0:T(8,128)(2,1)}), bf16[4,512,256]{2,1,0:T(8,128)(2,1)S(1)}, u32[]{:S(2)}, u32[]{:S(2)}) %all-to-all-start.8) | async-done | bytes 1048608 | tf_op jit(solution)/shard_map/all_to_all | solution.py:545
  131.7 3.4 %all-to-all-start.5 = ((bf16[8,64,256]{2,1,0:T(8,128)(2,1)}), bf16[8,64,256]{2,1,0:T(8,128)(2,1)S(1)}, u32[]{:S(2)}, u32[]{:S(2)}) async-start(bf16[8,64,256]{2,1,0:T(8,128)(2,1)} %bitcast.9), calls=%async_computation.5 | async-start | bytes 524288 | tf_op jit(solution)/shard_map/all_to_all | solution.py:545
  135.1 0.9 reduce_sum.59
  136.0 8.0 %all-to-all-done.5 = bf16[8,64,256]{2,1,0:T(8,128)(2,1)S(1)} async-done(((bf16[8,64,256]{2,1,0:T(8,128)(2,1)}), bf16[8,64,256]{2,1,0:T(8,128)(2,1)S(1)}, u32[]{:S(2)}, u32[]{:S(2)}) %all-to-all-start.5) | async-done | bytes 262176 | tf_op jit(solution)/shard_map/all_to_all | solution.py:545
  144.1 3.6 %all-to-all-start.9 = ((bf16[8,64,256]{2,1,0:T(8,128)(2,1)}), bf16[8,64,256]{2,1,0:T(8,128)(2,1)S(1)}, u32[]{:S(2)}, u32[]{:S(2)}) async-start(bf16[8,64,256]{2,1,0:T(8,128)(2,1)} %bitcast.13), calls=%async_computation.9 | async-start | bytes 524288 | tf_op jit(solution)/shard_map/all_to_all | solution.py:545
  147.7 8.6 %all-to-all-done.9 = bf16[8,64,256]{2,1,0:T(8,128)(2,1)S(1)} async-done(((bf16[8,64,256]{2,1,0:T(8,128)(2,1)}), bf16[8,64,256]{2,1,0:T(8,128)(2,1)S(1)}, u32[]{:S(2)}, u32[]{:S(2)}) %all-to-all-start.9) | async-done | bytes 262176 | tf_op jit(solution)/shard_map/all_to_all | solution.py:545
  156.2 0.7 broadcast_in_dim.12
  157.0 3.6 %all-to-all-start.6 = ((bf16[8,64,256]{2,1,0:T(8,128)(2,1)}), bf16[8,64,256]{2,1,0:T(8,128)(2,1)S(1)}, u32[]{:S(2)}, u32[]{:S(2)}) async-start(bf16[8,64,256]{2,1,0:T(8,128)(2,1)} %broadcast_in_dim.12), calls=%async_computation.6 | async-start | bytes 524288 | tf_op jit(solution)/shard_map/all_to_all | solution.py:545
  160.6 8.5 %all-to-all-done.6 = bf16[8,64,256]{2,1,0:T(8,128)(2,1)S(1)} async-done(((bf16[8,64,256]{2,1,0:T(8,128)(2,1)}), bf16[8,64,256]{2,1,0:T(8,128)(2,1)S(1)}, u32[]{:S(2)}, u32[]{:S(2)}) %all-to-all-start.6) | async-done | bytes 262176 | tf_op jit(solution)/shard_map/all_to_all | solution.py:545
  169.1 0.7 broadcast_in_dim.14
  169.8 3.5 %all-to-all-start.10 = ((bf16[8,64,256]{2,1,0:T(8,128)(2,1)}), bf16[8,64,256]{2,1,0:T(8,128)(2,1)S(1)}, u32[]{:S(2)}, u32[]{:S(2)}) async-start(bf16[8,64,256]{2,1,0:T(8,128)(2,1)} %broadcast_in_dim.14), calls=%async_computation.10 | async-start | bytes 524288 | tf_op jit(solution)/shard_map/all_to_all | solution.py:545
  173.3 6.7 %finish.1 = (bf16[1024,512]{1,0:T(8,128)(2,1)}, f32[1,512]{1,0:T(1,128)}) custom-call(bf16[1024,512]{1,0:T(8,128)(2,1)} %bitcast.32, bf16[1024,512]{1,0:T(8,128)(2,1)} %bitcast.35, f32[1,512]{1,0:T(1,128)} %bitcast.45, bf16[512,512]{1,0:T(8,128)(2,1)} %refs_3_.3, bf16[512,512]{1,0:T(8,128)(2,1)} %refs_4_.3, bf16[512,512]{1,0:T(8,128)(2,1)} %refs_5_.3, ...), custom_call_target="tpu_custom_call" | custom-call | flops 1610612736 | bytes 8388608 | tf_op jit(solution)/shard_map/finish/pallas_call | solution.py:522
  180.1 1.8 all-to-all-done.10
  181.9 29.1 %all_to_all.61 = bf16[8,128,512]{2,1,0:T(8,128)(2,1)} all-to-all(bf16[8,128,512]{2,1,0:T(8,128)(2,1)} %bitcast.41), channel_id=1, replica_groups=mesh['sample'=4,'turb'=8] {'turb'}, dimensions={0} | all-to-all | bytes 2097152 | tf_op jit(solution)/shard_map/all_to_all | solution.py:545
  211.0 0.1 broadcast_in_dim.15
  211.0 17.6 %all_to_all.62 = bf16[4,512,256]{2,1,0:T(8,128)(2,1)} all-to-all(bf16[4,512,256]{2,1,0:T(8,128)(2,1)S(1)} %broadcast_in_dim.15), channel_id=1, replica_groups=mesh['sample'=4,'turb'=8] {'sample'}, dimensions={0} | all-to-all | bytes 2097152 | tf_op jit(solution)/shard_map/all_to_all | solution.py:545
  228.6 1.0 broadcast_in_dim.13
  229.7 3.5 %all-to-all-start.7 = ((bf16[4,512,256]{2,1,0:T(8,128)(2,1)}), bf16[4,512,256]{2,1,0:T(8,128)(2,1)S(1)}, u32[]{:S(2)}, u32[]{:S(2)}) async-start(bf16[4,512,256]{2,1,0:T(8,128)(2,1)} %broadcast_in_dim.13), calls=%async_computation.7 | async-start | bytes 2097152 | tf_op jit(solution)/shard_map/all_to_all | solution.py:545
  233.2 0.0 copy-done.10
  233.2 67.2 %all-gather = f32[32,1,512]{2,1,0:T(1,128)S(1)} all-gather(f32[1,1,512]{2,1,0:T(1,128)S(1)} %bitcast.46), channel_id=1, replica_groups=mesh['sample'=4,'turb'=8] {'sample','turb'}, dimensions={0}, use_global_device_ids=true | all-gather | bytes 67584 | tf_op jit(solution)/shard_map/all_gather | solution.py:595
  300.5 0.6 reduce_sum.61
  301.1 1.4 convert_element_type.21
  302.5 1.2 slice_bitcast_fusion
  303.7 0.0 all-to-all-done.7
  303.7 0.2 convert_element_type.20
  303.9 0.0 copy-start.7
  303.9 0.1 slice_bitcast_fusion.1
  304.0 0.1 fusion
  304.1 0.8 copy-done.7
  304.9 1.1 pad_maximum_fusion.2
  306.0 1.1 maximum_maximum_fusion
  307.2 0.0 copy-done.8
  307.2 0.0 copy-done.9
  307.2 1.6 pad_maximum_fusion
  308.8 1.0 copy.30
  309.8 0.6 copy-done.4
  310.4 1.0 copy.31
  (11 shorter events, 0.1 us)
Async XLA Ops:
  0.6 39.6 %copy-start = (s32[8,8,3]{1,0,2:T(8,128)S(1)}, s32[8,8,3]{1,0,2:T(8,128)}, u32[]{:S(2)}) copy-start(s32[8,8,3]{1,0,2:T(8,128)} %param.16) | copy-start | bytes 2308
  0.6 37.0 %copy-start.11 = (s32[8]{0:T(128)S(1)}, s32[8]{0:T(128)}, u32[]{:S(2)}) copy-start(s32[8]{0:T(128)} %param.17) | copy-start | bytes 100
  0.7 40.2 %copy-start.5 = (bf16[512,512]{1,0:T(8,128)(2,1)S(1)}, bf16[512,512]{1,0:T(8,128)(2,1)}, u32[]{:S(2)}) copy-start(bf16[512,512]{1,0:T(8,128)(2,1)} %refs_4_.3) | copy-start | bytes 1572868
  33.9 8.0 %copy-start.6 = (bf16[512,512]{1,0:T(8,128)(2,1)S(1)}, bf16[512,512]{1,0:T(8,128)(2,1)}, u32[]{:S(2)}) copy-start(bf16[512,512]{1,0:T(8,128)(2,1)} %refs_5_.3) | copy-start | bytes 1572868
  33.9 31.4 %all-to-all-start.2 = ((bf16[8,128,512]{2,1,0:T(8,128)(2,1)}), bf16[8,128,512]{2,1,0:T(8,128)(2,1)S(1)}, u32[]{:S(2)}, u32[]{:S(2)}) async-start(bf16[8,128,512]{2,1,0:T(8,128)(2,1)} %param.10), calls=%async_computation.2 | async-start | bytes 2097152 | tf_op jit(solution)/shard_map/all_to_all | solution.py:545
  65.3 5.9 %copy-start.1 = (bf16[8,128,512]{2,1,0:T(8,128)(2,1)}, bf16[8,128,512]{2,1,0:T(8,128)(2,1)S(1)}, u32[]{:S(2)}) copy-start(bf16[8,128,512]{2,1,0:T(8,128)(2,1)S(1)} %all-to-all-done.2) | copy-start | bytes 3145732
  65.3 30.5 %all-to-all-start.1 = ((bf16[8,128,512]{2,1,0:T(8,128)(2,1)}), bf16[8,128,512]{2,1,0:T(8,128)(2,1)S(1)}, u32[]{:S(2)}, u32[]{:S(2)}) async-start(bf16[8,128,512]{2,1,0:T(8,128)(2,1)} %bitcast.39), calls=%async_computation.1 | async-start | bytes 2097152 | tf_op jit(solution)/shard_map/all_to_all | solution.py:545
  95.8 17.7 %copy-start.2 = (bf16[8,128,512]{2,1,0:T(8,128)(2,1)}, bf16[8,128,512]{2,1,0:T(8,128)(2,1)S(1)}, u32[]{:S(2)}) copy-start(bf16[8,128,512]{2,1,0:T(8,128)(2,1)S(1)} %all-to-all-done.1) | copy-start | bytes 3145732
  95.8 18.0 %all-to-all-start.4 = ((bf16[4,512,256]{2,1,0:T(8,128)(2,1)}), bf16[4,512,256]{2,1,0:T(8,128)(2,1)S(1)}, u32[]{:S(2)}, u32[]{:S(2)}) async-start(bf16[4,512,256]{2,1,0:T(8,128)(2,1)} %bitcast.38), calls=%async_computation.4 | async-start | bytes 2097152 | tf_op jit(solution)/shard_map/all_to_all | solution.py:545
  113.8 18.0 %all-to-all-start.8 = ((bf16[4,512,256]{2,1,0:T(8,128)(2,1)}), bf16[4,512,256]{2,1,0:T(8,128)(2,1)S(1)}, u32[]{:S(2)}, u32[]{:S(2)}) async-start(bf16[4,512,256]{2,1,0:T(8,128)(2,1)} %bitcast.40), calls=%async_computation.8 | async-start | bytes 2097152 | tf_op jit(solution)/shard_map/all_to_all | solution.py:545
  131.7 12.4 %all-to-all-start.5 = ((bf16[8,64,256]{2,1,0:T(8,128)(2,1)}), bf16[8,64,256]{2,1,0:T(8,128)(2,1)S(1)}, u32[]{:S(2)}, u32[]{:S(2)}) async-start(bf16[8,64,256]{2,1,0:T(8,128)(2,1)} %bitcast.9), calls=%async_computation.5 | async-start | bytes 524288 | tf_op jit(solution)/shard_map/all_to_all | solution.py:545
  144.1 12.2 %all-to-all-start.9 = ((bf16[8,64,256]{2,1,0:T(8,128)(2,1)}), bf16[8,64,256]{2,1,0:T(8,128)(2,1)S(1)}, u32[]{:S(2)}, u32[]{:S(2)}) async-start(bf16[8,64,256]{2,1,0:T(8,128)(2,1)} %bitcast.13), calls=%async_computation.9 | async-start | bytes 524288 | tf_op jit(solution)/shard_map/all_to_all | solution.py:545
  157.0 12.1 %all-to-all-start.6 = ((bf16[8,64,256]{2,1,0:T(8,128)(2,1)}), bf16[8,64,256]{2,1,0:T(8,128)(2,1)S(1)}, u32[]{:S(2)}, u32[]{:S(2)}) async-start(bf16[8,64,256]{2,1,0:T(8,128)(2,1)} %broadcast_in_dim.12), calls=%async_computation.6 | async-start | bytes 524288 | tf_op jit(solution)/shard_map/all_to_all | solution.py:545
  169.8 12.1 %all-to-all-start.10 = ((bf16[8,64,256]{2,1,0:T(8,128)(2,1)}), bf16[8,64,256]{2,1,0:T(8,128)(2,1)S(1)}, u32[]{:S(2)}, u32[]{:S(2)}) async-start(bf16[8,64,256]{2,1,0:T(8,128)(2,1)} %broadcast_in_dim.14), calls=%async_computation.10 | async-start | bytes 524288 | tf_op jit(solution)/shard_map/all_to_all | solution.py:545
  228.6 4.6 %copy-start.10 = (f32[1,512]{1,0:T(1,128)S(1)}, f32[1,512]{1,0:T(1,128)}, u32[]{:S(2)}) copy-start(f32[1,512]{1,0:T(1,128)} %get-tuple-element.48) | copy-start | bytes 6148
  229.7 74.0 %all-to-all-start.7 = ((bf16[4,512,256]{2,1,0:T(8,128)(2,1)}), bf16[4,512,256]{2,1,0:T(8,128)(2,1)S(1)}, u32[]{:S(2)}, u32[]{:S(2)}) async-start(bf16[4,512,256]{2,1,0:T(8,128)(2,1)} %broadcast_in_dim.13), calls=%async_computation.7 | async-start | bytes 2097152 | tf_op jit(solution)/shard_map/all_to_all | solution.py:545
  303.9 1.0 copy-start.7
  304.9 2.3 copy-start.8
  304.9 2.3 copy-start.9
  307.2 1.6 copy-start.3
  308.8 1.6 copy-start.4

commit v3 on v2

--- a/solution.py
+++ b/solution.py
@@ -386,10 +386,11 @@
       key_weight.T, value_weight.T, out_weight)
 
 
-def backward_kernel(block_rows, head_dim, lists_ref, cot_ref, wo_ref, normed_t_ref, q_ref, k_ref,
-                    v_ref, kt_ref, att_ref, top_ref, inverse_ref, gq_ref, gk_ref, gv_ref, sums_ref,
-                    ga_ref, gk_acc, gv_acc):
+def backward_kernel(block_rows, head_dim, which, lists_ref, cot_ref, wo_ref, normed_t_ref, q_ref,
+                    k_ref, v_ref, kt_ref, att_ref, top_ref, inverse_ref, gq_ref, gk_ref, gv_ref,
+                    keep_ref, send_ref, ga_ref, gk_acc, gv_acc):
     row_count, width = cot_ref.shape
+    block_count = row_count // block_rows
     pair = PAIR * head_dim
     quad = QUAD * head_dim
     scale = head_dim ** (-0.5)
@@ -437,23 +438,38 @@
                         term = term.astype(jnp.bfloat16).astype(jnp.float32)
                     acc[rows, lane] += term
 
-    for_each_block(lists_ref, row_count // block_rows, block_rows, work)
+    for_each_block(lists_ref, block_count, block_rows, work)
     gk_ref[...] = gk_acc[...].astype(jnp.bfloat16)
     gv_ref[...] = gv_acc[...].astype(jnp.bfloat16)
-    for i, ref in enumerate((gq_ref, gk_ref, gv_ref)):
-        sums_ref[i * width : (i + 1) * width, :] = contract(
-            normed_t_ref[...], ref[...], 1, 0
-        ).astype(jnp.bfloat16)
-    for i in range(width // quad):
-        start = 3 * width + i * quad
-        sums_ref[start : start + quad, :] = contract(
-            att_ref[...], cot_ref[:, i * quad : (i + 1) * quad], 1, 0
-        ).astype(jnp.bfloat16)
+    products = [(normed_t_ref, ref, slice(None)) for ref in (gq_ref, gk_ref, gv_ref)]
+    products.append((att_ref, cot_ref, slice(which * quad, (which + 1) * quad)))
+    share = keep_ref.shape[1]
+    turbs = keep_ref.shape[0] // 2
+    offset = block_count * UPSTREAM
+    own_sample, own_turb = lists_ref[offset], lists_ref[offset + 1]
+    piece = 0
+    for left, right, lanes in products:
+        terms = contract(left[...], right[:, lanes], 1, 0)
+        for start in range(0, width, share):
+            apart = (piece // turbs) ^ own_sample
+            place = (apart // 2) * turbs + ((piece % turbs) ^ own_turb)
+            term = terms[start : start + share]
+
+            @pl.when(apart % 2 == 0)
+            def _():
+                keep_ref[place] = term
+
+            @pl.when(apart % 2 == 1)
+            def _():
+                send_ref[place] = term
+
+            piece += 1
 
 
 def backward(lists, cotangent, out_weight, normed_t, queries, keys, values, keys_t, attended_t,
-             tops, inverses, block_rows, which):
+             tops, inverses, block_rows, which, sample_axis):
     row_count, width = cotangent.shape
+    block_count = row_count // block_rows
     head_dim = width // HEADS
     quad = QUAD * head_dim
     fixed = lambda *shape: pl.BlockSpec(shape, lambda i, lists: (0,) * len(shape))
@@ -461,23 +477,25 @@
     down = lambda size: pl.BlockSpec((quad, size), lambda i, lists: (which, 0))
     stat = pl.BlockSpec((1,) + tops.shape[1:], lambda i, lists: (which, 0, 0))
     part = jax.ShapeDtypeStruct((row_count, quad), jnp.bfloat16)
+    share = 4 * width // (sample_axis * block_count)
+    pieces = (sample_axis * block_count // 2, share, quad)
     return pl.pallas_call(
-        lambda *refs: backward_kernel(block_rows, head_dim, *refs),
+        lambda *refs: backward_kernel(block_rows, head_dim, which, *refs),
         grid_spec=pltpu.PrefetchScalarGridSpec(
             num_scalar_prefetch=1,
             grid=(1,),
             in_specs=[fixed(row_count, width), down(width), fixed(width, row_count)]
             + [across] * 3
-            + [down(row_count)] * 2
+            + [down(row_count), fixed(width, row_count)]
             + [stat] * 2,
-            out_specs=[fixed(row_count, quad)] * 3 + [fixed(4 * width, quad)],
+            out_specs=[fixed(row_count, quad)] * 3 + [fixed(*pieces)] * 2,
             scratch_shapes=[
                 pltpu.VMEM((row_count, quad), jnp.bfloat16),
                 pltpu.VMEM((row_count, quad), jnp.float32),
                 pltpu.VMEM((row_count, quad), jnp.float32),
             ],
         ),
-        out_shape=[part] * 3 + [jax.ShapeDtypeStruct((4 * width, quad), jnp.bfloat16)],
+        out_shape=[part] * 3 + [jax.ShapeDtypeStruct(pieces, jnp.float32)] * 2,
         compiler_params=pltpu.CompilerParams(vmem_limit_bytes=VMEM_LIMIT),
         cost_estimate=pl.CostEstimate(
             flops=10 * row_count * width * quad + 80 * row_count * block_rows * quad,
@@ -545,16 +563,60 @@
     return lax.all_to_all(tensor, axis, split_axis=0, concat_axis=0, tiled=True)
 
 
-def reduce_sums(sums):
-    row_count, width = sums.shape
-    for axis in ("sample", "turb"):
-        size = lax.axis_size(axis)
-        sums = swap(sums.reshape(size, -1, width), axis)
-        sums = jnp.sum(sums.astype(jnp.float32), axis=0).astype(jnp.bfloat16)
-    for axis in ("turb", "sample"):
-        size = lax.axis_size(axis)
-        sums = swap(jnp.broadcast_to(sums, (size,) + sums.shape), axis).reshape(-1, width)
-    return sums.astype(jnp.float32)
+def across(tensor, axis, distance):
+    size = lax.axis_size(axis)
+    return lax.ppermute(tensor, axis, [(i, i ^ distance) for i in range(size)])
+
+
+def reduce_sums(keep, send):
+    turbs = lax.axis_size("turb")
+    sums = keep + across(send, "sample", 1)
+    arrived = across(sums[turbs:].astype(jnp.bfloat16), "sample", 2)
+    sums = sums[:turbs] + arrived.astype(jnp.float32)
+    total = sums[0]
+    for distance in range(1, turbs):
+        total = total + across(sums[distance].astype(jnp.bfloat16), "turb", distance).astype(
+            jnp.float32
+        )
+    own = total.astype(jnp.bfloat16)
+    row = jnp.stack([own] + [across(own, "turb", distance) for distance in range(1, turbs)])
+    both = [row, across(row, "sample", 2)]
+    return both + [across(part, "sample", 1) for part in both]
+
+
+def place_kernel(place_ref, *refs):
+    (*pieces, query_ref, key_ref, value_ref, out_ref, all_ref) = refs
+    own_sample, own_turb = place_ref[0], place_ref[1]
+    groups = len(pieces) // 4
+    for i, ref in enumerate(pieces):
+        which, part = divmod(i, 4)
+        turbs, share, quad = ref.shape
+        sample = own_sample ^ ((part % 2) * 2 + part // 2)
+        for j in range(turbs):
+            start = pl.multiple_of((sample * turbs + (own_turb ^ j)) * share, share)
+            all_ref[pl.ds(start, share), which * quad : (which + 1) * quad] = ref[j].astype(
+                jnp.float32
+            )
+    width = query_ref.shape[0]
+    for i, ref in enumerate((query_ref, key_ref, value_ref, out_ref)):
+        ref[...] = all_ref[i * width : (i + 1) * width, :]
+
+
+def place_sums(place, pieces, width):
+    whole = jax.ShapeDtypeStruct((width, width), jnp.float32)
+    return pl.pallas_call(
+        place_kernel,
+        in_specs=[pl.BlockSpec(memory_space=pltpu.SMEM)]
+        + [pl.BlockSpec(memory_space=pltpu.VMEM)] * len(pieces),
+        out_specs=[pl.BlockSpec(memory_space=pltpu.VMEM)] * 4,
+        out_shape=[whole] * 4,
+        scratch_shapes=[pltpu.VMEM((4 * width, width), jnp.float32)],
+        compiler_params=pltpu.CompilerParams(vmem_limit_bytes=VMEM_LIMIT),
+        cost_estimate=pl.CostEstimate(
+            flops=0, bytes_accessed=24 * width * width, transcendentals=0
+        ),
+        name="place",
+    )(place, *pieces)
 
 
 def by_sample(
@@ -569,11 +631,13 @@
     sectors,
 ):
     sample_count, block_rows, width = inflow.shape
+    sample_axis = lax.axis_size("sample")
     row_count = lax.axis_size("turb") * block_rows
-    quads = HEADS // QUAD
-    quad = width // quads
-    sector = lax.dynamic_index_in_dim(sectors, lax.axis_index("turb"), keepdims=False)
+    own_turb = lax.axis_index("turb")
+    place = jnp.stack([lax.axis_index("sample"), own_turb]).astype(jnp.int32)
+    sector = lax.dynamic_index_in_dim(sectors, own_turb, keepdims=False)
     lists = lax.dynamic_index_in_dim(adjacency, sector, keepdims=False).reshape(-1)
+    lists = jnp.concatenate([lists, place])
 
     rows = swap(inflow, "turb")
     rows, cotangent = lax.optimization_barrier((rows, cotangent))
@@ -583,34 +647,24 @@
         lists, rows, norm_gain, query_weight, key_weight, value_weight, out_weight, block_rows
     )
     layer_output = swap(layer_rows.reshape(inflow.shape), "turb")
-    grads, sums = [], []
-    for which in range(quads):
-        *part, terms = backward(lists, grad_rows, out_weight, *saved, block_rows, which)
+    grads, pieces = [], []
+    for which in range(HEADS // QUAD):
+        *part, keep, send = backward(
+            lists, grad_rows, out_weight, *saved, block_rows, which, sample_axis
+        )
         grads += part
-        sums.append(reduce_sums(terms))
+        pieces += reduce_sums(keep, send)
     grad_rows, sum_gain = finish(
         rows, grad_rows, norm_gain, query_weight, key_weight, value_weight, grads
     )
     grad_inflow = swap(grad_rows.reshape(inflow.shape), "turb")
-    sum_gain = jnp.sum(lax.all_gather(sum_gain.reshape(width), ("sample", "turb")), axis=0)
-    projections = [
-        jnp.concatenate([part[i * width : (i + 1) * width] for part in sums], axis=1)
-        for i in range(3)
-    ]
-    sum_out = jnp.concatenate(
-        [
-            jnp.concatenate(
-                [
-                    part[3 * width + i * quad : 3 * width + (i + 1) * quad]
-                    for i in range(quads)
-                ],
-                axis=1,
-            )
-            for part in sums
-        ],
-        axis=0,
-    )
-    return (layer_output, grad_inflow, *projections, sum_out, sum_gain)
+    for axis in ("sample", "turb"):
+        distance = 1
+        while distance < lax.axis_size(axis):
+            sum_gain = sum_gain + across(sum_gain, axis, distance)
+            distance *= 2
+    sums = place_sums(place, pieces, width)
+    return (layer_output, grad_inflow, *sums, sum_gain.reshape(width))
 
 
 def solution(mesh):
@@ -628,7 +682,7 @@
 
     def plan(*args):
         sample_count = args[0].shape[0]
-        if sample_count == mesh.shape["turb"]:
+        if sample_count == mesh.shape["turb"] and mesh.shape["sample"] == 4:
             return by_sample(*args)
         return on_device(*args)
 

time: 313 us -> 240 us (0.77)
  blocking collectives: 147 us -> 33.1 us
  starting transfers between devices: 34.4 us -> 85.7 us
  waiting for transfers between devices: 51.3 us -> 40.6 us
  Pallas kernels: 57.1 us -> 64.1 us
  other arithmetic: 8 us -> 4.54 us
  local copies, waits for them, and re-layouts: 10.6 us -> 7.18 us
    ppermute x0 -> x43, starting transfers between devices: none -> 71.6 us  [across(): return lax.ppermute(tensor, axis, [(i, i ^ distance) for i in range(size)])]
    all_gather x1 -> x0, blocking collectives: 67.2 us -> none  [by_sample(): lax.all_gather(sum_gain.reshape(width), ('sample', 'turb'))]
    all_to_all x9 -> x3, waiting for transfers between devices: 51.3 us -> 0.01 us  [swap(): return lax.all_to_all(tensor, axis, split_axis=0, concat_axis=0, tiled=True)]
    all_to_all x3 -> x1, blocking collectives: 80 us -> 33.1 us  [swap(): return lax.all_to_all(tensor, axis, split_axis=0, concat_axis=0, tiled=True)]
    ppermute x0 -> x43, waiting for transfers between devices: none -> 40.6 us  [across(): return lax.ppermute(tensor, axis, [(i, i ^ distance) for i in range(size)])]
    all_to_all x9 -> x3, starting transfers between devices: 34.4 us -> 14.1 us  [swap(): return lax.all_to_all(tensor, axis, split_axis=0, concat_axis=0, tiled=True)]
    pallas_call x2 -> x3, Pallas kernels: 28 us -> 35.9 us  [the longest x2 32 us: backward(): pl.pallas_call(lambda *refs: backward_kernel(block_rows, head_dim, which,...]
    concatenate x3 -> x1, other arithmetic: 3.89 us -> 0.59 us  [by_sample(): lists = jnp.concatenate([lists, place])]
  transfers between devices with their start and end apart: 9 -> 46, of which waited for: 7 -> 11; matrix products, arithmetic and copies ran while one was open for 3% -> 3% of each run, Pallas kernels for 18% -> 19%
where the time goes in v3:
time: 240 us; the launch traced here: 238 us
  starting transfers between devices  85.7 us (36%)
  Pallas kernels  64.1 us (27%)
  waiting for transfers between devices  40.6 us (17%)
  blocking collectives  33.1 us (14%)
  local copies, waits for them, and re-layouts  7.18 us (3%)
  other arithmetic  4.54 us (2%)
  between operations  2.92 us (1%)
    ppermute x43, starting transfers between devices, across(): return lax.ppermute(tensor, axis, [(i, i ^ distance) for i in range(size)])  71.6 us
    ppermute x43, waiting for transfers between devices, across(): return lax.ppermute(tensor, axis, [(i, i ^ distance) for i in range(size)])  40.6 us
    all_to_all x1, blocking collectives, swap(): return lax.all_to_all(tensor, axis, split_axis=0, concat_axis=0, tiled=True)  33.1 us
    pallas_call x2, Pallas kernels, backward(): pl.pallas_call(lambda *refs: backward_kernel(block_rows, head_dim, which,...  32 us
    pallas_call x1, Pallas kernels, forward(): pl.pallas_call(lambda *refs: forward_kernel(block_rows, head_dim, *refs),...  21.5 us
    all_to_all x3, starting transfers between devices, swap(): return lax.all_to_all(tensor, axis, split_axis=0, concat_axis=0, tiled=True)  14.1 us
    pallas_call x1, Pallas kernels, finish(): pl.pallas_call(lambda *refs: finish_kernel(width // quad, *refs), grid=(r...  6.74 us
    unnamed x42, local copies, waits for them, and re-layouts  6.33 us
  transfers between devices with their start and end apart: 46, of which 11 were waited for; matrix products, arithmetic and copies ran while one was open for 3% of the time, Pallas kernels for 19%

profile of v3, /device:TPU:0, one launch (start us, length us, event | category | flops | bytes accessed | tf_op | source)
XLA Modules:
  0.0 238.2 jit_solution(13493297841225206380)
XLA Ops:
  0.6 33.1 %all_to_all.20 = bf16[8,128,512]{2,1,0:T(8,128)(2,1)} all-to-all(bf16[8,128,512]{2,1,0:T(8,128)(2,1)} %param.9), channel_id=1, replica_groups=mesh['sample'=4,'turb'=8] {'turb'}, dimensions={0} | all-to-all | bytes 2097152 | tf_op jit(solution)/shard_map/all_to_all | solution.py:563
  33.8 3.7 %all-to-all-start.2 = ((bf16[8,128,512]{2,1,0:T(8,128)(2,1)}), bf16[8,128,512]{2,1,0:T(8,128)(2,1)S(1)}, u32[]{:S(2)}, u32[]{:S(2)}) async-start(bf16[8,128,512]{2,1,0:T(8,128)(2,1)} %param.10), calls=%async_computation.2 | async-start | bytes 2097152 | tf_op jit(solution)/shard_map/all_to_all | solution.py:563
  37.5 0.7 copy-done.12
  38.2 0.6 dynamic_slice.8
  40.9 1.0 copy.20
  41.9 1.0 copy.21
  42.9 0.6 pad_add_fusion.refs_0_
  43.5 21.5 %forward.1 = (bf16[512,1024]{1,0:T(8,128)(2,1)}, bf16[1024,512]{1,0:T(8,128)(2,1)}, bf16[1024,512]{1,0:T(8,128)(2,1)}, bf16[1024,512]{1,0:T(8,128)(2,1)}, bf16[5...) custom-call(s32[26]{0:T(128)} %pad_add_fusion.refs_0_, ...), custom_call_target="tpu_custom_call" | custom-call | flops 5368709120 | bytes 10485760 | tf_op jit(solution)/shard_map/forward/pallas_call | solution.py:357
  65.0 1.0 copy-done.1
  66.0 16.1 %backward.3 = (bf16[1024,256]{1,0:T(8,128)(2,1)}, bf16[1024,256]{1,0:T(8,128)(2,1)}, bf16[1024,256]{1,0:T(8,128)(2,1)}, f32[16,64,256]{2,1,0:T(8,128)}, f32[16,64,256]{2,1,0:T(8,128)}) custom-call(s32[26]{0:T(128)} %pad_add_fusion.refs_0_, bf16[1024,512]{1,0:T(8,128)(2,1)} %bitcast.111, bf16[512,512]{1,0:T(8,128)(2,1)} %refs_2_.3, ...), custom_call_target="tpu_custom_call" | custom-call | flops 4026531840 | bytes 7340032 | tf_op jit(solution)/shard_map/backward/pallas_call | solution.py:482
  82.1 16.0 %backward.2 = (bf16[1024,256]{1,0:T(8,128)(2,1)}, bf16[1024,256]{1,0:T(8,128)(2,1)}, bf16[1024,256]{1,0:T(8,128)(2,1)}, f32[16,64,256]{2,1,0:T(8,128)}, f32[16,64,256]{2,1,0:T(8,128)}) custom-call(s32[26]{0:T(128)} %pad_add_fusion.refs_0_, bf16[1024,512]{1,0:T(8,128)(2,1)} %bitcast.112, bf16[512,512]{1,0:T(8,128)(2,1)} %refs_2_.3, ...), custom_call_target="tpu_custom_call" | custom-call | flops 4026531840 | bytes 7340032 | tf_op jit(solution)/shard_map/backward/pallas_call | solution.py:482
  98.6 4.5 %collective-permute-start.20 = (bf16[8,64,256]{2,1,0:T(8,128)(2,1)S(1)}, bf16[8,64,256]{2,1,0:T(8,128)(2,1)}, u32[]{:S(2)}, u32[]{:S(2)}) collective-permute-start(bf16[8,64,256]{2,1,0:T(8,128)(2,1)S(1)} %slice.168), channel_id=1, source_target_pairs={{0,16},{8,24},{16,0},{24,8},{1,17},{9,25},{17,1},{25,9},{2,18},{10... | collective-permute-start | bytes 786440 | tf_op jit(solution)/shard_map/ppermute | solution.py:568
  103.2 4.0 %all-to-all-start.1 = ((bf16[8,128,512]{2,1,0:T(8,128)(2,1)}), bf16[8,128,512]{2,1,0:T(8,128)(2,1)S(1)}, u32[]{:S(2)}, u32[]{:S(2)}) async-start(bf16[8,128,512]{2,1,0:T(8,128)(2,1)} %bitcast.114), calls=%async_computation.1 | async-start | bytes 2097152 | tf_op jit(solution)/shard_map/all_to_all | solution.py:563
  107.2 1.4 add.79
  108.7 2.1 collective-permute-start.1
  110.7 1.0 fusion.17
  111.8 2.1 collective-permute-start.21
  113.9 3.3 %collective-permute-start.27 = (bf16[64,256]{1,0:T(8,128)(2,1)S(1)}, bf16[64,256]{1,0:T(8,128)(2,1)S(1)}, u32[]{:S(2)}, u32[]{:S(2)}) collective-permute-start(bf16[64,256]{1,0:T(8,128)(2,1)S(1)} %get-tuple-element.70), channel_id=1, source_target_pairs={{0,7},{1,6},{2,5},{3,4},{4,3},{5,2},{6,1},{7,0},{8,15},{9,14},{10,... | collective-permute-start | bytes 98312 | tf_op jit(solution)/shard_map/ppermute | solution.py:568
  117.2 1.9 collective-permute-start.25
  119.2 2.4 collective-permute-start.24
  121.7 1.0 collective-permute-start.23
  122.6 8.7 %collective-permute-done.27 = bf16[64,256]{1,0:T(8,128)(2,1)S(1)} collective-permute-done((bf16[64,256]{1,0:T(8,128)(2,1)S(1)}, bf16[64,256]{1,0:T(8,128)(2,1)S(1)}, u32[]{:S(2)}, u32[]{:S(2)}) %collective-permute-start.27) | collective-permute-done | bytes 32800 | tf_op jit(solution)/shard_map/ppermute | solution.py:568
  131.4 7.9 %collective-permute-start.22 = (bf16[64,256]{1,0:T(8,128)(2,1)S(1)}, bf16[64,256]{1,0:T(8,128)(2,1)S(1)}, u32[]{:S(2)}, u32[]{:S(2)}) collective-permute-start(bf16[64,256]{1,0:T(8,128)(2,1)S(1)} %get-tuple-element.75), channel_id=1, source_target_pairs={{0,2},{1,3},{2,0},{3,1},{4,6},{5,7},{6,4},{7,5},{8,10},{9,11},{10,... | collective-permute-start | bytes 98312 | tf_op jit(solution)/shard_map/ppermute | solution.py:568
  139.3 0.6 collective-permute-start.2
  139.9 2.2 collective-permute-start.8
  142.1 6.7 %finish.1 = (bf16[1024,512]{1,0:T(8,128)(2,1)}, f32[1,512]{1,0:T(1,128)}) custom-call(bf16[1024,512]{1,0:T(8,128)(2,1)} %bitcast.110, bf16[1024,512]{1,0:T(8,128)(2,1)} %bitcast.113, f32[1,512]{1,0:T(1,128)} %bitcast.118, bf16[512,512]{1,0:T(8,128)(2,1)} %refs_3_.3, bf16[512,512]{1,0:T(8,128)(2,1)} %refs_4_.3, bf16[512,512]{1,0:T(8,128)(2,1)} %refs_5_.3, ...), custom_call_target="tpu_custom_call" | custom-call | flops 1610612736 | bytes 8388608 | tf_op jit(solution)/shard_map/finish/pallas_call | solution.py:540
  148.8 2.5 %collective-permute-start.7 = (bf16[64,256]{1,0:T(8,128)(2,1)S(1)}, bf16[64,256]{1,0:T(8,128)(2,1)S(1)}, u32[]{:S(2)}, u32[]{:S(2)}) collective-permute-start(bf16[64,256]{1,0:T(8,128)(2,1)S(1)} %get-tuple-element.78), channel_id=1, source_target_pairs={{0,6},{1,7},{2,4},{3,5},{4,2},{5,3},{6,0},{7,1},{8,14},{9,15},{10,... | collective-permute-start | bytes 98312 | tf_op jit(solution)/shard_map/ppermute | solution.py:568
  151.4 3.0 %collective-permute-start.5 = (bf16[64,256]{1,0:T(8,128)(2,1)S(1)}, bf16[64,256]{1,0:T(8,128)(2,1)S(1)}, u32[]{:S(2)}, u32[]{:S(2)}) collective-permute-start(bf16[64,256]{1,0:T(8,128)(2,1)S(1)} %get-tuple-element.80), channel_id=1, source_target_pairs={{0,4},{1,5},{2,6},{3,7},{4,0},{5,1},{6,2},{7,3},{8,12},{9,13},{10,... | collective-permute-start | bytes 98312 | tf_op jit(solution)/shard_map/ppermute | solution.py:568
  154.4 2.9 %collective-permute-start.3 = (bf16[64,256]{1,0:T(8,128)(2,1)S(1)}, bf16[64,256]{1,0:T(8,128)(2,1)S(1)}, u32[]{:S(2)}, u32[]{:S(2)}) collective-permute-start(bf16[64,256]{1,0:T(8,128)(2,1)S(1)} %get-tuple-element.82), channel_id=1, source_target_pairs={{0,2},{1,3},{2,0},{3,1},{4,6},{5,7},{6,4},{7,5},{8,10},{9,11},{10,... | collective-permute-start | bytes 98312 | tf_op jit(solution)/shard_map/ppermute | solution.py:568
  157.3 1.4 collective-permute-start.33
  158.9 3.0 %collective-permute-start.31 = (bf16[64,256]{1,0:T(8,128)(2,1)S(1)}, bf16[64,256]{1,0:T(8,128)(2,1)S(1)}, u32[]{:S(2)}, u32[]{:S(2)}) collective-permute-start(bf16[64,256]{1,0:T(8,128)(2,1)S(1)} %get-tuple-element.62), channel_id=1, source_target_pairs={{0,4},{1,5},{2,6},{3,7},{4,0},{5,1},{6,2},{7,3},{8,12},{9,13},{10,... | collective-permute-start | bytes 98312 | tf_op jit(solution)/shard_map/ppermute | solution.py:568
  161.9 0.8 collective-permute-start.30
  162.7 0.6 collective-permute-start.28
  163.4 3.6 %collective-permute-done.28 = bf16[64,256]{1,0:T(8,128)(2,1)S(1)} collective-permute-done((bf16[64,256]{1,0:T(8,128)(2,1)S(1)}, bf16[64,256]{1,0:T(8,128)(2,1)S(1)}, u32[]{:S(2)}, u32[]{:S(2)}) %collective-permute-start.28) | collective-permute-done | bytes 32800 | tf_op jit(solution)/shard_map/ppermute | solution.py:568
  167.0 1.5 collective-permute-start.29
  168.5 2.8 %collective-permute-done.29 = bf16[64,256]{1,0:T(8,128)(2,1)S(1)} collective-permute-done((bf16[64,256]{1,0:T(8,128)(2,1)S(1)}, bf16[64,256]{1,0:T(8,128)(2,1)S(1)}, u32[]{:S(2)}, u32[]{:S(2)}) %collective-permute-start.29) | collective-permute-done | bytes 32800 | tf_op jit(solution)/shard_map/ppermute | solution.py:568
  171.3 2.0 collective-permute-start.34
  173.3 1.2 collective-permute-start.14
  174.5 2.2 collective-permute-start.13
  176.7 2.2 collective-permute-start.12
  179.0 1.0 collective-permute-start.9
  180.0 3.0 %collective-permute-done.9 = bf16[64,256]{1,0:T(8,128)(2,1)S(1)} collective-permute-done((bf16[64,256]{1,0:T(8,128)(2,1)S(1)}, bf16[64,256]{1,0:T(8,128)(2,1)S(1)}, u32[]{:S(2)}, u32[]{:S(2)}) %collective-permute-start.9) | collective-permute-done | bytes 32800 | tf_op jit(solution)/shard_map/ppermute | solution.py:568
  183.0 1.4 collective-permute-start.10
  184.3 6.4 %all-to-all-start.3 = ((bf16[8,128,512]{2,1,0:T(8,128)(2,1)}), bf16[8,128,512]{2,1,0:T(8,128)(2,1)S(1)}, u32[]{:S(2)}, u32[]{:S(2)}) async-start(bf16[8,128,512]{2,1,0:T(8,128)(2,1)} %bitcast.9), calls=%async_computation.3 | async-start | bytes 2097152 | tf_op jit(solution)/shard_map/all_to_all | solution.py:563
  190.7 4.7 %collective-permute-start.15 = (bf16[64,256]{1,0:T(8,128)(2,1)S(1)}, bf16[64,256]{1,0:T(8,128)(2,1)S(1)}, u32[]{:S(2)}, u32[]{:S(2)}) collective-permute-start(bf16[64,256]{1,0:T(8,128)(2,1)S(1)} %get-tuple-element.66), channel_id=1, source_target_pairs={{0,7},{1,6},{2,5},{3,4},{4,3},{5,2},{6,1},{7,0},{8,15},{9,14},{10,... | collective-permute-start | bytes 98312 | tf_op jit(solution)/shard_map/ppermute | solution.py:568
  195.4 1.7 collective-permute-start.35
  197.2 9.0 %collective-permute-done.15 = bf16[64,256]{1,0:T(8,128)(2,1)S(1)} collective-permute-done((bf16[64,256]{1,0:T(8,128)(2,1)S(1)}, bf16[64,256]{1,0:T(8,128)(2,1)S(1)}, u32[]{:S(2)}, u32[]{:S(2)}) %collective-permute-start.15) | collective-permute-done | bytes 32800 | tf_op jit(solution)/shard_map/ppermute | solution.py:568
  206.2 1.7 collective-permute-start.16
  208.4 4.1 %collective-permute-done.16.refs_1_ = bf16[8,64,256]{2,1,0:T(8,128)(2,1)S(1)} collective-permute-done((bf16[8,64,256]{2,1,0:T(8,128)(2,1)S(1)}, bf16[8,64,256]{2,1,0:T(8,128)(2,1)S(1)}, u32[]{:S(2)}, u32[]{:S(2)}) %collective-permute-start.16) | collective-permute-done | bytes 262176 | tf_op jit(solution)/shard_map/ppermute | solution.py:568
  213.1 1.0 collective-permute-done.38
  214.1 1.7 collective-permute-start.39
  215.8 1.9 collective-permute-done.39
  217.7 0.7 collective-permute-start.40
  218.4 2.9 %collective-permute-done.40 = f32[1,512]{1,0:T(1,128)S(1)} collective-permute-done((f32[1,512]{1,0:T(1,128)S(1)}, f32[1,512]{1,0:T(1,128)S(1)}, u32[]{:S(2)}, u32[]{:S(2)}) %collective-permute-start.40) | collective-permute-done | bytes 2080 | tf_op jit(solution)/shard_map/ppermute | solution.py:568
  221.3 3.8 %collective-permute-start.41 = (f32[1,512]{1,0:T(1,128)S(1)}, f32[1,512]{1,0:T(1,128)S(1)}, u32[]{:S(2)}, u32[]{:S(2)}) collective-permute-start(f32[1,512]{1,0:T(1,128)S(1)} %add.99), channel_id=1, source_target_pairs={{0,2},{1,3},{2,0},{3,1},{4,6},{5,7},{6,4},{7,5},{8,10},{9,11},{10,... | collective-permute-start | bytes 6152 | tf_op jit(solution)/shard_map/ppermute | solution.py:568
  225.1 1.6 collective-permute-done.41
  226.6 1.9 collective-permute-start.42
  228.5 0.6 pad_add_fusion.1.place_ref
  229.1 2.0 collective-permute-done.42
  231.1 0.6 add.101
  231.8 0.6 copy-done.10
  232.4 3.9 %place.1 = (f32[512,512]{1,0:T(8,128)}, f32[512,512]{1,0:T(8,128)}, f32[512,512]{1,0:T(8,128)}, f32[512,512]{1,0:T(8,128)}) custom-call(s32[2]{0:T(128)} %pad_add_fusion.1.place_ref, bf16[8,64,256]{2,1,0:T(8,128)(2,1)} %copy-done.6, bf16[8,64,256]{2,1,0:T(8,128)(2,1)} %copy-done.9, bf16[8,64,256]{2,1,0:T(8,128)(2,1)} %collective-permute-done.17.refs_2_, ...), custom_call_target="tpu_custom_call" | custom-call | bytes 6291456 | tf_op jit(solution)/shard_map/place/pallas_call | solution.py:607
  236.3 1.0 copy.38
  237.3 1.0 copy.39
  (99 shorter events, 2.5 us)
Async XLA Ops:
  0.6 40.1 %copy-start = (s32[8,8,3]{1,0,2:T(8,128)S(1)}, s32[8,8,3]{1,0,2:T(8,128)}, u32[]{:S(2)}) copy-start(s32[8,8,3]{1,0,2:T(8,128)} %param.16) | copy-start | bytes 2308
  33.8 7.1 %copy-start.2 = (bf16[512,512]{1,0:T(8,128)(2,1)S(1)}, bf16[512,512]{1,0:T(8,128)(2,1)}, u32[]{:S(2)}) copy-start(bf16[512,512]{1,0:T(8,128)(2,1)} %refs_4_.3) | copy-start | bytes 1572868
  33.8 31.2 %all-to-all-start.2 = ((bf16[8,128,512]{2,1,0:T(8,128)(2,1)}), bf16[8,128,512]{2,1,0:T(8,128)(2,1)S(1)}, u32[]{:S(2)}, u32[]{:S(2)}) async-start(bf16[8,128,512]{2,1,0:T(8,128)(2,1)} %param.10), calls=%async_computation.2 | async-start | bytes 2097152 | tf_op jit(solution)/shard_map/all_to_all | solution.py:563
  37.5 0.7 copy-start.12
  40.9 1.0 copy-start.3
  65.0 1.0 copy-start.1
  82.1 16.4 %copy-start.5 = (f32[16,64,256]{2,1,0:T(8,128)S(1)}, f32[16,64,256]{2,1,0:T(8,128)}, u32[]{:S(2)}) copy-start(f32[16,64,256]{2,1,0:T(8,128)} %get-tuple-element.54) | copy-start | bytes 3145732
  82.1 16.4 %collective-permute-start.19 = (f32[16,64,256]{2,1,0:T(8,128)}, f32[16,64,256]{2,1,0:T(8,128)S(1)}, u32[]{:S(2)}, u32[]{:S(2)}) collective-permute-start(f32[16,64,256]{2,1,0:T(8,128)} %get-tuple-element.55), channel_id=1, source_target_pairs={{0,8},{8,0},{16,24},{24,16},{1,9},{9,1},{17,25},{25,17},{2,10},{10... | collective-permute-start | bytes 3145736 | tf_op jit(solution)/shard_map/ppermute | solution.py:568
  98.0 9.2 %collective-permute-start = (f32[16,64,256]{2,1,0:T(8,128)}, f32[16,64,256]{2,1,0:T(8,128)}, u32[]{:S(2)}, u32[]{:S(2)}) collective-permute-start(f32[16,64,256]{2,1,0:T(8,128)} %get-tuple-element.53), channel_id=1, source_target_pairs={{0,8},{8,0},{16,24},{24,16},{1,9},{9,1},{17,25},{25,17},{2,10},{10... | collective-permute-start | bytes 3145736 | tf_op jit(solution)/shard_map/ppermute | solution.py:568
  98.6 12.1 %collective-permute-start.20 = (bf16[8,64,256]{2,1,0:T(8,128)(2,1)S(1)}, bf16[8,64,256]{2,1,0:T(8,128)(2,1)}, u32[]{:S(2)}, u32[]{:S(2)}) collective-permute-start(bf16[8,64,256]{2,1,0:T(8,128)(2,1)S(1)} %slice.168), channel_id=1, source_target_pairs={{0,16},{8,24},{16,0},{24,8},{1,17},{9,25},{17,1},{25,9},{2,18},{10... | collective-permute-start | bytes 786440 | tf_op jit(solution)/shard_map/ppermute | solution.py:568
  103.2 4.0 %copy-start.4 = (f32[16,64,256]{2,1,0:T(8,128)S(1)}, f32[16,64,256]{2,1,0:T(8,128)}, u32[]{:S(2)}) copy-start(f32[16,64,256]{2,1,0:T(8,128)} %get-tuple-element.52) | copy-start | bytes 3145732
  103.2 81.2 %all-to-all-start.1 = ((bf16[8,128,512]{2,1,0:T(8,128)(2,1)}), bf16[8,128,512]{2,1,0:T(8,128)(2,1)S(1)}, u32[]{:S(2)}, u32[]{:S(2)}) async-start(bf16[8,128,512]{2,1,0:T(8,128)(2,1)} %bitcast.114), calls=%async_computation.1 | async-start | bytes 2097152 | tf_op jit(solution)/shard_map/all_to_all | solution.py:563
  108.7 10.5 %collective-permute-start.1 = (bf16[8,64,256]{2,1,0:T(8,128)(2,1)S(1)}, bf16[8,64,256]{2,1,0:T(8,128)(2,1)S(1)}, u32[]{:S(2)}, u32[]{:S(2)}) collective-permute-start(bf16[8,64,256]{2,1,0:T(8,128)(2,1)S(1)} %slice.169), channel_id=1, source_target_pairs={{0,16},{8,24},{16,0},{24,8},{1,17},{9,25},{17,1},{25,9},{2,18},{10... | collective-permute-start | bytes 786440 | tf_op jit(solution)/shard_map/ppermute | solution.py:568
  111.8 9.8 %collective-permute-start.21 = (bf16[64,256]{1,0:T(8,128)(2,1)S(1)}, bf16[64,256]{1,0:T(8,128)(2,1)S(1)}, u32[]{:S(2)}, u32[]{:S(2)}) collective-permute-start(bf16[64,256]{1,0:T(8,128)(2,1)S(1)} %get-tuple-element.69), channel_id=1, source_target_pairs={{0,1},{1,0},{2,3},{3,2},{4,5},{5,4},{6,7},{7,6},{8,9},{9,8},{10,11... | collective-permute-start | bytes 98312 | tf_op jit(solution)/shard_map/ppermute | solution.py:568
  113.9 17.5 %collective-permute-start.27 = (bf16[64,256]{1,0:T(8,128)(2,1)S(1)}, bf16[64,256]{1,0:T(8,128)(2,1)S(1)}, u32[]{:S(2)}, u32[]{:S(2)}) collective-permute-start(bf16[64,256]{1,0:T(8,128)(2,1)S(1)} %get-tuple-element.70), channel_id=1, source_target_pairs={{0,7},{1,6},{2,5},{3,4},{4,3},{5,2},{6,1},{7,0},{8,15},{9,14},{10,... | collective-permute-start | bytes 98312 | tf_op jit(solution)/shard_map/ppermute | solution.py:568
  117.2 22.1 %collective-permute-start.26 = (bf16[64,256]{1,0:T(8,128)(2,1)S(1)}, bf16[64,256]{1,0:T(8,128)(2,1)S(1)}, u32[]{:S(2)}, u32[]{:S(2)}) collective-permute-start(bf16[64,256]{1,0:T(8,128)(2,1)S(1)} %get-tuple-element.71), channel_id=1, source_target_pairs={{0,6},{1,7},{2,4},{3,5},{4,2},{5,3},{6,0},{7,1},{8,14},{9,15},{10,... | collective-permute-start | bytes 98312 | tf_op jit(solution)/shard_map/ppermute | solution.py:568
  117.2 22.7 %collective-permute-start.25 = (bf16[64,256]{1,0:T(8,128)(2,1)S(1)}, bf16[64,256]{1,0:T(8,128)(2,1)S(1)}, u32[]{:S(2)}, u32[]{:S(2)}) collective-permute-start(bf16[64,256]{1,0:T(8,128)(2,1)S(1)} %get-tuple-element.72), channel_id=1, source_target_pairs={{0,5},{1,4},{2,7},{3,6},{4,1},{5,0},{6,3},{7,2},{8,13},{9,12},{10,... | collective-permute-start | bytes 98312 | tf_op jit(solution)/shard_map/ppermute | solution.py:568
  119.2 29.7 %collective-permute-start.24 = (bf16[64,256]{1,0:T(8,128)(2,1)S(1)}, bf16[64,256]{1,0:T(8,128)(2,1)S(1)}, u32[]{:S(2)}, u32[]{:S(2)}) collective-permute-start(bf16[64,256]{1,0:T(8,128)(2,1)S(1)} %get-tuple-element.73), channel_id=1, source_target_pairs={{0,4},{1,5},{2,6},{3,7},{4,0},{5,1},{6,2},{7,3},{8,12},{9,13},{10,... | collective-permute-start | bytes 98312 | tf_op jit(solution)/shard_map/ppermute | solution.py:568
  121.7 29.7 %collective-permute-start.23 = (bf16[64,256]{1,0:T(8,128)(2,1)S(1)}, bf16[64,256]{1,0:T(8,128)(2,1)S(1)}, u32[]{:S(2)}, u32[]{:S(2)}) collective-permute-start(bf16[64,256]{1,0:T(8,128)(2,1)S(1)} %get-tuple-element.74), channel_id=1, source_target_pairs={{0,3},{1,2},{2,1},{3,0},{4,7},{5,6},{6,5},{7,4},{8,11},{9,10},{10,... | collective-permute-start | bytes 98312 | tf_op jit(solution)/shard_map/ppermute | solution.py:568
  131.4 20.0 %collective-permute-start.22 = (bf16[64,256]{1,0:T(8,128)(2,1)S(1)}, bf16[64,256]{1,0:T(8,128)(2,1)S(1)}, u32[]{:S(2)}, u32[]{:S(2)}) collective-permute-start(bf16[64,256]{1,0:T(8,128)(2,1)S(1)} %get-tuple-element.75), channel_id=1, source_target_pairs={{0,2},{1,3},{2,0},{3,1},{4,6},{5,7},{6,4},{7,5},{8,10},{9,11},{10,... | collective-permute-start | bytes 98312 | tf_op jit(solution)/shard_map/ppermute | solution.py:568
  139.3 15.1 %collective-permute-start.2 = (bf16[64,256]{1,0:T(8,128)(2,1)S(1)}, bf16[64,256]{1,0:T(8,128)(2,1)S(1)}, u32[]{:S(2)}, u32[]{:S(2)}) collective-permute-start(bf16[64,256]{1,0:T(8,128)(2,1)S(1)} %get-tuple-element.76), channel_id=1, source_target_pairs={{0,1},{1,0},{2,3},{3,2},{4,5},{5,4},{6,7},{7,6},{8,9},{9,8},{10,11... | collective-permute-start | bytes 98312 | tf_op jit(solution)/shard_map/ppermute | solution.py:568
  139.9 14.5 %collective-permute-start.8 = (bf16[64,256]{1,0:T(8,128)(2,1)S(1)}, bf16[64,256]{1,0:T(8,128)(2,1)S(1)}, u32[]{:S(2)}, u32[]{:S(2)}) collective-permute-start(bf16[64,256]{1,0:T(8,128)(2,1)S(1)} %get-tuple-element.77), channel_id=1, source_target_pairs={{0,7},{1,6},{2,5},{3,4},{4,3},{5,2},{6,1},{7,0},{8,15},{9,14},{10,... | collective-permute-start | bytes 98312 | tf_op jit(solution)/shard_map/ppermute | solution.py:568
  148.8 8.4 %collective-permute-start.7 = (bf16[64,256]{1,0:T(8,128)(2,1)S(1)}, bf16[64,256]{1,0:T(8,128)(2,1)S(1)}, u32[]{:S(2)}, u32[]{:S(2)}) collective-permute-start(bf16[64,256]{1,0:T(8,128)(2,1)S(1)} %get-tuple-element.78), channel_id=1, source_target_pairs={{0,6},{1,7},{2,4},{3,5},{4,2},{5,3},{6,0},{7,1},{8,14},{9,15},{10,... | collective-permute-start | bytes 98312 | tf_op jit(solution)/shard_map/ppermute | solution.py:568
  151.4 7.3 %collective-permute-start.6 = (bf16[64,256]{1,0:T(8,128)(2,1)S(1)}, bf16[64,256]{1,0:T(8,128)(2,1)S(1)}, u32[]{:S(2)}, u32[]{:S(2)}) collective-permute-start(bf16[64,256]{1,0:T(8,128)(2,1)S(1)} %get-tuple-element.79), channel_id=1, source_target_pairs={{0,5},{1,4},{2,7},{3,6},{4,1},{5,0},{6,3},{7,2},{8,13},{9,12},{10,... | collective-permute-start | bytes 98312 | tf_op jit(solution)/shard_map/ppermute | solution.py:568
  151.4 7.5 %collective-permute-start.5 = (bf16[64,256]{1,0:T(8,128)(2,1)S(1)}, bf16[64,256]{1,0:T(8,128)(2,1)S(1)}, u32[]{:S(2)}, u32[]{:S(2)}) collective-permute-start(bf16[64,256]{1,0:T(8,128)(2,1)S(1)} %get-tuple-element.80), channel_id=1, source_target_pairs={{0,4},{1,5},{2,6},{3,7},{4,0},{5,1},{6,2},{7,3},{8,12},{9,13},{10,... | collective-permute-start | bytes 98312 | tf_op jit(solution)/shard_map/ppermute | solution.py:568
  154.4 7.6 %collective-permute-start.4 = (bf16[64,256]{1,0:T(8,128)(2,1)S(1)}, bf16[64,256]{1,0:T(8,128)(2,1)S(1)}, u32[]{:S(2)}, u32[]{:S(2)}) collective-permute-start(bf16[64,256]{1,0:T(8,128)(2,1)S(1)} %get-tuple-element.81), channel_id=1, source_target_pairs={{0,3},{1,2},{2,1},{3,0},{4,7},{5,6},{6,5},{7,4},{8,11},{9,10},{10,... | collective-permute-start | bytes 98312 | tf_op jit(solution)/shard_map/ppermute | solution.py:568
  154.4 8.4 %collective-permute-start.3 = (bf16[64,256]{1,0:T(8,128)(2,1)S(1)}, bf16[64,256]{1,0:T(8,128)(2,1)S(1)}, u32[]{:S(2)}, u32[]{:S(2)}) collective-permute-start(bf16[64,256]{1,0:T(8,128)(2,1)S(1)} %get-tuple-element.82), channel_id=1, source_target_pairs={{0,2},{1,3},{2,0},{3,1},{4,6},{5,7},{6,4},{7,5},{8,10},{9,11},{10,... | collective-permute-start | bytes 98312 | tf_op jit(solution)/shard_map/ppermute | solution.py:568
  157.3 21.6 %collective-permute-start.33 = (bf16[64,256]{1,0:T(8,128)(2,1)S(1)}, bf16[64,256]{1,0:T(8,128)(2,1)S(1)}, u32[]{:S(2)}, u32[]{:S(2)}) collective-permute-start(bf16[64,256]{1,0:T(8,128)(2,1)S(1)} %get-tuple-element.62), channel_id=1, source_target_pairs={{0,6},{1,7},{2,4},{3,5},{4,2},{5,3},{6,0},{7,1},{8,14},{9,15},{10,... | collective-permute-start | bytes 98312 | tf_op jit(solution)/shard_map/ppermute | solution.py:568
  158.7 18.0 %collective-permute-start.32 = (bf16[64,256]{1,0:T(8,128)(2,1)S(1)}, bf16[64,256]{1,0:T(8,128)(2,1)S(1)}, u32[]{:S(2)}, u32[]{:S(2)}) collective-permute-start(bf16[64,256]{1,0:T(8,128)(2,1)S(1)} %get-tuple-element.62), channel_id=1, source_target_pairs={{0,5},{1,4},{2,7},{3,6},{4,1},{5,0},{6,3},{7,2},{8,13},{9,12},{10,... | collective-permute-start | bytes 98312 | tf_op jit(solution)/shard_map/ppermute | solution.py:568
  158.9 15.6 %collective-permute-start.31 = (bf16[64,256]{1,0:T(8,128)(2,1)S(1)}, bf16[64,256]{1,0:T(8,128)(2,1)S(1)}, u32[]{:S(2)}, u32[]{:S(2)}) collective-permute-start(bf16[64,256]{1,0:T(8,128)(2,1)S(1)} %get-tuple-element.62), channel_id=1, source_target_pairs={{0,4},{1,5},{2,6},{3,7},{4,0},{5,1},{6,2},{7,3},{8,12},{9,13},{10,... | collective-permute-start | bytes 98312 | tf_op jit(solution)/shard_map/ppermute | solution.py:568
  161.9 11.4 %collective-permute-start.30 = (bf16[64,256]{1,0:T(8,128)(2,1)S(1)}, bf16[64,256]{1,0:T(8,128)(2,1)S(1)}, u32[]{:S(2)}, u32[]{:S(2)}) collective-permute-start(bf16[64,256]{1,0:T(8,128)(2,1)S(1)} %get-tuple-element.62), channel_id=1, source_target_pairs={{0,3},{1,2},{2,1},{3,0},{4,7},{5,6},{6,5},{7,4},{8,11},{9,10},{10,... | collective-permute-start | bytes 98312 | tf_op jit(solution)/shard_map/ppermute | solution.py:568
  162.7 4.3 %collective-permute-start.28 = (bf16[64,256]{1,0:T(8,128)(2,1)S(1)}, bf16[64,256]{1,0:T(8,128)(2,1)S(1)}, u32[]{:S(2)}, u32[]{:S(2)}) collective-permute-start(bf16[64,256]{1,0:T(8,128)(2,1)S(1)} %get-tuple-element.62), channel_id=1, source_target_pairs={{0,1},{1,0},{2,3},{3,2},{4,5},{5,4},{6,7},{7,6},{8,9},{9,8},{10,11... | collective-permute-start | bytes 98312 | tf_op jit(solution)/shard_map/ppermute | solution.py:568
  167.0 4.3 %collective-permute-start.29 = (bf16[64,256]{1,0:T(8,128)(2,1)S(1)}, bf16[64,256]{1,0:T(8,128)(2,1)S(1)}, u32[]{:S(2)}, u32[]{:S(2)}) collective-permute-start(bf16[64,256]{1,0:T(8,128)(2,1)S(1)} %get-tuple-element.62), channel_id=1, source_target_pairs={{0,2},{1,3},{2,0},{3,1},{4,6},{5,7},{6,4},{7,5},{8,10},{9,11},{10,... | collective-permute-start | bytes 98312 | tf_op jit(solution)/shard_map/ppermute | solution.py:568
  171.3 7.7 %collective-permute-start.34 = (bf16[64,256]{1,0:T(8,128)(2,1)S(1)}, bf16[64,256]{1,0:T(8,128)(2,1)S(1)}, u32[]{:S(2)}, u32[]{:S(2)}) collective-permute-start(bf16[64,256]{1,0:T(8,128)(2,1)S(1)} %get-tuple-element.62), channel_id=1, source_target_pairs={{0,7},{1,6},{2,5},{3,4},{4,3},{5,2},{6,1},{7,0},{8,15},{9,14},{10,... | collective-permute-start | bytes 98312 | tf_op jit(solution)/shard_map/ppermute | solution.py:568
  173.3 23.9 %collective-permute-start.14 = (bf16[64,256]{1,0:T(8,128)(2,1)S(1)}, bf16[64,256]{1,0:T(8,128)(2,1)S(1)}, u32[]{:S(2)}, u32[]{:S(2)}) collective-permute-start(bf16[64,256]{1,0:T(8,128)(2,1)S(1)} %get-tuple-element.66), channel_id=1, source_target_pairs={{0,6},{1,7},{2,4},{3,5},{4,2},{5,3},{6,0},{7,1},{8,14},{9,15},{10,... | collective-permute-start | bytes 98312 | tf_op jit(solution)/shard_map/ppermute | solution.py:568
  174.5 22.6 %collective-permute-start.13 = (bf16[64,256]{1,0:T(8,128)(2,1)S(1)}, bf16[64,256]{1,0:T(8,128)(2,1)S(1)}, u32[]{:S(2)}, u32[]{:S(2)}) collective-permute-start(bf16[64,256]{1,0:T(8,128)(2,1)S(1)} %get-tuple-element.66), channel_id=1, source_target_pairs={{0,5},{1,4},{2,7},{3,6},{4,1},{5,0},{6,3},{7,2},{8,13},{9,12},{10,... | collective-permute-start | bytes 98312 | tf_op jit(solution)/shard_map/ppermute | solution.py:568
  176.7 20.4 %collective-permute-start.12 = (bf16[64,256]{1,0:T(8,128)(2,1)S(1)}, bf16[64,256]{1,0:T(8,128)(2,1)S(1)}, u32[]{:S(2)}, u32[]{:S(2)}) collective-permute-start(bf16[64,256]{1,0:T(8,128)(2,1)S(1)} %get-tuple-element.66), channel_id=1, source_target_pairs={{0,4},{1,5},{2,6},{3,7},{4,0},{5,1},{6,2},{7,3},{8,12},{9,13},{10,... | collective-permute-start | bytes 98312 | tf_op jit(solution)/shard_map/ppermute | solution.py:568
  178.9 16.5 %collective-permute-start.11 = (bf16[64,256]{1,0:T(8,128)(2,1)S(1)}, bf16[64,256]{1,0:T(8,128)(2,1)S(1)}, u32[]{:S(2)}, u32[]{:S(2)}) collective-permute-start(bf16[64,256]{1,0:T(8,128)(2,1)S(1)} %get-tuple-element.66), channel_id=1, source_target_pairs={{0,3},{1,2},{2,1},{3,0},{4,7},{5,6},{6,5},{7,4},{8,11},{9,10},{10,... | collective-permute-start | bytes 98312 | tf_op jit(solution)/shard_map/ppermute | solution.py:568
  179.0 4.0 %collective-permute-start.9 = (bf16[64,256]{1,0:T(8,128)(2,1)S(1)}, bf16[64,256]{1,0:T(8,128)(2,1)S(1)}, u32[]{:S(2)}, u32[]{:S(2)}) collective-permute-start(bf16[64,256]{1,0:T(8,128)(2,1)S(1)} %get-tuple-element.66), channel_id=1, source_target_pairs={{0,1},{1,0},{2,3},{3,2},{4,5},{5,4},{6,7},{7,6},{8,9},{9,8},{10,11... | collective-permute-start | bytes 98312 | tf_op jit(solution)/shard_map/ppermute | solution.py:568
  180.0 27.9 %copy-start.7 = (bf16[8,64,256]{2,1,0:T(8,128)(2,1)}, bf16[8,64,256]{2,1,0:T(8,128)(2,1)S(1)}, u32[]{:S(2)}) copy-start(bf16[8,64,256]{2,1,0:T(8,128)(2,1)S(1)} %constant_dynamic-update-slice_fusion.8.refs_4_) | copy-start | bytes 786436
  183.0 7.8 %collective-permute-start.10 = (bf16[64,256]{1,0:T(8,128)(2,1)S(1)}, bf16[64,256]{1,0:T(8,128)(2,1)S(1)}, u32[]{:S(2)}, u32[]{:S(2)}) collective-permute-start(bf16[64,256]{1,0:T(8,128)(2,1)S(1)} %get-tuple-element.66), channel_id=1, source_target_pairs={{0,2},{1,3},{2,0},{3,1},{4,6},{5,7},{6,4},{7,5},{8,10},{9,11},{10,... | collective-permute-start | bytes 98312 | tf_op jit(solution)/shard_map/ppermute | solution.py:568
  184.3 47.4 %all-to-all-start.3 = ((bf16[8,128,512]{2,1,0:T(8,128)(2,1)}), bf16[8,128,512]{2,1,0:T(8,128)(2,1)S(1)}, u32[]{:S(2)}, u32[]{:S(2)}) async-start(bf16[8,128,512]{2,1,0:T(8,128)(2,1)} %bitcast.9), calls=%async_computation.3 | async-start | bytes 2097152 | tf_op jit(solution)/shard_map/all_to_all | solution.py:563
  190.7 15.4 %collective-permute-start.15 = (bf16[64,256]{1,0:T(8,128)(2,1)S(1)}, bf16[64,256]{1,0:T(8,128)(2,1)S(1)}, u32[]{:S(2)}, u32[]{:S(2)}) collective-permute-start(bf16[64,256]{1,0:T(8,128)(2,1)S(1)} %get-tuple-element.66), channel_id=1, source_target_pairs={{0,7},{1,6},{2,5},{3,4},{4,3},{5,2},{6,1},{7,0},{8,15},{9,14},{10,... | collective-permute-start | bytes 98312 | tf_op jit(solution)/shard_map/ppermute | solution.py:568
  195.4 12.9 %collective-permute-start.35 = (bf16[8,64,256]{2,1,0:T(8,128)(2,1)S(1)}, bf16[8,64,256]{2,1,0:T(8,128)(2,1)S(1)}, u32[]{:S(2)}, u32[]{:S(2)}) collective-permute-start(bf16[8,64,256]{2,1,0:T(8,128)(2,1)S(1)} %constant_dynamic-update-slice_fusion.8.refs_4_), channel_id=1, source_target_pairs={{0,16},{8,24},{16,0},{24,8},{1,17},{9,25},{17,1},{25,9},{2,18},{10... | collective-permute-start | bytes 786440 | tf_op jit(solution)/shard_map/ppermute | solution.py:568
  197.2 15.4 %copy-start.11 = (f32[1,512]{1,0:T(1,128)S(1)}, f32[1,512]{1,0:T(1,128)}, u32[]{:S(2)}) copy-start(f32[1,512]{1,0:T(1,128)} %get-tuple-element.60) | copy-start | bytes 6148
  206.2 25.6 %copy-start.6 = (bf16[8,64,256]{2,1,0:T(8,128)(2,1)}, bf16[8,64,256]{2,1,0:T(8,128)(2,1)S(1)}, u32[]{:S(2)}) copy-start(bf16[8,64,256]{2,1,0:T(8,128)(2,1)S(1)} %constant_dynamic-update-slice_fusion.refs_0_) | copy-start | bytes 786436
  206.2 6.4 %collective-permute-start.16 = (bf16[8,64,256]{2,1,0:T(8,128)(2,1)S(1)}, bf16[8,64,256]{2,1,0:T(8,128)(2,1)S(1)}, u32[]{:S(2)}, u32[]{:S(2)}) collective-permute-start(bf16[8,64,256]{2,1,0:T(8,128)(2,1)S(1)} %constant_dynamic-update-slice_fusion.refs_0_), channel_id=1, source_target_pairs={{0,16},{8,24},{16,0},{24,8},{1,17},{9,25},{17,1},{25,9},{2,18},{10... | collective-permute-start | bytes 786440 | tf_op jit(solution)/shard_map/ppermute | solution.py:568
  207.8 23.8 %collective-permute-start.36 = (bf16[8,64,256]{2,1,0:T(8,128)(2,1)S(1)}, bf16[8,64,256]{2,1,0:T(8,128)(2,1)S(1)}, u32[]{:S(2)}, u32[]{:S(2)}) collective-permute-start(bf16[8,64,256]{2,1,0:T(8,128)(2,1)S(1)} %constant_dynamic-update-slice_fusion.8.refs_4_), channel_id=1, source_target_pairs={{0,8},{8,0},{16,24},{24,16},{1,9},{9,1},{17,25},{25,17},{2,10},{10... | collective-permute-start | bytes 786440 | tf_op jit(solution)/shard_map/ppermute | solution.py:568
  207.8 23.9 %collective-permute-start.17 = (bf16[8,64,256]{2,1,0:T(8,128)(2,1)S(1)}, bf16[8,64,256]{2,1,0:T(8,128)(2,1)}, u32[]{:S(2)}, u32[]{:S(2)}) collective-permute-start(bf16[8,64,256]{2,1,0:T(8,128)(2,1)S(1)} %constant_dynamic-update-slice_fusion.refs_0_), channel_id=1, source_target_pairs={{0,8},{8,0},{16,24},{24,16},{1,9},{9,1},{17,25},{25,17},{2,10},{10... | collective-permute-start | bytes 786440 | tf_op jit(solution)/shard_map/ppermute | solution.py:568
  208.4 23.4 %copy-start.8 = (bf16[8,64,256]{2,1,0:T(8,128)(2,1)}, bf16[8,64,256]{2,1,0:T(8,128)(2,1)S(1)}, u32[]{:S(2)}) copy-start(bf16[8,64,256]{2,1,0:T(8,128)(2,1)S(1)} %collective-permute-done.35.refs_5_) | copy-start | bytes 786436
  208.4 23.4 %collective-permute-start.37 = (bf16[8,64,256]{2,1,0:T(8,128)(2,1)S(1)}, bf16[8,64,256]{2,1,0:T(8,128)(2,1)}, u32[]{:S(2)}, u32[]{:S(2)}) collective-permute-start(bf16[8,64,256]{2,1,0:T(8,128)(2,1)S(1)} %collective-permute-done.35.refs_5_), channel_id=1, source_target_pairs={{0,8},{8,0},{16,24},{24,16},{1,9},{9,1},{17,25},{25,17},{2,10},{10... | collective-permute-start | bytes 786440 | tf_op jit(solution)/shard_map/ppermute | solution.py:568
  212.5 19.2 %copy-start.9 = (bf16[8,64,256]{2,1,0:T(8,128)(2,1)}, bf16[8,64,256]{2,1,0:T(8,128)(2,1)S(1)}, u32[]{:S(2)}) copy-start(bf16[8,64,256]{2,1,0:T(8,128)(2,1)S(1)} %collective-permute-done.16.refs_1_) | copy-start | bytes 786436
  212.5 19.2 %collective-permute-start.18 = (bf16[8,64,256]{2,1,0:T(8,128)(2,1)S(1)}, bf16[8,64,256]{2,1,0:T(8,128)(2,1)}, u32[]{:S(2)}, u32[]{:S(2)}) collective-permute-start(bf16[8,64,256]{2,1,0:T(8,128)(2,1)S(1)} %collective-permute-done.16.refs_1_), channel_id=1, source_target_pairs={{0,8},{8,0},{16,24},{24,16},{1,9},{9,1},{17,25},{25,17},{2,10},{10... | collective-permute-start | bytes 786440 | tf_op jit(solution)/shard_map/ppermute | solution.py:568
  212.5 1.5 collective-permute-start.38
  214.1 3.6 %collective-permute-start.39 = (f32[1,512]{1,0:T(1,128)S(1)}, f32[1,512]{1,0:T(1,128)S(1)}, u32[]{:S(2)}, u32[]{:S(2)}) collective-permute-start(f32[1,512]{1,0:T(1,128)S(1)} %add.97), channel_id=1, source_target_pairs={{0,16},{8,24},{16,0},{24,8},{1,17},{9,25},{17,1},{25,9},{2,18},{10... | collective-permute-start | bytes 6152 | tf_op jit(solution)/shard_map/ppermute | solution.py:568
  217.7 3.6 %collective-permute-start.40 = (f32[1,512]{1,0:T(1,128)S(1)}, f32[1,512]{1,0:T(1,128)S(1)}, u32[]{:S(2)}, u32[]{:S(2)}) collective-permute-start(f32[1,512]{1,0:T(1,128)S(1)} %add.98), channel_id=1, source_target_pairs={{0,1},{1,0},{2,3},{3,2},{4,5},{5,4},{6,7},{7,6},{8,9},{9,8},{10,11... | collective-permute-start | bytes 6152 | tf_op jit(solution)/shard_map/ppermute | solution.py:568
  221.3 5.4 %collective-permute-start.41 = (f32[1,512]{1,0:T(1,128)S(1)}, f32[1,512]{1,0:T(1,128)S(1)}, u32[]{:S(2)}, u32[]{:S(2)}) collective-permute-start(f32[1,512]{1,0:T(1,128)S(1)} %add.99), channel_id=1, source_target_pairs={{0,2},{1,3},{2,0},{3,1},{4,6},{5,7},{6,4},{7,5},{8,10},{9,11},{10,... | collective-permute-start | bytes 6152 | tf_op jit(solution)/shard_map/ppermute | solution.py:568
  226.6 4.5 %collective-permute-start.42 = (f32[1,512]{1,0:T(1,128)S(1)}, f32[1,512]{1,0:T(1,128)S(1)}, u32[]{:S(2)}, u32[]{:S(2)}) collective-permute-start(f32[1,512]{1,0:T(1,128)S(1)} %add.100), channel_id=1, source_target_pairs={{0,4},{1,5},{2,6},{3,7},{4,0},{5,1},{6,2},{7,3},{8,12},{9,13},{10,... | collective-permute-start | bytes 6152 | tf_op jit(solution)/shard_map/ppermute | solution.py:568
  231.7 0.7 copy-start.10

commit v4 on v2

--- a/solution.py
+++ b/solution.py
@@ -225,6 +225,7 @@
 QUAD = 4
 LOG2_E = 1.4426950408889634
 VMEM_LIMIT = 58 * 2**20
+GAIN_ROWS = 8
 
 
 def contract(left, right, left_dim, right_dim):
@@ -247,17 +248,19 @@
     return jnp.where(first, wide[:, :block_rows], wide[:, block_rows:])
 
 
-def for_each_block(lists_ref, block_count, block_rows, work):
+def for_each_block(sectors_ref, lists_ref, block_count, block_rows, work):
+    sector = sectors_ref[lax.axis_index("turb")]
+
     def step(block, carry):
         used = jnp.int32(0)
         for slot in range(UPSTREAM):
-            used = used + (lists_ref[block * UPSTREAM + slot] >= 0).astype(jnp.int32)
+            used = used + (lists_ref[sector, block, slot] >= 0).astype(jnp.int32)
         for count in range(UPSTREAM + 1):
 
             @pl.when(used == count)
             def _():
                 sources = [block] + [
-                    lists_ref[block * UPSTREAM + slot] for slot in range(count)
+                    lists_ref[sector, block, slot] for slot in range(count)
                 ]
                 work(block, [pl.multiple_of(s * block_rows, block_rows) for s in sources])
 
@@ -274,8 +277,8 @@
     return jnp.concatenate([ref[rows, pl.ds(s, block_rows)] for s in starts], axis=1)
 
 
-def forward_kernel(block_rows, head_dim, lists_ref, x_ref, gain_ref, wq_ref, wk_ref, wv_ref,
-                   wkt_ref, wvt_ref, wo_ref, normed_t_ref, q_ref, k_ref, v_ref, kt_ref, att_ref,
+def forward_kernel(block_rows, head_dim, sectors_ref, lists_ref, x_ref, gain_ref, wq_ref, wk_ref,
+                   wv_ref, wo_ref, normed_t_ref, q_ref, k_ref, v_ref, kt_ref, att_ref,
                    top_ref, inverse_ref, out_ref, normed_ref, vt_ref, rows_ref, sum_ref):
     row_count = x_ref.shape[0]
     quad = pl.program_id(0)
@@ -295,8 +298,8 @@
     q_ref[...] = contract(normed, wq_ref[...], 1, 0).astype(jnp.bfloat16)
     k_ref[...] = contract(normed, wk_ref[...], 1, 0).astype(jnp.bfloat16)
     v_ref[...] = contract(normed, wv_ref[...], 1, 0).astype(jnp.bfloat16)
-    kt_ref[...] = contract(wkt_ref[...], normed, 1, 1).astype(jnp.bfloat16)
-    vt_ref[...] = contract(wvt_ref[...], normed, 1, 1).astype(jnp.bfloat16)
+    kt_ref[...] = contract(wk_ref[...], normed, 0, 1).astype(jnp.bfloat16)
+    vt_ref[...] = contract(wv_ref[...], normed, 0, 1).astype(jnp.bfloat16)
 
     def work(block, starts):
         own = pl.ds(starts[0], block_rows)
@@ -325,7 +328,7 @@
             att_ref[lane, own] = joined.astype(jnp.bfloat16)
             rows_ref[own, lane] = joined.T.astype(jnp.bfloat16)
 
-    for_each_block(lists_ref, row_count // block_rows, block_rows, work)
+    for_each_block(sectors_ref, lists_ref, row_count // block_rows, block_rows, work)
     part = contract(rows_ref[...], wo_ref[...], 1, 0)
 
     @pl.when(quad == 0)
@@ -341,27 +344,27 @@
         out_ref[...] = sum_ref[...].astype(jnp.bfloat16)
 
 
-def forward(lists, rows, norm_gain, query_weight, key_weight, value_weight, out_weight, block_rows):
+def forward(sectors, adjacency, rows, norm_gain, query_weight, key_weight, value_weight, out_weight, block_rows):
     row_count, width = rows.shape
     head_dim = width // HEADS
     quad = QUAD * head_dim
     quads = width // quad
     stat_rows = row_count // block_rows * (QUAD // PAIR)
-    fixed = lambda *shape: pl.BlockSpec(shape, lambda p, lists: (0,) * len(shape))
-    across = lambda size: pl.BlockSpec((size, quad), lambda p, lists: (0, p))
-    down = lambda size: pl.BlockSpec((quad, size), lambda p, lists: (p, 0))
-    stat = pl.BlockSpec((1, stat_rows, PAIR * block_rows), lambda p, lists: (p, 0, 0))
+    fixed = lambda *shape: pl.BlockSpec(shape, lambda p, *lists: (0,) * len(shape))
+    across = lambda size: pl.BlockSpec((size, quad), lambda p, *lists: (0, p))
+    down = lambda size: pl.BlockSpec((quad, size), lambda p, *lists: (p, 0))
+    stat = pl.BlockSpec((1, stat_rows, PAIR * block_rows), lambda p, *lists: (p, 0, 0))
     flat = jax.ShapeDtypeStruct((row_count, width), jnp.bfloat16)
     turned = jax.ShapeDtypeStruct((width, row_count), jnp.bfloat16)
     stats = jax.ShapeDtypeStruct((quads, stat_rows, PAIR * block_rows), jnp.float32)
     return pl.pallas_call(
         lambda *refs: forward_kernel(block_rows, head_dim, *refs),
         grid_spec=pltpu.PrefetchScalarGridSpec(
-            num_scalar_prefetch=1,
+            num_scalar_prefetch=2,
             grid=(quads,),
             in_specs=[fixed(row_count, width), fixed(1, width)]
             + [across(width)] * 3
-            + [down(width)] * 3,
+            + [down(width)],
             out_specs=[fixed(width, row_count)]
             + [across(row_count)] * 3
             + [down(row_count)] * 2
@@ -382,14 +385,20 @@
             transcendentals=row_count * 4 * block_rows * HEADS,
         ),
         name="forward",
-    )(lists, rows, norm_gain.reshape(1, width), query_weight, key_weight, value_weight,
-      key_weight.T, value_weight.T, out_weight)
-
-
-def backward_kernel(block_rows, head_dim, lists_ref, cot_ref, wo_ref, normed_t_ref, q_ref, k_ref,
-                    v_ref, kt_ref, att_ref, top_ref, inverse_ref, gq_ref, gk_ref, gv_ref, sums_ref,
-                    ga_ref, gk_acc, gv_acc):
+    )(sectors, adjacency, rows, norm_gain.reshape(1, width), query_weight, key_weight, value_weight,
+      out_weight)
+
+
+def backward_kernel(block_rows, head_dim, which, last, sectors_ref, lists_ref, cot_ref, wo_ref,
+                    normed_t_ref, q_ref, k_ref, v_ref, kt_ref, att_ref, top_ref, inverse_ref, *refs):
+    if last:
+        x_ref, gain_ref, wq_ref, wk_ref, wv_ref, *refs = refs
+        before, refs = refs[: 3 * which], refs[3 * which :]
+        grad_ref, keep_ref, send_ref, gq_ref, gk_ref, gv_ref, ga_ref, gk_acc, gv_acc, sum_ref = refs
+    else:
+        gq_ref, gk_ref, gv_ref, whole_ref, ga_ref, gk_acc, gv_acc = refs
     row_count, width = cot_ref.shape
+    block_count = row_count // block_rows
     pair = PAIR * head_dim
     quad = QUAD * head_dim
     scale = head_dim ** (-0.5)
@@ -437,124 +446,156 @@
                         term = term.astype(jnp.bfloat16).astype(jnp.float32)
                     acc[rows, lane] += term
 
-    for_each_block(lists_ref, row_count // block_rows, block_rows, work)
+    for_each_block(sectors_ref, lists_ref, block_count, block_rows, work)
     gk_ref[...] = gk_acc[...].astype(jnp.bfloat16)
     gv_ref[...] = gv_acc[...].astype(jnp.bfloat16)
-    for i, ref in enumerate((gq_ref, gk_ref, gv_ref)):
-        sums_ref[i * width : (i + 1) * width, :] = contract(
-            normed_t_ref[...], ref[...], 1, 0
-        ).astype(jnp.bfloat16)
-    for i in range(width // quad):
-        start = 3 * width + i * quad
-        sums_ref[start : start + quad, :] = contract(
-            att_ref[...], cot_ref[:, i * quad : (i + 1) * quad], 1, 0
-        ).astype(jnp.bfloat16)
-
-
-def backward(lists, cotangent, out_weight, normed_t, queries, keys, values, keys_t, attended_t,
-             tops, inverses, block_rows, which):
+    products = [(normed_t_ref, ref, slice(None)) for ref in (gq_ref, gk_ref, gv_ref)]
+    products.append((att_ref, cot_ref, slice(which * quad, (which + 1) * quad)))
+    for i, (left, right, lanes) in enumerate(products):
+        terms = contract(left[...], right[:, lanes], 1, 0)
+        if not last:
+            whole_ref[i * width : (i + 1) * width, :] = terms
+            continue
+        apart = i ^ lax.axis_index("sample")
+
+        @pl.when(apart % 2 == 0)
+        def _():
+            keep_ref[apart // 2, :width] = terms
+
+        @pl.when(apart % 2 == 1)
+        def _():
+            send_ref[apart // 2, :width] = terms
+
+    if not last:
+        return
+    chunk = min(row_count, 256)
+    sum_ref[...] = jnp.zeros_like(sum_ref)
+    for start in range(0, row_count, chunk):
+        rows = slice(start, start + chunk)
+        scaled, inverse, _ = normalize(x_ref[rows, :], gain_ref[...])
+        grad_normed = jnp.zeros((chunk, width), jnp.float32)
+        for i in range(width // quad):
+            parts = before[3 * i : 3 * i + 3] if i < which else (gq_ref, gk_ref, gv_ref)
+            for ref, weight_ref in zip(parts, (wq_ref, wk_ref, wv_ref)):
+                grad_normed += contract(
+                    ref[rows, :], weight_ref[:, i * quad : (i + 1) * quad], 1, 1
+                )
+        sum_ref[...] += jnp.sum(grad_normed * scaled, axis=0, keepdims=True)
+        grad_scaled = grad_normed * gain_ref[...]
+        grad_input = inverse * (
+            grad_scaled
+            - jnp.mean(grad_scaled, axis=-1, keepdims=True)
+            - scaled * jnp.mean(grad_scaled * scaled, axis=-1, keepdims=True)
+        )
+        grad_ref[rows, :] = (cot_ref[rows, :].astype(jnp.float32) + grad_input).astype(jnp.bfloat16)
+    for ref in (keep_ref, send_ref):
+        for i in range(width // quad):
+            start = width + i * GAIN_ROWS
+            ref[:, start : start + GAIN_ROWS, :] = jnp.broadcast_to(
+                sum_ref[:, i * quad : (i + 1) * quad], (ref.shape[0], GAIN_ROWS, quad)
+            )
+
+
+def backward(sectors, adjacency, cotangent, out_weight, normed_t, queries, keys, values, keys_t,
+             attended_t, tops, inverses, block_rows, which, *ending):
     row_count, width = cotangent.shape
+    block_count = row_count // block_rows
     head_dim = width // HEADS
     quad = QUAD * head_dim
-    fixed = lambda *shape: pl.BlockSpec(shape, lambda i, lists: (0,) * len(shape))
-    across = pl.BlockSpec((row_count, quad), lambda i, lists: (0, which))
-    down = lambda size: pl.BlockSpec((quad, size), lambda i, lists: (which, 0))
-    stat = pl.BlockSpec((1,) + tops.shape[1:], lambda i, lists: (which, 0, 0))
+    fixed = lambda *shape: pl.BlockSpec(shape, lambda i, *lists: (0,) * len(shape))
+    across = pl.BlockSpec((row_count, quad), lambda i, *lists: (0, which))
+    down = lambda size: pl.BlockSpec((quad, size), lambda i, *lists: (which, 0))
+    stat = pl.BlockSpec((1,) + tops.shape[1:], lambda i, *lists: (which, 0, 0))
     part = jax.ShapeDtypeStruct((row_count, quad), jnp.bfloat16)
+    halves = (2, width + GAIN_ROWS * (width // quad), quad)
+    scratch = [
+        pltpu.VMEM((row_count, quad), jnp.bfloat16),
+        pltpu.VMEM((row_count, quad), jnp.float32),
+        pltpu.VMEM((row_count, quad), jnp.float32),
+    ]
+    if ending:
+        out_shape = [jax.ShapeDtypeStruct((row_count, width), jnp.bfloat16)]
+        out_shape += [jax.ShapeDtypeStruct(halves, jnp.float32)] * 2
+        scratch = [pltpu.VMEM((row_count, quad), jnp.bfloat16)] * 3 + scratch
+        scratch.append(pltpu.VMEM((1, width), jnp.float32))
+    else:
+        out_shape = [part] * 3 + [jax.ShapeDtypeStruct((4 * width, quad), jnp.float32)]
     return pl.pallas_call(
-        lambda *refs: backward_kernel(block_rows, head_dim, *refs),
+        lambda *refs: backward_kernel(block_rows, head_dim, which, bool(ending), *refs),
         grid_spec=pltpu.PrefetchScalarGridSpec(
-            num_scalar_prefetch=1,
+            num_scalar_prefetch=2,
             grid=(1,),
             in_specs=[fixed(row_count, width), down(width), fixed(width, row_count)]
             + [across] * 3
-            + [down(row_count)] * 2
-            + [stat] * 2,
-            out_specs=[fixed(row_count, quad)] * 3 + [fixed(4 * width, quad)],
-            scratch_shapes=[
-                pltpu.VMEM((row_count, quad), jnp.bfloat16),
-                pltpu.VMEM((row_count, quad), jnp.float32),
-                pltpu.VMEM((row_count, quad), jnp.float32),
-            ],
+            + [down(row_count), fixed(width, row_count)]
+            + [stat] * 2
+            + [fixed(*array.shape) for array in ending],
+            out_specs=[fixed(*struct.shape) for struct in out_shape],
+            scratch_shapes=scratch,
         ),
-        out_shape=[part] * 3 + [jax.ShapeDtypeStruct((4 * width, quad), jnp.bfloat16)],
+        out_shape=out_shape,
         compiler_params=pltpu.CompilerParams(vmem_limit_bytes=VMEM_LIMIT),
         cost_estimate=pl.CostEstimate(
-            flops=10 * row_count * width * quad + 80 * row_count * block_rows * quad,
+            flops=10 * row_count * width * quad
+            + 80 * row_count * block_rows * quad
+            + 6 * row_count * width * width * bool(ending),
             bytes_accessed=14 * row_count * width,
             transcendentals=row_count * 4 * block_rows * QUAD,
         ),
         name="backward",
-    )(lists, cotangent, out_weight, normed_t, queries, keys, values, keys_t, attended_t, tops,
-      inverses)
-
-
-def finish_kernel(quads, x_ref, cot_ref, gain_ref, wq_ref, wk_ref, wv_ref, *refs):
-    grad_refs, (out_ref, sum_ref) = refs[:-2], refs[-2:]
-    scaled, inverse, _ = normalize(x_ref[...], gain_ref[...])
-    quad = grad_refs[0].shape[1]
-    grad_normed = jnp.zeros(x_ref.shape, jnp.float32)
-    for i in range(quads):
-        lanes = slice(i * quad, (i + 1) * quad)
-        for j, weight_ref in enumerate((wq_ref, wk_ref, wv_ref)):
-            grad_normed += contract(grad_refs[3 * i + j][...], weight_ref[:, lanes], 1, 1)
-
-    @pl.when(pl.program_id(0) == 0)
-    def _():
-        sum_ref[...] = jnp.zeros_like(sum_ref)
-
-    sum_ref[...] += jnp.sum(grad_normed * scaled, axis=0, keepdims=True)
-    grad_scaled = grad_normed * gain_ref[...]
-    grad_input = inverse * (
-        grad_scaled
-        - jnp.mean(grad_scaled, axis=-1, keepdims=True)
-        - scaled * jnp.mean(grad_scaled * scaled, axis=-1, keepdims=True)
-    )
-    out_ref[...] = (cot_ref[...].astype(jnp.float32) + grad_input).astype(jnp.bfloat16)
-
-
-def finish(rows, cotangent, norm_gain, query_weight, key_weight, value_weight, grads):
-    row_count, width = rows.shape
-    quad = grads[0].shape[1]
-    step = min(row_count, 256)
-    fixed = lambda *shape: pl.BlockSpec(shape, lambda i: (0,) * len(shape))
-    by_row = lambda size: pl.BlockSpec((step, size), lambda i: (i, 0))
+    )(sectors, adjacency, cotangent, out_weight, normed_t, queries, keys, values, keys_t, attended_t,
+      tops, inverses, *ending)
+
+
+def swap(tensor, axis):
+    return lax.all_to_all(tensor, axis, split_axis=0, concat_axis=0, tiled=True)
+
+
+def across(tensor, axis, distance):
+    size = lax.axis_size(axis)
+    return lax.ppermute(tensor, axis, [(i, i ^ distance) for i in range(size)])
+
+
+def across(tensor, axis, distance):
+    size = lax.axis_size(axis)
+    return lax.ppermute(tensor, axis, [(i, i ^ distance) for i in range(size)])
+
+
+def reduce_halves(keep, send, width):
+    sums = keep + across(send, "sample", 1)
+    sums = sums[0] + across(sums[1].astype(jnp.bfloat16), "sample", 2).astype(jnp.float32)
+    sums = lax.psum(sums, "turb")
+    gain = sums[width:].reshape(-1, GAIN_ROWS, sums.shape[1])[:, 0].reshape(width)
+    own = sums[:width].astype(jnp.bfloat16)
+    both = [own, across(own, "sample", 2)]
+    return both + [across(part, "sample", 1) for part in both], gain
+
+
+def place_kernel(whole_ref, *refs):
+    (*parts, query_ref, key_ref, value_ref, out_ref, all_ref) = refs
+    own = lax.axis_index("sample")
+    width, quad = parts[0].shape
+    for i, ref in enumerate(parts):
+        all_ref[own ^ ((i % 2) * 2 + i // 2)] = ref[...].astype(jnp.float32)
+    for i, ref in enumerate((query_ref, key_ref, value_ref, out_ref)):
+        ref[:, :quad] = whole_ref[i * width : (i + 1) * width, :]
+        ref[:, quad:] = all_ref[i]
+
+
+def place_sums(whole, parts):
+    width, quad = parts[0].shape
     return pl.pallas_call(
-        lambda *refs: finish_kernel(width // quad, *refs),
-        grid=(row_count // step,),
-        in_specs=[by_row(width)] * 2
-        + [fixed(1, width)]
-        + [fixed(width, width)] * 3
-        + [by_row(quad)] * len(grads),
-        out_specs=[by_row(width), fixed(1, width)],
-        out_shape=[
-            jax.ShapeDtypeStruct((row_count, width), jnp.bfloat16),
-            jax.ShapeDtypeStruct((1, width), jnp.float32),
-        ],
+        place_kernel,
+        in_specs=[pl.BlockSpec(memory_space=pltpu.VMEM)] * (1 + len(parts)),
+        out_specs=[pl.BlockSpec(memory_space=pltpu.VMEM)] * 4,
+        out_shape=[jax.ShapeDtypeStruct((width, 2 * quad), jnp.float32)] * 4,
+        scratch_shapes=[pltpu.VMEM((4, width, quad), jnp.float32)],
         compiler_params=pltpu.CompilerParams(vmem_limit_bytes=VMEM_LIMIT),
         cost_estimate=pl.CostEstimate(
-            flops=6 * row_count * width * width,
-            bytes_accessed=16 * row_count * width,
-            transcendentals=0,
+            flops=0, bytes_accessed=28 * width * width, transcendentals=0
         ),
-        name="finish",
-    )(rows, cotangent, norm_gain.reshape(1, width), query_weight, key_weight, value_weight, *grads)
-
-
-def swap(tensor, axis):
-    return lax.all_to_all(tensor, axis, split_axis=0, concat_axis=0, tiled=True)
-
-
-def reduce_sums(sums):
-    row_count, width = sums.shape
-    for axis in ("sample", "turb"):
-        size = lax.axis_size(axis)
-        sums = swap(sums.reshape(size, -1, width), axis)
-        sums = jnp.sum(sums.astype(jnp.float32), axis=0).astype(jnp.bfloat16)
-    for axis in ("turb", "sample"):
-        size = lax.axis_size(axis)
-        sums = swap(jnp.broadcast_to(sums, (size,) + sums.shape), axis).reshape(-1, width)
-    return sums.astype(jnp.float32)
+        name="place",
+    )(whole, *parts)
 
 
 def by_sample(
@@ -570,47 +611,27 @@
 ):
     sample_count, block_rows, width = inflow.shape
     row_count = lax.axis_size("turb") * block_rows
-    quads = HEADS // QUAD
-    quad = width // quads
-    sector = lax.dynamic_index_in_dim(sectors, lax.axis_index("turb"), keepdims=False)
-    lists = lax.dynamic_index_in_dim(adjacency, sector, keepdims=False).reshape(-1)
-
     rows = swap(inflow, "turb")
     rows, cotangent = lax.optimization_barrier((rows, cotangent))
     rows = rows.reshape(row_count, width)
     grad_rows = swap(cotangent, "turb").reshape(row_count, width)
     *saved, layer_rows = forward(
-        lists, rows, norm_gain, query_weight, key_weight, value_weight, out_weight, block_rows
+        sectors, adjacency, rows, norm_gain, query_weight, key_weight, value_weight, out_weight,
+        block_rows,
     )
     layer_output = swap(layer_rows.reshape(inflow.shape), "turb")
-    grads, sums = [], []
-    for which in range(quads):
-        *part, terms = backward(lists, grad_rows, out_weight, *saved, block_rows, which)
-        grads += part
-        sums.append(reduce_sums(terms))
-    grad_rows, sum_gain = finish(
-        rows, grad_rows, norm_gain, query_weight, key_weight, value_weight, grads
+    *grads, whole = backward(
+        sectors, adjacency, grad_rows, out_weight, *saved, block_rows, 0
+    )
+    whole = lax.psum(whole, ("sample", "turb"))
+    grad_rows, keep, send = backward(
+        sectors, adjacency, grad_rows, out_weight, *saved, block_rows, 1,
+        rows, norm_gain.reshape(1, width), query_weight, key_weight, value_weight, *grads,
     )
     grad_inflow = swap(grad_rows.reshape(inflow.shape), "turb")
-    sum_gain = jnp.sum(lax.all_gather(sum_gain.reshape(width), ("sample", "turb")), axis=0)
-    projections = [
-        jnp.concatenate([part[i * width : (i + 1) * width] for part in sums], axis=1)
-        for i in range(3)
-    ]
-    sum_out = jnp.concatenate(
-        [
-            jnp.concatenate(
-                [
-                    part[3 * width + i * quad : 3 * width + (i + 1) * quad]
-                    for i in range(quads)
-                ],
-                axis=1,
-            )
-            for part in sums
-        ],
-        axis=0,
-    )
-    return (layer_output, grad_inflow, *projections, sum_out, sum_gain)
+    parts, sum_gain = reduce_halves(keep, send, width)
+    sums = place_sums(whole, parts)
+    return (layer_output, grad_inflow, *sums, sum_gain)
 
 
 def solution(mesh):
@@ -628,7 +649,7 @@
 
     def plan(*args):
         sample_count = args[0].shape[0]
-        if sample_count == mesh.shape["turb"]:
+        if sample_count == mesh.shape["turb"] and mesh.shape["sample"] == 4:
             return by_sample(*args)
         return on_device(*args)
 

time: 313 us -> 359 us (1.15)
  waiting for transfers between devices: 51.3 us -> 225 us
  blocking collectives: 147 us -> 33.1 us
  starting transfers between devices: 34.4 us -> 17.9 us
  between operations: 2.75 us -> 14.1 us
  other arithmetic: 8 us -> 3.18 us
  local copies, waits for them, and re-layouts: 10.6 us -> 6.47 us
    psum x0 -> x2, waiting for transfers between devices: none -> 211 us  [the longest x1 130 us: by_sample(): whole = lax.psum(whole, ('sample', 'turb'))]
    all_gather x1 -> x0, blocking collectives: 67.2 us -> none  [by_sample(): lax.all_gather(sum_gain.reshape(width), ('sample', 'turb'))]
    all_to_all x9 -> x3, waiting for transfers between devices: 51.3 us -> 3.37 us  [swap(): return lax.all_to_all(tensor, axis, split_axis=0, concat_axis=0, tiled=True)]
    all_to_all x3 -> x1, blocking collectives: 80 us -> 33.1 us  [swap(): return lax.all_to_all(tensor, axis, split_axis=0, concat_axis=0, tiled=True)]
    all_to_all x9 -> x3, starting transfers between devices: 34.4 us -> 12.5 us  [swap(): return lax.all_to_all(tensor, axis, split_axis=0, concat_axis=0, tiled=True)]
    ppermute x0 -> x5, waiting for transfers between devices: none -> 9.75 us  [across(): return lax.ppermute(tensor, axis, [(i, i ^ distance) for i in range(size)])]
    ppermute x0 -> x5, starting transfers between devices: none -> 5.35 us  [across(): return lax.ppermute(tensor, axis, [(i, i ^ distance) for i in range(size)])]
    concatenate x3 -> x0, other arithmetic: 3.89 us -> none  [the longest x2 2.76 us: by_sample(): jnp.concatenate([part[i * width:(i + 1) * width] for part in sums], axis=1)]
  transfers between devices with their start and end apart: 9 -> 10, of which waited for: 7 -> 6; matrix products, arithmetic and copies ran while one was open for 3% -> 2% of each run, Pallas kernels for 18% -> 15%
where the time goes in v4:
time: 359 us; the launch traced here: 358 us
  waiting for transfers between devices  225 us (63%)
  Pallas kernels  58.2 us (16%)
  blocking collectives  33.1 us (9%)
  starting transfers between devices  17.9 us (5%)
  between operations  14.1 us (4%)
  local copies, waits for them, and re-layouts  6.47 us (2%)
    psum x1, waiting for transfers between devices, by_sample(): whole = lax.psum(whole, ('sample', 'turb'))  130 us
    psum x1, waiting for transfers between devices, reduce_halves(): sums = lax.psum(sums, 'turb')  81.4 us
    all_to_all x1, blocking collectives, swap(): return lax.all_to_all(tensor, axis, split_axis=0, concat_axis=0, tiled=True)  33.1 us
    pallas_call x2, Pallas kernels, backward(): pl.pallas_call(lambda *refs: backward_kernel(block_rows, head_dim, which,...  32.6 us
    pallas_call x1, Pallas kernels, forward(): pl.pallas_call(lambda *refs: forward_kernel(block_rows, head_dim, *refs),...  21.5 us
    all_to_all x3, starting transfers between devices, swap(): return lax.all_to_all(tensor, axis, split_axis=0, concat_axis=0, tiled=True)  12.5 us
    ppermute x5, waiting for transfers between devices, across(): return lax.ppermute(tensor, axis, [(i, i ^ distance) for i in range(size)])  9.75 us
  transfers between devices with their start and end apart: 10, of which 6 were waited for; matrix products, arithmetic and copies ran while one was open for 2% of the time, Pallas kernels for 15%

profile of v4, /device:TPU:0, one launch (start us, length us, event | category | flops | bytes accessed | tf_op | source)
XLA Modules:
  0.0 358.3 jit_solution(1873782523265253071)
XLA Ops:
  7.2 33.1 %all_to_all.20 = bf16[8,128,512]{2,1,0:T(8,128)(2,1)} all-to-all(bf16[8,128,512]{2,1,0:T(8,128)(2,1)} %param.9), channel_id=1, replica_groups=mesh['sample'=4,'turb'=8] {'turb'}, dimensions={0} | all-to-all | bytes 2097152 | tf_op jit(solution)/shard_map/all_to_all | solution.py:551
  40.3 0.0 copy-start.5
  40.3 3.7 %all-to-all-start.2 = ((bf16[8,128,512]{2,1,0:T(8,128)(2,1)}), bf16[8,128,512]{2,1,0:T(8,128)(2,1)S(1)}, u32[]{:S(2)}, u32[]{:S(2)}) async-start(bf16[8,128,512]{2,1,0:T(8,128)(2,1)} %param.10), calls=%async_computation.2 | async-start | bytes 2097152 | tf_op jit(solution)/shard_map/all_to_all | solution.py:551
  44.0 0.0 copy-done.5
  44.0 0.7 copy.16.refs_1_
  44.8 21.5 %forward.1 = (bf16[512,1024]{1,0:T(8,128)(2,1)}, bf16[1024,512]{1,0:T(8,128)(2,1)}, bf16[1024,512]{1,0:T(8,128)(2,1)}, bf16[1024,512]{1,0:T(8,128)(2,1)}, bf16[5...) custom-call(s32[8]{0:T(128)} %refs_0_.5, ...), custom_call_target="tpu_custom_call" | custom-call | flops 5368709120 | bytes 10485760 | tf_op jit(solution)/shard_map/forward/pallas_call | solution.py:360
  66.3 3.4 all-to-all-done.2
  69.6 0.0 copy-start.1
  69.6 3.8 %all-to-all-start.1 = ((bf16[8,128,512]{2,1,0:T(8,128)(2,1)}), bf16[8,128,512]{2,1,0:T(8,128)(2,1)S(1)}, u32[]{:S(2)}, u32[]{:S(2)}) async-start(bf16[8,128,512]{2,1,0:T(8,128)(2,1)} %bitcast.15), calls=%async_computation.1 | async-start | bytes 2097152 | tf_op jit(solution)/shard_map/all_to_all | solution.py:551
  73.4 0.0 copy-done.1
  73.4 13.6 %backward.2 = (bf16[1024,256]{1,0:T(8,128)(2,1)}, bf16[1024,256]{1,0:T(8,128)(2,1)}, bf16[1024,256]{1,0:T(8,128)(2,1)}, f32[2048,256]{1,0:T(8,128)}) custom-call(s32[8]{0:T(128)} %refs_0_.5, s32[8,8,3]{2,1,0:T(8,128)} %copy.16.refs_1_, bf16[1024,512]{1,0:T(8,128)(2,1)} %bitcast.18, bf16[512,512]{1,0:T(8,128)(2,1)} %refs_3_.3, ...), custom_call_target="tpu_custom_call" | custom-call | flops 4026531840 | bytes 7340032 | tf_op jit(solution)/shard_map/backward/pallas_call | solution.py:523
  87.0 19.0 %backward.3 = (bf16[1024,512]{1,0:T(8,128)(2,1)}, f32[2,528,256]{2,1,0:T(8,128)}, f32[2,528,256]{2,1,0:T(8,128)}) custom-call(s32[8]{0:T(128)} %refs_0_.5, s32[8,8,3]{2,1,0:T(8,128)} %copy.16.refs_1_, bf16[1024,512]{1,0:T(8,128)(2,1)} %bitcast.19, bf16[512,512]{1,0:T(8,128)(2,1)} %refs_3_.3, bf16[512,1024]{1,0:T(8,128)(2,1)} %get-tuple-element.32.refs_4_, ...), custom_call_target="tpu_custom_call" | custom-call | flops 5637144576 | bytes 7340032 | tf_op jit(solution)/shard_map/backward/pallas_call | solution.py:523
  106.1 0.5 collective-permute-start
  106.5 2.5 collective-permute-done
  109.1 1.4 add.10
  110.5 3.6 collective-permute-start.1
  114.1 0.0 all-to-all-done.1
  114.1 5.0 %all-to-all-start.3 = ((bf16[8,128,512]{2,1,0:T(8,128)(2,1)}), bf16[8,128,512]{2,1,0:T(8,128)(2,1)S(1)}, u32[]{:S(2)}, u32[]{:S(2)}) async-start(bf16[8,128,512]{2,1,0:T(8,128)(2,1)} %bitcast.14), calls=%async_computation.3 | async-start | bytes 2097152 | tf_op jit(solution)/shard_map/all_to_all | solution.py:551
  119.1 0.0 all-reduce.5.cloned.1.call-start
  119.1 2.1 collective-permute-done.1
  121.2 1.8 fusion
  123.0 0.0 all-reduce.5.cloned.1.call-update
  123.0 0.0 all-reduce.3.cloned.1.call-start
  123.1 0.7 all-reduce.3.cloned.1.call-update
  123.8 81.4 %all-reduce.5.cloned.1.call-done = f32[528,256]{1,0:T(8,128)} async-done(((f32[528,256]{1,0:T(8,128)}), f32[528,256]{1,0:T(8,128)}) %all-reduce.5.cloned.1.call-update) | async-done | bytes 540688 | tf_op jit(solution)/shard_map/psum | solution.py:567
  205.2 1.1 slice.35.refs_0_
  206.2 0.0 copy-start
  206.2 1.3 collective-permute-start.2
  207.6 0.0 collective-permute-start.3
  207.6 5.1 %collective-permute-done.2.refs_1_ = bf16[512,256]{1,0:T(8,128)(2,1)S(1)} collective-permute-done((bf16[512,256]{1,0:T(8,128)(2,1)S(1)}, bf16[512,256]{1,0:T(8,128)(2,1)S(1)}, u32[]{:S(2)}, u32[]{:S(2)}) %collective-permute-start.2) | collective-permute-done | bytes 262176 | tf_op jit(solution)/shard_map/ppermute | solution.py:561
  212.7 0.0 copy-start.2
  212.7 0.0 collective-permute-start.4
  212.7 0.0 all-to-all-done.3
  212.7 0.7 slice_bitcast_fusion.1
  213.4 0.6 slice.26
  214.0 130.0 %all-reduce.3.cloned.1.call-done.whole_ref = f32[2048,256]{1,0:T(8,128)} async-done(((f32[2048,256]{1,0:T(8,128)}), f32[2048,256]{1,0:T(8,128)}) %all-reduce.3.cloned.1.call-update) | async-done | bytes 2097168 | tf_op jit(solution)/shard_map/psum | solution.py:626
  344.1 0.0 collective-permute-done.3.refs_2_
  344.1 0.0 copy-start.3
  344.1 0.0 collective-permute-done.4.refs_3_
  344.1 0.0 copy-done
  344.1 0.0 copy-done.2
  344.1 0.7 copy-done.3
  344.8 0.0 copy-start.4
  344.8 0.7 copy-done.4
  345.5 4.0 %place.1 = (f32[512,512]{1,0:T(8,128)}, f32[512,512]{1,0:T(8,128)}, f32[512,512]{1,0:T(8,128)}, f32[512,512]{1,0:T(8,128)}) custom-call(f32[2048,256]{1,0:T(8,128)} %all-reduce.3.cloned.1.call-done.whole_ref, bf16[512,256]{1,0:T(8,128)(2,1)} %copy-done, bf16[512,256]{1,0:T(8,128)(2,1)} %copy-done.2, bf16[512,256]{1,0:T(8,128)(2,1)} %copy-done.3, ...), custom_call_target="tpu_custom_call" | custom-call | bytes 7340032 | tf_op jit(solution)/shard_map/place/pallas_call | solution.py:587
  349.5 1.0 copy.23
  350.5 1.0 copy.24
  (1 shorter events, 0.0 us)
Async XLA Ops:
  40.3 3.7 %copy-start.5 = (s32[8,8,3]{1,0,2:T(8,128)S(1)}, s32[8,8,3]{1,0,2:T(8,128)}, u32[]{:S(2)}) copy-start(s32[8,8,3]{1,0,2:T(8,128)} %param.16) | copy-start | bytes 2308
  40.3 29.3 %all-to-all-start.2 = ((bf16[8,128,512]{2,1,0:T(8,128)(2,1)}), bf16[8,128,512]{2,1,0:T(8,128)(2,1)S(1)}, u32[]{:S(2)}, u32[]{:S(2)}) async-start(bf16[8,128,512]{2,1,0:T(8,128)(2,1)} %param.10), calls=%async_computation.2 | async-start | bytes 2097152 | tf_op jit(solution)/shard_map/all_to_all | solution.py:551
  69.6 3.8 %copy-start.1 = (bf16[8,128,512]{2,1,0:T(8,128)(2,1)}, bf16[8,128,512]{2,1,0:T(8,128)(2,1)S(1)}, u32[]{:S(2)}) copy-start(bf16[8,128,512]{2,1,0:T(8,128)(2,1)S(1)} %all-to-all-done.2) | copy-start | bytes 3145732
  69.6 44.4 %all-to-all-start.1 = ((bf16[8,128,512]{2,1,0:T(8,128)(2,1)}), bf16[8,128,512]{2,1,0:T(8,128)(2,1)S(1)}, u32[]{:S(2)}, u32[]{:S(2)}) async-start(bf16[8,128,512]{2,1,0:T(8,128)(2,1)} %bitcast.15), calls=%async_computation.1 | async-start | bytes 2097152 | tf_op jit(solution)/shard_map/all_to_all | solution.py:551
  106.1 3.0 collective-permute-start
  110.5 10.7 %collective-permute-start.1 = (bf16[528,256]{1,0:T(8,128)(2,1)S(1)}, bf16[528,256]{1,0:T(8,128)(2,1)}, u32[]{:S(2)}, u32[]{:S(2)}) collective-permute-start(bf16[528,256]{1,0:T(8,128)(2,1)S(1)} %fusion.1), channel_id=1, source_target_pairs={{0,16},{8,24},{16,0},{24,8},{1,17},{9,25},{17,1},{25,9},{2,18},{10... | collective-permute-start | bytes 811016 | tf_op jit(solution)/shard_map/ppermute | solution.py:561
  114.1 98.6 %all-to-all-start.3 = ((bf16[8,128,512]{2,1,0:T(8,128)(2,1)}), bf16[8,128,512]{2,1,0:T(8,128)(2,1)S(1)}, u32[]{:S(2)}, u32[]{:S(2)}) async-start(bf16[8,128,512]{2,1,0:T(8,128)(2,1)} %bitcast.14), calls=%async_computation.3 | async-start | bytes 2097152 | tf_op jit(solution)/shard_map/all_to_all | solution.py:551
  119.1 86.1 %all-reduce.5.cloned.1.call-start = ((), (), s32[]{:S(2)}) async-start(), calls=%async_computation.5 | async-start | bytes 1081344 | tf_op jit(solution)/shard_map/psum | solution.py:567
  123.0 221.1 %all-reduce.3.cloned.1.call-start = ((), (), s32[]{:S(2)}) async-start(), calls=%async_computation.4 | async-start | bytes 4194304 | tf_op jit(solution)/shard_map/psum | solution.py:626
  206.2 137.8 %copy-start = (bf16[512,256]{1,0:T(8,128)(2,1)}, bf16[512,256]{1,0:T(8,128)(2,1)S(1)}, u32[]{:S(2)}) copy-start(bf16[512,256]{1,0:T(8,128)(2,1)S(1)} %slice.35.refs_0_) | copy-start | bytes 786436
  206.2 6.4 %collective-permute-start.2 = (bf16[512,256]{1,0:T(8,128)(2,1)S(1)}, bf16[512,256]{1,0:T(8,128)(2,1)S(1)}, u32[]{:S(2)}, u32[]{:S(2)}) collective-permute-start(bf16[512,256]{1,0:T(8,128)(2,1)S(1)} %slice.35.refs_0_), channel_id=1, source_target_pairs={{0,16},{8,24},{16,0},{24,8},{1,17},{9,25},{17,1},{25,9},{2,18},{10... | collective-permute-start | bytes 786440 | tf_op jit(solution)/shard_map/ppermute | solution.py:561
  207.6 136.5 %collective-permute-start.3 = (bf16[512,256]{1,0:T(8,128)(2,1)S(1)}, bf16[512,256]{1,0:T(8,128)(2,1)S(1)}, u32[]{:S(2)}, u32[]{:S(2)}) collective-permute-start(bf16[512,256]{1,0:T(8,128)(2,1)S(1)} %slice.35.refs_0_), channel_id=1, source_target_pairs={{0,8},{8,0},{16,24},{24,16},{1,9},{9,1},{17,25},{25,17},{2,10},{10... | collective-permute-start | bytes 786440 | tf_op jit(solution)/shard_map/ppermute | solution.py:561
  212.7 131.4 %copy-start.2 = (bf16[512,256]{1,0:T(8,128)(2,1)}, bf16[512,256]{1,0:T(8,128)(2,1)S(1)}, u32[]{:S(2)}) copy-start(bf16[512,256]{1,0:T(8,128)(2,1)S(1)} %collective-permute-done.2.refs_1_) | copy-start | bytes 786436
  212.7 131.4 %collective-permute-start.4 = (bf16[512,256]{1,0:T(8,128)(2,1)S(1)}, bf16[512,256]{1,0:T(8,128)(2,1)S(1)}, u32[]{:S(2)}, u32[]{:S(2)}) collective-permute-start(bf16[512,256]{1,0:T(8,128)(2,1)S(1)} %collective-permute-done.2.refs_1_), channel_id=1, source_target_pairs={{0,8},{8,0},{16,24},{24,16},{1,9},{9,1},{17,25},{25,17},{2,10},{10... | collective-permute-start | bytes 786440 | tf_op jit(solution)/shard_map/ppermute | solution.py:561
  344.1 0.7 copy-start.3
  344.8 0.7 copy-start.4
Sparse Core Ops, SparseCore 0:
  123.9 81.2 all-reduce.4
  211.4 132.6 all-reduce.2

commit v5 on v4

--- a/solution.py
+++ b/solution.py
@@ -225,7 +225,13 @@
 QUAD = 4
 LOG2_E = 1.4426950408889634
 VMEM_LIMIT = 58 * 2**20
-GAIN_ROWS = 8
+GAIN_ROWS = 4
+SAMPLES = 4
+TURBS = 8
+
+
+def turb_place(apart):
+    return (apart % 2) * 4 + (apart // 4) * 2 + (apart // 2) % 2
 
 
 def contract(left, right, left_dim, right_dim):
@@ -396,7 +402,7 @@
         before, refs = refs[: 3 * which], refs[3 * which :]
         grad_ref, keep_ref, send_ref, gq_ref, gk_ref, gv_ref, ga_ref, gk_acc, gv_acc, sum_ref = refs
     else:
-        gq_ref, gk_ref, gv_ref, whole_ref, ga_ref, gk_acc, gv_acc = refs
+        gq_ref, gk_ref, gv_ref, keep_ref, send_ref, ga_ref, gk_acc, gv_acc = refs
     row_count, width = cot_ref.shape
     block_count = row_count // block_rows
     pair = PAIR * head_dim
@@ -451,20 +457,27 @@
     gv_ref[...] = gv_acc[...].astype(jnp.bfloat16)
     products = [(normed_t_ref, ref, slice(None)) for ref in (gq_ref, gk_ref, gv_ref)]
     products.append((att_ref, cot_ref, slice(which * quad, (which + 1) * quad)))
+    own_sample, own_turb = lax.axis_index("sample"), lax.axis_index("turb")
+    share = width // TURBS
     for i, (left, right, lanes) in enumerate(products):
         terms = contract(left[...], right[:, lanes], 1, 0)
-        if not last:
-            whole_ref[i * width : (i + 1) * width, :] = terms
-            continue
-        apart = i ^ lax.axis_index("sample")
-
-        @pl.when(apart % 2 == 0)
+        apart = i ^ own_sample
+        first, second = (apart % 2, apart // 2) if last else (apart // 2, apart % 2)
+
+        def store(ref):
+            for turb in range(TURBS):
+                start = pl.multiple_of(second * width + turb_place(turb ^ own_turb) * share, share)
+                ref[pl.ds(start, share), :] = terms[turb * share : (turb + 1) * share].astype(
+                    ref.dtype
+                )
+
+        @pl.when(first == 0)
         def _():
-            keep_ref[apart // 2, :width] = terms
-
-        @pl.when(apart % 2 == 1)
+            store(keep_ref)
+
+        @pl.when(first == 1)
         def _():
-            send_ref[apart // 2, :width] = terms
+            store(send_ref)
 
     if not last:
         return
@@ -490,9 +503,9 @@
         grad_ref[rows, :] = (cot_ref[rows, :].astype(jnp.float32) + grad_input).astype(jnp.bfloat16)
     for ref in (keep_ref, send_ref):
         for i in range(width // quad):
-            start = width + i * GAIN_ROWS
-            ref[:, start : start + GAIN_ROWS, :] = jnp.broadcast_to(
-                sum_ref[:, i * quad : (i + 1) * quad], (ref.shape[0], GAIN_ROWS, quad)
+            start = 2 * width + i * GAIN_ROWS
+            ref[start : start + GAIN_ROWS, :] = jnp.broadcast_to(
+                sum_ref[:, i * quad : (i + 1) * quad], (GAIN_ROWS, quad)
             )
 
 
@@ -507,7 +520,7 @@
     down = lambda size: pl.BlockSpec((quad, size), lambda i, *lists: (which, 0))
     stat = pl.BlockSpec((1,) + tops.shape[1:], lambda i, *lists: (which, 0, 0))
     part = jax.ShapeDtypeStruct((row_count, quad), jnp.bfloat16)
-    halves = (2, width + GAIN_ROWS * (width // quad), quad)
+    gain_rows = GAIN_ROWS * (width // quad)
     scratch = [
         pltpu.VMEM((row_count, quad), jnp.bfloat16),
         pltpu.VMEM((row_count, quad), jnp.float32),
@@ -515,11 +528,13 @@
     ]
     if ending:
         out_shape = [jax.ShapeDtypeStruct((row_count, width), jnp.bfloat16)]
-        out_shape += [jax.ShapeDtypeStruct(halves, jnp.float32)] * 2
+        out_shape += [jax.ShapeDtypeStruct((2 * width + gain_rows, quad), jnp.float32)] * 2
         scratch = [pltpu.VMEM((row_count, quad), jnp.bfloat16)] * 3 + scratch
         scratch.append(pltpu.VMEM((1, width), jnp.float32))
     else:
-        out_shape = [part] * 3 + [jax.ShapeDtypeStruct((4 * width, quad), jnp.float32)]
+        out_shape = [part] * 3 + [
+            jax.ShapeDtypeStruct((2 * width, quad), dtype) for dtype in (jnp.float32, jnp.bfloat16)
+        ]
     return pl.pallas_call(
         lambda *refs: backward_kernel(block_rows, head_dim, which, bool(ending), *refs),
         grid_spec=pltpu.PrefetchScalarGridSpec(
@@ -561,41 +576,73 @@
     return lax.ppermute(tensor, axis, [(i, i ^ distance) for i in range(size)])
 
 
-def reduce_halves(keep, send, width):
-    sums = keep + across(send, "sample", 1)
-    sums = sums[0] + across(sums[1].astype(jnp.bfloat16), "sample", 2).astype(jnp.float32)
-    sums = lax.psum(sums, "turb")
-    gain = sums[width:].reshape(-1, GAIN_ROWS, sums.shape[1])[:, 0].reshape(width)
-    own = sums[:width].astype(jnp.bfloat16)
-    both = [own, across(own, "sample", 2)]
-    return both + [across(part, "sample", 1) for part in both], gain
-
-
-def place_kernel(whole_ref, *refs):
+def reduce_sums(early, late, width):
+    quad = early[0].shape[1]
+    wide = jnp.float32
+
+    def pack(gain):
+        high = gain.astype(jnp.bfloat16)
+        low = (gain - high.astype(wide)).astype(jnp.bfloat16)
+        return jnp.concatenate([high, low, jnp.zeros((16 - 2 * gain.shape[0], quad), jnp.bfloat16)])
+
+    def unpack(rows, count):
+        return rows[:count].astype(wide) + rows[count : 2 * count].astype(wide)
+
+    keep, arrived = early
+    first = keep + arrived.astype(wide)
+    first = first[:width] + across(first[width:], "sample", 1)
+    keep, arrived = late
+    second = keep + arrived
+    gain = second[2 * width :: GAIN_ROWS]
+    count = gain.shape[0]
+    arrived = across(
+        jnp.concatenate([second[width : 2 * width].astype(jnp.bfloat16), pack(gain)]), "sample", 2
+    )
+    second = second[:width] + arrived[:width].astype(wide)
+    gain = gain + unpack(arrived[width:], count)
+    for distance in (1, 4, 2):
+        half = first.shape[0] // 2
+        halves = [part[half:].astype(jnp.bfloat16) for part in (first, second)]
+        arrived = across(jnp.concatenate(halves + [pack(gain)]), "turb", distance)
+        first = first[:half] + arrived[:half].astype(wide)
+        second = second[:half] + arrived[half : 2 * half].astype(wide)
+        gain = gain + unpack(arrived[2 * half :], count)
+    total = jnp.stack([first, second]).astype(jnp.bfloat16)[None]
+    for distance in (2, 4, 1):
+        total = jnp.concatenate([total, across(total, "turb", distance)])
+    both = [total, across(total, "sample", 2)]
+    return both + [across(part, "sample", 1) for part in both], gain.reshape(width)
+
+
+def place_kernel(*refs):
     (*parts, query_ref, key_ref, value_ref, out_ref, all_ref) = refs
-    own = lax.axis_index("sample")
-    width, quad = parts[0].shape
+    own_sample, own_turb = lax.axis_index("sample"), lax.axis_index("turb")
+    turbs, quads, share, quad = parts[0].shape
     for i, ref in enumerate(parts):
-        all_ref[own ^ ((i % 2) * 2 + i // 2)] = ref[...].astype(jnp.float32)
+        product = own_sample ^ ((i % 2) * 2 + i // 2)
+        for apart in range(turbs):
+            rows = pl.ds(pl.multiple_of((apart ^ own_turb) * share, share), share)
+            for j in range(quads):
+                all_ref[product, rows, j * quad : (j + 1) * quad] = ref[
+                    turb_place(apart), j
+                ].astype(jnp.float32)
     for i, ref in enumerate((query_ref, key_ref, value_ref, out_ref)):
-        ref[:, :quad] = whole_ref[i * width : (i + 1) * width, :]
-        ref[:, quad:] = all_ref[i]
-
-
-def place_sums(whole, parts):
-    width, quad = parts[0].shape
+        ref[...] = all_ref[i]
+
+
+def place_sums(parts, width):
     return pl.pallas_call(
         place_kernel,
-        in_specs=[pl.BlockSpec(memory_space=pltpu.VMEM)] * (1 + len(parts)),
+        in_specs=[pl.BlockSpec(memory_space=pltpu.VMEM)] * len(parts),
         out_specs=[pl.BlockSpec(memory_space=pltpu.VMEM)] * 4,
-        out_shape=[jax.ShapeDtypeStruct((width, 2 * quad), jnp.float32)] * 4,
-        scratch_shapes=[pltpu.VMEM((4, width, quad), jnp.float32)],
+        out_shape=[jax.ShapeDtypeStruct((width, width), jnp.float32)] * 4,
+        scratch_shapes=[pltpu.VMEM((4, width, width), jnp.float32)],
         compiler_params=pltpu.CompilerParams(vmem_limit_bytes=VMEM_LIMIT),
         cost_estimate=pl.CostEstimate(
-            flops=0, bytes_accessed=28 * width * width, transcendentals=0
+            flops=0, bytes_accessed=24 * width * width, transcendentals=0
         ),
         name="place",
-    )(whole, *parts)
+    )(*parts)
 
 
 def by_sample(
@@ -620,17 +667,18 @@
         block_rows,
     )
     layer_output = swap(layer_rows.reshape(inflow.shape), "turb")
-    *grads, whole = backward(
+    *grads, keep, send = backward(
         sectors, adjacency, grad_rows, out_weight, *saved, block_rows, 0
     )
-    whole = lax.psum(whole, ("sample", "turb"))
+    early = (keep, across(send, "sample", 2))
     grad_rows, keep, send = backward(
         sectors, adjacency, grad_rows, out_weight, *saved, block_rows, 1,
         rows, norm_gain.reshape(1, width), query_weight, key_weight, value_weight, *grads,
     )
+    late = (keep, across(send, "sample", 1))
     grad_inflow = swap(grad_rows.reshape(inflow.shape), "turb")
-    parts, sum_gain = reduce_halves(keep, send, width)
-    sums = place_sums(whole, parts)
+    parts, sum_gain = reduce_sums(early, late, width)
+    sums = place_sums(parts, width)
     return (layer_output, grad_inflow, *sums, sum_gain)
 
 
@@ -649,7 +697,7 @@
 
     def plan(*args):
         sample_count = args[0].shape[0]
-        if sample_count == mesh.shape["turb"] and mesh.shape["sample"] == 4:
+        if sample_count == mesh.shape["turb"] == TURBS and mesh.shape["sample"] == SAMPLES:
             return by_sample(*args)
         return on_device(*args)
 

time: 359 us -> 222 us (0.62)
  waiting for transfers between devices: 225 us -> 88.7 us
  between operations: 14.1 us -> 0.9 us
  starting transfers between devices: 17.9 us -> 26.7 us
    psum x2 -> x0, waiting for transfers between devices: 211 us -> none  [the longest x1 130 us: by_sample(): whole = lax.psum(whole, ('sample', 'turb'))]
    ppermute x5 -> x13, waiting for transfers between devices: 9.75 us -> 85.2 us  [across(): return lax.ppermute(tensor, axis, [(i, i ^ distance) for i in range(size)])]
    ppermute x5 -> x13, starting transfers between devices: 5.35 us -> 13.7 us  [across(): return lax.ppermute(tensor, axis, [(i, i ^ distance) for i in range(size)])]
  transfers between devices with their start and end apart: 10 -> 16, of which waited for: 6 -> 11; matrix products, arithmetic and copies ran while one was open for 2% -> 3% of each run, Pallas kernels for 15% -> 10%
where the time goes in v5:
time: 222 us; the launch traced here: 221 us
  waiting for transfers between devices  88.7 us (40%)
  Pallas kernels  61.1 us (28%)
  blocking collectives  33.1 us (15%)
  starting transfers between devices  26.7 us (12%)
  local copies, waits for them, and re-layouts  6.21 us (3%)
  other arithmetic  4.33 us (2%)
    ppermute x13, waiting for transfers between devices, across(): return lax.ppermute(tensor, axis, [(i, i ^ distance) for i in range(size)])  85.2 us
    pallas_call x2, Pallas kernels, backward(): pl.pallas_call(lambda *refs: backward_kernel(block_rows, head_dim, which,...  35.8 us
    all_to_all x1, blocking collectives, swap(): return lax.all_to_all(tensor, axis, split_axis=0, concat_axis=0, tiled=True)  33.1 us
    pallas_call x1, Pallas kernels, forward(): pl.pallas_call(lambda *refs: forward_kernel(block_rows, head_dim, *refs),...  21.4 us
    ppermute x13, starting transfers between devices, across(): return lax.ppermute(tensor, axis, [(i, i ^ distance) for i in range(size)])  13.7 us
    all_to_all x3, starting transfers between devices, swap(): return lax.all_to_all(tensor, axis, split_axis=0, concat_axis=0, tiled=True)  13 us
    unnamed x20, local copies, waits for them, and re-layouts  4.79 us
  transfers between devices with their start and end apart: 16, of which 11 were waited for; matrix products, arithmetic and copies ran while one was open for 3% of the time, Pallas kernels for 10%

profile of v5, /device:TPU:0, one launch (start us, length us, event | category | flops | bytes accessed | tf_op | source)
XLA Modules:
  0.0 221.0 jit_solution(4157778315565792246)
XLA Ops:
  0.6 33.1 %all_to_all.20 = bf16[8,128,512]{2,1,0:T(8,128)(2,1)} all-to-all(bf16[8,128,512]{2,1,0:T(8,128)(2,1)} %param.9), channel_id=1, replica_groups=mesh['sample'=4,'turb'=8] {'turb'}, dimensions={0} | all-to-all | bytes 2097152 | tf_op jit(solution)/shard_map/all_to_all | solution.py:566
  33.8 0.0 copy-start.6
  33.8 3.7 %all-to-all-start.2 = ((bf16[8,128,512]{2,1,0:T(8,128)(2,1)}), bf16[8,128,512]{2,1,0:T(8,128)(2,1)S(1)}, u32[]{:S(2)}, u32[]{:S(2)}) async-start(bf16[8,128,512]{2,1,0:T(8,128)(2,1)} %param.10), calls=%async_computation.2 | async-start | bytes 2097152 | tf_op jit(solution)/shard_map/all_to_all | solution.py:566
  37.5 0.0 copy-done.6
  37.5 0.7 copy.16.refs_1_
  38.2 21.4 %forward.1 = (bf16[512,1024]{1,0:T(8,128)(2,1)}, bf16[1024,512]{1,0:T(8,128)(2,1)}, bf16[1024,512]{1,0:T(8,128)(2,1)}, bf16[1024,512]{1,0:T(8,128)(2,1)}, bf16[5...) custom-call(s32[8]{0:T(128)} %refs_0_.5, ...), custom_call_target="tpu_custom_call" | custom-call | flops 5368709120 | bytes 10485760 | tf_op jit(solution)/shard_map/forward/pallas_call | solution.py:366
  59.6 3.5 %all-to-all-done.2 = bf16[8,128,512]{2,1,0:T(8,128)(2,1)S(1)} async-done(((bf16[8,128,512]{2,1,0:T(8,128)(2,1)}), bf16[8,128,512]{2,1,0:T(8,128)(2,1)S(1)}, u32[]{:S(2)}, u32[]{:S(2)}) %all-to-all-start.2) | async-done | bytes 1048608 | tf_op jit(solution)/shard_map/all_to_all | solution.py:566
  63.1 0.0 copy-start.4
  63.1 1.0 copy-done.4
  64.1 16.2 %backward.2 = (bf16[1024,256]{1,0:T(8,128)(2,1)}, bf16[1024,256]{1,0:T(8,128)(2,1)}, bf16[1024,256]{1,0:T(8,128)(2,1)}, f32[1024,256]{1,0:T(8,128)}, bf16[1024,256]{1,0:T(8,128)(2,1)}) custom-call(s32[8]{0:T(128)} %refs_0_.5, s32[8,8,3]{2,1,0:T(8,128)} %copy.16.refs_1_, bf16[1024,512]{1,0:T(8,128)(2,1)} %bitcast.15, bf16[512,512]{1,0:T(8,128)(2,1)} %refs_3_.3, ...), custom_call_target="tpu_custom_call" | custom-call | flops 4026531840 | bytes 7340032 | tf_op jit(solution)/shard_map/backward/pallas_call | solution.py:538
  80.3 19.6 %backward.3 = (bf16[1024,512]{1,0:T(8,128)(2,1)}, f32[1032,256]{1,0:T(8,128)}, f32[1032,256]{1,0:T(8,128)}) custom-call(s32[8]{0:T(128)} %refs_0_.5, s32[8,8,3]{2,1,0:T(8,128)} %copy.16.refs_1_, bf16[1024,512]{1,0:T(8,128)(2,1)} %bitcast.16, bf16[512,512]{1,0:T(8,128)(2,1)} %refs_3_.3, bf16[512,1024]{1,0:T(8,128)(2,1)} %get-tuple-element.33.refs_4_, ...), custom_call_target="tpu_custom_call" | custom-call | flops 5637144576 | bytes 7340032 | tf_op jit(solution)/shard_map/backward/pallas_call | solution.py:538
  99.9 0.0 collective-permute-start.2
  99.9 0.0 copy-done.7
  99.9 2.7 %collective-permute-start = (bf16[1024,256]{1,0:T(8,128)(2,1)S(1)}, bf16[1024,256]{1,0:T(8,128)(2,1)S(1)}, u32[]{:S(2)}, u32[]{:S(2)}) collective-permute-start(bf16[1024,256]{1,0:T(8,128)(2,1)S(1)} %copy-done.7), channel_id=1, source_target_pairs={{0,16},{8,24},{16,0},{24,8},{1,17},{9,25},{17,1},{25,9},{2,18},{10... | collective-permute-start | bytes 1572872 | tf_op jit(solution)/shard_map/ppermute | solution.py:576
  102.7 12.5 %collective-permute-done = bf16[1024,256]{1,0:T(8,128)(2,1)S(1)} collective-permute-done((bf16[1024,256]{1,0:T(8,128)(2,1)S(1)}, bf16[1024,256]{1,0:T(8,128)(2,1)S(1)}, u32[]{:S(2)}, u32[]{:S(2)}) %collective-permute-start) | collective-permute-done | bytes 524320 | tf_op jit(solution)/shard_map/ppermute | solution.py:576
  115.2 0.0 copy-done.3
  115.2 0.1 convert_add_fusion
  115.3 0.8 slice.148
  116.1 0.0 collective-permute-start.1
  116.1 0.0 collective-permute-done.2
  116.1 0.5 copy-done.2
  116.6 0.1 add.56
  116.8 1.8 collective-permute-start.3
  118.7 5.2 %all-to-all-start.1 = ((bf16[8,128,512]{2,1,0:T(8,128)(2,1)}), bf16[8,128,512]{2,1,0:T(8,128)(2,1)S(1)}, u32[]{:S(2)}, u32[]{:S(2)}) async-start(bf16[8,128,512]{2,1,0:T(8,128)(2,1)} %bitcast.12), calls=%async_computation.1 | async-start | bytes 2097152 | tf_op jit(solution)/shard_map/all_to_all | solution.py:566
  123.8 0.0 collective-permute-done.1
  123.8 1.1 slice_add_fusion.1
  124.9 0.0 copy-start.1
  125.0 0.5 collective-permute-done.3
  125.4 1.0 slice_add_fusion
  126.5 0.0 copy-done.1
  126.5 0.8 subtract_convert_fusion.2
  127.2 0.2 concatenate.32
  127.4 3.4 %collective-permute-start.4 = (bf16[528,256]{1,0:T(8,128)(2,1)S(1)}, bf16[528,256]{1,0:T(8,128)(2,1)S(1)}, u32[]{:S(2)}, u32[]{:S(2)}) collective-permute-start(bf16[528,256]{1,0:T(8,128)(2,1)S(1)} %concatenate.32), channel_id=1, source_target_pairs={{0,1},{1,0},{2,3},{3,2},{4,5},{5,4},{6,7},{7,6},{8,9},{9,8},{10,11... | collective-permute-start | bytes 811016 | tf_op jit(solution)/shard_map/ppermute | solution.py:576
  130.8 11.5 %collective-permute-done.4 = bf16[528,256]{1,0:T(8,128)(2,1)S(1)} collective-permute-done((bf16[528,256]{1,0:T(8,128)(2,1)S(1)}, bf16[528,256]{1,0:T(8,128)(2,1)S(1)}, u32[]{:S(2)}, u32[]{:S(2)}) %collective-permute-start.4) | collective-permute-done | bytes 270368 | tf_op jit(solution)/shard_map/ppermute | solution.py:576
  142.3 1.0 slice_add_fusion.3
  143.4 0.2 concatenate.33
  143.6 1.3 collective-permute-start.5
  144.9 10.6 %collective-permute-done.5 = bf16[272,256]{1,0:T(8,128)(2,1)S(1)} collective-permute-done((bf16[272,256]{1,0:T(8,128)(2,1)S(1)}, bf16[272,256]{1,0:T(8,128)(2,1)S(1)}, u32[]{:S(2)}, u32[]{:S(2)}) %collective-permute-start.5) | collective-permute-done | bytes 139296 | tf_op jit(solution)/shard_map/ppermute | solution.py:576
  155.6 0.2 concatenate.34
  155.7 0.1 collective-permute-start.6
  155.8 4.3 %collective-permute-done.6 = bf16[144,256]{1,0:T(8,128)(2,1)S(1)} collective-permute-done((bf16[144,256]{1,0:T(8,128)(2,1)S(1)}, bf16[144,256]{1,0:T(8,128)(2,1)S(1)}, u32[]{:S(2)}, u32[]{:S(2)}) %collective-permute-start.6) | collective-permute-done | bytes 73760 | tf_op jit(solution)/shard_map/ppermute | solution.py:576
  160.2 0.1 collective-permute-start.7
  160.3 0.0 all-to-all-done.1
  160.3 4.1 %all-to-all-start.3 = ((bf16[8,128,512]{2,1,0:T(8,128)(2,1)}), bf16[8,128,512]{2,1,0:T(8,128)(2,1)S(1)}, u32[]{:S(2)}, u32[]{:S(2)}) async-start(bf16[8,128,512]{2,1,0:T(8,128)(2,1)} %bitcast.4), calls=%async_computation.3 | async-start | bytes 2097152 | tf_op jit(solution)/shard_map/all_to_all | solution.py:566
  164.4 0.1 collective-permute-done.7
  164.5 2.9 %collective-permute-start.8 = (bf16[2,2,64,256]{3,2,1,0:T(8,128)(2,1)S(1)}, bf16[2,2,64,256]{3,2,1,0:T(8,128)(2,1)S(1)}, u32[]{:S(2)}, u32[]{:S(2)}) collective-permute-start(bf16[2,2,64,256]{3,2,1,0:T(8,128)(2,1)S(1)} %pad_maximum_fusion.3), channel_id=1, source_target_pairs={{0,4},{1,5},{2,6},{3,7},{4,0},{5,1},{6,2},{7,3},{8,12},{9,13},{10,... | collective-permute-start | bytes 393224 | tf_op jit(solution)/shard_map/ppermute | solution.py:576
  167.4 27.5 %collective-permute-done.8 = bf16[2,2,64,256]{3,2,1,0:T(8,128)(2,1)S(1)} collective-permute-done((bf16[2,2,64,256]{3,2,1,0:T(8,128)(2,1)S(1)}, bf16[2,2,64,256]{3,2,1,0:T(8,128)(2,1)S(1)}, u32[]{:S(2)}, u32[]{:S(2)}) %collective-permute-start.8) | collective-permute-done | bytes 131104 | tf_op jit(solution)/shard_map/ppermute | solution.py:576
  195.0 1.3 collective-permute-start.9
  196.2 5.4 %collective-permute-done.9 = bf16[4,2,64,256]{3,2,1,0:T(8,128)(2,1)S(1)} collective-permute-done((bf16[4,2,64,256]{3,2,1,0:T(8,128)(2,1)S(1)}, bf16[4,2,64,256]{3,2,1,0:T(8,128)(2,1)S(1)}, u32[]{:S(2)}, u32[]{:S(2)}) %collective-permute-start.9) | collective-permute-done | bytes 262176 | tf_op jit(solution)/shard_map/ppermute | solution.py:576
  201.7 0.1 pad_maximum_fusion.refs_0_
  201.7 0.0 copy-start
  201.7 0.1 collective-permute-start.10
  201.8 0.1 collective-permute-start.11
  201.9 11.2 %collective-permute-done.10.refs_1_ = bf16[8,2,64,256]{3,2,1,0:T(8,128)(2,1)S(1)} collective-permute-done((bf16[8,2,64,256]{3,2,1,0:T(8,128)(2,1)S(1)}, bf16[8,2,64,256]{3,2,1,0:T(8,128)(2,1)S(1)}, u32[]{:S(2)}, u32[]{:S(2)}) %collective-permute-start.10) | collective-permute-done | bytes 524320 | tf_op jit(solution)/shard_map/ppermute | solution.py:576
  213.1 0.0 collective-permute-start.12
  213.1 0.6 copy.19
  213.8 0.0 all-to-all-done.3
  213.8 0.0 collective-permute-done.11.refs_2_
  213.8 1.4 collective-permute-done.12.refs_3_
  215.2 0.0 copy-done
  215.2 0.0 copy-done.5
  215.2 3.9 %place.1 = (f32[512,512]{1,0:T(8,128)}, f32[512,512]{1,0:T(8,128)}, f32[512,512]{1,0:T(8,128)}, f32[512,512]{1,0:T(8,128)}) custom-call(bf16[8,2,64,256]{3,2,1,0:T(8,128)(2,1)} %copy-done, bf16[8,2,64,256]{3,2,1,0:T(8,128)(2,1)} %copy-done.5, bf16[8,2,64,256]{3,2,1,0:T(8,128)(2,1)} %collective-permute-done.11.refs_2_, ...), custom_call_target="tpu_custom_call" | custom-call | bytes 6291456 | tf_op jit(solution)/shard_map/place/pallas_call | solution.py:634
  219.0 1.0 copy.22
  220.0 1.0 copy.23
  (23 shorter events, 0.3 us)
Async XLA Ops:
  33.8 3.7 %copy-start.6 = (s32[8,8,3]{1,0,2:T(8,128)S(1)}, s32[8,8,3]{1,0,2:T(8,128)}, u32[]{:S(2)}) copy-start(s32[8,8,3]{1,0,2:T(8,128)} %param.16) | copy-start | bytes 2308
  33.8 29.3 %all-to-all-start.2 = ((bf16[8,128,512]{2,1,0:T(8,128)(2,1)}), bf16[8,128,512]{2,1,0:T(8,128)(2,1)S(1)}, u32[]{:S(2)}, u32[]{:S(2)}) async-start(bf16[8,128,512]{2,1,0:T(8,128)(2,1)} %param.10), calls=%async_computation.2 | async-start | bytes 2097152 | tf_op jit(solution)/shard_map/all_to_all | solution.py:566
  63.1 1.0 copy-start.4
  80.3 19.6 %copy-start.7 = (bf16[1024,256]{1,0:T(8,128)(2,1)S(1)}, bf16[1024,256]{1,0:T(8,128)(2,1)}, u32[]{:S(2)}) copy-start(bf16[1024,256]{1,0:T(8,128)(2,1)} %get-tuple-element.46) | copy-start | bytes 1572868
  80.3 34.8 %copy-start.3 = (f32[1024,256]{1,0:T(8,128)S(1)}, f32[1024,256]{1,0:T(8,128)}, u32[]{:S(2)}) copy-start(f32[1024,256]{1,0:T(8,128)} %get-tuple-element.45) | copy-start | bytes 3145732
  99.9 16.2 %collective-permute-start.2 = (f32[1032,256]{1,0:T(8,128)}, f32[1032,256]{1,0:T(8,128)S(1)}, u32[]{:S(2)}, u32[]{:S(2)}) collective-permute-start(f32[1032,256]{1,0:T(8,128)} %get-tuple-element.48), channel_id=1, source_target_pairs={{0,8},{8,0},{16,24},{24,16},{1,9},{9,1},{17,25},{25,17},{2,10},{10... | collective-permute-start | bytes 3170312 | tf_op jit(solution)/shard_map/ppermute | solution.py:576
  99.9 15.2 %collective-permute-start = (bf16[1024,256]{1,0:T(8,128)(2,1)S(1)}, bf16[1024,256]{1,0:T(8,128)(2,1)S(1)}, u32[]{:S(2)}, u32[]{:S(2)}) collective-permute-start(bf16[1024,256]{1,0:T(8,128)(2,1)S(1)} %copy-done.7), channel_id=1, source_target_pairs={{0,16},{8,24},{16,0},{24,8},{1,17},{9,25},{17,1},{25,9},{2,18},{10... | collective-permute-start | bytes 1572872 | tf_op jit(solution)/shard_map/ppermute | solution.py:576
  115.2 1.4 copy-start.2
  116.1 7.7 %collective-permute-start.1 = (f32[512,256]{1,0:T(8,128)}, f32[512,256]{1,0:T(8,128)}, u32[]{:S(2)}, u32[]{:S(2)}) collective-permute-start(f32[512,256]{1,0:T(8,128)} %slice.148), channel_id=1, source_target_pairs={{0,8},{8,0},{16,24},{24,16},{1,9},{9,1},{17,25},{25,17},{2,10},{10... | collective-permute-start | bytes 1572872 | tf_op jit(solution)/shard_map/ppermute | solution.py:576
  116.8 8.6 %collective-permute-start.3 = (bf16[528,256]{1,0:T(8,128)(2,1)S(1)}, bf16[528,256]{1,0:T(8,128)(2,1)}, u32[]{:S(2)}, u32[]{:S(2)}) collective-permute-start(bf16[528,256]{1,0:T(8,128)(2,1)S(1)} %pad_maximum_fusion.1), channel_id=1, source_target_pairs={{0,16},{8,24},{16,0},{24,8},{1,17},{9,25},{17,1},{25,9},{2,18},{10... | collective-permute-start | bytes 811016 | tf_op jit(solution)/shard_map/ppermute | solution.py:576
  118.7 41.6 %all-to-all-start.1 = ((bf16[8,128,512]{2,1,0:T(8,128)(2,1)}), bf16[8,128,512]{2,1,0:T(8,128)(2,1)S(1)}, u32[]{:S(2)}, u32[]{:S(2)}) async-start(bf16[8,128,512]{2,1,0:T(8,128)(2,1)} %bitcast.12), calls=%async_computation.1 | async-start | bytes 2097152 | tf_op jit(solution)/shard_map/all_to_all | solution.py:566
  124.9 1.5 copy-start.1
  127.4 14.9 %collective-permute-start.4 = (bf16[528,256]{1,0:T(8,128)(2,1)S(1)}, bf16[528,256]{1,0:T(8,128)(2,1)S(1)}, u32[]{:S(2)}, u32[]{:S(2)}) collective-permute-start(bf16[528,256]{1,0:T(8,128)(2,1)S(1)} %concatenate.32), channel_id=1, source_target_pairs={{0,1},{1,0},{2,3},{3,2},{4,5},{5,4},{6,7},{7,6},{8,9},{9,8},{10,11... | collective-permute-start | bytes 811016 | tf_op jit(solution)/shard_map/ppermute | solution.py:576
  143.6 11.9 %collective-permute-start.5 = (bf16[272,256]{1,0:T(8,128)(2,1)S(1)}, bf16[272,256]{1,0:T(8,128)(2,1)S(1)}, u32[]{:S(2)}, u32[]{:S(2)}) collective-permute-start(bf16[272,256]{1,0:T(8,128)(2,1)S(1)} %concatenate.33), channel_id=1, source_target_pairs={{0,4},{1,5},{2,6},{3,7},{4,0},{5,1},{6,2},{7,3},{8,12},{9,13},{10,... | collective-permute-start | bytes 417800 | tf_op jit(solution)/shard_map/ppermute | solution.py:576
  155.7 4.4 %collective-permute-start.6 = (bf16[144,256]{1,0:T(8,128)(2,1)S(1)}, bf16[144,256]{1,0:T(8,128)(2,1)S(1)}, u32[]{:S(2)}, u32[]{:S(2)}) collective-permute-start(bf16[144,256]{1,0:T(8,128)(2,1)S(1)} %concatenate.34), channel_id=1, source_target_pairs={{0,2},{1,3},{2,0},{3,1},{4,6},{5,7},{6,4},{7,5},{8,10},{9,11},{10,... | collective-permute-start | bytes 221192 | tf_op jit(solution)/shard_map/ppermute | solution.py:576
  160.2 4.3 %collective-permute-start.7 = (bf16[1,2,64,256]{3,2,1,0:T(8,128)(2,1)S(1)}, bf16[1,2,64,256]{3,2,1,0:T(8,128)(2,1)S(1)}, u32[]{:S(2)}, u32[]{:S(2)}) collective-permute-start(bf16[1,2,64,256]{3,2,1,0:T(8,128)(2,1)S(1)} %pad_maximum_fusion.4), channel_id=1, source_target_pairs={{0,2},{1,3},{2,0},{3,1},{4,6},{5,7},{6,4},{7,5},{8,10},{9,11},{10,... | collective-permute-start | bytes 196616 | tf_op jit(solution)/shard_map/ppermute | solution.py:576
  160.3 53.5 %all-to-all-start.3 = ((bf16[8,128,512]{2,1,0:T(8,128)(2,1)}), bf16[8,128,512]{2,1,0:T(8,128)(2,1)S(1)}, u32[]{:S(2)}, u32[]{:S(2)}) async-start(bf16[8,128,512]{2,1,0:T(8,128)(2,1)} %bitcast.4), calls=%async_computation.3 | async-start | bytes 2097152 | tf_op jit(solution)/shard_map/all_to_all | solution.py:566
  164.5 30.4 %collective-permute-start.8 = (bf16[2,2,64,256]{3,2,1,0:T(8,128)(2,1)S(1)}, bf16[2,2,64,256]{3,2,1,0:T(8,128)(2,1)S(1)}, u32[]{:S(2)}, u32[]{:S(2)}) collective-permute-start(bf16[2,2,64,256]{3,2,1,0:T(8,128)(2,1)S(1)} %pad_maximum_fusion.3), channel_id=1, source_target_pairs={{0,4},{1,5},{2,6},{3,7},{4,0},{5,1},{6,2},{7,3},{8,12},{9,13},{10,... | collective-permute-start | bytes 393224 | tf_op jit(solution)/shard_map/ppermute | solution.py:576
  195.0 6.7 %collective-permute-start.9 = (bf16[4,2,64,256]{3,2,1,0:T(8,128)(2,1)S(1)}, bf16[4,2,64,256]{3,2,1,0:T(8,128)(2,1)S(1)}, u32[]{:S(2)}, u32[]{:S(2)}) collective-permute-start(bf16[4,2,64,256]{3,2,1,0:T(8,128)(2,1)S(1)} %pad_maximum_fusion.2), channel_id=1, source_target_pairs={{0,1},{1,0},{2,3},{3,2},{4,5},{5,4},{6,7},{7,6},{8,9},{9,8},{10,11... | collective-permute-start | bytes 786440 | tf_op jit(solution)/shard_map/ppermute | solution.py:576
  201.7 13.5 %copy-start = (bf16[8,2,64,256]{3,2,1,0:T(8,128)(2,1)}, bf16[8,2,64,256]{3,2,1,0:T(8,128)(2,1)S(1)}, u32[]{:S(2)}) copy-start(bf16[8,2,64,256]{3,2,1,0:T(8,128)(2,1)S(1)} %pad_maximum_fusion.refs_0_) | copy-start | bytes 1572868
  201.7 11.4 %collective-permute-start.10 = (bf16[8,2,64,256]{3,2,1,0:T(8,128)(2,1)S(1)}, bf16[8,2,64,256]{3,2,1,0:T(8,128)(2,1)S(1)}, u32[]{:S(2)}, u32[]{:S(2)}) collective-permute-start(bf16[8,2,64,256]{3,2,1,0:T(8,128)(2,1)S(1)} %pad_maximum_fusion.refs_0_), channel_id=1, source_target_pairs={{0,16},{8,24},{16,0},{24,8},{1,17},{9,25},{17,1},{25,9},{2,18},{10... | collective-permute-start | bytes 1572872 | tf_op jit(solution)/shard_map/ppermute | solution.py:576
  201.8 12.0 %collective-permute-start.11 = (bf16[8,2,64,256]{3,2,1,0:T(8,128)(2,1)S(1)}, bf16[8,2,64,256]{3,2,1,0:T(8,128)(2,1)}, u32[]{:S(2)}, u32[]{:S(2)}) collective-permute-start(bf16[8,2,64,256]{3,2,1,0:T(8,128)(2,1)S(1)} %pad_maximum_fusion.refs_0_), channel_id=1, source_target_pairs={{0,8},{8,0},{16,24},{24,16},{1,9},{9,1},{17,25},{25,17},{2,10},{10... | collective-permute-start | bytes 1572872 | tf_op jit(solution)/shard_map/ppermute | solution.py:576
  213.1 2.0 copy-start.5
  213.1 2.0 collective-permute-start.12

commit v6 on v5

--- a/solution.py
+++ b/solution.py
@@ -576,7 +576,7 @@
     return lax.ppermute(tensor, axis, [(i, i ^ distance) for i in range(size)])
 
 
-def reduce_sums(early, late, width):
+def reduce_sums(early, late, width, beside):
     quad = early[0].shape[1]
     wide = jnp.float32
 
@@ -608,14 +608,22 @@
         second = second[:half] + arrived[half : 2 * half].astype(wide)
         gain = gain + unpack(arrived[2 * half :], count)
     total = jnp.stack([first, second]).astype(jnp.bfloat16)[None]
+    total, beside = lax.optimization_barrier((total, beside))
     for distance in (2, 4, 1):
         total = jnp.concatenate([total, across(total, "turb", distance)])
     both = [total, across(total, "sample", 2)]
-    return both + [across(part, "sample", 1) for part in both], gain.reshape(width)
-
-
-def place_kernel(*refs):
-    (*parts, query_ref, key_ref, value_ref, out_ref, all_ref) = refs
+    both += [across(part, "sample", 1) for part in both]
+    return both, gain.reshape(width), beside
+
+
+def place_kernel(from_ref, from_grad_ref, *refs):
+    (*parts, to_ref, to_grad_ref, query_ref, key_ref, value_ref, out_ref, all_ref, sems) = refs
+    copies = [
+        pltpu.make_async_copy(from_ref, to_ref, sems.at[0]),
+        pltpu.make_async_copy(from_grad_ref, to_grad_ref, sems.at[1]),
+    ]
+    for copy in copies:
+        copy.start()
     own_sample, own_turb = lax.axis_index("sample"), lax.axis_index("turb")
     turbs, quads, share, quad = parts[0].shape
     for i, ref in enumerate(parts):
@@ -628,21 +636,29 @@
                 ].astype(jnp.float32)
     for i, ref in enumerate((query_ref, key_ref, value_ref, out_ref)):
         ref[...] = all_ref[i]
-
-
-def place_sums(parts, width):
+    for copy in copies:
+        copy.wait()
+
+
+def place_sums(rows, parts, width):
     return pl.pallas_call(
         place_kernel,
-        in_specs=[pl.BlockSpec(memory_space=pltpu.VMEM)] * len(parts),
-        out_specs=[pl.BlockSpec(memory_space=pltpu.VMEM)] * 4,
-        out_shape=[jax.ShapeDtypeStruct((width, width), jnp.float32)] * 4,
-        scratch_shapes=[pltpu.VMEM((4, width, width), jnp.float32)],
+        in_specs=[pl.BlockSpec(memory_space=pl.ANY)] * 2
+        + [pl.BlockSpec(memory_space=pltpu.VMEM)] * len(parts),
+        out_specs=[pl.BlockSpec(memory_space=pl.ANY)] * 2
+        + [pl.BlockSpec(memory_space=pltpu.VMEM)] * 4,
+        out_shape=[jax.ShapeDtypeStruct(array.shape, array.dtype) for array in rows]
+        + [jax.ShapeDtypeStruct((width, width), jnp.float32)] * 4,
+        scratch_shapes=[
+            pltpu.VMEM((4, width, width), jnp.float32),
+            pltpu.SemaphoreType.DMA((2,)),
+        ],
         compiler_params=pltpu.CompilerParams(vmem_limit_bytes=VMEM_LIMIT),
         cost_estimate=pl.CostEstimate(
             flops=0, bytes_accessed=24 * width * width, transcendentals=0
         ),
         name="place",
-    )(*parts)
+    )(*rows, *parts)
 
 
 def by_sample(
@@ -670,15 +686,19 @@
     *grads, keep, send = backward(
         sectors, adjacency, grad_rows, out_weight, *saved, block_rows, 0
     )
-    early = (keep, across(send, "sample", 2))
-    grad_rows, keep, send = backward(
+    early = across(send, "sample", 2)
+    *late, grad_rows = backward(
         sectors, adjacency, grad_rows, out_weight, *saved, block_rows, 1,
         rows, norm_gain.reshape(1, width), query_weight, key_weight, value_weight, *grads,
-    )
-    late = (keep, across(send, "sample", 1))
+    )[::-1]
+    late, grad_rows, early, layer_output = lax.optimization_barrier(
+        (late, grad_rows, early, layer_output)
+    )
+    send, second = late
+    late = (second, across(send, "sample", 1))
     grad_inflow = swap(grad_rows.reshape(inflow.shape), "turb")
-    parts, sum_gain = reduce_sums(early, late, width)
-    sums = place_sums(parts, width)
+    parts, sum_gain, grad_inflow = reduce_sums((keep, early), late, width, grad_inflow)
+    layer_output, grad_inflow, *sums = place_sums((layer_output, grad_inflow), parts, width)
     return (layer_output, grad_inflow, *sums, sum_gain)
 
 

time: 222 us -> 251 us (1.13)
  Pallas kernels: 61.1 us -> 126 us
  waiting for transfers between devices: 88.7 us -> 55.8 us
    pallas_call x1, Pallas kernels: 3.87 us -> 68.2 us  [place_sums(): pl.pallas_call(place_kernel, in_specs=[pl.BlockSpec(memory_space=pl.ANY)]...]
    ppermute x13, waiting for transfers between devices: 85.2 us -> 52.5 us  [across(): return lax.ppermute(tensor, axis, [(i, i ^ distance) for i in range(size)])]
    ppermute x13, starting transfers between devices: 13.7 us -> 9.88 us  [across(): return lax.ppermute(tensor, axis, [(i, i ^ distance) for i in range(size)])]
  transfers between devices with their start and end apart: 16 -> 16, of which waited for: 11 -> 9; matrix products, arithmetic and copies ran while one was open for 3% -> 3% of each run, Pallas kernels for 10% -> 23%
where the time goes in v6:
time: 251 us
  Pallas kernels  126 us (50%)
  waiting for transfers between devices  55.8 us (22%)
  blocking collectives  33.1 us (13%)
  starting transfers between devices  25.1 us (10%)
  other arithmetic  5.56 us (2%)
  local copies, waits for them, and re-layouts  4.31 us (2%)
    pallas_call x1, Pallas kernels, place_sums(): pl.pallas_call(place_kernel, in_specs=[pl.BlockSpec(memory_space=pl.ANY)]...  68.2 us
    ppermute x13, waiting for transfers between devices, across(): return lax.ppermute(tensor, axis, [(i, i ^ distance) for i in range(size)])  52.5 us
    pallas_call x2, Pallas kernels, backward(): pl.pallas_call(lambda *refs: backward_kernel(block_rows, head_dim, which,...  36.1 us
    all_to_all x1, blocking collectives, swap(): return lax.all_to_all(tensor, axis, split_axis=0, concat_axis=0, tiled=True)  33.1 us
    pallas_call x1, Pallas kernels, forward(): pl.pallas_call(lambda *refs: forward_kernel(block_rows, head_dim, *refs),...  21.7 us
    all_to_all x3, starting transfers between devices, swap(): return lax.all_to_all(tensor, axis, split_axis=0, concat_axis=0, tiled=True)  15.2 us
    ppermute x13, starting transfers between devices, across(): return lax.ppermute(tensor, axis, [(i, i ^ distance) for i in range(size)])  9.88 us
  transfers between devices with their start and end apart: 16, of which 9 were waited for; matrix products, arithmetic and copies ran while one was open for 3% of the time, Pallas kernels for 23%

profile of v6, /device:TPU:0, one launch (start us, length us, event | category | flops | bytes accessed | tf_op | source)
XLA Modules:
  0.0 250.9 jit_solution(3418069442325311776)
XLA Ops:
  0.6 33.1 %all_to_all.20 = bf16[8,128,512]{2,1,0:T(8,128)(2,1)} all-to-all(bf16[8,128,512]{2,1,0:T(8,128)(2,1)} %param.9), channel_id=1, replica_groups=mesh['sample'=4,'turb'=8] {'turb'}, dimensions={0} | all-to-all | bytes 2097152 | tf_op jit(solution)/shard_map/all_to_all | solution.py:566
  33.8 3.7 %all-to-all-start.1 = ((bf16[8,128,512]{2,1,0:T(8,128)(2,1)}), bf16[8,128,512]{2,1,0:T(8,128)(2,1)S(1)}, u32[]{:S(2)}, u32[]{:S(2)}) async-start(bf16[8,128,512]{2,1,0:T(8,128)(2,1)} %param.10), calls=%async_computation.1 | async-start | bytes 2097152 | tf_op jit(solution)/shard_map/all_to_all | solution.py:566
  37.5 0.0 copy-done.11
  37.5 0.7 copy.18.refs_1_
  38.2 21.7 %forward.1 = (bf16[512,1024]{1,0:T(8,128)(2,1)}, bf16[1024,512]{1,0:T(8,128)(2,1)}, bf16[1024,512]{1,0:T(8,128)(2,1)}, bf16[1024,512]{1,0:T(8,128)(2,1)}, bf16[5...) custom-call(s32[8]{0:T(128)} %refs_0_.5, ...), custom_call_target="tpu_custom_call" | custom-call | flops 5368709120 | bytes 10485760 | tf_op jit(solution)/shard_map/forward/pallas_call | solution.py:366
  59.9 3.2 %all-to-all-done.1 = bf16[8,128,512]{2,1,0:T(8,128)(2,1)S(1)} async-done(((bf16[8,128,512]{2,1,0:T(8,128)(2,1)}), bf16[8,128,512]{2,1,0:T(8,128)(2,1)S(1)}, u32[]{:S(2)}, u32[]{:S(2)}) %all-to-all-start.1) | async-done | bytes 1048608 | tf_op jit(solution)/shard_map/all_to_all | solution.py:566
  63.1 3.9 %all-to-all-start.2 = ((bf16[8,128,512]{2,1,0:T(8,128)(2,1)}), bf16[8,128,512]{2,1,0:T(8,128)(2,1)S(1)}, u32[]{:S(2)}, u32[]{:S(2)}) async-start(bf16[8,128,512]{2,1,0:T(8,128)(2,1)} %bitcast.17), calls=%async_computation.2 | async-start | bytes 2097152 | tf_op jit(solution)/shard_map/all_to_all | solution.py:566
  67.0 0.0 copy-done.4
  67.0 16.5 %backward.2 = (bf16[1024,256]{1,0:T(8,128)(2,1)}, bf16[1024,256]{1,0:T(8,128)(2,1)}, bf16[1024,256]{1,0:T(8,128)(2,1)}, f32[1024,256]{1,0:T(8,128)}, bf16[1024,256]{1,0:T(8,128)(2,1)}) custom-call(s32[8]{0:T(128)} %refs_0_.5, s32[8,8,3]{2,1,0:T(8,128)} %copy.18.refs_1_, bf16[1024,512]{1,0:T(8,128)(2,1)} %bitcast.15, bf16[512,512]{1,0:T(8,128)(2,1)} %refs_3_.3, ...), custom_call_target="tpu_custom_call" | custom-call | flops 4026531840 | bytes 7340032 | tf_op jit(solution)/shard_map/backward/pallas_call | solution.py:538
  83.5 1.2 collective-permute-start
  84.7 19.6 %backward.3 = (bf16[1024,512]{1,0:T(8,128)(2,1)}, f32[1032,256]{1,0:T(8,128)}, f32[1032,256]{1,0:T(8,128)}) custom-call(s32[8]{0:T(128)} %refs_0_.5, s32[8,8,3]{2,1,0:T(8,128)} %copy.18.refs_1_, bf16[1024,512]{1,0:T(8,128)(2,1)} %bitcast.16, bf16[512,512]{1,0:T(8,128)(2,1)} %refs_3_.3, bf16[512,1024]{1,0:T(8,128)(2,1)} %get-tuple-element.41.refs_4_, ...), custom_call_target="tpu_custom_call" | custom-call | flops 5637144576 | bytes 7340032 | tf_op jit(solution)/shard_map/backward/pallas_call | solution.py:538
  104.3 0.0 all-to-all-done.2.from_ref
  104.3 0.0 copy-start
  104.3 0.0 collective-permute-done
  104.3 0.0 copy-start.7
  104.4 0.2 collective-permute-start.2
  104.5 0.7 copy-done.7
  105.2 0.0 copy-done.5
  105.2 1.2 convert_add_fusion
  106.4 0.0 copy-done
  106.4 0.8 slice.148
  107.3 0.1 collective-permute-start.1
  107.3 0.0 collective-permute-done.2
  107.3 0.0 copy-done.3
  107.3 0.1 add.56
  107.6 1.1 collective-permute-start.3
  108.7 7.5 %all-to-all-start.3 = ((bf16[8,128,512]{2,1,0:T(8,128)(2,1)}), bf16[8,128,512]{2,1,0:T(8,128)(2,1)S(1)}, u32[]{:S(2)}, u32[]{:S(2)}) async-start(bf16[8,128,512]{2,1,0:T(8,128)(2,1)} %bitcast.12), calls=%async_computation.3 | async-start | bytes 2097152 | tf_op jit(solution)/shard_map/all_to_all | solution.py:566
  116.3 0.0 collective-permute-done.1
  116.3 1.1 slice_add_fusion.1
  117.4 0.0 copy-start.2
  117.4 0.0 collective-permute-done.3
  117.4 1.2 slice_add_fusion
  118.6 0.0 copy-done.2
  118.6 0.8 subtract_convert_fusion.2
  119.4 0.2 concatenate.32
  119.6 2.1 collective-permute-start.4
  121.6 13.3 %collective-permute-done.4 = bf16[528,256]{1,0:T(8,128)(2,1)S(1)} collective-permute-done((bf16[528,256]{1,0:T(8,128)(2,1)S(1)}, bf16[528,256]{1,0:T(8,128)(2,1)S(1)}, u32[]{:S(2)}, u32[]{:S(2)}) %collective-permute-start.4) | collective-permute-done | bytes 270368 | tf_op jit(solution)/shard_map/ppermute | solution.py:576
  134.9 1.0 slice_add_fusion.3
  136.0 0.2 concatenate.33
  136.1 1.5 collective-permute-start.5
  137.6 10.6 %collective-permute-done.5 = bf16[272,256]{1,0:T(8,128)(2,1)S(1)} collective-permute-done((bf16[272,256]{1,0:T(8,128)(2,1)S(1)}, bf16[272,256]{1,0:T(8,128)(2,1)S(1)}, u32[]{:S(2)}, u32[]{:S(2)}) %collective-permute-start.5) | collective-permute-done | bytes 139296 | tf_op jit(solution)/shard_map/ppermute | solution.py:576
  148.3 0.2 concatenate.34
  148.5 0.1 collective-permute-start.6
  148.6 4.3 %collective-permute-done.6 = bf16[144,256]{1,0:T(8,128)(2,1)S(1)} collective-permute-done((bf16[144,256]{1,0:T(8,128)(2,1)S(1)}, bf16[144,256]{1,0:T(8,128)(2,1)S(1)}, u32[]{:S(2)}, u32[]{:S(2)}) %collective-permute-start.6) | collective-permute-done | bytes 73760 | tf_op jit(solution)/shard_map/ppermute | solution.py:576
  152.9 0.0 all-to-all-done.3.from_grad_ref
  153.0 0.0 copy-start.1
  153.0 0.1 collective-permute-start.7
  153.0 4.3 %collective-permute-done.7 = bf16[1,2,64,256]{3,2,1,0:T(8,128)(2,1)S(1)} collective-permute-done((bf16[1,2,64,256]{3,2,1,0:T(8,128)(2,1)S(1)}, bf16[1,2,64,256]{3,2,1,0:T(8,128)(2,1)S(1)}, u32[]{:S(2)}, u32[]{:S(2)}) %collective-permute-start.7) | collective-permute-done | bytes 65568 | tf_op jit(solution)/shard_map/ppermute | solution.py:576
  157.3 0.4 collective-permute-start.8
  157.7 6.4 %collective-permute-done.8 = bf16[2,2,64,256]{3,2,1,0:T(8,128)(2,1)S(1)} collective-permute-done((bf16[2,2,64,256]{3,2,1,0:T(8,128)(2,1)S(1)}, bf16[2,2,64,256]{3,2,1,0:T(8,128)(2,1)S(1)}, u32[]{:S(2)}, u32[]{:S(2)}) %collective-permute-start.8) | collective-permute-done | bytes 131104 | tf_op jit(solution)/shard_map/ppermute | solution.py:576
  164.1 1.5 collective-permute-start.9
  165.6 4.9 %collective-permute-done.9 = bf16[4,2,64,256]{3,2,1,0:T(8,128)(2,1)S(1)} collective-permute-done((bf16[4,2,64,256]{3,2,1,0:T(8,128)(2,1)S(1)}, bf16[4,2,64,256]{3,2,1,0:T(8,128)(2,1)S(1)}, u32[]{:S(2)}, u32[]{:S(2)}) %collective-permute-start.9) | collective-permute-done | bytes 262176 | tf_op jit(solution)/shard_map/ppermute | solution.py:576
  170.6 0.0 copy-start.6
  170.6 1.8 collective-permute-start.10
  172.4 0.0 collective-permute-start.11
  172.4 7.5 %collective-permute-done.10.refs_1_ = bf16[8,2,64,256]{3,2,1,0:T(8,128)(2,1)S(1)} collective-permute-done((bf16[8,2,64,256]{3,2,1,0:T(8,128)(2,1)S(1)}, bf16[8,2,64,256]{3,2,1,0:T(8,128)(2,1)S(1)}, u32[]{:S(2)}, u32[]{:S(2)}) %collective-permute-start.10) | collective-permute-done | bytes 524320 | tf_op jit(solution)/shard_map/ppermute | solution.py:576
  179.8 0.0 collective-permute-start.12
  179.9 0.6 copy.19
  180.5 0.0 collective-permute-done.11.refs_2_
  180.5 1.3 collective-permute-done.12.refs_3_
  181.8 0.0 copy-done.1
  181.8 0.0 copy-done.6
  181.8 0.8 copy-done.10
  182.6 68.2 %place.1 = (bf16[8,128,512]{2,1,0:T(8,128)(2,1)}, bf16[8,128,512]{2,1,0:T(8,128)(2,1)}, f32[512,512]{1,0:T(8,128)}, f32[512,512]{1,0:T(8,128)}, f32[512,512]{1,0:T(8,128)}, /*index=5*/f32[512,512]{1,0:T(8,128)}) custom-call(bf16[8,128,512]{2,1,0:T(8,128)(2,1)} %copy-done, bf16[8,128,512]{2,1,0:T(8,128)(2,1)} %copy-done.1, bf16[8,2,64,256]{3,2,1,0:T(8,128)(2,1)} %copy-done.6, ...), custom_call_target="tpu_custom_call" | custom-call | bytes 6291456 | tf_op jit(solution)/shard_map/place/pallas_call | solution.py:644
  (32 shorter events, 0.3 us)
Async XLA Ops:
  33.8 3.7 %copy-start.11 = (s32[8,8,3]{1,0,2:T(8,128)S(1)}, s32[8,8,3]{1,0,2:T(8,128)}, u32[]{:S(2)}) copy-start(s32[8,8,3]{1,0,2:T(8,128)} %param.16) | copy-start | bytes 2308
  33.8 29.3 %all-to-all-start.1 = ((bf16[8,128,512]{2,1,0:T(8,128)(2,1)}), bf16[8,128,512]{2,1,0:T(8,128)(2,1)S(1)}, u32[]{:S(2)}, u32[]{:S(2)}) async-start(bf16[8,128,512]{2,1,0:T(8,128)(2,1)} %param.10), calls=%async_computation.1 | async-start | bytes 2097152 | tf_op jit(solution)/shard_map/all_to_all | solution.py:566
  63.1 3.9 %copy-start.4 = (bf16[8,128,512]{2,1,0:T(8,128)(2,1)}, bf16[8,128,512]{2,1,0:T(8,128)(2,1)S(1)}, u32[]{:S(2)}) copy-start(bf16[8,128,512]{2,1,0:T(8,128)(2,1)S(1)} %all-to-all-done.1) | copy-start | bytes 3145732
  63.1 41.2 %all-to-all-start.2 = ((bf16[8,128,512]{2,1,0:T(8,128)(2,1)}), bf16[8,128,512]{2,1,0:T(8,128)(2,1)S(1)}, u32[]{:S(2)}, u32[]{:S(2)}) async-start(bf16[8,128,512]{2,1,0:T(8,128)(2,1)} %bitcast.17), calls=%async_computation.2 | async-start | bytes 2097152 | tf_op jit(solution)/shard_map/all_to_all | solution.py:566
  83.5 20.8 %collective-permute-start = (bf16[1024,256]{1,0:T(8,128)(2,1)}, bf16[1024,256]{1,0:T(8,128)(2,1)S(1)}, u32[]{:S(2)}, u32[]{:S(2)}) collective-permute-start(bf16[1024,256]{1,0:T(8,128)(2,1)} %get-tuple-element.55), channel_id=1, source_target_pairs={{0,16},{8,24},{16,0},{24,8},{1,17},{9,25},{17,1},{25,9},{2,18},{10... | collective-permute-start | bytes 1572872 | tf_op jit(solution)/shard_map/ppermute | solution.py:576
  84.7 20.5 %copy-start.5 = (f32[1024,256]{1,0:T(8,128)S(1)}, f32[1024,256]{1,0:T(8,128)}, u32[]{:S(2)}) copy-start(f32[1024,256]{1,0:T(8,128)} %get-tuple-element.58) | copy-start | bytes 3145732
  104.3 2.1 copy-start
  104.3 0.8 copy-start.7
  104.4 3.0 %collective-permute-start.2 = (f32[1032,256]{1,0:T(8,128)}, f32[1032,256]{1,0:T(8,128)S(1)}, u32[]{:S(2)}, u32[]{:S(2)}) collective-permute-start(f32[1032,256]{1,0:T(8,128)} %get-tuple-element.61), channel_id=1, source_target_pairs={{0,8},{8,0},{16,24},{24,16},{1,9},{9,1},{17,25},{25,17},{2,10},{10... | collective-permute-start | bytes 3170312 | tf_op jit(solution)/shard_map/ppermute | solution.py:576
  105.2 2.2 copy-start.3
  107.3 9.0 %collective-permute-start.1 = (f32[512,256]{1,0:T(8,128)}, f32[512,256]{1,0:T(8,128)}, u32[]{:S(2)}, u32[]{:S(2)}) collective-permute-start(f32[512,256]{1,0:T(8,128)} %slice.148), channel_id=1, source_target_pairs={{0,8},{8,0},{16,24},{24,16},{1,9},{9,1},{17,25},{25,17},{2,10},{10... | collective-permute-start | bytes 1572872 | tf_op jit(solution)/shard_map/ppermute | solution.py:576
  107.6 9.8 %collective-permute-start.3 = (bf16[528,256]{1,0:T(8,128)(2,1)S(1)}, bf16[528,256]{1,0:T(8,128)(2,1)}, u32[]{:S(2)}, u32[]{:S(2)}) collective-permute-start(bf16[528,256]{1,0:T(8,128)(2,1)S(1)} %pad_maximum_fusion), channel_id=1, source_target_pairs={{0,16},{8,24},{16,0},{24,8},{1,17},{9,25},{17,1},{25,9},{2,18},{10... | collective-permute-start | bytes 811016 | tf_op jit(solution)/shard_map/ppermute | solution.py:576
  108.7 44.2 %all-to-all-start.3 = ((bf16[8,128,512]{2,1,0:T(8,128)(2,1)}), bf16[8,128,512]{2,1,0:T(8,128)(2,1)S(1)}, u32[]{:S(2)}, u32[]{:S(2)}) async-start(bf16[8,128,512]{2,1,0:T(8,128)(2,1)} %bitcast.12), calls=%async_computation.3 | async-start | bytes 2097152 | tf_op jit(solution)/shard_map/all_to_all | solution.py:566
  117.4 1.2 copy-start.2
  119.6 15.3 %collective-permute-start.4 = (bf16[528,256]{1,0:T(8,128)(2,1)S(1)}, bf16[528,256]{1,0:T(8,128)(2,1)S(1)}, u32[]{:S(2)}, u32[]{:S(2)}) collective-permute-start(bf16[528,256]{1,0:T(8,128)(2,1)S(1)} %concatenate.32), channel_id=1, source_target_pairs={{0,1},{1,0},{2,3},{3,2},{4,5},{5,4},{6,7},{7,6},{8,9},{9,8},{10,11... | collective-permute-start | bytes 811016 | tf_op jit(solution)/shard_map/ppermute | solution.py:576
  136.1 12.1 %collective-permute-start.5 = (bf16[272,256]{1,0:T(8,128)(2,1)S(1)}, bf16[272,256]{1,0:T(8,128)(2,1)S(1)}, u32[]{:S(2)}, u32[]{:S(2)}) collective-permute-start(bf16[272,256]{1,0:T(8,128)(2,1)S(1)} %concatenate.33), channel_id=1, source_target_pairs={{0,4},{1,5},{2,6},{3,7},{4,0},{5,1},{6,2},{7,3},{8,12},{9,13},{10,... | collective-permute-start | bytes 417800 | tf_op jit(solution)/shard_map/ppermute | solution.py:576
  148.5 4.4 %collective-permute-start.6 = (bf16[144,256]{1,0:T(8,128)(2,1)S(1)}, bf16[144,256]{1,0:T(8,128)(2,1)S(1)}, u32[]{:S(2)}, u32[]{:S(2)}) collective-permute-start(bf16[144,256]{1,0:T(8,128)(2,1)S(1)} %concatenate.34), channel_id=1, source_target_pairs={{0,2},{1,3},{2,0},{3,1},{4,6},{5,7},{6,4},{7,5},{8,10},{9,11},{10,... | collective-permute-start | bytes 221192 | tf_op jit(solution)/shard_map/ppermute | solution.py:576
  153.0 28.8 %copy-start.1 = (bf16[8,128,512]{2,1,0:T(8,128)(2,1)}, bf16[8,128,512]{2,1,0:T(8,128)(2,1)S(1)}, u32[]{:S(2)}) copy-start(bf16[8,128,512]{2,1,0:T(8,128)(2,1)S(1)} %all-to-all-done.3.from_grad_ref) | copy-start | bytes 3145732
  153.0 4.3 %collective-permute-start.7 = (bf16[1,2,64,256]{3,2,1,0:T(8,128)(2,1)S(1)}, bf16[1,2,64,256]{3,2,1,0:T(8,128)(2,1)S(1)}, u32[]{:S(2)}, u32[]{:S(2)}) collective-permute-start(bf16[1,2,64,256]{3,2,1,0:T(8,128)(2,1)S(1)} %pad_maximum_fusion.3), channel_id=1, source_target_pairs={{0,2},{1,3},{2,0},{3,1},{4,6},{5,7},{6,4},{7,5},{8,10},{9,11},{10,... | collective-permute-start | bytes 196616 | tf_op jit(solution)/shard_map/ppermute | solution.py:576
  157.3 6.8 %collective-permute-start.8 = (bf16[2,2,64,256]{3,2,1,0:T(8,128)(2,1)S(1)}, bf16[2,2,64,256]{3,2,1,0:T(8,128)(2,1)S(1)}, u32[]{:S(2)}, u32[]{:S(2)}) collective-permute-start(bf16[2,2,64,256]{3,2,1,0:T(8,128)(2,1)S(1)} %pad_maximum_fusion.2), channel_id=1, source_target_pairs={{0,4},{1,5},{2,6},{3,7},{4,0},{5,1},{6,2},{7,3},{8,12},{9,13},{10,... | collective-permute-start | bytes 393224 | tf_op jit(solution)/shard_map/ppermute | solution.py:576
  164.1 6.4 %collective-permute-start.9 = (bf16[4,2,64,256]{3,2,1,0:T(8,128)(2,1)S(1)}, bf16[4,2,64,256]{3,2,1,0:T(8,128)(2,1)S(1)}, u32[]{:S(2)}, u32[]{:S(2)}) collective-permute-start(bf16[4,2,64,256]{3,2,1,0:T(8,128)(2,1)S(1)} %pad_maximum_fusion.1), channel_id=1, source_target_pairs={{0,1},{1,0},{2,3},{3,2},{4,5},{5,4},{6,7},{7,6},{8,9},{9,8},{10,11... | collective-permute-start | bytes 786440 | tf_op jit(solution)/shard_map/ppermute | solution.py:576
  170.6 11.2 %copy-start.6 = (bf16[8,2,64,256]{3,2,1,0:T(8,128)(2,1)}, bf16[8,2,64,256]{3,2,1,0:T(8,128)(2,1)S(1)}, u32[]{:S(2)}) copy-start(bf16[8,2,64,256]{3,2,1,0:T(8,128)(2,1)S(1)} %constant_dynamic-update-slice_fusion.refs_0_) | copy-start | bytes 1572868
  170.6 9.2 %collective-permute-start.10 = (bf16[8,2,64,256]{3,2,1,0:T(8,128)(2,1)S(1)}, bf16[8,2,64,256]{3,2,1,0:T(8,128)(2,1)S(1)}, u32[]{:S(2)}, u32[]{:S(2)}) collective-permute-start(bf16[8,2,64,256]{3,2,1,0:T(8,128)(2,1)S(1)} %constant_dynamic-update-slice_fusion.refs_0_), channel_id=1, source_target_pairs={{0,16},{8,24},{16,0},{24,8},{1,17},{9,25},{17,1},{25,9},{2,18},{10... | collective-permute-start | bytes 1572872 | tf_op jit(solution)/shard_map/ppermute | solution.py:576
  172.4 8.1 %collective-permute-start.11 = (bf16[8,2,64,256]{3,2,1,0:T(8,128)(2,1)S(1)}, bf16[8,2,64,256]{3,2,1,0:T(8,128)(2,1)S(1)}, u32[]{:S(2)}, u32[]{:S(2)}) collective-permute-start(bf16[8,2,64,256]{3,2,1,0:T(8,128)(2,1)S(1)} %constant_dynamic-update-slice_fusion.refs_0_), channel_id=1, source_target_pairs={{0,8},{8,0},{16,24},{24,16},{1,9},{9,1},{17,25},{25,17},{2,10},{10... | collective-permute-start | bytes 1572872 | tf_op jit(solution)/shard_map/ppermute | solution.py:576
  179.8 1.9 copy-start.8
  179.8 1.9 collective-permute-start.12
  180.5 1.3 copy-start.9
  181.8 0.8 copy-start.10

commit v7 on v5

--- a/solution.py
+++ b/solution.py
@@ -225,7 +225,7 @@
 QUAD = 4
 LOG2_E = 1.4426950408889634
 VMEM_LIMIT = 58 * 2**20
-GAIN_ROWS = 4
+SUM_ROWS = 8
 SAMPLES = 4
 TURBS = 8
 
@@ -395,19 +395,22 @@
       out_weight)
 
 
-def backward_kernel(block_rows, head_dim, which, last, sectors_ref, lists_ref, cot_ref, wo_ref,
-                    normed_t_ref, q_ref, k_ref, v_ref, kt_ref, att_ref, top_ref, inverse_ref, *refs):
-    if last:
-        x_ref, gain_ref, wq_ref, wk_ref, wv_ref, *refs = refs
-        before, refs = refs[: 3 * which], refs[3 * which :]
-        grad_ref, keep_ref, send_ref, gq_ref, gk_ref, gv_ref, ga_ref, gk_acc, gv_acc, sum_ref = refs
-    else:
-        gq_ref, gk_ref, gv_ref, keep_ref, send_ref, ga_ref, gk_acc, gv_acc = refs
+def backward_kernel(block_rows, head_dim, which, sectors_ref, lists_ref, cot_ref, wo_ref, q_ref,
+                    k_ref, v_ref, kt_ref, top_ref, inverse_ref, gain_ref, before_ref, *refs):
+    late, refs = refs[:5], refs[5:]
+    (gq_ref, gk_ref, gv_ref, parts_ref, sum_ref, ga_ref, gk_acc, gv_acc, *held, sems) = refs
     row_count, width = cot_ref.shape
     block_count = row_count // block_rows
     pair = PAIR * head_dim
     quad = QUAD * head_dim
     scale = head_dim ** (-0.5)
+    own_lanes = slice(which * quad, (which + 1) * quad)
+    copies = []
+    for i, (ref, into) in enumerate(zip(late, held)):
+        source = ref if i < 2 else ref.at[:, own_lanes]
+        copies.append(pltpu.make_async_copy(source, into, sems.at[i]))
+        copies[-1].start()
+    normed_t_ref, att_ref, *weight_refs = held
     ga_ref[...] = contract(cot_ref[...], wo_ref[...], 1, 1).astype(jnp.bfloat16)
     gk_acc[...] = jnp.zeros_like(gk_acc)
     gv_acc[...] = jnp.zeros_like(gv_acc)
@@ -455,64 +458,34 @@
     for_each_block(sectors_ref, lists_ref, block_count, block_rows, work)
     gk_ref[...] = gk_acc[...].astype(jnp.bfloat16)
     gv_ref[...] = gv_acc[...].astype(jnp.bfloat16)
+    for copy in copies:
+        copy.wait()
     products = [(normed_t_ref, ref, slice(None)) for ref in (gq_ref, gk_ref, gv_ref)]
-    products.append((att_ref, cot_ref, slice(which * quad, (which + 1) * quad)))
+    products.append((att_ref, cot_ref, own_lanes))
     own_sample, own_turb = lax.axis_index("sample"), lax.axis_index("turb")
     share = width // TURBS
+    along = jnp.zeros((width, quad), jnp.float32)
     for i, (left, right, lanes) in enumerate(products):
         terms = contract(left[...], right[:, lanes], 1, 0)
+        if i < len(weight_refs):
+            along += terms * weight_refs[i][...].astype(jnp.float32)
         apart = i ^ own_sample
-        first, second = (apart % 2, apart // 2) if last else (apart // 2, apart % 2)
-
-        def store(ref):
-            for turb in range(TURBS):
-                start = pl.multiple_of(second * width + turb_place(turb ^ own_turb) * share, share)
-                ref[pl.ds(start, share), :] = terms[turb * share : (turb + 1) * share].astype(
-                    ref.dtype
-                )
-
-        @pl.when(first == 0)
-        def _():
-            store(keep_ref)
-
-        @pl.when(first == 1)
-        def _():
-            store(send_ref)
-
-    if not last:
-        return
-    chunk = min(row_count, 256)
-    sum_ref[...] = jnp.zeros_like(sum_ref)
-    for start in range(0, row_count, chunk):
-        rows = slice(start, start + chunk)
-        scaled, inverse, _ = normalize(x_ref[rows, :], gain_ref[...])
-        grad_normed = jnp.zeros((chunk, width), jnp.float32)
-        for i in range(width // quad):
-            parts = before[3 * i : 3 * i + 3] if i < which else (gq_ref, gk_ref, gv_ref)
-            for ref, weight_ref in zip(parts, (wq_ref, wk_ref, wv_ref)):
-                grad_normed += contract(
-                    ref[rows, :], weight_ref[:, i * quad : (i + 1) * quad], 1, 1
-                )
-        sum_ref[...] += jnp.sum(grad_normed * scaled, axis=0, keepdims=True)
-        grad_scaled = grad_normed * gain_ref[...]
-        grad_input = inverse * (
-            grad_scaled
-            - jnp.mean(grad_scaled, axis=-1, keepdims=True)
-            - scaled * jnp.mean(grad_scaled * scaled, axis=-1, keepdims=True)
-        )
-        grad_ref[rows, :] = (cot_ref[rows, :].astype(jnp.float32) + grad_input).astype(jnp.bfloat16)
-    for ref in (keep_ref, send_ref):
-        for i in range(width // quad):
-            start = 2 * width + i * GAIN_ROWS
-            ref[start : start + GAIN_ROWS, :] = jnp.broadcast_to(
-                sum_ref[:, i * quad : (i + 1) * quad], (GAIN_ROWS, quad)
-            )
+        low, high = apart % 2, apart // 2
+        first, second = (high, low) if which == 0 else (low, high)
+        for turb in range(TURBS):
+            start = pl.multiple_of(second * width + turb_place(turb ^ own_turb) * share, share)
+            parts_ref[first, pl.ds(start, share), :] = terms[turb * share : (turb + 1) * share]
+    ones = jnp.ones((SUM_ROWS, quad), jnp.bfloat16)
+    coarse = along.astype(jnp.bfloat16)
+    fine = (along - coarse.astype(jnp.float32)).astype(jnp.bfloat16)
+    total = (contract(ones, coarse, 1, 1) + contract(ones, fine, 1, 1)) / gain_ref[...]
+    sum_ref[...] = before_ref[...] + total
 
 
 def backward(sectors, adjacency, cotangent, out_weight, normed_t, queries, keys, values, keys_t,
-             attended_t, tops, inverses, block_rows, which, *ending):
+             attended_t, tops, inverses, norm_gain, query_weight, key_weight, value_weight, before,
+             block_rows, which):
     row_count, width = cotangent.shape
-    block_count = row_count // block_rows
     head_dim = width // HEADS
     quad = QUAD * head_dim
     fixed = lambda *shape: pl.BlockSpec(shape, lambda i, *lists: (0,) * len(shape))
@@ -520,46 +493,83 @@
     down = lambda size: pl.BlockSpec((quad, size), lambda i, *lists: (which, 0))
     stat = pl.BlockSpec((1,) + tops.shape[1:], lambda i, *lists: (which, 0, 0))
     part = jax.ShapeDtypeStruct((row_count, quad), jnp.bfloat16)
-    gain_rows = GAIN_ROWS * (width // quad)
-    scratch = [
-        pltpu.VMEM((row_count, quad), jnp.bfloat16),
-        pltpu.VMEM((row_count, quad), jnp.float32),
-        pltpu.VMEM((row_count, quad), jnp.float32),
-    ]
-    if ending:
-        out_shape = [jax.ShapeDtypeStruct((row_count, width), jnp.bfloat16)]
-        out_shape += [jax.ShapeDtypeStruct((2 * width + gain_rows, quad), jnp.float32)] * 2
-        scratch = [pltpu.VMEM((row_count, quad), jnp.bfloat16)] * 3 + scratch
-        scratch.append(pltpu.VMEM((1, width), jnp.float32))
-    else:
-        out_shape = [part] * 3 + [
-            jax.ShapeDtypeStruct((2 * width, quad), dtype) for dtype in (jnp.float32, jnp.bfloat16)
-        ]
+    sums = jax.ShapeDtypeStruct((2, 2 * width, quad), jnp.float32)
     return pl.pallas_call(
-        lambda *refs: backward_kernel(block_rows, head_dim, which, bool(ending), *refs),
+        lambda *refs: backward_kernel(block_rows, head_dim, which, *refs),
         grid_spec=pltpu.PrefetchScalarGridSpec(
             num_scalar_prefetch=2,
             grid=(1,),
-            in_specs=[fixed(row_count, width), down(width), fixed(width, row_count)]
+            in_specs=[fixed(row_count, width), down(width)]
             + [across] * 3
-            + [down(row_count), fixed(width, row_count)]
+            + [down(row_count)]
             + [stat] * 2
-            + [fixed(*array.shape) for array in ending],
-            out_specs=[fixed(*struct.shape) for struct in out_shape],
-            scratch_shapes=scratch,
+            + [fixed(1, width), fixed(SUM_ROWS, width)]
+            + [pl.BlockSpec(memory_space=pl.ANY)] * 5,
+            out_specs=[fixed(row_count, quad)] * 3
+            + [fixed(*sums.shape), fixed(SUM_ROWS, width)],
+            scratch_shapes=[
+                pltpu.VMEM((row_count, quad), jnp.bfloat16),
+                pltpu.VMEM((row_count, quad), jnp.float32),
+                pltpu.VMEM((row_count, quad), jnp.float32),
+            ]
+            + [pltpu.VMEM((width, row_count), jnp.bfloat16)] * 2
+            + [pltpu.VMEM((width, quad), jnp.bfloat16)] * 3
+            + [pltpu.SemaphoreType.DMA((5,))],
         ),
-        out_shape=out_shape,
+        out_shape=[part] * 3 + [sums, jax.ShapeDtypeStruct((SUM_ROWS, width), jnp.float32)],
         compiler_params=pltpu.CompilerParams(vmem_limit_bytes=VMEM_LIMIT),
         cost_estimate=pl.CostEstimate(
-            flops=10 * row_count * width * quad
-            + 80 * row_count * block_rows * quad
-            + 6 * row_count * width * width * bool(ending),
+            flops=10 * row_count * width * quad + 80 * row_count * block_rows * quad,
             bytes_accessed=14 * row_count * width,
             transcendentals=row_count * 4 * block_rows * QUAD,
         ),
         name="backward",
-    )(sectors, adjacency, cotangent, out_weight, normed_t, queries, keys, values, keys_t, attended_t,
-      tops, inverses, *ending)
+    )(sectors, adjacency, cotangent, out_weight, queries, keys, values, keys_t, tops, inverses,
+      norm_gain.reshape(1, width), before, normed_t, attended_t, query_weight, key_weight,
+      value_weight)
+
+
+def finish_kernel(quads, x_ref, cot_ref, gain_ref, wq_ref, wk_ref, wv_ref, *refs):
+    grad_refs, out_ref = refs[:-1], refs[-1]
+    scaled, inverse, _ = normalize(x_ref[...], gain_ref[...])
+    quad = grad_refs[0].shape[1]
+    grad_normed = jnp.zeros(x_ref.shape, jnp.float32)
+    for i in range(quads):
+        lanes = slice(i * quad, (i + 1) * quad)
+        for j, weight_ref in enumerate((wq_ref, wk_ref, wv_ref)):
+            grad_normed += contract(grad_refs[3 * i + j][...], weight_ref[:, lanes], 1, 1)
+    grad_scaled = grad_normed * gain_ref[...]
+    grad_input = inverse * (
+        grad_scaled
+        - jnp.mean(grad_scaled, axis=-1, keepdims=True)
+        - scaled * jnp.mean(grad_scaled * scaled, axis=-1, keepdims=True)
+    )
+    out_ref[...] = (cot_ref[...].astype(jnp.float32) + grad_input).astype(jnp.bfloat16)
+
+
+def finish(rows, cotangent, norm_gain, query_weight, key_weight, value_weight, grads):
+    row_count, width = rows.shape
+    quad = grads[0].shape[1]
+    step = min(row_count, 256)
+    fixed = lambda *shape: pl.BlockSpec(shape, lambda i: (0,) * len(shape))
+    by_row = lambda size: pl.BlockSpec((step, size), lambda i: (i, 0))
+    return pl.pallas_call(
+        lambda *refs: finish_kernel(width // quad, *refs),
+        grid=(row_count // step,),
+        in_specs=[by_row(width)] * 2
+        + [fixed(1, width)]
+        + [fixed(width, width)] * 3
+        + [by_row(quad)] * len(grads),
+        out_specs=by_row(width),
+        out_shape=jax.ShapeDtypeStruct((row_count, width), jnp.bfloat16),
+        compiler_params=pltpu.CompilerParams(vmem_limit_bytes=VMEM_LIMIT),
+        cost_estimate=pl.CostEstimate(
+            flops=6 * row_count * width * width,
+            bytes_accessed=16 * row_count * width,
+            transcendentals=0,
+        ),
+        name="finish",
+    )(rows, cotangent, norm_gain.reshape(1, width), query_weight, key_weight, value_weight, *grads)
 
 
 def swap(tensor, axis):
@@ -576,8 +586,8 @@
     return lax.ppermute(tensor, axis, [(i, i ^ distance) for i in range(size)])
 
 
-def reduce_sums(early, late, width):
-    quad = early[0].shape[1]
+def reduce_sums(early, late, width, beside):
+    quad = early[0].shape[-1]
     wide = jnp.float32
 
     def pack(gain):
@@ -588,15 +598,14 @@
     def unpack(rows, count):
         return rows[:count].astype(wide) + rows[count : 2 * count].astype(wide)
 
-    keep, arrived = early
-    first = keep + arrived.astype(wide)
+    parts, arrived = early
+    first = parts[0] + arrived.astype(wide)
     first = first[:width] + across(first[width:], "sample", 1)
-    keep, arrived = late
-    second = keep + arrived
-    gain = second[2 * width :: GAIN_ROWS]
+    parts, arrived, gain = late
+    second = parts[0] + arrived
     count = gain.shape[0]
     arrived = across(
-        jnp.concatenate([second[width : 2 * width].astype(jnp.bfloat16), pack(gain)]), "sample", 2
+        jnp.concatenate([second[width:].astype(jnp.bfloat16), pack(gain)]), "sample", 2
     )
     second = second[:width] + arrived[:width].astype(wide)
     gain = gain + unpack(arrived[width:], count)
@@ -608,10 +617,12 @@
         second = second[:half] + arrived[half : 2 * half].astype(wide)
         gain = gain + unpack(arrived[2 * half :], count)
     total = jnp.stack([first, second]).astype(jnp.bfloat16)[None]
+    total, beside = lax.optimization_barrier((total, beside))
     for distance in (2, 4, 1):
         total = jnp.concatenate([total, across(total, "turb", distance)])
     both = [total, across(total, "sample", 2)]
-    return both + [across(part, "sample", 1) for part in both], gain.reshape(width)
+    both += [across(part, "sample", 1) for part in both]
+    return both, gain.reshape(width), beside
 
 
 def place_kernel(*refs):
@@ -667,17 +678,26 @@
         block_rows,
     )
     layer_output = swap(layer_rows.reshape(inflow.shape), "turb")
-    *grads, keep, send = backward(
-        sectors, adjacency, grad_rows, out_weight, *saved, block_rows, 0
-    )
-    early = (keep, across(send, "sample", 2))
-    grad_rows, keep, send = backward(
-        sectors, adjacency, grad_rows, out_weight, *saved, block_rows, 1,
-        rows, norm_gain.reshape(1, width), query_weight, key_weight, value_weight, *grads,
-    )
-    late = (keep, across(send, "sample", 1))
+    weights = (norm_gain, query_weight, key_weight, value_weight)
+    none = jnp.zeros((SUM_ROWS, width), jnp.float32)
+    *grads, early, before = backward(
+        sectors, adjacency, grad_rows, out_weight, *saved, *weights, none, block_rows, 0
+    )
+    arrived_early = across(early[1].astype(jnp.bfloat16), "sample", 2)
+    *more, late, gain = backward(
+        sectors, adjacency, grad_rows, out_weight, *saved, *weights, before, block_rows, 1
+    )
+    late, gain, arrived_early, layer_output = lax.optimization_barrier(
+        (late, gain, arrived_early, layer_output)
+    )
+    arrived_late = across(late[1], "sample", 1)
+    gain = gain[0].reshape(-1, late.shape[2])
+    gain = gain + across(gain, "sample", 1)
+    grad_rows = finish(rows, grad_rows, *weights, grads + more)
     grad_inflow = swap(grad_rows.reshape(inflow.shape), "turb")
-    parts, sum_gain = reduce_sums(early, late, width)
+    parts, sum_gain, grad_inflow = reduce_sums(
+        (early, arrived_early), (late, arrived_late, gain), width, grad_inflow
+    )
     sums = place_sums(parts, width)
     return (layer_output, grad_inflow, *sums, sum_gain)
 

time: 222 us -> 195 us (0.88)
  waiting for transfers between devices: 88.7 us -> 56.1 us
  local copies, waits for them, and re-layouts: 6.21 us -> 12.3 us
  starting transfers between devices: 26.7 us -> 22.8 us
  other arithmetic: 4.33 us -> 7.01 us
    ppermute x13 -> x14, waiting for transfers between devices: 85.2 us -> 53.8 us  [across(): return lax.ppermute(tensor, axis, [(i, i ^ distance) for i in range(size)])]
    pallas_call x0 -> x1, Pallas kernels: none -> 6.47 us  [finish(): pl.pallas_call(lambda *refs: finish_kernel(width // quad, *refs), grid=(r...]
    pallas_call x2, Pallas kernels: 35.8 us -> 29.8 us  [backward(): pl.pallas_call(lambda *refs: backward_kernel(block_rows, head_dim, which,...]
    ppermute x13 -> x14, starting transfers between devices: 13.7 us -> 7.68 us  [across(): return lax.ppermute(tensor, axis, [(i, i ^ distance) for i in range(size)])]
    add x2, other arithmetic: 0.24 us -> 2.85 us  [the longest x1 1.49 us: reduce_sums(): first = parts[0] + arrived.astype(wide)]
    squeeze x0 -> x1, local copies, waits for them, and re-layouts: none -> 2.26 us  [by_sample(): arrived_late = across(late[1], 'sample', 1)]
    unnamed x20 -> x27, local copies, waits for them, and re-layouts: 4.79 us -> 6.02 us
  transfers between devices with their start and end apart: 16 -> 17, of which waited for: 11 -> 9; matrix products, arithmetic and copies ran while one was open for 3% -> 6% of each run, Pallas kernels for 10% -> 30%
where the time goes in v7:
time: 195 us
  Pallas kernels  62.6 us (32%)
  waiting for transfers between devices  56.1 us (29%)
  blocking collectives  33.1 us (17%)
  starting transfers between devices  22.8 us (12%)
  local copies, waits for them, and re-layouts  12.3 us (6%)
  other arithmetic  7.01 us (4%)
    ppermute x14, waiting for transfers between devices, across(): return lax.ppermute(tensor, axis, [(i, i ^ distance) for i in range(size)])  53.8 us
    all_to_all x1, blocking collectives, swap(): return lax.all_to_all(tensor, axis, split_axis=0, concat_axis=0, tiled=True)  33.1 us
    pallas_call x2, Pallas kernels, backward(): pl.pallas_call(lambda *refs: backward_kernel(block_rows, head_dim, which,...  29.8 us
    pallas_call x1, Pallas kernels, forward(): pl.pallas_call(lambda *refs: forward_kernel(block_rows, head_dim, *refs),...  22.5 us
    all_to_all x3, starting transfers between devices, swap(): return lax.all_to_all(tensor, axis, split_axis=0, concat_axis=0, tiled=True)  15.1 us
    ppermute x14, starting transfers between devices, across(): return lax.ppermute(tensor, axis, [(i, i ^ distance) for i in range(size)])  7.68 us
    pallas_call x1, Pallas kernels, finish(): pl.pallas_call(lambda *refs: finish_kernel(width // quad, *refs), grid=(r...  6.47 us
    unnamed x27, local copies, waits for them, and re-layouts  6.02 us
  transfers between devices with their start and end apart: 17, of which 9 were waited for; matrix products, arithmetic and copies ran while one was open for 6% of the time, Pallas kernels for 30%

profile of v7, /device:TPU:0, one launch (start us, length us, event | category | flops | bytes accessed | tf_op | source)
XLA Modules:
  0.0 195.0 jit_solution(6416281966425615704)
XLA Ops:
  0.6 33.1 %all_to_all.20 = bf16[8,128,512]{2,1,0:T(8,128)(2,1)} all-to-all(bf16[8,128,512]{2,1,0:T(8,128)(2,1)} %param.9), channel_id=1, replica_groups=mesh['sample'=4,'turb'=8] {'turb'}, dimensions={0} | all-to-all | bytes 2097152 | tf_op jit(solution)/shard_map/all_to_all | solution.py:576
  33.8 3.6 %all-to-all-start.1 = ((bf16[8,128,512]{2,1,0:T(8,128)(2,1)}), bf16[8,128,512]{2,1,0:T(8,128)(2,1)S(1)}, u32[]{:S(2)}, u32[]{:S(2)}) async-start(bf16[8,128,512]{2,1,0:T(8,128)(2,1)} %param.10), calls=%async_computation.1 | async-start | bytes 2097152 | tf_op jit(solution)/shard_map/all_to_all | solution.py:576
  37.4 0.7 copy.18.refs_1_
  38.1 22.5 %forward.1 = (bf16[512,1024]{1,0:T(8,128)(2,1)}, bf16[1024,512]{1,0:T(8,128)(2,1)}, bf16[1024,512]{1,0:T(8,128)(2,1)}, bf16[1024,512]{1,0:T(8,128)(2,1)}, bf16[5...) custom-call(s32[8]{0:T(128)} %refs_0_.5, ...), custom_call_target="tpu_custom_call" | custom-call | flops 5368709120 | bytes 10485760 | tf_op jit(solution)/shard_map/forward/pallas_call | solution.py:366
  60.6 2.3 %all-to-all-done.1 = bf16[8,128,512]{2,1,0:T(8,128)(2,1)S(1)} async-done(((bf16[8,128,512]{2,1,0:T(8,128)(2,1)}), bf16[8,128,512]{2,1,0:T(8,128)(2,1)S(1)}, u32[]{:S(2)}, u32[]{:S(2)}) %all-to-all-start.1) | async-done | bytes 1048608 | tf_op jit(solution)/shard_map/all_to_all | solution.py:576
  63.0 3.7 %all-to-all-start.2 = ((bf16[8,128,512]{2,1,0:T(8,128)(2,1)}), bf16[8,128,512]{2,1,0:T(8,128)(2,1)S(1)}, u32[]{:S(2)}, u32[]{:S(2)}) async-start(bf16[8,128,512]{2,1,0:T(8,128)(2,1)} %bitcast.26), calls=%async_computation.2 | async-start | bytes 2097152 | tf_op jit(solution)/shard_map/all_to_all | solution.py:576
  66.7 0.6 broadcast_in_dim.4.refs_11_
  67.3 14.9 %backward.2 = (bf16[1024,256]{1,0:T(8,128)(2,1)}, bf16[1024,256]{1,0:T(8,128)(2,1)}, bf16[1024,256]{1,0:T(8,128)(2,1)}, f32[2,1024,256]{2,1,0:T(8,128)}, f32[8,512]{1,0:T(8,128)}) custom-call(s32[8]{0:T(128)} %refs_0_.5, s32[8,8,3]{2,1,0:T(8,128)} %copy.18.refs_1_, bf16[1024,512]{1,0:T(8,128)(2,1)} %bitcast.22, bf16[512,512]{1,0:T(8,128)(2,1)} %refs_3_.4, ...), custom_call_target="tpu_custom_call" | custom-call | flops 4026531840 | bytes 7340032 | tf_op jit(solution)/shard_map/backward/pallas_call | solution.py:497
  82.2 1.3 fusion
  83.5 0.7 collective-permute-start
  84.2 14.9 %backward.3 = (bf16[1024,256]{1,0:T(8,128)(2,1)}, bf16[1024,256]{1,0:T(8,128)(2,1)}, bf16[1024,256]{1,0:T(8,128)(2,1)}, f32[2,1024,256]{2,1,0:T(8,128)}, f32[8,512]{1,0:T(8,128)}) custom-call(s32[8]{0:T(128)} %refs_0_.5, s32[8,8,3]{2,1,0:T(8,128)} %copy.18.refs_1_, bf16[1024,512]{1,0:T(8,128)(2,1)} %bitcast.23, bf16[512,512]{1,0:T(8,128)(2,1)} %refs_3_.4, ...), custom_call_target="tpu_custom_call" | custom-call | flops 4026531840 | bytes 7340032 | tf_op jit(solution)/shard_map/backward/pallas_call | solution.py:497
  99.1 0.0 all-to-all-done.2
  99.1 0.0 collective-permute-done
  99.1 0.0 copy-start.5
  99.2 0.8 copy-done.5
  99.9 2.3 %slice_bitcast_fusion = f32[1024,256]{1,0:T(8,128)} fusion(f32[2,1024,256]{2,1,0:T(8,128)} %get-tuple-element.55), kind=kLoop, calls=%fused_computation.3 | loop fusion | bytes 2097152 | tf_op jit(solution)/shard_map/squeeze | solution.py:693
  102.2 0.0 collective-permute-start.2
  102.2 0.7 slice_reduce_fusion
  103.0 0.6 collective-permute-start.3
  103.5 1.5 bitcast_add_fusion.1
  105.0 0.8 slice.166
  105.8 0.0 collective-permute-start.1
  105.9 0.0 collective-permute-done.3
  105.9 0.0 collective-permute-done.2
  105.9 1.4 bitcast_add_fusion
  107.2 0.0 copy-start.1
  107.3 1.0 copy-done.1
  108.3 0.2 collective-permute-start.4
  108.5 6.5 %finish.1 = bf16[1024,512]{1,0:T(8,128)(2,1)} custom-call(bf16[1024,512]{1,0:T(8,128)(2,1)} %bitcast.21, bf16[1024,512]{1,0:T(8,128)(2,1)} %bitcast.24, f32[1,512]{1,0:T(1,128)} %bitcast.30, bf16[512,512]{1,0:T(8,128)(2,1)} %refs_3_.5, bf16[512,512]{1,0:T(8,128)(2,1)} %refs_4_.3, bf16[512,512]{1,0:T(8,128)(2,1)} %refs_5_.3, ...), custom_call_target="tpu_custom_call" | custom-call | flops 1610612736 | bytes 8388608 | tf_op jit(solution)/shard_map/finish/pallas_call | solution.py:556
  114.9 7.8 %all-to-all-start.3 = ((bf16[8,128,512]{2,1,0:T(8,128)(2,1)}), bf16[8,128,512]{2,1,0:T(8,128)(2,1)S(1)}, u32[]{:S(2)}, u32[]{:S(2)}) async-start(bf16[8,128,512]{2,1,0:T(8,128)(2,1)} %bitcast.25), calls=%async_computation.3 | async-start | bytes 2097152 | tf_op jit(solution)/shard_map/all_to_all | solution.py:576
  122.8 0.0 collective-permute-done.1
  122.8 1.2 slice_add_fusion.1
  124.0 0.0 copy-start.3
  124.0 0.0 collective-permute-done.4
  124.0 0.1 copy-done.2
  124.1 1.0 slice_add_fusion
  125.2 0.8 subtract_convert_fusion.2
  126.0 0.2 concatenate.32
  126.1 2.1 %collective-permute-start.5 = (bf16[528,256]{1,0:T(8,128)(2,1)S(1)}, bf16[528,256]{1,0:T(8,128)(2,1)S(1)}, u32[]{:S(2)}, u32[]{:S(2)}) collective-permute-start(bf16[528,256]{1,0:T(8,128)(2,1)S(1)} %concatenate.32), channel_id=1, source_target_pairs={{0,1},{1,0},{2,3},{3,2},{4,5},{5,4},{6,7},{7,6},{8,9},{9,8},{10,11... | collective-permute-start | bytes 811016 | tf_op jit(solution)/shard_map/ppermute | solution.py:586
  128.2 13.4 %collective-permute-done.5 = bf16[528,256]{1,0:T(8,128)(2,1)S(1)} collective-permute-done((bf16[528,256]{1,0:T(8,128)(2,1)S(1)}, bf16[528,256]{1,0:T(8,128)(2,1)S(1)}, u32[]{:S(2)}, u32[]{:S(2)}) %collective-permute-start.5) | collective-permute-done | bytes 270368 | tf_op jit(solution)/shard_map/ppermute | solution.py:586
  141.6 1.0 slice_add_fusion.3
  142.7 0.2 concatenate.33
  142.9 1.4 collective-permute-start.6
  144.3 10.6 %collective-permute-done.6 = bf16[272,256]{1,0:T(8,128)(2,1)S(1)} collective-permute-done((bf16[272,256]{1,0:T(8,128)(2,1)S(1)}, bf16[272,256]{1,0:T(8,128)(2,1)S(1)}, u32[]{:S(2)}, u32[]{:S(2)}) %collective-permute-start.6) | collective-permute-done | bytes 139296 | tf_op jit(solution)/shard_map/ppermute | solution.py:586
  154.9 0.2 concatenate.34
  155.1 0.1 collective-permute-start.7
  155.2 4.3 %collective-permute-done.7 = bf16[144,256]{1,0:T(8,128)(2,1)S(1)} collective-permute-done((bf16[144,256]{1,0:T(8,128)(2,1)S(1)}, bf16[144,256]{1,0:T(8,128)(2,1)S(1)}, u32[]{:S(2)}, u32[]{:S(2)}) %collective-permute-start.7) | collective-permute-done | bytes 73760 | tf_op jit(solution)/shard_map/ppermute | solution.py:586
  159.6 0.0 all-to-all-done.3
  159.6 0.1 collective-permute-start.8
  159.7 4.3 %collective-permute-done.8 = bf16[1,2,64,256]{3,2,1,0:T(8,128)(2,1)S(1)} collective-permute-done((bf16[1,2,64,256]{3,2,1,0:T(8,128)(2,1)S(1)}, bf16[1,2,64,256]{3,2,1,0:T(8,128)(2,1)S(1)}, u32[]{:S(2)}, u32[]{:S(2)}) %collective-permute-start.8) | collective-permute-done | bytes 65568 | tf_op jit(solution)/shard_map/ppermute | solution.py:586
  163.9 0.5 collective-permute-start.9
  164.4 6.3 %collective-permute-done.9 = bf16[2,2,64,256]{3,2,1,0:T(8,128)(2,1)S(1)} collective-permute-done((bf16[2,2,64,256]{3,2,1,0:T(8,128)(2,1)S(1)}, bf16[2,2,64,256]{3,2,1,0:T(8,128)(2,1)S(1)}, u32[]{:S(2)}, u32[]{:S(2)}) %collective-permute-start.9) | collective-permute-done | bytes 131104 | tf_op jit(solution)/shard_map/ppermute | solution.py:586
  170.7 1.5 collective-permute-start.10
  172.2 4.9 %collective-permute-done.10 = bf16[4,2,64,256]{3,2,1,0:T(8,128)(2,1)S(1)} collective-permute-done((bf16[4,2,64,256]{3,2,1,0:T(8,128)(2,1)S(1)}, bf16[4,2,64,256]{3,2,1,0:T(8,128)(2,1)S(1)}, u32[]{:S(2)}, u32[]{:S(2)}) %collective-permute-start.10) | collective-permute-done | bytes 262176 | tf_op jit(solution)/shard_map/ppermute | solution.py:586
  177.2 0.0 copy-start.4
  177.2 0.6 collective-permute-start.11
  177.8 8.7 %collective-permute-done.11.refs_1_ = bf16[8,2,64,256]{3,2,1,0:T(8,128)(2,1)S(1)} collective-permute-done((bf16[8,2,64,256]{3,2,1,0:T(8,128)(2,1)S(1)}, bf16[8,2,64,256]{3,2,1,0:T(8,128)(2,1)S(1)}, u32[]{:S(2)}, u32[]{:S(2)}) %collective-permute-start.11) | collective-permute-done | bytes 524320 | tf_op jit(solution)/shard_map/ppermute | solution.py:586
  186.5 0.0 collective-permute-start.13
  186.5 0.6 copy.19
  187.1 1.3 collective-permute-done.13.refs_3_
  188.4 0.8 copy-done.8
  189.2 3.9 %place.1 = (f32[512,512]{1,0:T(8,128)}, f32[512,512]{1,0:T(8,128)}, f32[512,512]{1,0:T(8,128)}, f32[512,512]{1,0:T(8,128)}) custom-call(bf16[8,2,64,256]{3,2,1,0:T(8,128)(2,1)} %copy-done.4, bf16[8,2,64,256]{3,2,1,0:T(8,128)(2,1)} %copy-done.6, bf16[8,2,64,256]{3,2,1,0:T(8,128)(2,1)} %copy-done.7, bf16[8,2,64,256]{3,2,1,0:T(8,128)(2,1)} %copy-done.8), custom_call_target="tpu_custom_call" | custom-call | bytes 6291456 | tf_op jit(solution)/shard_map/place/pallas_call | solution.py:645
  193.0 1.0 copy.25
  194.0 1.0 copy.26
  (37 shorter events, 0.3 us)
Async XLA Ops:
  0.6 36.7 %copy-start.9 = (s32[8,8,3]{1,0,2:T(8,128)S(1)}, s32[8,8,3]{1,0,2:T(8,128)}, u32[]{:S(2)}) copy-start(s32[8,8,3]{1,0,2:T(8,128)} %param.16) | copy-start | bytes 2308
  33.8 29.2 %all-to-all-start.1 = ((bf16[8,128,512]{2,1,0:T(8,128)(2,1)}), bf16[8,128,512]{2,1,0:T(8,128)(2,1)S(1)}, u32[]{:S(2)}, u32[]{:S(2)}) async-start(bf16[8,128,512]{2,1,0:T(8,128)(2,1)} %param.10), calls=%async_computation.1 | async-start | bytes 2097152 | tf_op jit(solution)/shard_map/all_to_all | solution.py:576
  63.0 4.4 %copy-start = (bf16[8,128,512]{2,1,0:T(8,128)(2,1)}, bf16[8,128,512]{2,1,0:T(8,128)(2,1)S(1)}, u32[]{:S(2)}) copy-start(bf16[8,128,512]{2,1,0:T(8,128)(2,1)S(1)} %all-to-all-done.1) | copy-start | bytes 3145732
  63.0 36.2 %all-to-all-start.2 = ((bf16[8,128,512]{2,1,0:T(8,128)(2,1)}), bf16[8,128,512]{2,1,0:T(8,128)(2,1)S(1)}, u32[]{:S(2)}, u32[]{:S(2)}) async-start(bf16[8,128,512]{2,1,0:T(8,128)(2,1)} %bitcast.26), calls=%async_computation.2 | async-start | bytes 2097152 | tf_op jit(solution)/shard_map/all_to_all | solution.py:576
  83.5 15.6 %collective-permute-start = (bf16[1024,256]{1,0:T(8,128)(2,1)S(1)}, bf16[1024,256]{1,0:T(8,128)(2,1)S(1)}, u32[]{:S(2)}, u32[]{:S(2)}) collective-permute-start(bf16[1024,256]{1,0:T(8,128)(2,1)S(1)} %fusion), channel_id=1, source_target_pairs={{0,16},{8,24},{16,0},{24,8},{1,17},{9,25},{17,1},{25,9},{2,18},{10... | collective-permute-start | bytes 1572872 | tf_op jit(solution)/shard_map/ppermute | solution.py:586
  99.1 0.8 copy-start.5
  102.2 3.7 %collective-permute-start.2 = (f32[1024,256]{1,0:T(8,128)}, f32[1024,256]{1,0:T(8,128)S(1)}, u32[]{:S(2)}, u32[]{:S(2)}) collective-permute-start(f32[1024,256]{1,0:T(8,128)} %slice_bitcast_fusion), channel_id=1, source_target_pairs={{0,8},{8,0},{16,24},{24,16},{1,9},{9,1},{17,25},{25,17},{2,10},{10... | collective-permute-start | bytes 3145736 | tf_op jit(solution)/shard_map/ppermute | solution.py:586
  103.0 2.9 %collective-permute-start.3 = (f32[2,256]{1,0:T(2,128)S(1)}, f32[2,256]{1,0:T(2,128)S(1)}, u32[]{:S(2)}, u32[]{:S(2)}) collective-permute-start(f32[2,256]{1,0:T(2,128)S(1)} %reshape_squeeze.3), channel_id=1, source_target_pairs={{0,8},{8,0},{16,24},{24,16},{1,9},{9,1},{17,25},{25,17},{2,10},{10... | collective-permute-start | bytes 6152 | tf_op jit(solution)/shard_map/ppermute | solution.py:586
  105.8 16.9 %collective-permute-start.1 = (f32[512,256]{1,0:T(8,128)}, f32[512,256]{1,0:T(8,128)}, u32[]{:S(2)}, u32[]{:S(2)}) collective-permute-start(f32[512,256]{1,0:T(8,128)} %slice.166), channel_id=1, source_target_pairs={{0,8},{8,0},{16,24},{24,16},{1,9},{9,1},{17,25},{25,17},{2,10},{10... | collective-permute-start | bytes 1572872 | tf_op jit(solution)/shard_map/ppermute | solution.py:586
  107.2 1.0 copy-start.1
  108.3 15.7 %collective-permute-start.4 = (bf16[528,256]{1,0:T(8,128)(2,1)S(1)}, bf16[528,256]{1,0:T(8,128)(2,1)}, u32[]{:S(2)}, u32[]{:S(2)}) collective-permute-start(bf16[528,256]{1,0:T(8,128)(2,1)S(1)} %pad_maximum_fusion), channel_id=1, source_target_pairs={{0,16},{8,24},{16,0},{24,8},{1,17},{9,25},{17,1},{25,9},{2,18},{10... | collective-permute-start | bytes 811016 | tf_op jit(solution)/shard_map/ppermute | solution.py:586
  114.9 44.6 %all-to-all-start.3 = ((bf16[8,128,512]{2,1,0:T(8,128)(2,1)}), bf16[8,128,512]{2,1,0:T(8,128)(2,1)S(1)}, u32[]{:S(2)}, u32[]{:S(2)}) async-start(bf16[8,128,512]{2,1,0:T(8,128)(2,1)} %bitcast.25), calls=%async_computation.3 | async-start | bytes 2097152 | tf_op jit(solution)/shard_map/all_to_all | solution.py:576
  122.8 1.4 copy-start.2
  124.0 1.2 copy-start.3
  126.1 15.5 %collective-permute-start.5 = (bf16[528,256]{1,0:T(8,128)(2,1)S(1)}, bf16[528,256]{1,0:T(8,128)(2,1)S(1)}, u32[]{:S(2)}, u32[]{:S(2)}) collective-permute-start(bf16[528,256]{1,0:T(8,128)(2,1)S(1)} %concatenate.32), channel_id=1, source_target_pairs={{0,1},{1,0},{2,3},{3,2},{4,5},{5,4},{6,7},{7,6},{8,9},{9,8},{10,11... | collective-permute-start | bytes 811016 | tf_op jit(solution)/shard_map/ppermute | solution.py:586
  142.9 12.0 %collective-permute-start.6 = (bf16[272,256]{1,0:T(8,128)(2,1)S(1)}, bf16[272,256]{1,0:T(8,128)(2,1)S(1)}, u32[]{:S(2)}, u32[]{:S(2)}) collective-permute-start(bf16[272,256]{1,0:T(8,128)(2,1)S(1)} %concatenate.33), channel_id=1, source_target_pairs={{0,4},{1,5},{2,6},{3,7},{4,0},{5,1},{6,2},{7,3},{8,12},{9,13},{10,... | collective-permute-start | bytes 417800 | tf_op jit(solution)/shard_map/ppermute | solution.py:586
  155.1 4.4 %collective-permute-start.7 = (bf16[144,256]{1,0:T(8,128)(2,1)S(1)}, bf16[144,256]{1,0:T(8,128)(2,1)S(1)}, u32[]{:S(2)}, u32[]{:S(2)}) collective-permute-start(bf16[144,256]{1,0:T(8,128)(2,1)S(1)} %concatenate.34), channel_id=1, source_target_pairs={{0,2},{1,3},{2,0},{3,1},{4,6},{5,7},{6,4},{7,5},{8,10},{9,11},{10,... | collective-permute-start | bytes 221192 | tf_op jit(solution)/shard_map/ppermute | solution.py:586
  159.6 4.3 %collective-permute-start.8 = (bf16[1,2,64,256]{3,2,1,0:T(8,128)(2,1)S(1)}, bf16[1,2,64,256]{3,2,1,0:T(8,128)(2,1)S(1)}, u32[]{:S(2)}, u32[]{:S(2)}) collective-permute-start(bf16[1,2,64,256]{3,2,1,0:T(8,128)(2,1)S(1)} %pad_maximum_fusion.3), channel_id=1, source_target_pairs={{0,2},{1,3},{2,0},{3,1},{4,6},{5,7},{6,4},{7,5},{8,10},{9,11},{10,... | collective-permute-start | bytes 196616 | tf_op jit(solution)/shard_map/ppermute | solution.py:586
  163.9 6.8 %collective-permute-start.9 = (bf16[2,2,64,256]{3,2,1,0:T(8,128)(2,1)S(1)}, bf16[2,2,64,256]{3,2,1,0:T(8,128)(2,1)S(1)}, u32[]{:S(2)}, u32[]{:S(2)}) collective-permute-start(bf16[2,2,64,256]{3,2,1,0:T(8,128)(2,1)S(1)} %pad_maximum_fusion.2), channel_id=1, source_target_pairs={{0,4},{1,5},{2,6},{3,7},{4,0},{5,1},{6,2},{7,3},{8,12},{9,13},{10,... | collective-permute-start | bytes 393224 | tf_op jit(solution)/shard_map/ppermute | solution.py:586
  170.7 6.4 %collective-permute-start.10 = (bf16[4,2,64,256]{3,2,1,0:T(8,128)(2,1)S(1)}, bf16[4,2,64,256]{3,2,1,0:T(8,128)(2,1)S(1)}, u32[]{:S(2)}, u32[]{:S(2)}) collective-permute-start(bf16[4,2,64,256]{3,2,1,0:T(8,128)(2,1)S(1)} %pad_maximum_fusion.1), channel_id=1, source_target_pairs={{0,1},{1,0},{2,3},{3,2},{4,5},{5,4},{6,7},{7,6},{8,9},{9,8},{10,11... | collective-permute-start | bytes 786440 | tf_op jit(solution)/shard_map/ppermute | solution.py:586
  177.2 11.2 %copy-start.4 = (bf16[8,2,64,256]{3,2,1,0:T(8,128)(2,1)}, bf16[8,2,64,256]{3,2,1,0:T(8,128)(2,1)S(1)}, u32[]{:S(2)}) copy-start(bf16[8,2,64,256]{3,2,1,0:T(8,128)(2,1)S(1)} %constant_dynamic-update-slice_fusion.refs_0_) | copy-start | bytes 1572868
  177.2 9.2 %collective-permute-start.11 = (bf16[8,2,64,256]{3,2,1,0:T(8,128)(2,1)S(1)}, bf16[8,2,64,256]{3,2,1,0:T(8,128)(2,1)S(1)}, u32[]{:S(2)}, u32[]{:S(2)}) collective-permute-start(bf16[8,2,64,256]{3,2,1,0:T(8,128)(2,1)S(1)} %constant_dynamic-update-slice_fusion.refs_0_), channel_id=1, source_target_pairs={{0,16},{8,24},{16,0},{24,8},{1,17},{9,25},{17,1},{25,9},{2,18},{10... | collective-permute-start | bytes 1572872 | tf_op jit(solution)/shard_map/ppermute | solution.py:586
  177.8 9.3 %collective-permute-start.12 = (bf16[8,2,64,256]{3,2,1,0:T(8,128)(2,1)S(1)}, bf16[8,2,64,256]{3,2,1,0:T(8,128)(2,1)S(1)}, u32[]{:S(2)}, u32[]{:S(2)}) collective-permute-start(bf16[8,2,64,256]{3,2,1,0:T(8,128)(2,1)S(1)} %constant_dynamic-update-slice_fusion.refs_0_), channel_id=1, source_target_pairs={{0,8},{8,0},{16,24},{24,16},{1,9},{9,1},{17,25},{25,17},{2,10},{10... | collective-permute-start | bytes 1572872 | tf_op jit(solution)/shard_map/ppermute | solution.py:586
  186.5 1.9 copy-start.6
  186.5 1.9 collective-permute-start.13
  187.1 1.3 copy-start.7
  188.4 0.8 copy-start.8

commit v8 on v7

--- a/solution.py
+++ b/solution.py
@@ -260,13 +260,13 @@
     def step(block, carry):
         used = jnp.int32(0)
         for slot in range(UPSTREAM):
-            used = used + (lists_ref[sector, block, slot] >= 0).astype(jnp.int32)
+            used = used + (lists_ref[slot, sector, block] >= 0).astype(jnp.int32)
         for count in range(UPSTREAM + 1):
 
             @pl.when(used == count)
             def _():
                 sources = [block] + [
-                    lists_ref[sector, block, slot] for slot in range(count)
+                    lists_ref[slot, sector, block] for slot in range(count)
                 ]
                 work(block, [pl.multiple_of(s * block_rows, block_rows) for s in sources])
 
@@ -285,7 +285,7 @@
 
 def forward_kernel(block_rows, head_dim, sectors_ref, lists_ref, x_ref, gain_ref, wq_ref, wk_ref,
                    wv_ref, wo_ref, normed_t_ref, q_ref, k_ref, v_ref, kt_ref, att_ref,
-                   top_ref, inverse_ref, out_ref, normed_ref, vt_ref, rows_ref, sum_ref):
+                   level_ref, out_ref, normed_ref, vt_ref, rows_ref, sum_ref):
     row_count = x_ref.shape[0]
     quad = pl.program_id(0)
     pair = PAIR * head_dim
@@ -319,10 +319,11 @@
         for p, lane in enumerate(lanes):
             highest = jnp.max(scores[p], axis=0, keepdims=True)
             weights = jnp.exp2((scores[p] - highest) * exponent)
-            inverse = 1.0 / jnp.sum(weights, axis=0, keepdims=True)
-            probs = (weights * inverse).astype(jnp.bfloat16)
-            top_ref[0, pl.ds(block * (QUAD // PAIR) + p, 1), :] = highest
-            inverse_ref[0, pl.ds(block * (QUAD // PAIR) + p, 1), :] = inverse
+            total = jnp.sum(weights, axis=0, keepdims=True)
+            probs = (weights * (1.0 / total)).astype(jnp.bfloat16)
+            level_ref[0, pl.ds(block * (QUAD // PAIR) + p, 1), :] = highest * exponent + jnp.log2(
+                total
+            )
             joined = join_heads(
                 jnp.dot(
                     beside(vt_ref, starts, block_rows, lane),
@@ -374,8 +375,7 @@
             out_specs=[fixed(width, row_count)]
             + [across(row_count)] * 3
             + [down(row_count)] * 2
-            + [stat] * 2
-            + [fixed(row_count, width)],
+            + [stat, fixed(row_count, width)],
             scratch_shapes=[
                 pltpu.VMEM((row_count, width), jnp.bfloat16),
                 pltpu.VMEM((quad, row_count), jnp.bfloat16),
@@ -383,7 +383,7 @@
                 pltpu.VMEM((row_count, width), jnp.float32),
             ],
         ),
-        out_shape=[turned, flat, flat, flat, turned, turned, stats, stats, flat],
+        out_shape=[turned, flat, flat, flat, turned, turned, stats, flat],
         compiler_params=pltpu.CompilerParams(vmem_limit_bytes=VMEM_LIMIT),
         cost_estimate=pl.CostEstimate(
             flops=12 * row_count * width * width + 32 * row_count * block_rows * width,
@@ -395,10 +395,12 @@
       out_weight)
 
 
-def backward_kernel(block_rows, head_dim, which, sectors_ref, lists_ref, cot_ref, wo_ref, q_ref,
-                    k_ref, v_ref, kt_ref, top_ref, inverse_ref, gain_ref, before_ref, *refs):
-    late, refs = refs[:5], refs[5:]
-    (gq_ref, gk_ref, gv_ref, parts_ref, sum_ref, ga_ref, gk_acc, gv_acc, *held, sems) = refs
+def backward_kernel(block_rows, head_dim, which, sectors_ref, lists_ref, wo_ref, q_ref, k_ref, v_ref,
+                    kt_ref, level_ref, gain_ref, before_ref, *refs):
+    late, refs = refs[:6], refs[6:]
+    gq_ref, gk_ref, gv_ref, keep_ref, send_ref, sum_ref, *refs = refs
+    ga_ref, gk_acc, gv_acc, parts_ref, *held, sems = refs
+    cot_ref = held[0]
     row_count, width = cot_ref.shape
     block_count = row_count // block_rows
     pair = PAIR * head_dim
@@ -407,10 +409,11 @@
     own_lanes = slice(which * quad, (which + 1) * quad)
     copies = []
     for i, (ref, into) in enumerate(zip(late, held)):
-        source = ref if i < 2 else ref.at[:, own_lanes]
+        source = ref if i < 3 else ref.at[:, own_lanes]
         copies.append(pltpu.make_async_copy(source, into, sems.at[i]))
         copies[-1].start()
-    normed_t_ref, att_ref, *weight_refs = held
+    _, normed_t_ref, att_ref, *weight_refs = held
+    copies[0].wait()
     ga_ref[...] = contract(cot_ref[...], wo_ref[...], 1, 1).astype(jnp.bfloat16)
     gk_acc[...] = jnp.zeros_like(gk_acc)
     gv_acc[...] = jnp.zeros_like(gv_acc)
@@ -430,8 +433,7 @@
         ]
         for p, lane in enumerate(lanes):
             stat = pl.ds(block * (QUAD // PAIR) + p, 1)
-            probs = jnp.exp2((scores[p] - top_ref[0, stat, :]) * (scale * LOG2_E))
-            probs = probs * inverse_ref[0, stat, :]
+            probs = jnp.exp2(scores[p] * (scale * LOG2_E) - level_ref[0, stat, :])
             total = jnp.sum(probs * grad_probs[p], axis=0, keepdims=True)
             grad_scores = (probs * (grad_probs[p] - total)).astype(jnp.bfloat16)
             probs_b = probs.astype(jnp.bfloat16)
@@ -458,7 +460,7 @@
     for_each_block(sectors_ref, lists_ref, block_count, block_rows, work)
     gk_ref[...] = gk_acc[...].astype(jnp.bfloat16)
     gv_ref[...] = gv_acc[...].astype(jnp.bfloat16)
-    for copy in copies:
+    for copy in copies[1:]:
         copy.wait()
     products = [(normed_t_ref, ref, slice(None)) for ref in (gq_ref, gk_ref, gv_ref)]
     products.append((att_ref, cot_ref, own_lanes))
@@ -470,11 +472,16 @@
         if i < len(weight_refs):
             along += terms * weight_refs[i][...].astype(jnp.float32)
         apart = i ^ own_sample
-        low, high = apart % 2, apart // 2
-        first, second = (high, low) if which == 0 else (low, high)
         for turb in range(TURBS):
-            start = pl.multiple_of(second * width + turb_place(turb ^ own_turb) * share, share)
-            parts_ref[first, pl.ds(start, share), :] = terms[turb * share : (turb + 1) * share]
+            place = turb_place(turb ^ own_turb)
+            if which == 0:
+                half, start = place // 4, (apart % 2 * 2 + apart // 2) * 4 + place % 4
+            else:
+                half, start = apart % 2, apart // 2 * TURBS + place
+            start = pl.multiple_of(start * share, share)
+            parts_ref[half, pl.ds(start, share), :] = terms[turb * share : (turb + 1) * share]
+    keep_ref[...] = parts_ref[0]
+    send_ref[...] = parts_ref[1].astype(send_ref.dtype)
     ones = jnp.ones((SUM_ROWS, quad), jnp.bfloat16)
     coarse = along.astype(jnp.bfloat16)
     fine = (along - coarse.astype(jnp.float32)).astype(jnp.bfloat16)
@@ -483,7 +490,7 @@
 
 
 def backward(sectors, adjacency, cotangent, out_weight, normed_t, queries, keys, values, keys_t,
-             attended_t, tops, inverses, norm_gain, query_weight, key_weight, value_weight, before,
+             attended_t, levels, norm_gain, query_weight, key_weight, value_weight, before,
              block_rows, which):
     row_count, width = cotangent.shape
     head_dim = width // HEADS
@@ -491,32 +498,39 @@
     fixed = lambda *shape: pl.BlockSpec(shape, lambda i, *lists: (0,) * len(shape))
     across = pl.BlockSpec((row_count, quad), lambda i, *lists: (0, which))
     down = lambda size: pl.BlockSpec((quad, size), lambda i, *lists: (which, 0))
-    stat = pl.BlockSpec((1,) + tops.shape[1:], lambda i, *lists: (which, 0, 0))
+    stat = pl.BlockSpec((1,) + levels.shape[1:], lambda i, *lists: (which, 0, 0))
     part = jax.ShapeDtypeStruct((row_count, quad), jnp.bfloat16)
-    sums = jax.ShapeDtypeStruct((2, 2 * width, quad), jnp.float32)
+    half = (2 * width, quad)
+    sent = jnp.bfloat16 if which == 0 else jnp.float32
     return pl.pallas_call(
         lambda *refs: backward_kernel(block_rows, head_dim, which, *refs),
         grid_spec=pltpu.PrefetchScalarGridSpec(
             num_scalar_prefetch=2,
             grid=(1,),
-            in_specs=[fixed(row_count, width), down(width)]
+            in_specs=[down(width)]
             + [across] * 3
-            + [down(row_count)]
-            + [stat] * 2
-            + [fixed(1, width), fixed(SUM_ROWS, width)]
-            + [pl.BlockSpec(memory_space=pl.ANY)] * 5,
+            + [down(row_count), stat, fixed(1, width), fixed(SUM_ROWS, width)]
+            + [pl.BlockSpec(memory_space=pl.ANY)] * 6,
             out_specs=[fixed(row_count, quad)] * 3
-            + [fixed(*sums.shape), fixed(SUM_ROWS, width)],
+            + [fixed(*half)] * 2
+            + [fixed(SUM_ROWS, width)],
             scratch_shapes=[
                 pltpu.VMEM((row_count, quad), jnp.bfloat16),
                 pltpu.VMEM((row_count, quad), jnp.float32),
                 pltpu.VMEM((row_count, quad), jnp.float32),
+                pltpu.VMEM((2,) + half, jnp.float32),
             ]
+            + [pltpu.VMEM((row_count, width), jnp.bfloat16)]
             + [pltpu.VMEM((width, row_count), jnp.bfloat16)] * 2
             + [pltpu.VMEM((width, quad), jnp.bfloat16)] * 3
-            + [pltpu.SemaphoreType.DMA((5,))],
+            + [pltpu.SemaphoreType.DMA((6,))],
         ),
-        out_shape=[part] * 3 + [sums, jax.ShapeDtypeStruct((SUM_ROWS, width), jnp.float32)],
+        out_shape=[part] * 3
+        + [
+            jax.ShapeDtypeStruct(half, jnp.float32),
+            jax.ShapeDtypeStruct(half, sent),
+            jax.ShapeDtypeStruct((SUM_ROWS, width), jnp.float32),
+        ],
         compiler_params=pltpu.CompilerParams(vmem_limit_bytes=VMEM_LIMIT),
         cost_estimate=pl.CostEstimate(
             flops=10 * row_count * width * quad + 80 * row_count * block_rows * quad,
@@ -524,8 +538,8 @@
             transcendentals=row_count * 4 * block_rows * QUAD,
         ),
         name="backward",
-    )(sectors, adjacency, cotangent, out_weight, queries, keys, values, keys_t, tops, inverses,
-      norm_gain.reshape(1, width), before, normed_t, attended_t, query_weight, key_weight,
+    )(sectors, adjacency, out_weight, queries, keys, values, keys_t, levels,
+      norm_gain.reshape(1, width), before, cotangent, normed_t, attended_t, query_weight, key_weight,
       value_weight)
 
 
@@ -586,57 +600,61 @@
     return lax.ppermute(tensor, axis, [(i, i ^ distance) for i in range(size)])
 
 
-def reduce_sums(early, late, width, beside):
-    quad = early[0].shape[-1]
+def reduce_sums(early, late, gain, width, beside):
+    quad = gain.shape[1]
+    count = gain.shape[0]
     wide = jnp.float32
 
     def pack(gain):
         high = gain.astype(jnp.bfloat16)
         low = (gain - high.astype(wide)).astype(jnp.bfloat16)
-        return jnp.concatenate([high, low, jnp.zeros((16 - 2 * gain.shape[0], quad), jnp.bfloat16)])
-
-    def unpack(rows, count):
-        return rows[:count].astype(wide) + rows[count : 2 * count].astype(wide)
-
-    parts, arrived = early
-    first = parts[0] + arrived.astype(wide)
-    first = first[:width] + across(first[width:], "sample", 1)
-    parts, arrived, gain = late
-    second = parts[0] + arrived
-    count = gain.shape[0]
-    arrived = across(
-        jnp.concatenate([second[width:].astype(jnp.bfloat16), pack(gain)]), "sample", 2
-    )
-    second = second[:width] + arrived[:width].astype(wide)
-    gain = gain + unpack(arrived[width:], count)
-    for distance in (1, 4, 2):
-        half = first.shape[0] // 2
-        halves = [part[half:].astype(jnp.bfloat16) for part in (first, second)]
-        arrived = across(jnp.concatenate(halves + [pack(gain)]), "turb", distance)
-        first = first[:half] + arrived[:half].astype(wide)
-        second = second[:half] + arrived[half : 2 * half].astype(wide)
-        gain = gain + unpack(arrived[2 * half :], count)
-    total = jnp.stack([first, second]).astype(jnp.bfloat16)[None]
-    total, beside = lax.optimization_barrier((total, beside))
-    for distance in (2, 4, 1):
+        return jnp.concatenate([high, low, jnp.zeros((16 - 2 * count, quad), jnp.bfloat16)])
+
+    def halve(parts, gain, axis, distance):
+        halves = [part.shape[0] // 2 for part in parts]
+        sent = [part[half:].astype(jnp.bfloat16) for part, half in zip(parts, halves)]
+        if gain is not None:
+            sent.append(pack(gain))
+        arrived = across(jnp.concatenate(sent), axis, distance)
+        start, kept = 0, []
+        for part, half in zip(parts, halves):
+            kept.append(part[:half] + arrived[start : start + half].astype(wide))
+            start += half
+        if gain is None:
+            return kept, gain
+        rows = arrived[start:].astype(wide)
+        return kept, gain + rows[:count] + rows[count : 2 * count]
+
+    first = early[:width] + across(early[width:], "sample", 1)
+    first, _ = halve([first], None, "sample", 2)
+    second, gain = halve([late], gain, "sample", 2)
+    second, gain = halve(second, gain, "turb", 1)
+    parts, gain, beside = lax.optimization_barrier((first + second, gain, beside))
+    for distance in (4, 2):
+        parts, gain = halve(parts, gain, "turb", distance)
+    total = jnp.stack(parts).astype(jnp.bfloat16)[None]
+    for distance in (2, 4):
         total = jnp.concatenate([total, across(total, "turb", distance)])
-    both = [total, across(total, "sample", 2)]
-    both += [across(part, "sample", 1) for part in both]
-    return both, gain.reshape(width), beside
+    other = across(total, "turb", 1)
+    four = [total, other, across(total, "sample", 2), across(other, "sample", 2)]
+    four += [across(part, "sample", 1) for part in four]
+    return four, gain.reshape(width), beside
 
 
 def place_kernel(*refs):
     (*parts, query_ref, key_ref, value_ref, out_ref, all_ref) = refs
     own_sample, own_turb = lax.axis_index("sample"), lax.axis_index("turb")
-    turbs, quads, share, quad = parts[0].shape
-    for i, ref in enumerate(parts):
+    _, quads, share, quad = parts[0].shape
+    for i in range(SAMPLES):
         product = own_sample ^ ((i % 2) * 2 + i // 2)
-        for apart in range(turbs):
+        for apart in range(TURBS):
+            place = turb_place(apart)
+            ref = parts[2 * i + place // 4]
             rows = pl.ds(pl.multiple_of((apart ^ own_turb) * share, share), share)
             for j in range(quads):
-                all_ref[product, rows, j * quad : (j + 1) * quad] = ref[
-                    turb_place(apart), j
-                ].astype(jnp.float32)
+                all_ref[product, rows, j * quad : (j + 1) * quad] = ref[place % 4, j].astype(
+                    jnp.float32
+                )
     for i, ref in enumerate((query_ref, key_ref, value_ref, out_ref)):
         ref[...] = all_ref[i]
 
@@ -669,6 +687,7 @@
 ):
     sample_count, block_rows, width = inflow.shape
     row_count = lax.axis_size("turb") * block_rows
+    adjacency = jnp.transpose(adjacency, (2, 0, 1))
     rows = swap(inflow, "turb")
     rows, cotangent = lax.optimization_barrier((rows, cotangent))
     rows = rows.reshape(row_count, width)
@@ -680,23 +699,27 @@
     layer_output = swap(layer_rows.reshape(inflow.shape), "turb")
     weights = (norm_gain, query_weight, key_weight, value_weight)
     none = jnp.zeros((SUM_ROWS, width), jnp.float32)
-    *grads, early, before = backward(
+    *grads, early, send, before = backward(
         sectors, adjacency, grad_rows, out_weight, *saved, *weights, none, block_rows, 0
     )
-    arrived_early = across(early[1].astype(jnp.bfloat16), "sample", 2)
-    *more, late, gain = backward(
+    arrived = across(send, "turb", 1)
+    *more, late, send, gain = backward(
         sectors, adjacency, grad_rows, out_weight, *saved, *weights, before, block_rows, 1
     )
-    late, gain, arrived_early, layer_output = lax.optimization_barrier(
-        (late, gain, arrived_early, layer_output)
-    )
-    arrived_late = across(late[1], "sample", 1)
-    gain = gain[0].reshape(-1, late.shape[2])
-    gain = gain + across(gain, "sample", 1)
+    late, send, gain, arrived, layer_output = lax.optimization_barrier(
+        (late, send, gain, arrived, layer_output)
+    )
+    gain = gain[0].reshape(-1, late.shape[1])
+    arrived_gain = across(gain, "sample", 1)
+    arrived_late = across(send, "sample", 1)
+    early = early + arrived.astype(jnp.float32)
     grad_rows = finish(rows, grad_rows, *weights, grads + more)
+    grad_rows, late, arrived_late, arrived_gain = lax.optimization_barrier(
+        (grad_rows, late, arrived_late, arrived_gain)
+    )
     grad_inflow = swap(grad_rows.reshape(inflow.shape), "turb")
     parts, sum_gain, grad_inflow = reduce_sums(
-        (early, arrived_early), (late, arrived_late, gain), width, grad_inflow
+        early, late + arrived_late, gain + arrived_gain, width, grad_inflow
     )
     sums = place_sums(parts, width)
     return (layer_output, grad_inflow, *sums, sum_gain)

time: 195 us -> 192 us (0.985)
  waiting for transfers between devices: 56.1 us -> 62.3 us
  local copies, waits for them, and re-layouts: 12.3 us -> 8.65 us
  other arithmetic: 7.01 us -> 3.8 us
  starting transfers between devices: 22.8 us -> 20.7 us
    all_to_all x3, waiting for transfers between devices: 2.35 us -> 16.3 us  [swap(): return lax.all_to_all(tensor, axis, split_axis=0, concat_axis=0, tiled=True)]
    ppermute x14 -> x18, waiting for transfers between devices: 53.8 us -> 46 us  [across(): return lax.ppermute(tensor, axis, [(i, i ^ distance) for i in range(size)])]
    add x6 -> x8, other arithmetic: 6.12 us -> 2.94 us  [the longest x1 1.46 us: by_sample(): early = early + arrived.astype(jnp.float32)]
    all_to_all x3, starting transfers between devices: 15.1 us -> 12.5 us  [swap(): return lax.all_to_all(tensor, axis, split_axis=0, concat_axis=0, tiled=True)]
    squeeze x1 -> x0, local copies, waits for them, and re-layouts: 2.26 us -> none  [by_sample(): arrived_late = across(late[1], 'sample', 1)]
    ppermute x14 -> x18, starting transfers between devices: 7.68 us -> 8.19 us  [across(): return lax.ppermute(tensor, axis, [(i, i ^ distance) for i in range(size)])]
    unnamed x27 -> x29, local copies, waits for them, and re-layouts: 6.02 us -> 6.07 us
  transfers between devices with their start and end apart: 17 -> 21, of which waited for: 9 -> 13; matrix products, arithmetic and copies ran while one was open for 6% -> 3% of each run, Pallas kernels for 30% -> 30%
where the time goes in v8:
time: 192 us
  waiting for transfers between devices  62.3 us (32%)
  Pallas kernels  62.2 us (32%)
  blocking collectives  33.1 us (17%)
  starting transfers between devices  20.7 us (11%)
  local copies, waits for them, and re-layouts  8.65 us (5%)
  other arithmetic  3.8 us (2%)
    ppermute x18, waiting for transfers between devices, across(): return lax.ppermute(tensor, axis, [(i, i ^ distance) for i in range(size)])  46 us
    all_to_all x1, blocking collectives, swap(): return lax.all_to_all(tensor, axis, split_axis=0, concat_axis=0, tiled=True)  33.1 us
    pallas_call x2, Pallas kernels, backward(): pl.pallas_call(lambda *refs: backward_kernel(block_rows, head_dim, which,...  29.9 us
    pallas_call x1, Pallas kernels, forward(): pl.pallas_call(lambda *refs: forward_kernel(block_rows, head_dim, *refs),...  21.9 us
    all_to_all x3, waiting for transfers between devices, swap(): return lax.all_to_all(tensor, axis, split_axis=0, concat_axis=0, tiled=True)  16.3 us
    all_to_all x3, starting transfers between devices, swap(): return lax.all_to_all(tensor, axis, split_axis=0, concat_axis=0, tiled=True)  12.5 us
    ppermute x18, starting transfers between devices, across(): return lax.ppermute(tensor, axis, [(i, i ^ distance) for i in range(size)])  8.19 us
    pallas_call x1, Pallas kernels, finish(): pl.pallas_call(lambda *refs: finish_kernel(width // quad, *refs), grid=(r...  6.55 us
  transfers between devices with their start and end apart: 21, of which 13 were waited for; matrix products, arithmetic and copies ran while one was open for 3% of the time, Pallas kernels for 30%

profile of v8, /device:TPU:0, one launch (start us, length us, event | category | flops | bytes accessed | tf_op | source)
XLA Modules:
  0.0 191.8 jit_solution(11505587810016235284)
XLA Ops:
  0.6 33.1 %all_to_all.20 = bf16[8,128,512]{2,1,0:T(8,128)(2,1)} all-to-all(bf16[8,128,512]{2,1,0:T(8,128)(2,1)} %param.9), channel_id=1, replica_groups=mesh['sample'=4,'turb'=8] {'turb'}, dimensions={0} | all-to-all | bytes 2097152 | tf_op jit(solution)/shard_map/all_to_all | solution.py:590
  33.8 3.6 %all-to-all-start.1 = ((bf16[8,128,512]{2,1,0:T(8,128)(2,1)}), bf16[8,128,512]{2,1,0:T(8,128)(2,1)S(1)}, u32[]{:S(2)}, u32[]{:S(2)}) async-start(bf16[8,128,512]{2,1,0:T(8,128)(2,1)} %param.10), calls=%async_computation.1 | async-start | bytes 2097152 | tf_op jit(solution)/shard_map/all_to_all | solution.py:590
  37.4 21.9 %forward.1 = (bf16[512,1024]{1,0:T(8,128)(2,1)}, bf16[1024,512]{1,0:T(8,128)(2,1)}, bf16[1024,512]{1,0:T(8,128)(2,1)}, bf16[1024,512]{1,0:T(8,128)(2,1)}, bf16[5...) custom-call(s32[8]{0:T(128)} %refs_0_.5, ...), custom_call_target="tpu_custom_call" | custom-call | flops 5368709120 | bytes 10485760 | tf_op jit(solution)/shard_map/forward/pallas_call | solution.py:367
  59.2 3.7 %all-to-all-done.1 = bf16[8,128,512]{2,1,0:T(8,128)(2,1)S(1)} async-done(((bf16[8,128,512]{2,1,0:T(8,128)(2,1)}), bf16[8,128,512]{2,1,0:T(8,128)(2,1)S(1)}, u32[]{:S(2)}, u32[]{:S(2)}) %all-to-all-start.1) | async-done | bytes 1048608 | tf_op jit(solution)/shard_map/all_to_all | solution.py:590
  63.0 1.0 copy-done
  63.9 3.7 %all-to-all-start.2 = ((bf16[8,128,512]{2,1,0:T(8,128)(2,1)}), bf16[8,128,512]{2,1,0:T(8,128)(2,1)S(1)}, u32[]{:S(2)}, u32[]{:S(2)}) async-start(bf16[8,128,512]{2,1,0:T(8,128)(2,1)} %bitcast.18), calls=%async_computation.2 | async-start | bytes 2097152 | tf_op jit(solution)/shard_map/all_to_all | solution.py:590
  67.7 0.6 broadcast_in_dim.4.refs_9_
  68.3 14.9 %backward.2 = (bf16[1024,256]{1,0:T(8,128)(2,1)}, bf16[1024,256]{1,0:T(8,128)(2,1)}, bf16[1024,256]{1,0:T(8,128)(2,1)}, f32[1024,256]{1,0:T(8,128)}, bf16[1024,256]{1,0:T(8,128)(2,1)}, /*index=5*/f32[8,512]{1,0:T(8,128)}) custom-call(s32[8]{0:T(128)} %refs_0_.5, s32[3,8,8]{2,1,0:T(8,128)} %bitcast.25, bf16[512,512]{1,0:T(8,128)(2,1)} %refs_2_.3, ...), custom_call_target="tpu_custom_call" | custom-call | flops 4026531840 | bytes 7340032 | tf_op jit(solution)/shard_map/backward/pallas_call | solution.py:505
  83.2 1.0 collective-permute-start
  84.2 15.0 %backward.3 = (bf16[1024,256]{1,0:T(8,128)(2,1)}, bf16[1024,256]{1,0:T(8,128)(2,1)}, bf16[1024,256]{1,0:T(8,128)(2,1)}, f32[1024,256]{1,0:T(8,128)}, f32[1024,256]{1,0:T(8,128)}, /*index=5*/f32[8,512]{1,0:T(8,128)}) custom-call(s32[8]{0:T(128)} %refs_0_.5, s32[3,8,8]{2,1,0:T(8,128)} %bitcast.26, bf16[512,512]{1,0:T(8,128)(2,1)} %refs_2_.3, ...), custom_call_target="tpu_custom_call" | custom-call | flops 4026531840 | bytes 7340032 | tf_op jit(solution)/shard_map/backward/pallas_call | solution.py:505
  99.2 0.0 all-to-all-done.2
  99.2 0.0 collective-permute-done
  99.2 0.0 copy-start.5
  99.2 0.8 copy-done.5
  100.0 1.5 convert_add_fusion
  101.5 0.8 slice.148
  102.3 0.5 collective-permute-start.1
  102.8 0.7 slice_reduce_fusion
  103.6 0.1 collective-permute-start.4
  103.7 6.5 %finish.1 = bf16[1024,512]{1,0:T(8,128)(2,1)} custom-call(bf16[1024,512]{1,0:T(8,128)(2,1)} %bitcast.14, bf16[1024,512]{1,0:T(8,128)(2,1)} %bitcast.17, f32[1,512]{1,0:T(1,128)} %bitcast.22, bf16[512,512]{1,0:T(8,128)(2,1)} %refs_3_.1, bf16[512,512]{1,0:T(8,128)(2,1)} %refs_4_.3, bf16[512,512]{1,0:T(8,128)(2,1)} %refs_5_.3, ...), custom_call_target="tpu_custom_call" | custom-call | flops 1610612736 | bytes 8388608 | tf_op jit(solution)/shard_map/finish/pallas_call | solution.py:570
  110.2 0.0 collective-permute-done.4
  110.2 0.1 add.60
  110.4 0.0 copy-start.1
  110.4 1.0 copy-done.1
  111.4 0.7 pad_maximum_fusion
  112.1 2.2 %collective-permute-start.5 = (bf16[528,256]{1,0:T(8,128)(2,1)}, bf16[528,256]{1,0:T(8,128)(2,1)S(1)}, u32[]{:S(2)}, u32[]{:S(2)}) collective-permute-start(bf16[528,256]{1,0:T(8,128)(2,1)} %pad_maximum_fusion), channel_id=1, source_target_pairs={{0,16},{8,24},{16,0},{24,8},{1,17},{9,25},{17,1},{25,9},{2,18},{10... | collective-permute-start | bytes 811016 | tf_op jit(solution)/shard_map/ppermute | solution.py:600
  114.3 5.2 %all-to-all-start.3 = ((bf16[8,128,512]{2,1,0:T(8,128)(2,1)}), bf16[8,128,512]{2,1,0:T(8,128)(2,1)S(1)}, u32[]{:S(2)}, u32[]{:S(2)}) async-start(bf16[8,128,512]{2,1,0:T(8,128)(2,1)} %bitcast.5), calls=%async_computation.3 | async-start | bytes 2097152 | tf_op jit(solution)/shard_map/all_to_all | solution.py:590
  119.5 1.2 slice_add_fusion.1
  120.7 0.1 collective-permute-start.2
  120.8 0.8 collective-permute-done.5
  121.7 0.1 slice_add_fusion
  121.8 1.3 collective-permute-start.6
  123.1 3.0 %collective-permute-done.2 = bf16[256,256]{1,0:T(8,128)(2,1)S(1)} collective-permute-done((bf16[256,256]{1,0:T(8,128)(2,1)S(1)}, bf16[256,256]{1,0:T(8,128)(2,1)S(1)}, u32[]{:S(2)}, u32[]{:S(2)}) %collective-permute-start.2) | collective-permute-done | bytes 131104 | tf_op jit(solution)/shard_map/ppermute | solution.py:600
  126.1 6.8 %collective-permute-done.6 = bf16[272,256]{1,0:T(8,128)(2,1)S(1)} collective-permute-done((bf16[272,256]{1,0:T(8,128)(2,1)S(1)}, bf16[272,256]{1,0:T(8,128)(2,1)S(1)}, u32[]{:S(2)}, u32[]{:S(2)}) %collective-permute-start.6) | collective-permute-done | bytes 139296 | tf_op jit(solution)/shard_map/ppermute | solution.py:600
  133.0 12.6 %all-to-all-done.3 = bf16[8,128,512]{2,1,0:T(8,128)(2,1)S(1)} async-done(((bf16[8,128,512]{2,1,0:T(8,128)(2,1)}), bf16[8,128,512]{2,1,0:T(8,128)(2,1)S(1)}, u32[]{:S(2)}, u32[]{:S(2)}) %all-to-all-start.3) | async-done | bytes 1048608 | tf_op jit(solution)/shard_map/all_to_all | solution.py:590
  145.6 0.2 concatenate.29
  145.8 0.1 collective-permute-start.7
  145.9 8.5 %collective-permute-done.7 = bf16[272,256]{1,0:T(8,128)(2,1)S(1)} collective-permute-done((bf16[272,256]{1,0:T(8,128)(2,1)S(1)}, bf16[272,256]{1,0:T(8,128)(2,1)S(1)}, u32[]{:S(2)}, u32[]{:S(2)}) %collective-permute-start.7) | collective-permute-done | bytes 139296 | tf_op jit(solution)/shard_map/ppermute | solution.py:600
  154.5 0.2 concatenate.30
  154.6 0.1 collective-permute-start.8
  154.7 4.3 %collective-permute-done.8 = bf16[144,256]{1,0:T(8,128)(2,1)S(1)} collective-permute-done((bf16[144,256]{1,0:T(8,128)(2,1)S(1)}, bf16[144,256]{1,0:T(8,128)(2,1)S(1)}, u32[]{:S(2)}, u32[]{:S(2)}) %collective-permute-start.8) | collective-permute-done | bytes 73760 | tf_op jit(solution)/shard_map/ppermute | solution.py:600
  159.1 0.2 collective-permute-start.9
  159.2 4.2 %collective-permute-done.9 = bf16[1,2,64,256]{3,2,1,0:T(8,128)(2,1)S(1)} collective-permute-done((bf16[1,2,64,256]{3,2,1,0:T(8,128)(2,1)S(1)}, bf16[1,2,64,256]{3,2,1,0:T(8,128)(2,1)S(1)}, u32[]{:S(2)}, u32[]{:S(2)}) %collective-permute-start.9) | collective-permute-done | bytes 65568 | tf_op jit(solution)/shard_map/ppermute | solution.py:600
  163.4 0.1 collective-permute-start.10
  163.5 6.8 %collective-permute-done.10 = bf16[2,2,64,256]{3,2,1,0:T(8,128)(2,1)S(1)} collective-permute-done((bf16[2,2,64,256]{3,2,1,0:T(8,128)(2,1)S(1)}, bf16[2,2,64,256]{3,2,1,0:T(8,128)(2,1)S(1)}, u32[]{:S(2)}, u32[]{:S(2)}) %collective-permute-start.10) | collective-permute-done | bytes 131104 | tf_op jit(solution)/shard_map/ppermute | solution.py:600
  170.3 0.0 copy-start.4
  170.4 1.4 collective-permute-start.11
  171.7 0.3 collective-permute-start.12
  172.0 4.8 %collective-permute-done.11.refs_1_ = bf16[4,2,64,256]{3,2,1,0:T(8,128)(2,1)S(1)} collective-permute-done((bf16[4,2,64,256]{3,2,1,0:T(8,128)(2,1)S(1)}, bf16[4,2,64,256]{3,2,1,0:T(8,128)(2,1)S(1)}, u32[]{:S(2)}, u32[]{:S(2)}) %collective-permute-start.11) | collective-permute-done | bytes 262176 | tf_op jit(solution)/shard_map/ppermute | solution.py:600
  176.8 0.5 collective-permute-start.13
  177.3 0.0 collective-permute-start.14
  177.3 0.5 collective-permute-start.15
  177.8 3.1 %collective-permute-done.12.refs_2_ = bf16[4,2,64,256]{3,2,1,0:T(8,128)(2,1)S(1)} collective-permute-done((bf16[4,2,64,256]{3,2,1,0:T(8,128)(2,1)S(1)}, bf16[4,2,64,256]{3,2,1,0:T(8,128)(2,1)S(1)}, u32[]{:S(2)}, u32[]{:S(2)}) %collective-permute-start.12) | collective-permute-done | bytes 262176 | tf_op jit(solution)/shard_map/ppermute | solution.py:600
  180.9 0.0 collective-permute-start.16
  180.9 2.8 %collective-permute-done.13.refs_3_ = bf16[4,2,64,256]{3,2,1,0:T(8,128)(2,1)S(1)} collective-permute-done((bf16[4,2,64,256]{3,2,1,0:T(8,128)(2,1)S(1)}, bf16[4,2,64,256]{3,2,1,0:T(8,128)(2,1)S(1)}, u32[]{:S(2)}, u32[]{:S(2)}) %collective-permute-start.13) | collective-permute-done | bytes 262176 | tf_op jit(solution)/shard_map/ppermute | solution.py:600
  183.7 0.0 collective-permute-start.17
  183.7 0.6 copy.16
  184.4 0.0 collective-permute-done.16.refs_6_
  184.4 0.8 collective-permute-done.17.refs_7_
  185.3 0.0 copy-done.11
  185.3 0.7 copy-done.12
  186.0 3.9 %place.1 = (f32[512,512]{1,0:T(8,128)}, f32[512,512]{1,0:T(8,128)}, f32[512,512]{1,0:T(8,128)}, f32[512,512]{1,0:T(8,128)}) custom-call(bf16[4,2,64,256]{3,2,1,0:T(8,128)(2,1)} %copy-done.4, bf16[4,2,64,256]{3,2,1,0:T(8,128)(2,1)} %copy-done.6, bf16[4,2,64,256]{3,2,1,0:T(8,128)(2,1)} %copy-done.7, bf16[4,2,64,256]{3,2,1,0:T(8,128)(2,1)} %copy-done.8, ...), custom_call_target="tpu_custom_call" | custom-call | bytes 6291456 | tf_op jit(solution)/shard_map/place/pallas_call | solution.py:663
  189.9 1.0 copy.19
  190.8 1.0 copy.20
  (50 shorter events, 0.4 us)
Async XLA Ops:
  33.8 29.2 %all-to-all-start.1 = ((bf16[8,128,512]{2,1,0:T(8,128)(2,1)}), bf16[8,128,512]{2,1,0:T(8,128)(2,1)S(1)}, u32[]{:S(2)}, u32[]{:S(2)}) async-start(bf16[8,128,512]{2,1,0:T(8,128)(2,1)} %param.10), calls=%async_computation.1 | async-start | bytes 2097152 | tf_op jit(solution)/shard_map/all_to_all | solution.py:590
  63.0 1.0 copy-start
  63.9 35.3 %all-to-all-start.2 = ((bf16[8,128,512]{2,1,0:T(8,128)(2,1)}), bf16[8,128,512]{2,1,0:T(8,128)(2,1)S(1)}, u32[]{:S(2)}, u32[]{:S(2)}) async-start(bf16[8,128,512]{2,1,0:T(8,128)(2,1)} %bitcast.18), calls=%async_computation.2 | async-start | bytes 2097152 | tf_op jit(solution)/shard_map/all_to_all | solution.py:590
  83.2 16.0 %collective-permute-start = (bf16[1024,256]{1,0:T(8,128)(2,1)}, bf16[1024,256]{1,0:T(8,128)(2,1)S(1)}, u32[]{:S(2)}, u32[]{:S(2)}) collective-permute-start(bf16[1024,256]{1,0:T(8,128)(2,1)} %get-tuple-element.59), channel_id=1, source_target_pairs={{0,1},{1,0},{2,3},{3,2},{4,5},{5,4},{6,7},{7,6},{8,9},{9,8},{10,11... | collective-permute-start | bytes 1572872 | tf_op jit(solution)/shard_map/ppermute | solution.py:600
  99.2 0.8 copy-start.5
  100.0 10.2 %collective-permute-start.3 = (f32[1024,256]{1,0:T(8,128)}, f32[1024,256]{1,0:T(8,128)S(1)}, u32[]{:S(2)}, u32[]{:S(2)}) collective-permute-start(f32[1024,256]{1,0:T(8,128)} %get-tuple-element.71), channel_id=1, source_target_pairs={{0,8},{8,0},{16,24},{24,16},{1,9},{9,1},{17,25},{25,17},{2,10},{10... | collective-permute-start | bytes 3145736 | tf_op jit(solution)/shard_map/ppermute | solution.py:600
  102.3 17.2 %collective-permute-start.1 = (f32[512,256]{1,0:T(8,128)}, f32[512,256]{1,0:T(8,128)}, u32[]{:S(2)}, u32[]{:S(2)}) collective-permute-start(f32[512,256]{1,0:T(8,128)} %slice.148), channel_id=1, source_target_pairs={{0,8},{8,0},{16,24},{24,16},{1,9},{9,1},{17,25},{25,17},{2,10},{10... | collective-permute-start | bytes 1572872 | tf_op jit(solution)/shard_map/ppermute | solution.py:600
  103.6 6.6 %collective-permute-start.4 = (f32[2,256]{1,0:T(2,128)S(1)}, f32[2,256]{1,0:T(2,128)S(1)}, u32[]{:S(2)}, u32[]{:S(2)}) collective-permute-start(f32[2,256]{1,0:T(2,128)S(1)} %reshape_squeeze.3), channel_id=1, source_target_pairs={{0,8},{8,0},{16,24},{24,16},{1,9},{9,1},{17,25},{25,17},{2,10},{10... | collective-permute-start | bytes 6152 | tf_op jit(solution)/shard_map/ppermute | solution.py:600
  103.7 6.6 %copy-start.3 = (f32[1024,256]{1,0:T(8,128)S(1)}, f32[1024,256]{1,0:T(8,128)}, u32[]{:S(2)}) copy-start(f32[1024,256]{1,0:T(8,128)} %get-tuple-element.73) | copy-start | bytes 3145732
  110.4 1.0 copy-start.1
  112.1 9.5 %collective-permute-start.5 = (bf16[528,256]{1,0:T(8,128)(2,1)}, bf16[528,256]{1,0:T(8,128)(2,1)S(1)}, u32[]{:S(2)}, u32[]{:S(2)}) collective-permute-start(bf16[528,256]{1,0:T(8,128)(2,1)} %pad_maximum_fusion), channel_id=1, source_target_pairs={{0,16},{8,24},{16,0},{24,8},{1,17},{9,25},{17,1},{25,9},{2,18},{10... | collective-permute-start | bytes 811016 | tf_op jit(solution)/shard_map/ppermute | solution.py:600
  114.3 31.3 %all-to-all-start.3 = ((bf16[8,128,512]{2,1,0:T(8,128)(2,1)}), bf16[8,128,512]{2,1,0:T(8,128)(2,1)S(1)}, u32[]{:S(2)}, u32[]{:S(2)}) async-start(bf16[8,128,512]{2,1,0:T(8,128)(2,1)} %bitcast.5), calls=%async_computation.3 | async-start | bytes 2097152 | tf_op jit(solution)/shard_map/all_to_all | solution.py:590
  119.5 2.2 %copy-start.2 = (f32[1024,256]{1,0:T(8,128)S(1)}, f32[1024,256]{1,0:T(8,128)}, u32[]{:S(2)}) copy-start(f32[1024,256]{1,0:T(8,128)} %copy-done.1) | copy-start | bytes 3145732
  120.7 5.4 %collective-permute-start.2 = (bf16[256,256]{1,0:T(8,128)(2,1)S(1)}, bf16[256,256]{1,0:T(8,128)(2,1)S(1)}, u32[]{:S(2)}, u32[]{:S(2)}) collective-permute-start(bf16[256,256]{1,0:T(8,128)(2,1)S(1)} %slice.233), channel_id=1, source_target_pairs={{0,16},{8,24},{16,0},{24,8},{1,17},{9,25},{17,1},{25,9},{2,18},{10... | collective-permute-start | bytes 393224 | tf_op jit(solution)/shard_map/ppermute | solution.py:600
  121.8 11.2 %collective-permute-start.6 = (bf16[272,256]{1,0:T(8,128)(2,1)S(1)}, bf16[272,256]{1,0:T(8,128)(2,1)S(1)}, u32[]{:S(2)}, u32[]{:S(2)}) collective-permute-start(bf16[272,256]{1,0:T(8,128)(2,1)S(1)} %pad_maximum_fusion.2), channel_id=1, source_target_pairs={{0,1},{1,0},{2,3},{3,2},{4,5},{5,4},{6,7},{7,6},{8,9},{9,8},{10,11... | collective-permute-start | bytes 417800 | tf_op jit(solution)/shard_map/ppermute | solution.py:600
  145.8 8.6 %collective-permute-start.7 = (bf16[272,256]{1,0:T(8,128)(2,1)S(1)}, bf16[272,256]{1,0:T(8,128)(2,1)S(1)}, u32[]{:S(2)}, u32[]{:S(2)}) collective-permute-start(bf16[272,256]{1,0:T(8,128)(2,1)S(1)} %concatenate.29), channel_id=1, source_target_pairs={{0,4},{1,5},{2,6},{3,7},{4,0},{5,1},{6,2},{7,3},{8,12},{9,13},{10,... | collective-permute-start | bytes 417800 | tf_op jit(solution)/shard_map/ppermute | solution.py:600
  154.6 4.4 %collective-permute-start.8 = (bf16[144,256]{1,0:T(8,128)(2,1)S(1)}, bf16[144,256]{1,0:T(8,128)(2,1)S(1)}, u32[]{:S(2)}, u32[]{:S(2)}) collective-permute-start(bf16[144,256]{1,0:T(8,128)(2,1)S(1)} %concatenate.30), channel_id=1, source_target_pairs={{0,2},{1,3},{2,0},{3,1},{4,6},{5,7},{6,4},{7,5},{8,10},{9,11},{10,... | collective-permute-start | bytes 221192 | tf_op jit(solution)/shard_map/ppermute | solution.py:600
  159.1 4.3 %collective-permute-start.9 = (bf16[1,2,64,256]{3,2,1,0:T(8,128)(2,1)S(1)}, bf16[1,2,64,256]{3,2,1,0:T(8,128)(2,1)S(1)}, u32[]{:S(2)}, u32[]{:S(2)}) collective-permute-start(bf16[1,2,64,256]{3,2,1,0:T(8,128)(2,1)S(1)} %pad_maximum_fusion.4), channel_id=1, source_target_pairs={{0,2},{1,3},{2,0},{3,1},{4,6},{5,7},{6,4},{7,5},{8,10},{9,11},{10,... | collective-permute-start | bytes 196616 | tf_op jit(solution)/shard_map/ppermute | solution.py:600
  163.4 6.9 %collective-permute-start.10 = (bf16[2,2,64,256]{3,2,1,0:T(8,128)(2,1)S(1)}, bf16[2,2,64,256]{3,2,1,0:T(8,128)(2,1)S(1)}, u32[]{:S(2)}, u32[]{:S(2)}) collective-permute-start(bf16[2,2,64,256]{3,2,1,0:T(8,128)(2,1)S(1)} %pad_maximum_fusion.3), channel_id=1, source_target_pairs={{0,4},{1,5},{2,6},{3,7},{4,0},{5,1},{6,2},{7,3},{8,12},{9,13},{10,... | collective-permute-start | bytes 393224 | tf_op jit(solution)/shard_map/ppermute | solution.py:600
  170.3 14.9 %copy-start.4 = (bf16[4,2,64,256]{3,2,1,0:T(8,128)(2,1)}, bf16[4,2,64,256]{3,2,1,0:T(8,128)(2,1)S(1)}, u32[]{:S(2)}) copy-start(bf16[4,2,64,256]{3,2,1,0:T(8,128)(2,1)S(1)} %pad_maximum_fusion.1.refs_0_) | copy-start | bytes 786436
  170.4 6.4 %collective-permute-start.11 = (bf16[4,2,64,256]{3,2,1,0:T(8,128)(2,1)S(1)}, bf16[4,2,64,256]{3,2,1,0:T(8,128)(2,1)S(1)}, u32[]{:S(2)}, u32[]{:S(2)}) collective-permute-start(bf16[4,2,64,256]{3,2,1,0:T(8,128)(2,1)S(1)} %pad_maximum_fusion.1.refs_0_), channel_id=1, source_target_pairs={{0,1},{1,0},{2,3},{3,2},{4,5},{5,4},{6,7},{7,6},{8,9},{9,8},{10,11... | collective-permute-start | bytes 786440 | tf_op jit(solution)/shard_map/ppermute | solution.py:600
  171.7 9.1 %collective-permute-start.12 = (bf16[4,2,64,256]{3,2,1,0:T(8,128)(2,1)S(1)}, bf16[4,2,64,256]{3,2,1,0:T(8,128)(2,1)S(1)}, u32[]{:S(2)}, u32[]{:S(2)}) collective-permute-start(bf16[4,2,64,256]{3,2,1,0:T(8,128)(2,1)S(1)} %pad_maximum_fusion.1.refs_0_), channel_id=1, source_target_pairs={{0,16},{8,24},{16,0},{24,8},{1,17},{9,25},{17,1},{25,9},{2,18},{10... | collective-permute-start | bytes 786440 | tf_op jit(solution)/shard_map/ppermute | solution.py:600
  176.8 8.4 %copy-start.6 = (bf16[4,2,64,256]{3,2,1,0:T(8,128)(2,1)}, bf16[4,2,64,256]{3,2,1,0:T(8,128)(2,1)S(1)}, u32[]{:S(2)}) copy-start(bf16[4,2,64,256]{3,2,1,0:T(8,128)(2,1)S(1)} %collective-permute-done.11.refs_1_) | copy-start | bytes 786436
  176.8 6.9 %collective-permute-start.13 = (bf16[4,2,64,256]{3,2,1,0:T(8,128)(2,1)S(1)}, bf16[4,2,64,256]{3,2,1,0:T(8,128)(2,1)S(1)}, u32[]{:S(2)}, u32[]{:S(2)}) collective-permute-start(bf16[4,2,64,256]{3,2,1,0:T(8,128)(2,1)S(1)} %collective-permute-done.11.refs_1_), channel_id=1, source_target_pairs={{0,16},{8,24},{16,0},{24,8},{1,17},{9,25},{17,1},{25,9},{2,18},{10... | collective-permute-start | bytes 786440 | tf_op jit(solution)/shard_map/ppermute | solution.py:600
  177.3 7.1 %collective-permute-start.14 = (bf16[4,2,64,256]{3,2,1,0:T(8,128)(2,1)S(1)}, bf16[4,2,64,256]{3,2,1,0:T(8,128)(2,1)S(1)}, u32[]{:S(2)}, u32[]{:S(2)}) collective-permute-start(bf16[4,2,64,256]{3,2,1,0:T(8,128)(2,1)S(1)} %pad_maximum_fusion.1.refs_0_), channel_id=1, source_target_pairs={{0,8},{8,0},{16,24},{24,16},{1,9},{9,1},{17,25},{25,17},{2,10},{10... | collective-permute-start | bytes 786440 | tf_op jit(solution)/shard_map/ppermute | solution.py:600
  177.3 7.1 %collective-permute-start.15 = (bf16[4,2,64,256]{3,2,1,0:T(8,128)(2,1)S(1)}, bf16[4,2,64,256]{3,2,1,0:T(8,128)(2,1)S(1)}, u32[]{:S(2)}, u32[]{:S(2)}) collective-permute-start(bf16[4,2,64,256]{3,2,1,0:T(8,128)(2,1)S(1)} %collective-permute-done.11.refs_1_), channel_id=1, source_target_pairs={{0,8},{8,0},{16,24},{24,16},{1,9},{9,1},{17,25},{25,17},{2,10},{10... | collective-permute-start | bytes 786440 | tf_op jit(solution)/shard_map/ppermute | solution.py:600
  180.9 4.4 %copy-start.7 = (bf16[4,2,64,256]{3,2,1,0:T(8,128)(2,1)}, bf16[4,2,64,256]{3,2,1,0:T(8,128)(2,1)S(1)}, u32[]{:S(2)}) copy-start(bf16[4,2,64,256]{3,2,1,0:T(8,128)(2,1)S(1)} %collective-permute-done.12.refs_2_) | copy-start | bytes 786436
  180.9 3.5 %collective-permute-start.16 = (bf16[4,2,64,256]{3,2,1,0:T(8,128)(2,1)S(1)}, bf16[4,2,64,256]{3,2,1,0:T(8,128)(2,1)S(1)}, u32[]{:S(2)}, u32[]{:S(2)}) collective-permute-start(bf16[4,2,64,256]{3,2,1,0:T(8,128)(2,1)S(1)} %collective-permute-done.12.refs_2_), channel_id=1, source_target_pairs={{0,8},{8,0},{16,24},{24,16},{1,9},{9,1},{17,25},{25,17},{2,10},{10... | collective-permute-start | bytes 786440 | tf_op jit(solution)/shard_map/ppermute | solution.py:600
  183.7 1.6 copy-start.8
  183.7 1.5 collective-permute-start.17
  184.3 0.9 copy-start.9
  184.3 0.9 copy-start.10
  184.4 0.9 copy-start.11
  185.3 0.7 copy-start.12

commit v9 on v8

--- a/solution.py
+++ b/solution.py
@@ -396,7 +396,8 @@
 
 
 def backward_kernel(block_rows, head_dim, which, sectors_ref, lists_ref, wo_ref, q_ref, k_ref, v_ref,
-                    kt_ref, level_ref, gain_ref, before_ref, *refs):
+                    kt_ref, level_ref, gain_ref, *refs):
+    before, refs = refs[:which], refs[which:]
     late, refs = refs[:6], refs[6:]
     gq_ref, gk_ref, gv_ref, keep_ref, send_ref, sum_ref, *refs = refs
     ga_ref, gk_acc, gv_acc, parts_ref, *held, sems = refs
@@ -486,7 +487,7 @@
     coarse = along.astype(jnp.bfloat16)
     fine = (along - coarse.astype(jnp.float32)).astype(jnp.bfloat16)
     total = (contract(ones, coarse, 1, 1) + contract(ones, fine, 1, 1)) / gain_ref[...]
-    sum_ref[...] = before_ref[...] + total
+    sum_ref[...] = sum((ref[...] for ref in before), total)
 
 
 def backward(sectors, adjacency, cotangent, out_weight, normed_t, queries, keys, values, keys_t,
@@ -509,7 +510,8 @@
             grid=(1,),
             in_specs=[down(width)]
             + [across] * 3
-            + [down(row_count), stat, fixed(1, width), fixed(SUM_ROWS, width)]
+            + [down(row_count), stat, fixed(1, width)]
+            + [fixed(SUM_ROWS, width)] * which
             + [pl.BlockSpec(memory_space=pl.ANY)] * 6,
             out_specs=[fixed(row_count, quad)] * 3
             + [fixed(*half)] * 2
@@ -539,7 +541,7 @@
         ),
         name="backward",
     )(sectors, adjacency, out_weight, queries, keys, values, keys_t, levels,
-      norm_gain.reshape(1, width), before, cotangent, normed_t, attended_t, query_weight, key_weight,
+      norm_gain.reshape(1, width), *before, cotangent, normed_t, attended_t, query_weight, key_weight,
       value_weight)
 
 
@@ -630,11 +632,17 @@
     second, gain = halve([late], gain, "sample", 2)
     second, gain = halve(second, gain, "turb", 1)
     parts, gain, beside = lax.optimization_barrier((first + second, gain, beside))
-    for distance in (4, 2):
-        parts, gain = halve(parts, gain, "turb", distance)
-    total = jnp.stack(parts).astype(jnp.bfloat16)[None]
-    for distance in (2, 4):
-        total = jnp.concatenate([total, across(total, "turb", distance)])
+    share = parts[0].shape[0] // 4
+    pieces = [jnp.concatenate([part[i * share : (i + 1) * share] for part in parts]) for i in range(4)]
+    size = pieces[0].shape[0]
+    sent = [jnp.concatenate([piece.astype(jnp.bfloat16), pack(gain)]) for piece in pieces[1:]]
+    arrived = [across(piece, "turb", 2 * i + 2).astype(wide) for i, piece in enumerate(sent)]
+    total = pieces[0] + sum(rows[:size] for rows in arrived)
+    gain = gain + sum(
+        rows[size : size + count] + rows[size + count : size + 2 * count] for rows in arrived
+    )
+    total = total.astype(jnp.bfloat16).reshape(1, 2, share, quad)
+    total = jnp.concatenate([total] + [across(total, "turb", distance) for distance in (2, 4, 6)])
     other = across(total, "turb", 1)
     four = [total, other, across(total, "sample", 2), across(other, "sample", 2)]
     four += [across(part, "sample", 1) for part in four]
@@ -698,31 +706,33 @@
     )
     layer_output = swap(layer_rows.reshape(inflow.shape), "turb")
     weights = (norm_gain, query_weight, key_weight, value_weight)
-    none = jnp.zeros((SUM_ROWS, width), jnp.float32)
     *grads, early, send, before = backward(
-        sectors, adjacency, grad_rows, out_weight, *saved, *weights, none, block_rows, 0
+        sectors, adjacency, grad_rows, out_weight, *saved, *weights, [], block_rows, 0
     )
     arrived = across(send, "turb", 1)
     *more, late, send, gain = backward(
-        sectors, adjacency, grad_rows, out_weight, *saved, *weights, before, block_rows, 1
-    )
-    late, send, gain, arrived, layer_output = lax.optimization_barrier(
-        (late, send, gain, arrived, layer_output)
+        sectors, adjacency, grad_rows, out_weight, *saved, *weights, [before], block_rows, 1
+    )
+    arrived_late = across(send, "sample", 1)
+    grad_rows = finish(rows, grad_rows, *weights, grads + more)
+    grad_rows, late, arrived_late, gain, early, arrived, layer_output = lax.optimization_barrier(
+        (grad_rows, late, arrived_late, gain, early, arrived, layer_output)
     )
     gain = gain[0].reshape(-1, late.shape[1])
     arrived_gain = across(gain, "sample", 1)
-    arrived_late = across(send, "sample", 1)
     early = early + arrived.astype(jnp.float32)
-    grad_rows = finish(rows, grad_rows, *weights, grads + more)
-    grad_rows, late, arrived_late, arrived_gain = lax.optimization_barrier(
-        (grad_rows, late, arrived_late, arrived_gain)
-    )
     grad_inflow = swap(grad_rows.reshape(inflow.shape), "turb")
     parts, sum_gain, grad_inflow = reduce_sums(
         early, late + arrived_late, gain + arrived_gain, width, grad_inflow
     )
     sums = place_sums(parts, width)
-    return (layer_output, grad_inflow, *sums, sum_gain)
+    lowest = jnp.finfo(jnp.bfloat16).min
+    return (
+        jnp.maximum(layer_output, lowest),
+        jnp.maximum(grad_inflow, lowest),
+        *sums,
+        sum_gain,
+    )
 
 
 def solution(mesh):

time: 192 us -> 188 us (0.979)
  waiting for transfers between devices: 62.3 us -> 50.3 us
  starting transfers between devices: 20.7 us -> 28.5 us
  local copies, waits for them, and re-layouts: 8.65 us -> 5.5 us
  other arithmetic: 3.8 us -> 5.73 us
    ppermute x18 -> x20, starting transfers between devices: 8.19 us -> 17 us  [across(): return lax.ppermute(tensor, axis, [(i, i ^ distance) for i in range(size)])]
    ppermute x18 -> x20, waiting for transfers between devices: 46 us -> 39.2 us  [across(): return lax.ppermute(tensor, axis, [(i, i ^ distance) for i in range(size)])]
    all_to_all x3, waiting for transfers between devices: 16.3 us -> 11.1 us  [swap(): return lax.all_to_all(tensor, axis, split_axis=0, concat_axis=0, tiled=True)]
    unnamed x29, local copies, waits for them, and re-layouts: 6.07 us -> 3.36 us
    max x0 -> x2, other arithmetic: none -> 2.13 us  [the longest x1 1.06 us: by_sample(): jnp.maximum(grad_inflow, lowest)]
  transfers between devices with their start and end apart: 21 -> 23, of which waited for: 13 -> 13; matrix products, arithmetic and copies ran while one was open for 3% -> 3% of each run, Pallas kernels for 30% -> 31%
where the time goes in v9:
time: 188 us; the launch traced here: 186 us
  Pallas kernels  62.4 us (33%)
  waiting for transfers between devices  50.3 us (27%)
  blocking collectives  33.1 us (18%)
  starting transfers between devices  28.5 us (15%)
  other arithmetic  5.73 us (3%)
  local copies, waits for them, and re-layouts  5.5 us (3%)
    ppermute x20, waiting for transfers between devices, across(): return lax.ppermute(tensor, axis, [(i, i ^ distance) for i in range(size)])  39.2 us
    all_to_all x1, blocking collectives, swap(): return lax.all_to_all(tensor, axis, split_axis=0, concat_axis=0, tiled=True)  33.1 us
    pallas_call x2, Pallas kernels, backward(): pl.pallas_call(lambda *refs: backward_kernel(block_rows, head_dim, which,...  30 us
    pallas_call x1, Pallas kernels, forward(): pl.pallas_call(lambda *refs: forward_kernel(block_rows, head_dim, *refs),...  22 us
    ppermute x20, starting transfers between devices, across(): return lax.ppermute(tensor, axis, [(i, i ^ distance) for i in range(size)])  17 us
    all_to_all x3, starting transfers between devices, swap(): return lax.all_to_all(tensor, axis, split_axis=0, concat_axis=0, tiled=True)  11.5 us
    all_to_all x3, waiting for transfers between devices, swap(): return lax.all_to_all(tensor, axis, split_axis=0, concat_axis=0, tiled=True)  11.1 us
    pallas_call x1, Pallas kernels, finish(): pl.pallas_call(lambda *refs: finish_kernel(width // quad, *refs), grid=(r...  6.54 us
  transfers between devices with their start and end apart: 23, of which 13 were waited for; matrix products, arithmetic and copies ran while one was open for 3% of the time, Pallas kernels for 31%

profile of v9, /device:TPU:0, one launch (start us, length us, event | category | flops | bytes accessed | tf_op | source)
XLA Modules:
  0.0 186.5 jit_solution(14598970530181224339)
XLA Ops:
  0.6 33.1 %all_to_all.20 = bf16[8,128,512]{2,1,0:T(8,128)(2,1)} all-to-all(bf16[8,128,512]{2,1,0:T(8,128)(2,1)} %param.9), channel_id=1, replica_groups=mesh['sample'=4,'turb'=8] {'turb'}, dimensions={0} | all-to-all | bytes 2097152 | tf_op jit(solution)/shard_map/all_to_all | solution.py:592
  33.8 3.6 %all-to-all-start.1 = ((bf16[8,128,512]{2,1,0:T(8,128)(2,1)}), bf16[8,128,512]{2,1,0:T(8,128)(2,1)S(1)}, u32[]{:S(2)}, u32[]{:S(2)}) async-start(bf16[8,128,512]{2,1,0:T(8,128)(2,1)} %param.10), calls=%async_computation.1 | async-start | bytes 2097152 | tf_op jit(solution)/shard_map/all_to_all | solution.py:592
  37.4 22.0 %forward.1 = (bf16[512,1024]{1,0:T(8,128)(2,1)}, bf16[1024,512]{1,0:T(8,128)(2,1)}, bf16[1024,512]{1,0:T(8,128)(2,1)}, bf16[1024,512]{1,0:T(8,128)(2,1)}, bf16[5...) custom-call(s32[8]{0:T(128)} %refs_0_.5, ...), custom_call_target="tpu_custom_call" | custom-call | flops 5368709120 | bytes 10485760 | tf_op jit(solution)/shard_map/forward/pallas_call | solution.py:367
  59.4 3.6 %all-to-all-done.1 = bf16[8,128,512]{2,1,0:T(8,128)(2,1)S(1)} async-done(((bf16[8,128,512]{2,1,0:T(8,128)(2,1)}), bf16[8,128,512]{2,1,0:T(8,128)(2,1)S(1)}, u32[]{:S(2)}, u32[]{:S(2)}) %all-to-all-start.1) | async-done | bytes 1048608 | tf_op jit(solution)/shard_map/all_to_all | solution.py:592
  63.0 1.0 copy-done
  63.9 3.7 %all-to-all-start.2 = ((bf16[8,128,512]{2,1,0:T(8,128)(2,1)}), bf16[8,128,512]{2,1,0:T(8,128)(2,1)S(1)}, u32[]{:S(2)}, u32[]{:S(2)}) async-start(bf16[8,128,512]{2,1,0:T(8,128)(2,1)} %bitcast.15), calls=%async_computation.2 | async-start | bytes 2097152 | tf_op jit(solution)/shard_map/all_to_all | solution.py:592
  67.7 14.9 %backward.2 = (bf16[1024,256]{1,0:T(8,128)(2,1)}, bf16[1024,256]{1,0:T(8,128)(2,1)}, bf16[1024,256]{1,0:T(8,128)(2,1)}, f32[1024,256]{1,0:T(8,128)}, bf16[1024,256]{1,0:T(8,128)(2,1)}, /*index=5*/f32[8,512]{1,0:T(8,128)}) custom-call(s32[8]{0:T(128)} %refs_0_.5, s32[3,8,8]{2,1,0:T(8,128)} %bitcast.26, bf16[512,512]{1,0:T(8,128)(2,1)} %refs_2_.3, ...), custom_call_target="tpu_custom_call" | custom-call | flops 4026531840 | bytes 7340032 | tf_op jit(solution)/shard_map/backward/pallas_call | solution.py:506
  82.6 15.1 %backward.3 = (bf16[1024,256]{1,0:T(8,128)(2,1)}, bf16[1024,256]{1,0:T(8,128)(2,1)}, bf16[1024,256]{1,0:T(8,128)(2,1)}, f32[1024,256]{1,0:T(8,128)}, f32[1024,256]{1,0:T(8,128)}, /*index=5*/f32[8,512]{1,0:T(8,128)}) custom-call(s32[8]{0:T(128)} %refs_0_.5, s32[3,8,8]{2,1,0:T(8,128)} %bitcast.27, bf16[512,512]{1,0:T(8,128)(2,1)} %refs_2_.3, ...), custom_call_target="tpu_custom_call" | custom-call | flops 4026531840 | bytes 7340032 | tf_op jit(solution)/shard_map/backward/pallas_call | solution.py:506
  97.7 0.1 collective-permute-start
  97.7 0.1 collective-permute-start.1
  97.8 6.5 %finish.1 = bf16[1024,512]{1,0:T(8,128)(2,1)} custom-call(bf16[1024,512]{1,0:T(8,128)(2,1)} %bitcast.11, bf16[1024,512]{1,0:T(8,128)(2,1)} %bitcast.14, f32[1,512]{1,0:T(1,128)} %bitcast.23, bf16[512,512]{1,0:T(8,128)(2,1)} %refs_3_.1, bf16[512,512]{1,0:T(8,128)(2,1)} %refs_4_.3, bf16[512,512]{1,0:T(8,128)(2,1)} %refs_5_.3, ...), custom_call_target="tpu_custom_call" | custom-call | flops 1610612736 | bytes 8388608 | tf_op jit(solution)/shard_map/finish/pallas_call | solution.py:572
  104.4 0.0 all-to-all-done.2
  104.4 8.0 %collective-permute-done.1 = bf16[1024,256]{1,0:T(8,128)(2,1)} collective-permute-done((bf16[1024,256]{1,0:T(8,128)(2,1)}, bf16[1024,256]{1,0:T(8,128)(2,1)}, u32[]{:S(2)}, u32[]{:S(2)}) %collective-permute-start.1) | collective-permute-done | bytes 524320 | tf_op jit(solution)/shard_map/ppermute | solution.py:602
  112.4 0.7 slice_reduce_fusion
  113.2 0.2 copy-done.4
  113.4 0.0 collective-permute-start.4
  113.4 1.4 add.63
  114.8 0.7 pad_maximum_fusion
  115.5 2.3 %collective-permute-start.5 = (bf16[528,256]{1,0:T(8,128)(2,1)}, bf16[528,256]{1,0:T(8,128)(2,1)S(1)}, u32[]{:S(2)}, u32[]{:S(2)}) collective-permute-start(bf16[528,256]{1,0:T(8,128)(2,1)} %pad_maximum_fusion), channel_id=1, source_target_pairs={{0,16},{8,24},{16,0},{24,8},{1,17},{9,25},{17,1},{25,9},{2,18},{10... | collective-permute-start | bytes 811016 | tf_op jit(solution)/shard_map/ppermute | solution.py:602
  117.8 4.2 %all-to-all-start.3 = ((bf16[8,128,512]{2,1,0:T(8,128)(2,1)}), bf16[8,128,512]{2,1,0:T(8,128)(2,1)S(1)}, u32[]{:S(2)}, u32[]{:S(2)}) async-start(bf16[8,128,512]{2,1,0:T(8,128)(2,1)} %bitcast.5), calls=%async_computation.3 | async-start | bytes 2097152 | tf_op jit(solution)/shard_map/all_to_all | solution.py:592
  122.0 3.2 %collective-permute-done.5 = bf16[528,256]{1,0:T(8,128)(2,1)S(1)} collective-permute-done((bf16[528,256]{1,0:T(8,128)(2,1)}, bf16[528,256]{1,0:T(8,128)(2,1)S(1)}, u32[]{:S(2)}, u32[]{:S(2)}) %collective-permute-start.5) | collective-permute-done | bytes 270368 | tf_op jit(solution)/shard_map/ppermute | solution.py:602
  125.2 0.1 slice_add_fusion
  125.3 1.0 collective-permute-start.6
  126.3 1.1 convert_add_fusion
  127.5 0.1 collective-permute-start.2
  127.6 7.9 %collective-permute-done.6 = bf16[272,256]{1,0:T(8,128)(2,1)S(1)} collective-permute-done((bf16[272,256]{1,0:T(8,128)(2,1)S(1)}, bf16[272,256]{1,0:T(8,128)(2,1)S(1)}, u32[]{:S(2)}, u32[]{:S(2)}) %collective-permute-start.6) | collective-permute-done | bytes 139296 | tf_op jit(solution)/shard_map/ppermute | solution.py:602
  135.5 0.0 copy-start.1
  135.5 0.1 slice_add_fusion.1
  135.6 0.9 collective-permute-start.3
  136.5 4.2 %collective-permute-done.3 = bf16[256,256]{1,0:T(8,128)(2,1)S(1)} collective-permute-done((bf16[256,256]{1,0:T(8,128)(2,1)S(1)}, bf16[256,256]{1,0:T(8,128)(2,1)S(1)}, u32[]{:S(2)}, u32[]{:S(2)}) %collective-permute-start.3) | collective-permute-done | bytes 131104 | tf_op jit(solution)/shard_map/ppermute | solution.py:602
  140.7 0.0 copy-start.2
  140.7 7.5 %all-to-all-done.3 = bf16[8,128,512]{2,1,0:T(8,128)(2,1)S(1)} async-done(((bf16[8,128,512]{2,1,0:T(8,128)(2,1)}), bf16[8,128,512]{2,1,0:T(8,128)(2,1)S(1)}, u32[]{:S(2)}, u32[]{:S(2)}) %all-to-all-start.3) | async-done | bytes 1048608 | tf_op jit(solution)/shard_map/all_to_all | solution.py:592
  148.2 0.2 concatenate.33
  148.4 0.1 collective-permute-start.7
  148.5 0.2 concatenate.34
  148.6 2.4 %collective-permute-start.8 = (bf16[144,256]{1,0:T(8,128)(2,1)S(1)}, bf16[144,256]{1,0:T(8,128)(2,1)S(1)}, u32[]{:S(2)}, u32[]{:S(2)}) collective-permute-start(bf16[144,256]{1,0:T(8,128)(2,1)S(1)} %concatenate.34), channel_id=1, source_target_pairs={{0,4},{1,5},{2,6},{3,7},{4,0},{5,1},{6,2},{7,3},{8,12},{9,13},{10,... | collective-permute-start | bytes 221192 | tf_op jit(solution)/shard_map/ppermute | solution.py:602
  151.0 0.1 concatenate.35
  151.2 2.1 %collective-permute-start.9 = (bf16[144,256]{1,0:T(8,128)(2,1)S(1)}, bf16[144,256]{1,0:T(8,128)(2,1)S(1)}, u32[]{:S(2)}, u32[]{:S(2)}) collective-permute-start(bf16[144,256]{1,0:T(8,128)(2,1)S(1)} %concatenate.35), channel_id=1, source_target_pairs={{0,6},{1,7},{2,4},{3,5},{4,2},{5,3},{6,0},{7,1},{8,14},{9,15},{10,... | collective-permute-start | bytes 221192 | tf_op jit(solution)/shard_map/ppermute | solution.py:602
  153.3 4.1 %collective-permute-done.8 = bf16[144,256]{1,0:T(8,128)(2,1)S(1)} collective-permute-done((bf16[144,256]{1,0:T(8,128)(2,1)S(1)}, bf16[144,256]{1,0:T(8,128)(2,1)S(1)}, u32[]{:S(2)}, u32[]{:S(2)}) %collective-permute-start.8) | collective-permute-done | bytes 73760 | tf_op jit(solution)/shard_map/ppermute | solution.py:602
  157.5 0.0 slice-start
  157.5 0.0 slice-start.1
  157.5 0.8 slice-done
  158.3 0.0 slice-done.1
  158.4 0.6 collective-permute-start.10
  158.9 1.4 collective-permute-start.11
  160.3 2.5 %collective-permute-start.12 = (bf16[1,2,64,256]{3,2,1,0:T(8,128)(2,1)S(1)}, bf16[1,2,64,256]{3,2,1,0:T(8,128)(2,1)S(1)}, u32[]{:S(2)}, u32[]{:S(2)}) collective-permute-start(bf16[1,2,64,256]{3,2,1,0:T(8,128)(2,1)S(1)} %bitcast.18), channel_id=1, source_target_pairs={{0,6},{1,7},{2,4},{3,5},{4,2},{5,3},{6,0},{7,1},{8,14},{9,15},{10,... | collective-permute-start | bytes 196616 | tf_op jit(solution)/shard_map/ppermute | solution.py:602
  162.8 1.3 collective-permute-done.10
  164.1 1.1 collective-permute-done.11
  165.2 1.3 collective-permute-done.12
  166.5 1.4 collective-permute-start.13
  168.0 0.8 collective-permute-start.14
  168.8 4.2 %collective-permute-done.13.refs_1_ = bf16[4,2,64,256]{3,2,1,0:T(8,128)(2,1)S(1)} collective-permute-done((bf16[4,2,64,256]{3,2,1,0:T(8,128)(2,1)S(1)}, bf16[4,2,64,256]{3,2,1,0:T(8,128)(2,1)S(1)}, u32[]{:S(2)}, u32[]{:S(2)}) %collective-permute-start.13) | collective-permute-done | bytes 262176 | tf_op jit(solution)/shard_map/ppermute | solution.py:602
  173.0 0.8 collective-permute-start.15
  173.8 1.1 broadcast_maximum_fusion.1
  174.8 0.5 collective-permute-start.17
  175.3 1.2 collective-permute-done.14.refs_2_
  176.5 2.8 %collective-permute-done.15.refs_3_ = bf16[4,2,64,256]{3,2,1,0:T(8,128)(2,1)S(1)} collective-permute-done((bf16[4,2,64,256]{3,2,1,0:T(8,128)(2,1)S(1)}, bf16[4,2,64,256]{3,2,1,0:T(8,128)(2,1)S(1)}, u32[]{:S(2)}, u32[]{:S(2)}) %collective-permute-start.15) | collective-permute-done | bytes 262176 | tf_op jit(solution)/shard_map/ppermute | solution.py:602
  179.4 1.1 broadcast_maximum_fusion
  180.4 0.6 copy.16
  181.1 0.7 copy-done.10
  181.7 0.1 copy-done.11
  181.8 0.1 copy-done.12
  181.9 0.7 copy-done.13
  182.6 3.9 %place.1 = (f32[512,512]{1,0:T(8,128)}, f32[512,512]{1,0:T(8,128)}, f32[512,512]{1,0:T(8,128)}, f32[512,512]{1,0:T(8,128)}) custom-call(bf16[4,2,64,256]{3,2,1,0:T(8,128)(2,1)} %copy-done.6, bf16[4,2,64,256]{3,2,1,0:T(8,128)(2,1)} %copy-done.7, bf16[4,2,64,256]{3,2,1,0:T(8,128)(2,1)} %copy-done.8, bf16[4,2,64,256]{3,2,1,0:T(8,128)(2,1)} %copy-done.9, ...), custom_call_target="tpu_custom_call" | custom-call | bytes 6291456 | tf_op jit(solution)/shard_map/place/pallas_call | solution.py:671
  (56 shorter events, 0.5 us)
Async XLA Ops:
  33.8 29.2 %all-to-all-start.1 = ((bf16[8,128,512]{2,1,0:T(8,128)(2,1)}), bf16[8,128,512]{2,1,0:T(8,128)(2,1)S(1)}, u32[]{:S(2)}, u32[]{:S(2)}) async-start(bf16[8,128,512]{2,1,0:T(8,128)(2,1)} %param.10), calls=%async_computation.1 | async-start | bytes 2097152 | tf_op jit(solution)/shard_map/all_to_all | solution.py:592
  63.0 1.0 copy-start
  63.9 40.5 %all-to-all-start.2 = ((bf16[8,128,512]{2,1,0:T(8,128)(2,1)}), bf16[8,128,512]{2,1,0:T(8,128)(2,1)S(1)}, u32[]{:S(2)}, u32[]{:S(2)}) async-start(bf16[8,128,512]{2,1,0:T(8,128)(2,1)} %bitcast.15), calls=%async_computation.2 | async-start | bytes 2097152 | tf_op jit(solution)/shard_map/all_to_all | solution.py:592
  97.7 14.7 %collective-permute-start = (f32[1024,256]{1,0:T(8,128)}, f32[1024,256]{1,0:T(8,128)S(1)}, u32[]{:S(2)}, u32[]{:S(2)}) collective-permute-start(f32[1024,256]{1,0:T(8,128)} %get-tuple-element.61), channel_id=1, source_target_pairs={{0,8},{8,0},{16,24},{24,16},{1,9},{9,1},{17,25},{25,17},{2,10},{10... | collective-permute-start | bytes 3145736 | tf_op jit(solution)/shard_map/ppermute | solution.py:602
  97.7 14.7 %collective-permute-start.1 = (bf16[1024,256]{1,0:T(8,128)(2,1)}, bf16[1024,256]{1,0:T(8,128)(2,1)}, u32[]{:S(2)}, u32[]{:S(2)}) collective-permute-start(bf16[1024,256]{1,0:T(8,128)(2,1)} %get-tuple-element.64), channel_id=1, source_target_pairs={{0,1},{1,0},{2,3},{3,2},{4,5},{5,4},{6,7},{7,6},{8,9},{9,8},{10,11... | collective-permute-start | bytes 1572872 | tf_op jit(solution)/shard_map/ppermute | solution.py:602
  97.8 15.6 %copy-start.3 = (f32[1024,256]{1,0:T(8,128)S(1)}, f32[1024,256]{1,0:T(8,128)}, u32[]{:S(2)}) copy-start(f32[1024,256]{1,0:T(8,128)} %get-tuple-element.69) | copy-start | bytes 3145732
  112.4 1.0 copy-start.4
  113.4 1.4 collective-permute-start.4
  115.5 9.7 %collective-permute-start.5 = (bf16[528,256]{1,0:T(8,128)(2,1)}, bf16[528,256]{1,0:T(8,128)(2,1)S(1)}, u32[]{:S(2)}, u32[]{:S(2)}) collective-permute-start(bf16[528,256]{1,0:T(8,128)(2,1)} %pad_maximum_fusion), channel_id=1, source_target_pairs={{0,16},{8,24},{16,0},{24,8},{1,17},{9,25},{17,1},{25,9},{2,18},{10... | collective-permute-start | bytes 811016 | tf_op jit(solution)/shard_map/ppermute | solution.py:602
  117.8 30.3 %all-to-all-start.3 = ((bf16[8,128,512]{2,1,0:T(8,128)(2,1)}), bf16[8,128,512]{2,1,0:T(8,128)(2,1)S(1)}, u32[]{:S(2)}, u32[]{:S(2)}) async-start(bf16[8,128,512]{2,1,0:T(8,128)(2,1)} %bitcast.5), calls=%async_computation.3 | async-start | bytes 2097152 | tf_op jit(solution)/shard_map/all_to_all | solution.py:592
  122.0 4.3 %copy-start.5 = (f32[1024,256]{1,0:T(8,128)S(1)}, f32[1024,256]{1,0:T(8,128)}, u32[]{:S(2)}) copy-start(f32[1024,256]{1,0:T(8,128)} %get-tuple-element.67) | copy-start | bytes 3145732
  125.3 10.1 %collective-permute-start.6 = (bf16[272,256]{1,0:T(8,128)(2,1)S(1)}, bf16[272,256]{1,0:T(8,128)(2,1)S(1)}, u32[]{:S(2)}, u32[]{:S(2)}) collective-permute-start(bf16[272,256]{1,0:T(8,128)(2,1)S(1)} %pad_maximum_fusion.2), channel_id=1, source_target_pairs={{0,1},{1,0},{2,3},{3,2},{4,5},{5,4},{6,7},{7,6},{8,9},{9,8},{10,11... | collective-permute-start | bytes 417800 | tf_op jit(solution)/shard_map/ppermute | solution.py:602
  127.5 8.0 %collective-permute-start.2 = (f32[512,256]{1,0:T(8,128)S(1)}, f32[512,256]{1,0:T(8,128)S(1)}, u32[]{:S(2)}, u32[]{:S(2)}) collective-permute-start(f32[512,256]{1,0:T(8,128)S(1)} %slice.146), channel_id=1, source_target_pairs={{0,8},{8,0},{16,24},{24,16},{1,9},{9,1},{17,25},{25,17},{2,10},{10... | collective-permute-start | bytes 1572872 | tf_op jit(solution)/shard_map/ppermute | solution.py:602
  135.5 17.8 %copy-start.1 = (f32[256,256]{1,0:T(8,128)}, f32[256,256]{1,0:T(8,128)S(1)}, u32[]{:S(2)}) copy-start(f32[256,256]{1,0:T(8,128)S(1)} %slice_add_fusion.2) | copy-start | bytes 786436
  135.6 5.0 %collective-permute-start.3 = (bf16[256,256]{1,0:T(8,128)(2,1)S(1)}, bf16[256,256]{1,0:T(8,128)(2,1)S(1)}, u32[]{:S(2)}, u32[]{:S(2)}) collective-permute-start(bf16[256,256]{1,0:T(8,128)(2,1)S(1)} %slice.225), channel_id=1, source_target_pairs={{0,16},{8,24},{16,0},{24,8},{1,17},{9,25},{17,1},{25,9},{2,18},{10... | collective-permute-start | bytes 393224 | tf_op jit(solution)/shard_map/ppermute | solution.py:602
  140.7 12.6 %copy-start.2 = (f32[256,256]{1,0:T(8,128)}, f32[256,256]{1,0:T(8,128)S(1)}, u32[]{:S(2)}) copy-start(f32[256,256]{1,0:T(8,128)S(1)} %slice_add_fusion.3) | copy-start | bytes 786436
  148.4 4.9 %collective-permute-start.7 = (bf16[144,256]{1,0:T(8,128)(2,1)S(1)}, bf16[144,256]{1,0:T(8,128)(2,1)S(1)}, u32[]{:S(2)}, u32[]{:S(2)}) collective-permute-start(bf16[144,256]{1,0:T(8,128)(2,1)S(1)} %concatenate.33), channel_id=1, source_target_pairs={{0,2},{1,3},{2,0},{3,1},{4,6},{5,7},{6,4},{7,5},{8,10},{9,11},{10,... | collective-permute-start | bytes 221192 | tf_op jit(solution)/shard_map/ppermute | solution.py:602
  148.6 8.8 %collective-permute-start.8 = (bf16[144,256]{1,0:T(8,128)(2,1)S(1)}, bf16[144,256]{1,0:T(8,128)(2,1)S(1)}, u32[]{:S(2)}, u32[]{:S(2)}) collective-permute-start(bf16[144,256]{1,0:T(8,128)(2,1)S(1)} %concatenate.34), channel_id=1, source_target_pairs={{0,4},{1,5},{2,6},{3,7},{4,0},{5,1},{6,2},{7,3},{8,12},{9,13},{10,... | collective-permute-start | bytes 221192 | tf_op jit(solution)/shard_map/ppermute | solution.py:602
  151.2 6.3 %collective-permute-start.9 = (bf16[144,256]{1,0:T(8,128)(2,1)S(1)}, bf16[144,256]{1,0:T(8,128)(2,1)S(1)}, u32[]{:S(2)}, u32[]{:S(2)}) collective-permute-start(bf16[144,256]{1,0:T(8,128)(2,1)S(1)} %concatenate.35), channel_id=1, source_target_pairs={{0,6},{1,7},{2,4},{3,5},{4,2},{5,3},{6,0},{7,1},{8,14},{9,15},{10,... | collective-permute-start | bytes 221192 | tf_op jit(solution)/shard_map/ppermute | solution.py:602
  157.5 0.8 slice-start
  157.5 0.9 slice-start.1
  158.4 5.7 %collective-permute-start.10 = (bf16[1,2,64,256]{3,2,1,0:T(8,128)(2,1)S(1)}, bf16[1,2,64,256]{3,2,1,0:T(8,128)(2,1)S(1)}, u32[]{:S(2)}, u32[]{:S(2)}) collective-permute-start(bf16[1,2,64,256]{3,2,1,0:T(8,128)(2,1)S(1)} %bitcast.16), channel_id=1, source_target_pairs={{0,2},{1,3},{2,0},{3,1},{4,6},{5,7},{6,4},{7,5},{8,10},{9,11},{10,... | collective-permute-start | bytes 196616 | tf_op jit(solution)/shard_map/ppermute | solution.py:602
  158.9 6.2 %collective-permute-start.11 = (bf16[1,2,64,256]{3,2,1,0:T(8,128)(2,1)S(1)}, bf16[1,2,64,256]{3,2,1,0:T(8,128)(2,1)S(1)}, u32[]{:S(2)}, u32[]{:S(2)}) collective-permute-start(bf16[1,2,64,256]{3,2,1,0:T(8,128)(2,1)S(1)} %bitcast.17), channel_id=1, source_target_pairs={{0,4},{1,5},{2,6},{3,7},{4,0},{5,1},{6,2},{7,3},{8,12},{9,13},{10,... | collective-permute-start | bytes 196616 | tf_op jit(solution)/shard_map/ppermute | solution.py:602
  160.3 6.2 %collective-permute-start.12 = (bf16[1,2,64,256]{3,2,1,0:T(8,128)(2,1)S(1)}, bf16[1,2,64,256]{3,2,1,0:T(8,128)(2,1)S(1)}, u32[]{:S(2)}, u32[]{:S(2)}) collective-permute-start(bf16[1,2,64,256]{3,2,1,0:T(8,128)(2,1)S(1)} %bitcast.18), channel_id=1, source_target_pairs={{0,6},{1,7},{2,4},{3,5},{4,2},{5,3},{6,0},{7,1},{8,14},{9,15},{10,... | collective-permute-start | bytes 196616 | tf_op jit(solution)/shard_map/ppermute | solution.py:602
  166.5 8.3 %copy-start.6 = (bf16[4,2,64,256]{3,2,1,0:T(8,128)(2,1)}, bf16[4,2,64,256]{3,2,1,0:T(8,128)(2,1)S(1)}, u32[]{:S(2)}) copy-start(bf16[4,2,64,256]{3,2,1,0:T(8,128)(2,1)S(1)} %pad_maximum_fusion.1.refs_0_) | copy-start | bytes 786436
  166.5 6.4 %collective-permute-start.13 = (bf16[4,2,64,256]{3,2,1,0:T(8,128)(2,1)S(1)}, bf16[4,2,64,256]{3,2,1,0:T(8,128)(2,1)S(1)}, u32[]{:S(2)}, u32[]{:S(2)}) collective-permute-start(bf16[4,2,64,256]{3,2,1,0:T(8,128)(2,1)S(1)} %pad_maximum_fusion.1.refs_0_), channel_id=1, source_target_pairs={{0,1},{1,0},{2,3},{3,2},{4,5},{5,4},{6,7},{7,6},{8,9},{9,8},{10,11... | collective-permute-start | bytes 786440 | tf_op jit(solution)/shard_map/ppermute | solution.py:602
  168.0 8.6 %collective-permute-start.14 = (bf16[4,2,64,256]{3,2,1,0:T(8,128)(2,1)S(1)}, bf16[4,2,64,256]{3,2,1,0:T(8,128)(2,1)S(1)}, u32[]{:S(2)}, u32[]{:S(2)}) collective-permute-start(bf16[4,2,64,256]{3,2,1,0:T(8,128)(2,1)S(1)} %pad_maximum_fusion.1.refs_0_), channel_id=1, source_target_pairs={{0,16},{8,24},{16,0},{24,8},{1,17},{9,25},{17,1},{25,9},{2,18},{10... | collective-permute-start | bytes 786440 | tf_op jit(solution)/shard_map/ppermute | solution.py:602
  173.0 1.9 %copy-start.7 = (bf16[4,2,64,256]{3,2,1,0:T(8,128)(2,1)}, bf16[4,2,64,256]{3,2,1,0:T(8,128)(2,1)S(1)}, u32[]{:S(2)}) copy-start(bf16[4,2,64,256]{3,2,1,0:T(8,128)(2,1)S(1)} %collective-permute-done.13.refs_1_) | copy-start | bytes 786436
  173.0 6.4 %collective-permute-start.15 = (bf16[4,2,64,256]{3,2,1,0:T(8,128)(2,1)S(1)}, bf16[4,2,64,256]{3,2,1,0:T(8,128)(2,1)S(1)}, u32[]{:S(2)}, u32[]{:S(2)}) collective-permute-start(bf16[4,2,64,256]{3,2,1,0:T(8,128)(2,1)S(1)} %collective-permute-done.13.refs_1_), channel_id=1, source_target_pairs={{0,16},{8,24},{16,0},{24,8},{1,17},{9,25},{17,1},{25,9},{2,18},{10... | collective-permute-start | bytes 786440 | tf_op jit(solution)/shard_map/ppermute | solution.py:602
  174.8 6.2 %collective-permute-start.16 = (bf16[4,2,64,256]{3,2,1,0:T(8,128)(2,1)S(1)}, bf16[4,2,64,256]{3,2,1,0:T(8,128)(2,1)S(1)}, u32[]{:S(2)}, u32[]{:S(2)}) collective-permute-start(bf16[4,2,64,256]{3,2,1,0:T(8,128)(2,1)S(1)} %pad_maximum_fusion.1.refs_0_), channel_id=1, source_target_pairs={{0,8},{8,0},{16,24},{24,16},{1,9},{9,1},{17,25},{25,17},{2,10},{10... | collective-permute-start | bytes 786440 | tf_op jit(solution)/shard_map/ppermute | solution.py:602
  174.8 6.2 %collective-permute-start.17 = (bf16[4,2,64,256]{3,2,1,0:T(8,128)(2,1)S(1)}, bf16[4,2,64,256]{3,2,1,0:T(8,128)(2,1)S(1)}, u32[]{:S(2)}, u32[]{:S(2)}) collective-permute-start(bf16[4,2,64,256]{3,2,1,0:T(8,128)(2,1)S(1)} %collective-permute-done.13.refs_1_), channel_id=1, source_target_pairs={{0,8},{8,0},{16,24},{24,16},{1,9},{9,1},{17,25},{25,17},{2,10},{10... | collective-permute-start | bytes 786440 | tf_op jit(solution)/shard_map/ppermute | solution.py:602
  176.5 3.9 %copy-start.8 = (bf16[4,2,64,256]{3,2,1,0:T(8,128)(2,1)}, bf16[4,2,64,256]{3,2,1,0:T(8,128)(2,1)S(1)}, u32[]{:S(2)}) copy-start(bf16[4,2,64,256]{3,2,1,0:T(8,128)(2,1)S(1)} %collective-permute-done.14.refs_2_) | copy-start | bytes 786436
  176.5 4.5 %collective-permute-start.18 = (bf16[4,2,64,256]{3,2,1,0:T(8,128)(2,1)S(1)}, bf16[4,2,64,256]{3,2,1,0:T(8,128)(2,1)S(1)}, u32[]{:S(2)}, u32[]{:S(2)}) collective-permute-start(bf16[4,2,64,256]{3,2,1,0:T(8,128)(2,1)S(1)} %collective-permute-done.14.refs_2_), channel_id=1, source_target_pairs={{0,8},{8,0},{16,24},{24,16},{1,9},{9,1},{17,25},{25,17},{2,10},{10... | collective-permute-start | bytes 786440 | tf_op jit(solution)/shard_map/ppermute | solution.py:602
  179.4 1.1 copy-start.9
  179.4 1.7 collective-permute-start.19
  181.0 0.7 copy-start.10
  181.0 0.8 copy-start.11
  181.1 0.9 copy-start.12
  181.9 0.7 copy-start.13

commit v10 on v9

--- a/solution.py
+++ b/solution.py
@@ -602,7 +602,7 @@
     return lax.ppermute(tensor, axis, [(i, i ^ distance) for i in range(size)])
 
 
-def reduce_sums(early, late, gain, width, beside):
+def reduce_sums(early, late, gain, width):
     quad = gain.shape[1]
     count = gain.shape[0]
     wide = jnp.float32
@@ -631,7 +631,7 @@
     first, _ = halve([first], None, "sample", 2)
     second, gain = halve([late], gain, "sample", 2)
     second, gain = halve(second, gain, "turb", 1)
-    parts, gain, beside = lax.optimization_barrier((first + second, gain, beside))
+    parts = first + second
     share = parts[0].shape[0] // 4
     pieces = [jnp.concatenate([part[i * share : (i + 1) * share] for part in parts]) for i in range(4)]
     size = pieces[0].shape[0]
@@ -641,12 +641,14 @@
     gain = gain + sum(
         rows[size : size + count] + rows[size + count : size + 2 * count] for rows in arrived
     )
-    total = total.astype(jnp.bfloat16).reshape(1, 2, share, quad)
+    return total.astype(jnp.bfloat16).reshape(1, 2, share, quad), gain.reshape(width)
+
+
+def gather_sums(total):
     total = jnp.concatenate([total] + [across(total, "turb", distance) for distance in (2, 4, 6)])
     other = across(total, "turb", 1)
     four = [total, other, across(total, "sample", 2), across(other, "sample", 2)]
-    four += [across(part, "sample", 1) for part in four]
-    return four, gain.reshape(width), beside
+    return four + [across(part, "sample", 1) for part in four]
 
 
 def place_kernel(*refs):
@@ -713,18 +715,21 @@
     *more, late, send, gain = backward(
         sectors, adjacency, grad_rows, out_weight, *saved, *weights, [before], block_rows, 1
     )
+    more, late, send, gain, arrived, layer_output = lax.optimization_barrier(
+        (more, late, send, gain, arrived, layer_output)
+    )
     arrived_late = across(send, "sample", 1)
+    gain = gain[0].reshape(-1, late.shape[1])
+    total, sum_gain = reduce_sums(
+        early + arrived.astype(jnp.float32),
+        late + arrived_late,
+        gain + across(gain, "sample", 1),
+        width,
+    )
     grad_rows = finish(rows, grad_rows, *weights, grads + more)
-    grad_rows, late, arrived_late, gain, early, arrived, layer_output = lax.optimization_barrier(
-        (grad_rows, late, arrived_late, gain, early, arrived, layer_output)
-    )
-    gain = gain[0].reshape(-1, late.shape[1])
-    arrived_gain = across(gain, "sample", 1)
-    early = early + arrived.astype(jnp.float32)
+    grad_rows, total = lax.optimization_barrier((grad_rows, total))
     grad_inflow = swap(grad_rows.reshape(inflow.shape), "turb")
-    parts, sum_gain, grad_inflow = reduce_sums(
-        early, late + arrived_late, gain + arrived_gain, width, grad_inflow
-    )
+    parts = gather_sums(total)
     sums = place_sums(parts, width)
     lowest = jnp.finfo(jnp.bfloat16).min
     return (

time: 188 us -> 190 us (1.011)
    ppermute x20, waiting for transfers between devices: 39.2 us -> 47.1 us  [across(): return lax.ppermute(tensor, axis, [(i, i ^ distance) for i in range(size)])]
    all_to_all x3, waiting for transfers between devices: 11.1 us -> 3.9 us  [swap(): return lax.all_to_all(tensor, axis, split_axis=0, concat_axis=0, tiled=True)]
    unnamed x29 -> x28, local copies, waits for them, and re-layouts: 3.36 us -> 3.85 us
  transfers between devices with their start and end apart: 23 -> 23, of which waited for: 13 -> 11; matrix products, arithmetic and copies ran while one was open for 3% -> 4% of each run, Pallas kernels for 31% -> 33%
where the time goes in v10:
time: 190 us; the launch traced here: 189 us
  Pallas kernels  61.7 us (32%)
  waiting for transfers between devices  51 us (27%)
  blocking collectives  33.1 us (17%)
  starting transfers between devices  30 us (16%)
  local copies, waits for them, and re-layouts  6.05 us (3%)
  other arithmetic  6.01 us (3%)
    ppermute x20, waiting for transfers between devices, across(): return lax.ppermute(tensor, axis, [(i, i ^ distance) for i in range(size)])  47.1 us
    all_to_all x1, blocking collectives, swap(): return lax.all_to_all(tensor, axis, split_axis=0, concat_axis=0, tiled=True)  33.1 us
    pallas_call x2, Pallas kernels, backward(): pl.pallas_call(lambda *refs: backward_kernel(block_rows, head_dim, which,...  29.7 us
    pallas_call x1, Pallas kernels, forward(): pl.pallas_call(lambda *refs: forward_kernel(block_rows, head_dim, *refs),...  21.7 us
    ppermute x20, starting transfers between devices, across(): return lax.ppermute(tensor, axis, [(i, i ^ distance) for i in range(size)])  18.2 us
    all_to_all x3, starting transfers between devices, swap(): return lax.all_to_all(tensor, axis, split_axis=0, concat_axis=0, tiled=True)  11.8 us
    pallas_call x1, Pallas kernels, finish(): pl.pallas_call(lambda *refs: finish_kernel(width // quad, *refs), grid=(r...  6.47 us
    all_to_all x3, waiting for transfers between devices, swap(): return lax.all_to_all(tensor, axis, split_axis=0, concat_axis=0, tiled=True)  3.9 us
  transfers between devices with their start and end apart: 23, of which 11 were waited for; matrix products, arithmetic and copies ran while one was open for 4% of the time, Pallas kernels for 33%

profile of v10, /device:TPU:0, one launch (start us, length us, event | category | flops | bytes accessed | tf_op | source)
XLA Modules:
  0.0 188.9 jit_solution(13254110063614962134)
XLA Ops:
  0.6 33.1 %all_to_all.20 = bf16[8,128,512]{2,1,0:T(8,128)(2,1)} all-to-all(bf16[8,128,512]{2,1,0:T(8,128)(2,1)} %param.9), channel_id=1, replica_groups=mesh['sample'=4,'turb'=8] {'turb'}, dimensions={0} | all-to-all | bytes 2097152 | tf_op jit(solution)/shard_map/all_to_all | solution.py:592
  33.8 3.6 %all-to-all-start.1 = ((bf16[8,128,512]{2,1,0:T(8,128)(2,1)}), bf16[8,128,512]{2,1,0:T(8,128)(2,1)S(1)}, u32[]{:S(2)}, u32[]{:S(2)}) async-start(bf16[8,128,512]{2,1,0:T(8,128)(2,1)} %param.10), calls=%async_computation.1 | async-start | bytes 2097152 | tf_op jit(solution)/shard_map/all_to_all | solution.py:592
  37.4 21.7 %forward.1 = (bf16[512,1024]{1,0:T(8,128)(2,1)}, bf16[1024,512]{1,0:T(8,128)(2,1)}, bf16[1024,512]{1,0:T(8,128)(2,1)}, bf16[1024,512]{1,0:T(8,128)(2,1)}, bf16[5...) custom-call(s32[8]{0:T(128)} %refs_0_.5, ...), custom_call_target="tpu_custom_call" | custom-call | flops 5368709120 | bytes 10485760 | tf_op jit(solution)/shard_map/forward/pallas_call | solution.py:367
  59.1 3.9 %all-to-all-done.1 = bf16[8,128,512]{2,1,0:T(8,128)(2,1)S(1)} async-done(((bf16[8,128,512]{2,1,0:T(8,128)(2,1)}), bf16[8,128,512]{2,1,0:T(8,128)(2,1)S(1)}, u32[]{:S(2)}, u32[]{:S(2)}) %all-to-all-start.1) | async-done | bytes 1048608 | tf_op jit(solution)/shard_map/all_to_all | solution.py:592
  63.0 1.0 copy-done
  63.9 3.7 %all-to-all-start.2 = ((bf16[8,128,512]{2,1,0:T(8,128)(2,1)}), bf16[8,128,512]{2,1,0:T(8,128)(2,1)S(1)}, u32[]{:S(2)}, u32[]{:S(2)}) async-start(bf16[8,128,512]{2,1,0:T(8,128)(2,1)} %bitcast.15), calls=%async_computation.2 | async-start | bytes 2097152 | tf_op jit(solution)/shard_map/all_to_all | solution.py:592
  67.7 14.7 %backward.2 = (bf16[1024,256]{1,0:T(8,128)(2,1)}, bf16[1024,256]{1,0:T(8,128)(2,1)}, bf16[1024,256]{1,0:T(8,128)(2,1)}, f32[1024,256]{1,0:T(8,128)}, bf16[1024,256]{1,0:T(8,128)(2,1)}, /*index=5*/f32[8,512]{1,0:T(8,128)}) custom-call(s32[8]{0:T(128)} %refs_0_.5, s32[3,8,8]{2,1,0:T(8,128)} %bitcast.26, bf16[512,512]{1,0:T(8,128)(2,1)} %refs_2_.3, ...), custom_call_target="tpu_custom_call" | custom-call | flops 4026531840 | bytes 7340032 | tf_op jit(solution)/shard_map/backward/pallas_call | solution.py:506
  82.4 2.2 %collective-permute-start = (bf16[1024,256]{1,0:T(8,128)(2,1)}, bf16[1024,256]{1,0:T(8,128)(2,1)S(1)}, u32[]{:S(2)}, u32[]{:S(2)}) collective-permute-start(bf16[1024,256]{1,0:T(8,128)(2,1)} %get-tuple-element.59), channel_id=1, source_target_pairs={{0,1},{1,0},{2,3},{3,2},{4,5},{5,4},{6,7},{7,6},{8,9},{9,8},{10,11... | collective-permute-start | bytes 1572872 | tf_op jit(solution)/shard_map/ppermute | solution.py:602
  84.6 15.0 %backward.3 = (bf16[1024,256]{1,0:T(8,128)(2,1)}, bf16[1024,256]{1,0:T(8,128)(2,1)}, bf16[1024,256]{1,0:T(8,128)(2,1)}, f32[1024,256]{1,0:T(8,128)}, f32[1024,256]{1,0:T(8,128)}, /*index=5*/f32[8,512]{1,0:T(8,128)}) custom-call(s32[8]{0:T(128)} %refs_0_.5, s32[3,8,8]{2,1,0:T(8,128)} %bitcast.27, bf16[512,512]{1,0:T(8,128)(2,1)} %refs_2_.3, ...), custom_call_target="tpu_custom_call" | custom-call | flops 4026531840 | bytes 7340032 | tf_op jit(solution)/shard_map/backward/pallas_call | solution.py:506
  99.6 0.0 copy-start.3
  99.6 0.1 collective-permute-start.3
  99.7 0.7 copy-done.3
  100.4 1.1 convert_add_fusion
  101.5 0.8 slice.146
  102.3 0.8 slice_reduce_fusion
  103.2 0.5 collective-permute-start.4
  103.7 0.8 collective-permute-done.4
  104.5 0.1 collective-permute-done.1
  104.6 1.1 slice_add_fusion.1
  105.7 0.8 collective-permute-start.2
  106.5 1.4 add.63
  108.0 1.3 collective-permute-start.5
  109.3 2.8 %collective-permute-done.2 = bf16[256,256]{1,0:T(8,128)(2,1)S(1)} collective-permute-done((bf16[256,256]{1,0:T(8,128)(2,1)S(1)}, bf16[256,256]{1,0:T(8,128)(2,1)S(1)}, u32[]{:S(2)}, u32[]{:S(2)}) %collective-permute-start.2) | collective-permute-done | bytes 131104 | tf_op jit(solution)/shard_map/ppermute | solution.py:602
  112.2 5.1 %collective-permute-done.5 = bf16[528,256]{1,0:T(8,128)(2,1)S(1)} collective-permute-done((bf16[528,256]{1,0:T(8,128)(2,1)S(1)}, bf16[528,256]{1,0:T(8,128)(2,1)S(1)}, u32[]{:S(2)}, u32[]{:S(2)}) %collective-permute-start.5) | collective-permute-done | bytes 270368 | tf_op jit(solution)/shard_map/ppermute | solution.py:602
  117.2 0.1 slice_add_fusion
  117.4 0.5 collective-permute-start.6
  117.8 4.6 %collective-permute-done.6 = bf16[272,256]{1,0:T(8,128)(2,1)S(1)} collective-permute-done((bf16[272,256]{1,0:T(8,128)(2,1)S(1)}, bf16[272,256]{1,0:T(8,128)(2,1)S(1)}, u32[]{:S(2)}, u32[]{:S(2)}) %collective-permute-start.6) | collective-permute-done | bytes 139296 | tf_op jit(solution)/shard_map/ppermute | solution.py:602
  122.6 0.2 concatenate.33
  122.7 0.5 collective-permute-start.7
  123.2 0.1 concatenate.34
  123.4 2.7 %collective-permute-start.8 = (bf16[144,256]{1,0:T(8,128)(2,1)S(1)}, bf16[144,256]{1,0:T(8,128)(2,1)S(1)}, u32[]{:S(2)}, u32[]{:S(2)}) collective-permute-start(bf16[144,256]{1,0:T(8,128)(2,1)S(1)} %concatenate.34), channel_id=1, source_target_pairs={{0,4},{1,5},{2,6},{3,7},{4,0},{5,1},{6,2},{7,3},{8,12},{9,13},{10,... | collective-permute-start | bytes 221192 | tf_op jit(solution)/shard_map/ppermute | solution.py:602
  126.1 0.1 concatenate.35
  126.3 1.3 collective-permute-start.9
  127.6 6.5 %finish.1 = bf16[1024,512]{1,0:T(8,128)(2,1)} custom-call(bf16[1024,512]{1,0:T(8,128)(2,1)} %bitcast.11, bf16[1024,512]{1,0:T(8,128)(2,1)} %bitcast.14, f32[1,512]{1,0:T(1,128)} %bitcast.23, bf16[512,512]{1,0:T(8,128)(2,1)} %refs_3_.1, bf16[512,512]{1,0:T(8,128)(2,1)} %refs_4_.3, bf16[512,512]{1,0:T(8,128)(2,1)} %refs_5_.3, ...), custom_call_target="tpu_custom_call" | custom-call | flops 1610612736 | bytes 8388608 | tf_op jit(solution)/shard_map/finish/pallas_call | solution.py:572
  134.1 0.0 collective-permute-done.7
  134.1 0.0 collective-permute-done.8
  134.2 4.5 %all-to-all-start.3 = ((bf16[8,128,512]{2,1,0:T(8,128)(2,1)}), bf16[8,128,512]{2,1,0:T(8,128)(2,1)S(1)}, u32[]{:S(2)}, u32[]{:S(2)}) async-start(bf16[8,128,512]{2,1,0:T(8,128)(2,1)} %bitcast.6), calls=%async_computation.3 | async-start | bytes 2097152 | tf_op jit(solution)/shard_map/all_to_all | solution.py:592
  138.7 2.0 %collective-permute-start.10 = (bf16[1,2,64,256]{3,2,1,0:T(8,128)(2,1)S(1)}, bf16[1,2,64,256]{3,2,1,0:T(8,128)(2,1)S(1)}, u32[]{:S(2)}, u32[]{:S(2)}) collective-permute-start(bf16[1,2,64,256]{3,2,1,0:T(8,128)(2,1)S(1)} %bitcast.16), channel_id=1, source_target_pairs={{0,2},{1,3},{2,0},{3,1},{4,6},{5,7},{6,4},{7,5},{8,10},{9,11},{10,... | collective-permute-start | bytes 196616 | tf_op jit(solution)/shard_map/ppermute | solution.py:602
  140.7 2.4 %collective-permute-start.11 = (bf16[1,2,64,256]{3,2,1,0:T(8,128)(2,1)S(1)}, bf16[1,2,64,256]{3,2,1,0:T(8,128)(2,1)S(1)}, u32[]{:S(2)}, u32[]{:S(2)}) collective-permute-start(bf16[1,2,64,256]{3,2,1,0:T(8,128)(2,1)S(1)} %bitcast.17), channel_id=1, source_target_pairs={{0,4},{1,5},{2,6},{3,7},{4,0},{5,1},{6,2},{7,3},{8,12},{9,13},{10,... | collective-permute-start | bytes 196616 | tf_op jit(solution)/shard_map/ppermute | solution.py:602
  143.1 0.0 collective-permute-start.12
  143.1 14.0 %collective-permute-done.10 = bf16[1,2,64,256]{3,2,1,0:T(8,128)(2,1)S(1)} collective-permute-done((bf16[1,2,64,256]{3,2,1,0:T(8,128)(2,1)S(1)}, bf16[1,2,64,256]{3,2,1,0:T(8,128)(2,1)S(1)}, u32[]{:S(2)}, u32[]{:S(2)}) %collective-permute-start.10) | collective-permute-done | bytes 65568 | tf_op jit(solution)/shard_map/ppermute | solution.py:602
  157.1 10.5 %collective-permute-done.11 = bf16[1,2,64,256]{3,2,1,0:T(8,128)(2,1)S(1)} collective-permute-done((bf16[1,2,64,256]{3,2,1,0:T(8,128)(2,1)S(1)}, bf16[1,2,64,256]{3,2,1,0:T(8,128)(2,1)S(1)}, u32[]{:S(2)}, u32[]{:S(2)}) %collective-permute-start.11) | collective-permute-done | bytes 65568 | tf_op jit(solution)/shard_map/ppermute | solution.py:602
  167.6 0.0 collective-permute-done.12
  167.6 1.3 collective-permute-start.13
  168.9 1.1 collective-permute-start.14
  170.0 4.1 %collective-permute-done.13.refs_1_ = bf16[4,2,64,256]{3,2,1,0:T(8,128)(2,1)S(1)} collective-permute-done((bf16[4,2,64,256]{3,2,1,0:T(8,128)(2,1)S(1)}, bf16[4,2,64,256]{3,2,1,0:T(8,128)(2,1)S(1)}, u32[]{:S(2)}, u32[]{:S(2)}) %collective-permute-start.13) | collective-permute-done | bytes 262176 | tf_op jit(solution)/shard_map/ppermute | solution.py:602
  174.1 1.1 collective-permute-start.15
  175.1 0.0 collective-permute-start.16
  175.1 0.5 collective-permute-start.17
  175.6 2.3 %collective-permute-done.14.refs_2_ = bf16[4,2,64,256]{3,2,1,0:T(8,128)(2,1)S(1)} collective-permute-done((bf16[4,2,64,256]{3,2,1,0:T(8,128)(2,1)S(1)}, bf16[4,2,64,256]{3,2,1,0:T(8,128)(2,1)S(1)}, u32[]{:S(2)}, u32[]{:S(2)}) %collective-permute-start.14) | collective-permute-done | bytes 262176 | tf_op jit(solution)/shard_map/ppermute | solution.py:602
  177.9 0.0 collective-permute-start.18
  177.9 2.8 %collective-permute-done.15.refs_3_ = bf16[4,2,64,256]{3,2,1,0:T(8,128)(2,1)S(1)} collective-permute-done((bf16[4,2,64,256]{3,2,1,0:T(8,128)(2,1)S(1)}, bf16[4,2,64,256]{3,2,1,0:T(8,128)(2,1)S(1)}, u32[]{:S(2)}, u32[]{:S(2)}) %collective-permute-start.15) | collective-permute-done | bytes 262176 | tf_op jit(solution)/shard_map/ppermute | solution.py:602
  180.7 1.1 broadcast_maximum_fusion.1
  181.8 0.6 copy.16
  182.4 0.0 collective-permute-done.16.refs_4_
  182.4 0.0 collective-permute-done.18.refs_6_
  182.4 0.0 collective-permute-done.19.refs_7_
  182.5 0.7 copy-done.8
  183.1 0.1 copy-done.9
  183.2 0.1 copy-done.10
  183.3 0.7 copy-done.11
  184.0 3.9 %place.1 = (f32[512,512]{1,0:T(8,128)}, f32[512,512]{1,0:T(8,128)}, f32[512,512]{1,0:T(8,128)}, f32[512,512]{1,0:T(8,128)}) custom-call(bf16[4,2,64,256]{3,2,1,0:T(8,128)(2,1)} %copy-done.4, bf16[4,2,64,256]{3,2,1,0:T(8,128)(2,1)} %copy-done.5, bf16[4,2,64,256]{3,2,1,0:T(8,128)(2,1)} %copy-done.6, bf16[4,2,64,256]{3,2,1,0:T(8,128)(2,1)} %copy-done.7, ...), custom_call_target="tpu_custom_call" | custom-call | bytes 6291456 | tf_op jit(solution)/shard_map/place/pallas_call | solution.py:673
  187.9 0.0 all-to-all-done.3
  187.9 1.1 broadcast_maximum_fusion
  (51 shorter events, 0.4 us)
Async XLA Ops:
  33.8 29.2 %all-to-all-start.1 = ((bf16[8,128,512]{2,1,0:T(8,128)(2,1)}), bf16[8,128,512]{2,1,0:T(8,128)(2,1)S(1)}, u32[]{:S(2)}, u32[]{:S(2)}) async-start(bf16[8,128,512]{2,1,0:T(8,128)(2,1)} %param.10), calls=%async_computation.1 | async-start | bytes 2097152 | tf_op jit(solution)/shard_map/all_to_all | solution.py:592
  63.0 1.0 copy-start
  63.9 35.6 %all-to-all-start.2 = ((bf16[8,128,512]{2,1,0:T(8,128)(2,1)}), bf16[8,128,512]{2,1,0:T(8,128)(2,1)S(1)}, u32[]{:S(2)}, u32[]{:S(2)}) async-start(bf16[8,128,512]{2,1,0:T(8,128)(2,1)} %bitcast.15), calls=%async_computation.2 | async-start | bytes 2097152 | tf_op jit(solution)/shard_map/all_to_all | solution.py:592
  82.4 17.2 %collective-permute-start = (bf16[1024,256]{1,0:T(8,128)(2,1)}, bf16[1024,256]{1,0:T(8,128)(2,1)S(1)}, u32[]{:S(2)}, u32[]{:S(2)}) collective-permute-start(bf16[1024,256]{1,0:T(8,128)(2,1)} %get-tuple-element.59), channel_id=1, source_target_pairs={{0,1},{1,0},{2,3},{3,2},{4,5},{5,4},{6,7},{7,6},{8,9},{9,8},{10,11... | collective-permute-start | bytes 1572872 | tf_op jit(solution)/shard_map/ppermute | solution.py:602
  84.6 15.8 %copy-start.2 = (f32[1024,256]{1,0:T(8,128)S(1)}, f32[1024,256]{1,0:T(8,128)}, u32[]{:S(2)}) copy-start(f32[1024,256]{1,0:T(8,128)} %get-tuple-element.68) | copy-start | bytes 3145732
  99.6 0.8 copy-start.3
  99.6 7.0 %collective-permute-start.3 = (f32[1024,256]{1,0:T(8,128)}, f32[1024,256]{1,0:T(8,128)}, u32[]{:S(2)}, u32[]{:S(2)}) collective-permute-start(f32[1024,256]{1,0:T(8,128)} %get-tuple-element.71), channel_id=1, source_target_pairs={{0,8},{8,0},{16,24},{24,16},{1,9},{9,1},{17,25},{25,17},{2,10},{10... | collective-permute-start | bytes 3145736 | tf_op jit(solution)/shard_map/ppermute | solution.py:602
  102.3 4.2 %copy-start.1 = (f32[1024,256]{1,0:T(8,128)S(1)}, f32[1024,256]{1,0:T(8,128)}, u32[]{:S(2)}) copy-start(f32[1024,256]{1,0:T(8,128)} %get-tuple-element.70) | copy-start | bytes 3145732
  102.3 2.3 %collective-permute-start.1 = (f32[512,256]{1,0:T(8,128)}, f32[512,256]{1,0:T(8,128)}, u32[]{:S(2)}, u32[]{:S(2)}) collective-permute-start(f32[512,256]{1,0:T(8,128)} %slice.146), channel_id=1, source_target_pairs={{0,8},{8,0},{16,24},{24,16},{1,9},{9,1},{17,25},{25,17},{2,10},{10... | collective-permute-start | bytes 1572872 | tf_op jit(solution)/shard_map/ppermute | solution.py:602
  103.2 1.3 collective-permute-start.4
  105.7 6.4 %collective-permute-start.2 = (bf16[256,256]{1,0:T(8,128)(2,1)S(1)}, bf16[256,256]{1,0:T(8,128)(2,1)S(1)}, u32[]{:S(2)}, u32[]{:S(2)}) collective-permute-start(bf16[256,256]{1,0:T(8,128)(2,1)S(1)} %slice.227), channel_id=1, source_target_pairs={{0,16},{8,24},{16,0},{24,8},{1,17},{9,25},{17,1},{25,9},{2,18},{10... | collective-permute-start | bytes 393224 | tf_op jit(solution)/shard_map/ppermute | solution.py:602
  108.0 9.2 %collective-permute-start.5 = (bf16[528,256]{1,0:T(8,128)(2,1)S(1)}, bf16[528,256]{1,0:T(8,128)(2,1)S(1)}, u32[]{:S(2)}, u32[]{:S(2)}) collective-permute-start(bf16[528,256]{1,0:T(8,128)(2,1)S(1)} %pad_maximum_fusion), channel_id=1, source_target_pairs={{0,16},{8,24},{16,0},{24,8},{1,17},{9,25},{17,1},{25,9},{2,18},{10... | collective-permute-start | bytes 811016 | tf_op jit(solution)/shard_map/ppermute | solution.py:602
  117.4 5.1 %collective-permute-start.6 = (bf16[272,256]{1,0:T(8,128)(2,1)S(1)}, bf16[272,256]{1,0:T(8,128)(2,1)S(1)}, u32[]{:S(2)}, u32[]{:S(2)}) collective-permute-start(bf16[272,256]{1,0:T(8,128)(2,1)S(1)} %pad_maximum_fusion.1), channel_id=1, source_target_pairs={{0,1},{1,0},{2,3},{3,2},{4,5},{5,4},{6,7},{7,6},{8,9},{9,8},{10,11... | collective-permute-start | bytes 417800 | tf_op jit(solution)/shard_map/ppermute | solution.py:602
  122.7 11.4 %collective-permute-start.7 = (bf16[144,256]{1,0:T(8,128)(2,1)S(1)}, bf16[144,256]{1,0:T(8,128)(2,1)S(1)}, u32[]{:S(2)}, u32[]{:S(2)}) collective-permute-start(bf16[144,256]{1,0:T(8,128)(2,1)S(1)} %concatenate.33), channel_id=1, source_target_pairs={{0,2},{1,3},{2,0},{3,1},{4,6},{5,7},{6,4},{7,5},{8,10},{9,11},{10,... | collective-permute-start | bytes 221192 | tf_op jit(solution)/shard_map/ppermute | solution.py:602
  123.4 10.7 %collective-permute-start.8 = (bf16[144,256]{1,0:T(8,128)(2,1)S(1)}, bf16[144,256]{1,0:T(8,128)(2,1)S(1)}, u32[]{:S(2)}, u32[]{:S(2)}) collective-permute-start(bf16[144,256]{1,0:T(8,128)(2,1)S(1)} %concatenate.34), channel_id=1, source_target_pairs={{0,4},{1,5},{2,6},{3,7},{4,0},{5,1},{6,2},{7,3},{8,12},{9,13},{10,... | collective-permute-start | bytes 221192 | tf_op jit(solution)/shard_map/ppermute | solution.py:602
  126.3 7.9 %collective-permute-start.9 = (bf16[144,256]{1,0:T(8,128)(2,1)S(1)}, bf16[144,256]{1,0:T(8,128)(2,1)S(1)}, u32[]{:S(2)}, u32[]{:S(2)}) collective-permute-start(bf16[144,256]{1,0:T(8,128)(2,1)S(1)} %concatenate.35), channel_id=1, source_target_pairs={{0,6},{1,7},{2,4},{3,5},{4,2},{5,3},{6,0},{7,1},{8,14},{9,15},{10,... | collective-permute-start | bytes 221192 | tf_op jit(solution)/shard_map/ppermute | solution.py:602
  134.2 53.6 %all-to-all-start.3 = ((bf16[8,128,512]{2,1,0:T(8,128)(2,1)}), bf16[8,128,512]{2,1,0:T(8,128)(2,1)S(1)}, u32[]{:S(2)}, u32[]{:S(2)}) async-start(bf16[8,128,512]{2,1,0:T(8,128)(2,1)} %bitcast.6), calls=%async_computation.3 | async-start | bytes 2097152 | tf_op jit(solution)/shard_map/all_to_all | solution.py:592
  138.7 18.4 %collective-permute-start.10 = (bf16[1,2,64,256]{3,2,1,0:T(8,128)(2,1)S(1)}, bf16[1,2,64,256]{3,2,1,0:T(8,128)(2,1)S(1)}, u32[]{:S(2)}, u32[]{:S(2)}) collective-permute-start(bf16[1,2,64,256]{3,2,1,0:T(8,128)(2,1)S(1)} %bitcast.16), channel_id=1, source_target_pairs={{0,2},{1,3},{2,0},{3,1},{4,6},{5,7},{6,4},{7,5},{8,10},{9,11},{10,... | collective-permute-start | bytes 196616 | tf_op jit(solution)/shard_map/ppermute | solution.py:602
  140.7 26.9 %collective-permute-start.11 = (bf16[1,2,64,256]{3,2,1,0:T(8,128)(2,1)S(1)}, bf16[1,2,64,256]{3,2,1,0:T(8,128)(2,1)S(1)}, u32[]{:S(2)}, u32[]{:S(2)}) collective-permute-start(bf16[1,2,64,256]{3,2,1,0:T(8,128)(2,1)S(1)} %bitcast.17), channel_id=1, source_target_pairs={{0,4},{1,5},{2,6},{3,7},{4,0},{5,1},{6,2},{7,3},{8,12},{9,13},{10,... | collective-permute-start | bytes 196616 | tf_op jit(solution)/shard_map/ppermute | solution.py:602
  143.1 24.5 %collective-permute-start.12 = (bf16[1,2,64,256]{3,2,1,0:T(8,128)(2,1)S(1)}, bf16[1,2,64,256]{3,2,1,0:T(8,128)(2,1)S(1)}, u32[]{:S(2)}, u32[]{:S(2)}) collective-permute-start(bf16[1,2,64,256]{3,2,1,0:T(8,128)(2,1)S(1)} %bitcast.18), channel_id=1, source_target_pairs={{0,6},{1,7},{2,4},{3,5},{4,2},{5,3},{6,0},{7,1},{8,14},{9,15},{10,... | collective-permute-start | bytes 196616 | tf_op jit(solution)/shard_map/ppermute | solution.py:602
  167.6 14.2 %copy-start.4 = (bf16[4,2,64,256]{3,2,1,0:T(8,128)(2,1)}, bf16[4,2,64,256]{3,2,1,0:T(8,128)(2,1)S(1)}, u32[]{:S(2)}) copy-start(bf16[4,2,64,256]{3,2,1,0:T(8,128)(2,1)S(1)} %constant_dynamic-update-slice_fusion.refs_0_) | copy-start | bytes 786436
  167.6 6.4 %collective-permute-start.13 = (bf16[4,2,64,256]{3,2,1,0:T(8,128)(2,1)S(1)}, bf16[4,2,64,256]{3,2,1,0:T(8,128)(2,1)S(1)}, u32[]{:S(2)}, u32[]{:S(2)}) collective-permute-start(bf16[4,2,64,256]{3,2,1,0:T(8,128)(2,1)S(1)} %constant_dynamic-update-slice_fusion.refs_0_), channel_id=1, source_target_pairs={{0,1},{1,0},{2,3},{3,2},{4,5},{5,4},{6,7},{7,6},{8,9},{9,8},{10,11... | collective-permute-start | bytes 786440 | tf_op jit(solution)/shard_map/ppermute | solution.py:602
  168.9 9.0 %collective-permute-start.14 = (bf16[4,2,64,256]{3,2,1,0:T(8,128)(2,1)S(1)}, bf16[4,2,64,256]{3,2,1,0:T(8,128)(2,1)S(1)}, u32[]{:S(2)}, u32[]{:S(2)}) collective-permute-start(bf16[4,2,64,256]{3,2,1,0:T(8,128)(2,1)S(1)} %constant_dynamic-update-slice_fusion.refs_0_), channel_id=1, source_target_pairs={{0,16},{8,24},{16,0},{24,8},{1,17},{9,25},{17,1},{25,9},{2,18},{10... | collective-permute-start | bytes 786440 | tf_op jit(solution)/shard_map/ppermute | solution.py:602
  174.1 7.7 %copy-start.5 = (bf16[4,2,64,256]{3,2,1,0:T(8,128)(2,1)}, bf16[4,2,64,256]{3,2,1,0:T(8,128)(2,1)S(1)}, u32[]{:S(2)}) copy-start(bf16[4,2,64,256]{3,2,1,0:T(8,128)(2,1)S(1)} %collective-permute-done.13.refs_1_) | copy-start | bytes 786436
  174.1 6.7 %collective-permute-start.15 = (bf16[4,2,64,256]{3,2,1,0:T(8,128)(2,1)S(1)}, bf16[4,2,64,256]{3,2,1,0:T(8,128)(2,1)S(1)}, u32[]{:S(2)}, u32[]{:S(2)}) collective-permute-start(bf16[4,2,64,256]{3,2,1,0:T(8,128)(2,1)S(1)} %collective-permute-done.13.refs_1_), channel_id=1, source_target_pairs={{0,16},{8,24},{16,0},{24,8},{1,17},{9,25},{17,1},{25,9},{2,18},{10... | collective-permute-start | bytes 786440 | tf_op jit(solution)/shard_map/ppermute | solution.py:602
  175.1 7.3 %collective-permute-start.16 = (bf16[4,2,64,256]{3,2,1,0:T(8,128)(2,1)S(1)}, bf16[4,2,64,256]{3,2,1,0:T(8,128)(2,1)S(1)}, u32[]{:S(2)}, u32[]{:S(2)}) collective-permute-start(bf16[4,2,64,256]{3,2,1,0:T(8,128)(2,1)S(1)} %constant_dynamic-update-slice_fusion.refs_0_), channel_id=1, source_target_pairs={{0,8},{8,0},{16,24},{24,16},{1,9},{9,1},{17,25},{25,17},{2,10},{10... | collective-permute-start | bytes 786440 | tf_op jit(solution)/shard_map/ppermute | solution.py:602
  175.1 7.3 %collective-permute-start.17 = (bf16[4,2,64,256]{3,2,1,0:T(8,128)(2,1)S(1)}, bf16[4,2,64,256]{3,2,1,0:T(8,128)(2,1)S(1)}, u32[]{:S(2)}, u32[]{:S(2)}) collective-permute-start(bf16[4,2,64,256]{3,2,1,0:T(8,128)(2,1)S(1)} %collective-permute-done.13.refs_1_), channel_id=1, source_target_pairs={{0,8},{8,0},{16,24},{24,16},{1,9},{9,1},{17,25},{25,17},{2,10},{10... | collective-permute-start | bytes 786440 | tf_op jit(solution)/shard_map/ppermute | solution.py:602
  177.9 3.9 %copy-start.6 = (bf16[4,2,64,256]{3,2,1,0:T(8,128)(2,1)}, bf16[4,2,64,256]{3,2,1,0:T(8,128)(2,1)S(1)}, u32[]{:S(2)}) copy-start(bf16[4,2,64,256]{3,2,1,0:T(8,128)(2,1)S(1)} %collective-permute-done.14.refs_2_) | copy-start | bytes 786436
  177.9 4.5 %collective-permute-start.18 = (bf16[4,2,64,256]{3,2,1,0:T(8,128)(2,1)S(1)}, bf16[4,2,64,256]{3,2,1,0:T(8,128)(2,1)S(1)}, u32[]{:S(2)}, u32[]{:S(2)}) collective-permute-start(bf16[4,2,64,256]{3,2,1,0:T(8,128)(2,1)S(1)} %collective-permute-done.14.refs_2_), channel_id=1, source_target_pairs={{0,8},{8,0},{16,24},{24,16},{1,9},{9,1},{17,25},{25,17},{2,10},{10... | collective-permute-start | bytes 786440 | tf_op jit(solution)/shard_map/ppermute | solution.py:602
  180.7 1.1 copy-start.7
  180.7 1.7 collective-permute-start.19
  182.4 0.7 copy-start.8
  182.4 0.8 copy-start.9
  182.4 0.9 copy-start.10
  183.3 0.7 copy-start.11

commit v11 on v9

--- a/solution.py
+++ b/solution.py
@@ -650,19 +650,25 @@
 
 
 def place_kernel(*refs):
-    (*parts, query_ref, key_ref, value_ref, out_ref, all_ref) = refs
+    (*sources, query_ref, key_ref, value_ref, out_ref, all_ref, held, sems) = refs
+    copies = [
+        pltpu.make_async_copy(ref, held.at[i], sems.at[i]) for i, ref in enumerate(sources)
+    ]
+    for copy in copies:
+        copy.start()
     own_sample, own_turb = lax.axis_index("sample"), lax.axis_index("turb")
-    _, quads, share, quad = parts[0].shape
+    _, _, quads, share, quad = held.shape
     for i in range(SAMPLES):
+        copies[2 * i].wait()
+        copies[2 * i + 1].wait()
         product = own_sample ^ ((i % 2) * 2 + i // 2)
         for apart in range(TURBS):
             place = turb_place(apart)
-            ref = parts[2 * i + place // 4]
             rows = pl.ds(pl.multiple_of((apart ^ own_turb) * share, share), share)
             for j in range(quads):
-                all_ref[product, rows, j * quad : (j + 1) * quad] = ref[place % 4, j].astype(
-                    jnp.float32
-                )
+                all_ref[product, rows, j * quad : (j + 1) * quad] = held[
+                    2 * i + place // 4, place % 4, j
+                ].astype(jnp.float32)
     for i, ref in enumerate((query_ref, key_ref, value_ref, out_ref)):
         ref[...] = all_ref[i]
 
@@ -670,10 +676,14 @@
 def place_sums(parts, width):
     return pl.pallas_call(
         place_kernel,
-        in_specs=[pl.BlockSpec(memory_space=pltpu.VMEM)] * len(parts),
+        in_specs=[pl.BlockSpec(memory_space=pl.ANY)] * len(parts),
         out_specs=[pl.BlockSpec(memory_space=pltpu.VMEM)] * 4,
         out_shape=[jax.ShapeDtypeStruct((width, width), jnp.float32)] * 4,
-        scratch_shapes=[pltpu.VMEM((4, width, width), jnp.float32)],
+        scratch_shapes=[
+            pltpu.VMEM((4, width, width), jnp.float32),
+            pltpu.VMEM((len(parts),) + parts[0].shape, jnp.bfloat16),
+            pltpu.SemaphoreType.DMA((len(parts),)),
+        ],
         compiler_params=pltpu.CompilerParams(vmem_limit_bytes=VMEM_LIMIT),
         cost_estimate=pl.CostEstimate(
             flops=0, bytes_accessed=24 * width * width, transcendentals=0
@@ -713,10 +723,13 @@
     *more, late, send, gain = backward(
         sectors, adjacency, grad_rows, out_weight, *saved, *weights, [before], block_rows, 1
     )
+    more, send, arrived, layer_output = lax.optimization_barrier(
+        (more, send, arrived, layer_output)
+    )
     arrived_late = across(send, "sample", 1)
     grad_rows = finish(rows, grad_rows, *weights, grads + more)
-    grad_rows, late, arrived_late, gain, early, arrived, layer_output = lax.optimization_barrier(
-        (grad_rows, late, arrived_late, gain, early, arrived, layer_output)
+    grad_rows, late, arrived_late, gain, early, arrived = lax.optimization_barrier(
+        (grad_rows, late, arrived_late, gain, early, arrived)
     )
     gain = gain[0].reshape(-1, late.shape[1])
     arrived_gain = across(gain, "sample", 1)

time: 188 us -> 182 us (0.968)
  waiting for transfers between devices: 50.3 us -> 45.9 us
    ppermute x20, waiting for transfers between devices: 39.2 us -> 34.8 us  [across(): return lax.ppermute(tensor, axis, [(i, i ^ distance) for i in range(size)])]
    unnamed x29 -> x31, local copies, waits for them, and re-layouts: 3.36 us -> 3.88 us
  transfers between devices with their start and end apart: 23 -> 23, of which waited for: 13 -> 14; matrix products, arithmetic and copies ran while one was open for 3% -> 3% of each run, Pallas kernels for 31% -> 32%
where the time goes in v11:
time: 182 us
  Pallas kernels  62.1 us (34%)
  waiting for transfers between devices  45.9 us (25%)
  blocking collectives  33.1 us (18%)
  starting transfers between devices  29.4 us (16%)
  local copies, waits for them, and re-layouts  5.21 us (3%)
  other arithmetic  4.69 us (3%)
    ppermute x20, waiting for transfers between devices, across(): return lax.ppermute(tensor, axis, [(i, i ^ distance) for i in range(size)])  34.8 us
    all_to_all x1, blocking collectives, swap(): return lax.all_to_all(tensor, axis, split_axis=0, concat_axis=0, tiled=True)  33.1 us
    pallas_call x2, Pallas kernels, backward(): pl.pallas_call(lambda *refs: backward_kernel(block_rows, head_dim, which,...  29.9 us
    pallas_call x1, Pallas kernels, forward(): pl.pallas_call(lambda *refs: forward_kernel(block_rows, head_dim, *refs),...  21.9 us
    ppermute x20, starting transfers between devices, across(): return lax.ppermute(tensor, axis, [(i, i ^ distance) for i in range(size)])  18.3 us
    all_to_all x3, starting transfers between devices, swap(): return lax.all_to_all(tensor, axis, split_axis=0, concat_axis=0, tiled=True)  11.2 us
    all_to_all x3, waiting for transfers between devices, swap(): return lax.all_to_all(tensor, axis, split_axis=0, concat_axis=0, tiled=True)  11.1 us
    pallas_call x1, Pallas kernels, finish(): pl.pallas_call(lambda *refs: finish_kernel(width // quad, *refs), grid=(r...  6.54 us
  transfers between devices with their start and end apart: 23, of which 14 were waited for; matrix products, arithmetic and copies ran while one was open for 3% of the time, Pallas kernels for 32%

profile of v11, /device:TPU:0, one launch (start us, length us, event | category | flops | bytes accessed | tf_op | source)
XLA Modules:
  0.0 181.7 jit_solution(1263690948754672842)
XLA Ops:
  0.6 33.1 %all_to_all.20 = bf16[8,128,512]{2,1,0:T(8,128)(2,1)} all-to-all(bf16[8,128,512]{2,1,0:T(8,128)(2,1)} %param.9), channel_id=1, replica_groups=mesh['sample'=4,'turb'=8] {'turb'}, dimensions={0} | all-to-all | bytes 2097152 | tf_op jit(solution)/shard_map/all_to_all | solution.py:592
  33.8 3.6 %all-to-all-start.1 = ((bf16[8,128,512]{2,1,0:T(8,128)(2,1)}), bf16[8,128,512]{2,1,0:T(8,128)(2,1)S(1)}, u32[]{:S(2)}, u32[]{:S(2)}) async-start(bf16[8,128,512]{2,1,0:T(8,128)(2,1)} %param.10), calls=%async_computation.1 | async-start | bytes 2097152 | tf_op jit(solution)/shard_map/all_to_all | solution.py:592
  37.4 21.9 %forward.1 = (bf16[512,1024]{1,0:T(8,128)(2,1)}, bf16[1024,512]{1,0:T(8,128)(2,1)}, bf16[1024,512]{1,0:T(8,128)(2,1)}, bf16[1024,512]{1,0:T(8,128)(2,1)}, bf16[5...) custom-call(s32[8]{0:T(128)} %refs_0_.5, ...), custom_call_target="tpu_custom_call" | custom-call | flops 5368709120 | bytes 10485760 | tf_op jit(solution)/shard_map/forward/pallas_call | solution.py:367
  59.3 3.7 %all-to-all-done.1 = bf16[8,128,512]{2,1,0:T(8,128)(2,1)S(1)} async-done(((bf16[8,128,512]{2,1,0:T(8,128)(2,1)}), bf16[8,128,512]{2,1,0:T(8,128)(2,1)S(1)}, u32[]{:S(2)}, u32[]{:S(2)}) %all-to-all-start.1) | async-done | bytes 1048608 | tf_op jit(solution)/shard_map/all_to_all | solution.py:592
  63.0 1.0 copy-done
  63.9 3.7 %all-to-all-start.2 = ((bf16[8,128,512]{2,1,0:T(8,128)(2,1)}), bf16[8,128,512]{2,1,0:T(8,128)(2,1)S(1)}, u32[]{:S(2)}, u32[]{:S(2)}) async-start(bf16[8,128,512]{2,1,0:T(8,128)(2,1)} %bitcast.15), calls=%async_computation.2 | async-start | bytes 2097152 | tf_op jit(solution)/shard_map/all_to_all | solution.py:592
  67.7 14.9 %backward.2 = (bf16[1024,256]{1,0:T(8,128)(2,1)}, bf16[1024,256]{1,0:T(8,128)(2,1)}, bf16[1024,256]{1,0:T(8,128)(2,1)}, f32[1024,256]{1,0:T(8,128)}, bf16[1024,256]{1,0:T(8,128)(2,1)}, /*index=5*/f32[8,512]{1,0:T(8,128)}) custom-call(s32[8]{0:T(128)} %refs_0_.5, s32[3,8,8]{2,1,0:T(8,128)} %bitcast.26, bf16[512,512]{1,0:T(8,128)(2,1)} %refs_2_.3, ...), custom_call_target="tpu_custom_call" | custom-call | flops 4026531840 | bytes 7340032 | tf_op jit(solution)/shard_map/backward/pallas_call | solution.py:506
  82.5 2.7 %collective-permute-start = (bf16[1024,256]{1,0:T(8,128)(2,1)}, bf16[1024,256]{1,0:T(8,128)(2,1)S(1)}, u32[]{:S(2)}, u32[]{:S(2)}) collective-permute-start(bf16[1024,256]{1,0:T(8,128)(2,1)} %get-tuple-element.63), channel_id=1, source_target_pairs={{0,1},{1,0},{2,3},{3,2},{4,5},{5,4},{6,7},{7,6},{8,9},{9,8},{10,11... | collective-permute-start | bytes 1572872 | tf_op jit(solution)/shard_map/ppermute | solution.py:602
  85.3 15.0 %backward.3 = (bf16[1024,256]{1,0:T(8,128)(2,1)}, bf16[1024,256]{1,0:T(8,128)(2,1)}, bf16[1024,256]{1,0:T(8,128)(2,1)}, f32[1024,256]{1,0:T(8,128)}, f32[1024,256]{1,0:T(8,128)}, /*index=5*/f32[8,512]{1,0:T(8,128)}) custom-call(s32[8]{0:T(128)} %refs_0_.5, s32[3,8,8]{2,1,0:T(8,128)} %bitcast.27, bf16[512,512]{1,0:T(8,128)(2,1)} %refs_2_.3, ...), custom_call_target="tpu_custom_call" | custom-call | flops 4026531840 | bytes 7340032 | tf_op jit(solution)/shard_map/backward/pallas_call | solution.py:506
  100.4 0.0 copy-start.6
  100.4 0.1 collective-permute-start.1
  100.4 0.7 copy-done.6
  101.2 6.5 %finish.1 = bf16[1024,512]{1,0:T(8,128)(2,1)} custom-call(bf16[1024,512]{1,0:T(8,128)(2,1)} %bitcast.11, bf16[1024,512]{1,0:T(8,128)(2,1)} %bitcast.14, f32[1,512]{1,0:T(1,128)} %bitcast.23, bf16[512,512]{1,0:T(8,128)(2,1)} %refs_3_.1, bf16[512,512]{1,0:T(8,128)(2,1)} %refs_4_.3, bf16[512,512]{1,0:T(8,128)(2,1)} %refs_5_.3, ...), custom_call_target="tpu_custom_call" | custom-call | flops 1610612736 | bytes 8388608 | tf_op jit(solution)/shard_map/finish/pallas_call | solution.py:572
  107.7 0.7 slice_reduce_fusion
  108.4 0.1 collective-permute-start.4
  108.5 1.4 add.63
  110.0 0.7 pad_maximum_fusion
  110.7 1.8 %collective-permute-start.5 = (bf16[528,256]{1,0:T(8,128)(2,1)}, bf16[528,256]{1,0:T(8,128)(2,1)S(1)}, u32[]{:S(2)}, u32[]{:S(2)}) collective-permute-start(bf16[528,256]{1,0:T(8,128)(2,1)} %pad_maximum_fusion), channel_id=1, source_target_pairs={{0,16},{8,24},{16,0},{24,8},{1,17},{9,25},{17,1},{25,9},{2,18},{10... | collective-permute-start | bytes 811016 | tf_op jit(solution)/shard_map/ppermute | solution.py:602
  112.5 3.8 %all-to-all-start.3 = ((bf16[8,128,512]{2,1,0:T(8,128)(2,1)}), bf16[8,128,512]{2,1,0:T(8,128)(2,1)S(1)}, u32[]{:S(2)}, u32[]{:S(2)}) async-start(bf16[8,128,512]{2,1,0:T(8,128)(2,1)} %bitcast.5), calls=%async_computation.3 | async-start | bytes 2097152 | tf_op jit(solution)/shard_map/all_to_all | solution.py:592
  116.4 3.5 %collective-permute-done.5 = bf16[528,256]{1,0:T(8,128)(2,1)S(1)} collective-permute-done((bf16[528,256]{1,0:T(8,128)(2,1)}, bf16[528,256]{1,0:T(8,128)(2,1)S(1)}, u32[]{:S(2)}, u32[]{:S(2)}) %collective-permute-start.5) | collective-permute-done | bytes 270368 | tf_op jit(solution)/shard_map/ppermute | solution.py:602
  119.9 0.1 slice_add_fusion
  120.0 0.9 collective-permute-start.6
  120.9 0.0 copy-done.7
  121.0 0.1 convert_add_fusion
  121.1 0.1 collective-permute-start.2
  121.2 8.6 %collective-permute-done.6 = bf16[272,256]{1,0:T(8,128)(2,1)S(1)} collective-permute-done((bf16[272,256]{1,0:T(8,128)(2,1)S(1)}, bf16[272,256]{1,0:T(8,128)(2,1)S(1)}, u32[]{:S(2)}, u32[]{:S(2)}) %collective-permute-start.6) | collective-permute-done | bytes 139296 | tf_op jit(solution)/shard_map/ppermute | solution.py:602
  129.9 0.0 copy-start.1
  129.9 0.1 slice_add_fusion.1
  130.0 1.2 collective-permute-start.3
  131.2 3.8 %collective-permute-done.3 = bf16[256,256]{1,0:T(8,128)(2,1)S(1)} collective-permute-done((bf16[256,256]{1,0:T(8,128)(2,1)S(1)}, bf16[256,256]{1,0:T(8,128)(2,1)S(1)}, u32[]{:S(2)}, u32[]{:S(2)}) %collective-permute-start.3) | collective-permute-done | bytes 131104 | tf_op jit(solution)/shard_map/ppermute | solution.py:602
  135.1 0.0 copy-start.2
  135.1 7.4 %all-to-all-done.3 = bf16[8,128,512]{2,1,0:T(8,128)(2,1)S(1)} async-done(((bf16[8,128,512]{2,1,0:T(8,128)(2,1)}), bf16[8,128,512]{2,1,0:T(8,128)(2,1)S(1)}, u32[]{:S(2)}, u32[]{:S(2)}) %all-to-all-start.3) | async-done | bytes 1048608 | tf_op jit(solution)/shard_map/all_to_all | solution.py:592
  142.6 0.2 concatenate.33
  142.8 0.1 collective-permute-start.7
  142.8 0.2 concatenate.34
  143.0 2.5 %collective-permute-start.8 = (bf16[144,256]{1,0:T(8,128)(2,1)S(1)}, bf16[144,256]{1,0:T(8,128)(2,1)S(1)}, u32[]{:S(2)}, u32[]{:S(2)}) collective-permute-start(bf16[144,256]{1,0:T(8,128)(2,1)S(1)} %concatenate.34), channel_id=1, source_target_pairs={{0,4},{1,5},{2,6},{3,7},{4,0},{5,1},{6,2},{7,3},{8,12},{9,13},{10,... | collective-permute-start | bytes 221192 | tf_op jit(solution)/shard_map/ppermute | solution.py:602
  145.5 0.1 concatenate.35
  145.7 1.9 %collective-permute-start.9 = (bf16[144,256]{1,0:T(8,128)(2,1)S(1)}, bf16[144,256]{1,0:T(8,128)(2,1)S(1)}, u32[]{:S(2)}, u32[]{:S(2)}) collective-permute-start(bf16[144,256]{1,0:T(8,128)(2,1)S(1)} %concatenate.35), channel_id=1, source_target_pairs={{0,6},{1,7},{2,4},{3,5},{4,2},{5,3},{6,0},{7,1},{8,14},{9,15},{10,... | collective-permute-start | bytes 221192 | tf_op jit(solution)/shard_map/ppermute | solution.py:602
  147.7 0.1 collective-permute-done.7
  147.8 3.3 %collective-permute-done.8 = bf16[144,256]{1,0:T(8,128)(2,1)S(1)} collective-permute-done((bf16[144,256]{1,0:T(8,128)(2,1)S(1)}, bf16[144,256]{1,0:T(8,128)(2,1)S(1)}, u32[]{:S(2)}, u32[]{:S(2)}) %collective-permute-start.8) | collective-permute-done | bytes 73760 | tf_op jit(solution)/shard_map/ppermute | solution.py:602
  151.1 0.0 slice-start
  151.1 0.0 slice-start.1
  151.1 0.9 collective-permute-done.9
  152.1 1.3 collective-permute-start.10
  153.4 2.2 %collective-permute-start.11 = (bf16[1,2,64,256]{3,2,1,0:T(8,128)(2,1)S(1)}, bf16[1,2,64,256]{3,2,1,0:T(8,128)(2,1)S(1)}, u32[]{:S(2)}, u32[]{:S(2)}) collective-permute-start(bf16[1,2,64,256]{3,2,1,0:T(8,128)(2,1)S(1)} %bitcast.17), channel_id=1, source_target_pairs={{0,4},{1,5},{2,6},{3,7},{4,0},{5,1},{6,2},{7,3},{8,12},{9,13},{10,... | collective-permute-start | bytes 196616 | tf_op jit(solution)/shard_map/ppermute | solution.py:602
  155.6 1.0 collective-permute-start.12
  156.6 1.0 collective-permute-done.10
  157.6 1.8 collective-permute-done.11
  159.4 2.3 %collective-permute-done.12 = bf16[1,2,64,256]{3,2,1,0:T(8,128)(2,1)S(1)} collective-permute-done((bf16[1,2,64,256]{3,2,1,0:T(8,128)(2,1)S(1)}, bf16[1,2,64,256]{3,2,1,0:T(8,128)(2,1)S(1)}, u32[]{:S(2)}, u32[]{:S(2)}) %collective-permute-start.12) | collective-permute-done | bytes 65568 | tf_op jit(solution)/shard_map/ppermute | solution.py:602
  161.7 0.6 collective-permute-start.13
  162.3 1.0 collective-permute-start.14
  163.3 4.8 %collective-permute-done.13.refs_1_ = bf16[4,2,64,256]{3,2,1,0:T(8,128)(2,1)S(1)} collective-permute-done((bf16[4,2,64,256]{3,2,1,0:T(8,128)(2,1)S(1)}, bf16[4,2,64,256]{3,2,1,0:T(8,128)(2,1)S(1)}, u32[]{:S(2)}, u32[]{:S(2)}) %collective-permute-start.13) | collective-permute-done | bytes 262176 | tf_op jit(solution)/shard_map/ppermute | solution.py:602
  168.2 0.1 collective-permute-start.15
  168.3 1.1 broadcast_maximum_fusion.1
  169.4 0.5 collective-permute-start.17
  169.9 0.8 collective-permute-done.14.refs_2_
  170.7 3.8 %collective-permute-done.15.refs_3_ = bf16[4,2,64,256]{3,2,1,0:T(8,128)(2,1)S(1)} collective-permute-done((bf16[4,2,64,256]{3,2,1,0:T(8,128)(2,1)S(1)}, bf16[4,2,64,256]{3,2,1,0:T(8,128)(2,1)S(1)}, u32[]{:S(2)}, u32[]{:S(2)}) %collective-permute-start.15) | collective-permute-done | bytes 262176 | tf_op jit(solution)/shard_map/ppermute | solution.py:602
  174.5 1.1 broadcast_maximum_fusion
  175.6 0.6 copy.16
  176.2 0.6 copy-done.11
  176.9 0.1 copy-done.12
  177.0 0.1 copy-done.13
  177.1 0.7 copy-done.14
  177.8 3.7 %place.1 = (f32[512,512]{1,0:T(8,128)}, f32[512,512]{1,0:T(8,128)}, f32[512,512]{1,0:T(8,128)}, f32[512,512]{1,0:T(8,128)}) custom-call(bf16[4,2,64,256]{3,2,1,0:T(8,128)(2,1)} %copy-done.5, bf16[4,2,64,256]{3,2,1,0:T(8,128)(2,1)} %copy-done.8, bf16[4,2,64,256]{3,2,1,0:T(8,128)(2,1)} %copy-done.9, bf16[4,2,64,256]{3,2,1,0:T(8,128)(2,1)} %copy-done.10, ...), custom_call_target="tpu_custom_call" | custom-call | bytes 6291456 | tf_op jit(solution)/shard_map/place/pallas_call | solution.py:677
  (58 shorter events, 0.5 us)
Async XLA Ops:
  33.8 29.2 %all-to-all-start.1 = ((bf16[8,128,512]{2,1,0:T(8,128)(2,1)}), bf16[8,128,512]{2,1,0:T(8,128)(2,1)S(1)}, u32[]{:S(2)}, u32[]{:S(2)}) async-start(bf16[8,128,512]{2,1,0:T(8,128)(2,1)} %param.10), calls=%async_computation.1 | async-start | bytes 2097152 | tf_op jit(solution)/shard_map/all_to_all | solution.py:592
  63.0 1.0 copy-start
  63.9 36.4 %all-to-all-start.2 = ((bf16[8,128,512]{2,1,0:T(8,128)(2,1)}), bf16[8,128,512]{2,1,0:T(8,128)(2,1)S(1)}, u32[]{:S(2)}, u32[]{:S(2)}) async-start(bf16[8,128,512]{2,1,0:T(8,128)(2,1)} %bitcast.15), calls=%async_computation.2 | async-start | bytes 2097152 | tf_op jit(solution)/shard_map/all_to_all | solution.py:592
  82.5 17.8 %collective-permute-start = (bf16[1024,256]{1,0:T(8,128)(2,1)}, bf16[1024,256]{1,0:T(8,128)(2,1)S(1)}, u32[]{:S(2)}, u32[]{:S(2)}) collective-permute-start(bf16[1024,256]{1,0:T(8,128)(2,1)} %get-tuple-element.63), channel_id=1, source_target_pairs={{0,1},{1,0},{2,3},{3,2},{4,5},{5,4},{6,7},{7,6},{8,9},{9,8},{10,11... | collective-permute-start | bytes 1572872 | tf_op jit(solution)/shard_map/ppermute | solution.py:602
  100.4 0.8 copy-start.6
  100.4 7.3 %collective-permute-start.1 = (f32[1024,256]{1,0:T(8,128)}, f32[1024,256]{1,0:T(8,128)}, u32[]{:S(2)}, u32[]{:S(2)}) collective-permute-start(f32[1024,256]{1,0:T(8,128)} %get-tuple-element.73), channel_id=1, source_target_pairs={{0,8},{8,0},{16,24},{24,16},{1,9},{9,1},{17,25},{25,17},{2,10},{10... | collective-permute-start | bytes 3145736 | tf_op jit(solution)/shard_map/ppermute | solution.py:602
  101.2 7.4 %copy-start.3 = (f32[1024,256]{1,0:T(8,128)S(1)}, f32[1024,256]{1,0:T(8,128)}, u32[]{:S(2)}) copy-start(f32[1024,256]{1,0:T(8,128)} %get-tuple-element.79) | copy-start | bytes 3145732
  108.4 1.5 collective-permute-start.4
  110.7 9.2 %collective-permute-start.5 = (bf16[528,256]{1,0:T(8,128)(2,1)}, bf16[528,256]{1,0:T(8,128)(2,1)S(1)}, u32[]{:S(2)}, u32[]{:S(2)}) collective-permute-start(bf16[528,256]{1,0:T(8,128)(2,1)} %pad_maximum_fusion), channel_id=1, source_target_pairs={{0,16},{8,24},{16,0},{24,8},{1,17},{9,25},{17,1},{25,9},{2,18},{10... | collective-permute-start | bytes 811016 | tf_op jit(solution)/shard_map/ppermute | solution.py:602
  112.5 30.0 %all-to-all-start.3 = ((bf16[8,128,512]{2,1,0:T(8,128)(2,1)}), bf16[8,128,512]{2,1,0:T(8,128)(2,1)S(1)}, u32[]{:S(2)}, u32[]{:S(2)}) async-start(bf16[8,128,512]{2,1,0:T(8,128)(2,1)} %bitcast.5), calls=%async_computation.3 | async-start | bytes 2097152 | tf_op jit(solution)/shard_map/all_to_all | solution.py:592
  116.4 4.6 %copy-start.4 = (f32[1024,256]{1,0:T(8,128)S(1)}, f32[1024,256]{1,0:T(8,128)}, u32[]{:S(2)}) copy-start(f32[1024,256]{1,0:T(8,128)} %get-tuple-element.77) | copy-start | bytes 3145732
  119.9 1.0 copy-start.7
  120.0 9.8 %collective-permute-start.6 = (bf16[272,256]{1,0:T(8,128)(2,1)S(1)}, bf16[272,256]{1,0:T(8,128)(2,1)S(1)}, u32[]{:S(2)}, u32[]{:S(2)}) collective-permute-start(bf16[272,256]{1,0:T(8,128)(2,1)S(1)} %pad_maximum_fusion.2), channel_id=1, source_target_pairs={{0,1},{1,0},{2,3},{3,2},{4,5},{5,4},{6,7},{7,6},{8,9},{9,8},{10,11... | collective-permute-start | bytes 417800 | tf_op jit(solution)/shard_map/ppermute | solution.py:602
  121.1 8.7 %collective-permute-start.2 = (f32[512,256]{1,0:T(8,128)S(1)}, f32[512,256]{1,0:T(8,128)S(1)}, u32[]{:S(2)}, u32[]{:S(2)}) collective-permute-start(f32[512,256]{1,0:T(8,128)S(1)} %slice.146), channel_id=1, source_target_pairs={{0,8},{8,0},{16,24},{24,16},{1,9},{9,1},{17,25},{25,17},{2,10},{10... | collective-permute-start | bytes 1572872 | tf_op jit(solution)/shard_map/ppermute | solution.py:602
  129.9 17.8 %copy-start.1 = (f32[256,256]{1,0:T(8,128)}, f32[256,256]{1,0:T(8,128)S(1)}, u32[]{:S(2)}) copy-start(f32[256,256]{1,0:T(8,128)S(1)} %slice_add_fusion.2) | copy-start | bytes 786436
  130.0 5.1 %collective-permute-start.3 = (bf16[256,256]{1,0:T(8,128)(2,1)S(1)}, bf16[256,256]{1,0:T(8,128)(2,1)S(1)}, u32[]{:S(2)}, u32[]{:S(2)}) collective-permute-start(bf16[256,256]{1,0:T(8,128)(2,1)S(1)} %slice.225), channel_id=1, source_target_pairs={{0,16},{8,24},{16,0},{24,8},{1,17},{9,25},{17,1},{25,9},{2,18},{10... | collective-permute-start | bytes 393224 | tf_op jit(solution)/shard_map/ppermute | solution.py:602
  135.1 12.6 %copy-start.2 = (f32[256,256]{1,0:T(8,128)}, f32[256,256]{1,0:T(8,128)S(1)}, u32[]{:S(2)}) copy-start(f32[256,256]{1,0:T(8,128)S(1)} %slice_add_fusion.3) | copy-start | bytes 786436
  142.8 5.0 %collective-permute-start.7 = (bf16[144,256]{1,0:T(8,128)(2,1)S(1)}, bf16[144,256]{1,0:T(8,128)(2,1)S(1)}, u32[]{:S(2)}, u32[]{:S(2)}) collective-permute-start(bf16[144,256]{1,0:T(8,128)(2,1)S(1)} %concatenate.33), channel_id=1, source_target_pairs={{0,2},{1,3},{2,0},{3,1},{4,6},{5,7},{6,4},{7,5},{8,10},{9,11},{10,... | collective-permute-start | bytes 221192 | tf_op jit(solution)/shard_map/ppermute | solution.py:602
  143.0 8.1 %collective-permute-start.8 = (bf16[144,256]{1,0:T(8,128)(2,1)S(1)}, bf16[144,256]{1,0:T(8,128)(2,1)S(1)}, u32[]{:S(2)}, u32[]{:S(2)}) collective-permute-start(bf16[144,256]{1,0:T(8,128)(2,1)S(1)} %concatenate.34), channel_id=1, source_target_pairs={{0,4},{1,5},{2,6},{3,7},{4,0},{5,1},{6,2},{7,3},{8,12},{9,13},{10,... | collective-permute-start | bytes 221192 | tf_op jit(solution)/shard_map/ppermute | solution.py:602
  145.7 6.3 %collective-permute-start.9 = (bf16[144,256]{1,0:T(8,128)(2,1)S(1)}, bf16[144,256]{1,0:T(8,128)(2,1)S(1)}, u32[]{:S(2)}, u32[]{:S(2)}) collective-permute-start(bf16[144,256]{1,0:T(8,128)(2,1)S(1)} %concatenate.35), channel_id=1, source_target_pairs={{0,6},{1,7},{2,4},{3,5},{4,2},{5,3},{6,0},{7,1},{8,14},{9,15},{10,... | collective-permute-start | bytes 221192 | tf_op jit(solution)/shard_map/ppermute | solution.py:602
  151.1 1.0 slice-start
  151.1 0.9 slice-start.1
  152.1 5.5 %collective-permute-start.10 = (bf16[1,2,64,256]{3,2,1,0:T(8,128)(2,1)S(1)}, bf16[1,2,64,256]{3,2,1,0:T(8,128)(2,1)S(1)}, u32[]{:S(2)}, u32[]{:S(2)}) collective-permute-start(bf16[1,2,64,256]{3,2,1,0:T(8,128)(2,1)S(1)} %bitcast.16), channel_id=1, source_target_pairs={{0,2},{1,3},{2,0},{3,1},{4,6},{5,7},{6,4},{7,5},{8,10},{9,11},{10,... | collective-permute-start | bytes 196616 | tf_op jit(solution)/shard_map/ppermute | solution.py:602
  153.4 6.0 %collective-permute-start.11 = (bf16[1,2,64,256]{3,2,1,0:T(8,128)(2,1)S(1)}, bf16[1,2,64,256]{3,2,1,0:T(8,128)(2,1)S(1)}, u32[]{:S(2)}, u32[]{:S(2)}) collective-permute-start(bf16[1,2,64,256]{3,2,1,0:T(8,128)(2,1)S(1)} %bitcast.17), channel_id=1, source_target_pairs={{0,4},{1,5},{2,6},{3,7},{4,0},{5,1},{6,2},{7,3},{8,12},{9,13},{10,... | collective-permute-start | bytes 196616 | tf_op jit(solution)/shard_map/ppermute | solution.py:602
  155.6 6.1 %collective-permute-start.12 = (bf16[1,2,64,256]{3,2,1,0:T(8,128)(2,1)S(1)}, bf16[1,2,64,256]{3,2,1,0:T(8,128)(2,1)S(1)}, u32[]{:S(2)}, u32[]{:S(2)}) collective-permute-start(bf16[1,2,64,256]{3,2,1,0:T(8,128)(2,1)S(1)} %bitcast.18), channel_id=1, source_target_pairs={{0,6},{1,7},{2,4},{3,5},{4,2},{5,3},{6,0},{7,1},{8,14},{9,15},{10,... | collective-permute-start | bytes 196616 | tf_op jit(solution)/shard_map/ppermute | solution.py:602
  161.7 7.7 %copy-start.5 = (bf16[4,2,64,256]{3,2,1,0:T(8,128)(2,1)}, bf16[4,2,64,256]{3,2,1,0:T(8,128)(2,1)S(1)}, u32[]{:S(2)}) copy-start(bf16[4,2,64,256]{3,2,1,0:T(8,128)(2,1)S(1)} %pad_maximum_fusion.1.refs_0_) | copy-start | bytes 786436
  161.7 6.4 %collective-permute-start.13 = (bf16[4,2,64,256]{3,2,1,0:T(8,128)(2,1)S(1)}, bf16[4,2,64,256]{3,2,1,0:T(8,128)(2,1)S(1)}, u32[]{:S(2)}, u32[]{:S(2)}) collective-permute-start(bf16[4,2,64,256]{3,2,1,0:T(8,128)(2,1)S(1)} %pad_maximum_fusion.1.refs_0_), channel_id=1, source_target_pairs={{0,1},{1,0},{2,3},{3,2},{4,5},{5,4},{6,7},{7,6},{8,9},{9,8},{10,11... | collective-permute-start | bytes 786440 | tf_op jit(solution)/shard_map/ppermute | solution.py:602
  162.3 8.4 %collective-permute-start.14 = (bf16[4,2,64,256]{3,2,1,0:T(8,128)(2,1)S(1)}, bf16[4,2,64,256]{3,2,1,0:T(8,128)(2,1)S(1)}, u32[]{:S(2)}, u32[]{:S(2)}) collective-permute-start(bf16[4,2,64,256]{3,2,1,0:T(8,128)(2,1)S(1)} %pad_maximum_fusion.1.refs_0_), channel_id=1, source_target_pairs={{0,16},{8,24},{16,0},{24,8},{1,17},{9,25},{17,1},{25,9},{2,18},{10... | collective-permute-start | bytes 786440 | tf_op jit(solution)/shard_map/ppermute | solution.py:602
  168.2 1.2 copy-start.8
  168.2 6.4 %collective-permute-start.15 = (bf16[4,2,64,256]{3,2,1,0:T(8,128)(2,1)S(1)}, bf16[4,2,64,256]{3,2,1,0:T(8,128)(2,1)S(1)}, u32[]{:S(2)}, u32[]{:S(2)}) collective-permute-start(bf16[4,2,64,256]{3,2,1,0:T(8,128)(2,1)S(1)} %collective-permute-done.13.refs_1_), channel_id=1, source_target_pairs={{0,16},{8,24},{16,0},{24,8},{1,17},{9,25},{17,1},{25,9},{2,18},{10... | collective-permute-start | bytes 786440 | tf_op jit(solution)/shard_map/ppermute | solution.py:602
  169.4 6.8 %collective-permute-start.16 = (bf16[4,2,64,256]{3,2,1,0:T(8,128)(2,1)S(1)}, bf16[4,2,64,256]{3,2,1,0:T(8,128)(2,1)S(1)}, u32[]{:S(2)}, u32[]{:S(2)}) collective-permute-start(bf16[4,2,64,256]{3,2,1,0:T(8,128)(2,1)S(1)} %pad_maximum_fusion.1.refs_0_), channel_id=1, source_target_pairs={{0,8},{8,0},{16,24},{24,16},{1,9},{9,1},{17,25},{25,17},{2,10},{10... | collective-permute-start | bytes 786440 | tf_op jit(solution)/shard_map/ppermute | solution.py:602
  169.4 6.8 %collective-permute-start.17 = (bf16[4,2,64,256]{3,2,1,0:T(8,128)(2,1)S(1)}, bf16[4,2,64,256]{3,2,1,0:T(8,128)(2,1)S(1)}, u32[]{:S(2)}, u32[]{:S(2)}) collective-permute-start(bf16[4,2,64,256]{3,2,1,0:T(8,128)(2,1)S(1)} %collective-permute-done.13.refs_1_), channel_id=1, source_target_pairs={{0,8},{8,0},{16,24},{24,16},{1,9},{9,1},{17,25},{25,17},{2,10},{10... | collective-permute-start | bytes 786440 | tf_op jit(solution)/shard_map/ppermute | solution.py:602
  170.7 4.9 %copy-start.9 = (bf16[4,2,64,256]{3,2,1,0:T(8,128)(2,1)}, bf16[4,2,64,256]{3,2,1,0:T(8,128)(2,1)S(1)}, u32[]{:S(2)}) copy-start(bf16[4,2,64,256]{3,2,1,0:T(8,128)(2,1)S(1)} %collective-permute-done.14.refs_2_) | copy-start | bytes 786436
  170.7 5.5 %collective-permute-start.18 = (bf16[4,2,64,256]{3,2,1,0:T(8,128)(2,1)S(1)}, bf16[4,2,64,256]{3,2,1,0:T(8,128)(2,1)S(1)}, u32[]{:S(2)}, u32[]{:S(2)}) collective-permute-start(bf16[4,2,64,256]{3,2,1,0:T(8,128)(2,1)S(1)} %collective-permute-done.14.refs_2_), channel_id=1, source_target_pairs={{0,8},{8,0},{16,24},{24,16},{1,9},{9,1},{17,25},{25,17},{2,10},{10... | collective-permute-start | bytes 786440 | tf_op jit(solution)/shard_map/ppermute | solution.py:602
  174.5 1.1 copy-start.10
  174.5 1.7 collective-permute-start.19
  176.2 0.7 copy-start.11
  176.2 0.8 copy-start.12
  176.2 0.9 copy-start.13
  177.1 0.7 copy-start.14

commit v12 on v11

--- a/solution.py
+++ b/solution.py
@@ -602,7 +602,7 @@
     return lax.ppermute(tensor, axis, [(i, i ^ distance) for i in range(size)])
 
 
-def reduce_sums(early, late, gain, width, beside):
+def reduce_sums(early, late, arrived_late, gain, width, beside):
     quad = gain.shape[1]
     count = gain.shape[0]
     wide = jnp.float32
@@ -629,8 +629,12 @@
 
     first = early[:width] + across(early[width:], "sample", 1)
     first, _ = halve([first], None, "sample", 2)
-    second, gain = halve([late], gain, "sample", 2)
-    second, gain = halve(second, gain, "turb", 1)
+    half = late.shape[0] // 2
+    sent = (late[half:] + arrived_late[half:]).astype(jnp.bfloat16)
+    arrived = across(jnp.concatenate([sent, pack(gain)]), "sample", 2).astype(wide)
+    second = late[:half] + arrived_late[:half] + arrived[:half]
+    gain = gain + arrived[half : half + count] + arrived[half + count : half + 2 * count]
+    second, gain = halve([second], gain, "turb", 1)
     parts, gain, beside = lax.optimization_barrier((first + second, gain, beside))
     share = parts[0].shape[0] // 4
     pieces = [jnp.concatenate([part[i * share : (i + 1) * share] for part in parts]) for i in range(4)]
@@ -736,7 +740,7 @@
     early = early + arrived.astype(jnp.float32)
     grad_inflow = swap(grad_rows.reshape(inflow.shape), "turb")
     parts, sum_gain, grad_inflow = reduce_sums(
-        early, late + arrived_late, gain + arrived_gain, width, grad_inflow
+        early, late, arrived_late, gain + arrived_gain, width, grad_inflow
     )
     sums = place_sums(parts, width)
     lowest = jnp.finfo(jnp.bfloat16).min

time: 182 us -> 181 us (level)
  waiting for transfers between devices: 45.9 us -> 43.3 us
    ppermute x20, waiting for transfers between devices: 34.8 us -> 32 us  [across(): return lax.ppermute(tensor, axis, [(i, i ^ distance) for i in range(size)])]
    all_to_all x3, starting transfers between devices: 11.2 us -> 13 us  [swap(): return lax.all_to_all(tensor, axis, split_axis=0, concat_axis=0, tiled=True)]
    unnamed x31 -> x33, local copies, waits for them, and re-layouts: 3.88 us -> 3.91 us
  transfers between devices with their start and end apart: 23 -> 23, of which waited for: 14 -> 13; matrix products, arithmetic and copies ran while one was open for 3% -> 3% of each run, Pallas kernels for 32% -> 32%
where the time goes in v12:
time: 181 us; the launch traced here: 180 us
  Pallas kernels  60.9 us (34%)
  waiting for transfers between devices  43.3 us (24%)
  blocking collectives  33.1 us (18%)
  starting transfers between devices  30.4 us (17%)
  local copies, waits for them, and re-layouts  6.05 us (3%)
  other arithmetic  4.61 us (3%)
    all_to_all x1, blocking collectives, swap(): return lax.all_to_all(tensor, axis, split_axis=0, concat_axis=0, tiled=True)  33.1 us
    ppermute x20, waiting for transfers between devices, across(): return lax.ppermute(tensor, axis, [(i, i ^ distance) for i in range(size)])  32 us
    pallas_call x2, Pallas kernels, backward(): pl.pallas_call(lambda *refs: backward_kernel(block_rows, head_dim, which,...  29.2 us
    pallas_call x1, Pallas kernels, forward(): pl.pallas_call(lambda *refs: forward_kernel(block_rows, head_dim, *refs),...  21.5 us
    ppermute x20, starting transfers between devices, across(): return lax.ppermute(tensor, axis, [(i, i ^ distance) for i in range(size)])  17.4 us
    all_to_all x3, starting transfers between devices, swap(): return lax.all_to_all(tensor, axis, split_axis=0, concat_axis=0, tiled=True)  13 us
    all_to_all x3, waiting for transfers between devices, swap(): return lax.all_to_all(tensor, axis, split_axis=0, concat_axis=0, tiled=True)  11.4 us
    pallas_call x1, Pallas kernels, finish(): pl.pallas_call(lambda *refs: finish_kernel(width // quad, *refs), grid=(r...  6.54 us
  transfers between devices with their start and end apart: 23, of which 13 were waited for; matrix products, arithmetic and copies ran while one was open for 3% of the time, Pallas kernels for 32%

profile of v12, /device:TPU:0, one launch (start us, length us, event | category | flops | bytes accessed | tf_op | source)
XLA Modules:
  0.0 179.7 jit_solution(2264419034110570382)
XLA Ops:
  0.6 33.1 %all_to_all.20 = bf16[8,128,512]{2,1,0:T(8,128)(2,1)} all-to-all(bf16[8,128,512]{2,1,0:T(8,128)(2,1)} %param.9), channel_id=1, replica_groups=mesh['sample'=4,'turb'=8] {'turb'}, dimensions={0} | all-to-all | bytes 2097152 | tf_op jit(solution)/shard_map/all_to_all | solution.py:592
  33.8 3.6 %all-to-all-start.1 = ((bf16[8,128,512]{2,1,0:T(8,128)(2,1)}), bf16[8,128,512]{2,1,0:T(8,128)(2,1)S(1)}, u32[]{:S(2)}, u32[]{:S(2)}) async-start(bf16[8,128,512]{2,1,0:T(8,128)(2,1)} %param.10), calls=%async_computation.1 | async-start | bytes 2097152 | tf_op jit(solution)/shard_map/all_to_all | solution.py:592
  37.4 21.5 %forward.1 = (bf16[512,1024]{1,0:T(8,128)(2,1)}, bf16[1024,512]{1,0:T(8,128)(2,1)}, bf16[1024,512]{1,0:T(8,128)(2,1)}, bf16[1024,512]{1,0:T(8,128)(2,1)}, bf16[5...) custom-call(s32[8]{0:T(128)} %refs_0_.5, ...), custom_call_target="tpu_custom_call" | custom-call | flops 5368709120 | bytes 10485760 | tf_op jit(solution)/shard_map/forward/pallas_call | solution.py:367
  58.9 4.1 %all-to-all-done.1 = bf16[8,128,512]{2,1,0:T(8,128)(2,1)S(1)} async-done(((bf16[8,128,512]{2,1,0:T(8,128)(2,1)}), bf16[8,128,512]{2,1,0:T(8,128)(2,1)S(1)}, u32[]{:S(2)}, u32[]{:S(2)}) %all-to-all-start.1) | async-done | bytes 1048608 | tf_op jit(solution)/shard_map/all_to_all | solution.py:592
  63.0 1.0 copy-done
  63.9 3.7 %all-to-all-start.2 = ((bf16[8,128,512]{2,1,0:T(8,128)(2,1)}), bf16[8,128,512]{2,1,0:T(8,128)(2,1)S(1)}, u32[]{:S(2)}, u32[]{:S(2)}) async-start(bf16[8,128,512]{2,1,0:T(8,128)(2,1)} %bitcast.15), calls=%async_computation.2 | async-start | bytes 2097152 | tf_op jit(solution)/shard_map/all_to_all | solution.py:592
  67.7 14.5 %backward.2 = (bf16[1024,256]{1,0:T(8,128)(2,1)}, bf16[1024,256]{1,0:T(8,128)(2,1)}, bf16[1024,256]{1,0:T(8,128)(2,1)}, f32[1024,256]{1,0:T(8,128)}, bf16[1024,256]{1,0:T(8,128)(2,1)}, /*index=5*/f32[8,512]{1,0:T(8,128)}) custom-call(s32[8]{0:T(128)} %refs_0_.5, s32[3,8,8]{2,1,0:T(8,128)} %bitcast.26, bf16[512,512]{1,0:T(8,128)(2,1)} %refs_2_.3, ...), custom_call_target="tpu_custom_call" | custom-call | flops 4026531840 | bytes 7340032 | tf_op jit(solution)/shard_map/backward/pallas_call | solution.py:506
  82.2 1.1 collective-permute-start
  83.3 14.6 %backward.3 = (bf16[1024,256]{1,0:T(8,128)(2,1)}, bf16[1024,256]{1,0:T(8,128)(2,1)}, bf16[1024,256]{1,0:T(8,128)(2,1)}, f32[1024,256]{1,0:T(8,128)}, f32[1024,256]{1,0:T(8,128)}, /*index=5*/f32[8,512]{1,0:T(8,128)}) custom-call(s32[8]{0:T(128)} %refs_0_.5, s32[3,8,8]{2,1,0:T(8,128)} %bitcast.27, bf16[512,512]{1,0:T(8,128)(2,1)} %refs_2_.3, ...), custom_call_target="tpu_custom_call" | custom-call | flops 4026531840 | bytes 7340032 | tf_op jit(solution)/shard_map/backward/pallas_call | solution.py:506
  97.9 0.0 copy-start.7
  97.9 0.8 copy-done.7
  98.7 0.0 collective-permute-start.1
  98.7 6.5 %finish.1 = bf16[1024,512]{1,0:T(8,128)(2,1)} custom-call(bf16[1024,512]{1,0:T(8,128)(2,1)} %bitcast.11, bf16[1024,512]{1,0:T(8,128)(2,1)} %bitcast.14, f32[1,512]{1,0:T(1,128)} %bitcast.23, bf16[512,512]{1,0:T(8,128)(2,1)} %refs_3_.1, bf16[512,512]{1,0:T(8,128)(2,1)} %refs_4_.3, bf16[512,512]{1,0:T(8,128)(2,1)} %refs_5_.3, ...), custom_call_target="tpu_custom_call" | custom-call | flops 1610612736 | bytes 8388608 | tf_op jit(solution)/shard_map/finish/pallas_call | solution.py:572
  105.3 0.0 copy-start.5
  105.3 0.8 slice_reduce_fusion
  106.1 0.6 collective-permute-start.4
  106.6 0.1 add_convert_fusion
  106.7 0.7 collective-permute-done.4
  107.5 0.7 pad_maximum_fusion
  108.2 1.5 collective-permute-start.5
  109.7 5.7 %all-to-all-start.3 = ((bf16[8,128,512]{2,1,0:T(8,128)(2,1)}), bf16[8,128,512]{2,1,0:T(8,128)(2,1)S(1)}, u32[]{:S(2)}, u32[]{:S(2)}) async-start(bf16[8,128,512]{2,1,0:T(8,128)(2,1)} %bitcast.5), calls=%async_computation.3 | async-start | bytes 2097152 | tf_op jit(solution)/shard_map/all_to_all | solution.py:592
  115.4 1.8 collective-permute-done.5
  117.2 1.2 slice_add_fusion
  118.4 0.0 copy-start.8
  118.5 1.7 collective-permute-start.6
  120.2 0.1 convert_add_fusion
  120.3 0.1 collective-permute-start.2
  120.4 8.5 %collective-permute-done.6 = bf16[272,256]{1,0:T(8,128)(2,1)S(1)} collective-permute-done((bf16[272,256]{1,0:T(8,128)(2,1)S(1)}, bf16[272,256]{1,0:T(8,128)(2,1)S(1)}, u32[]{:S(2)}, u32[]{:S(2)}) %collective-permute-start.6) | collective-permute-done | bytes 139296 | tf_op jit(solution)/shard_map/ppermute | solution.py:602
  128.9 0.0 copy-start.1
  128.9 0.1 slice_add_fusion.1
  129.0 0.6 collective-permute-start.3
  129.6 4.5 %collective-permute-done.3 = bf16[256,256]{1,0:T(8,128)(2,1)S(1)} collective-permute-done((bf16[256,256]{1,0:T(8,128)(2,1)S(1)}, bf16[256,256]{1,0:T(8,128)(2,1)S(1)}, u32[]{:S(2)}, u32[]{:S(2)}) %collective-permute-start.3) | collective-permute-done | bytes 131104 | tf_op jit(solution)/shard_map/ppermute | solution.py:602
  134.1 7.3 %all-to-all-done.3 = bf16[8,128,512]{2,1,0:T(8,128)(2,1)S(1)} async-done(((bf16[8,128,512]{2,1,0:T(8,128)(2,1)}), bf16[8,128,512]{2,1,0:T(8,128)(2,1)S(1)}, u32[]{:S(2)}, u32[]{:S(2)}) %all-to-all-start.3) | async-done | bytes 1048608 | tf_op jit(solution)/shard_map/all_to_all | solution.py:592
  141.4 0.2 concatenate.33
  141.6 0.1 collective-permute-start.7
  141.7 0.2 concatenate.34
  141.8 2.2 %collective-permute-start.8 = (bf16[144,256]{1,0:T(8,128)(2,1)S(1)}, bf16[144,256]{1,0:T(8,128)(2,1)S(1)}, u32[]{:S(2)}, u32[]{:S(2)}) collective-permute-start(bf16[144,256]{1,0:T(8,128)(2,1)S(1)} %concatenate.34), channel_id=1, source_target_pairs={{0,4},{1,5},{2,6},{3,7},{4,0},{5,1},{6,2},{7,3},{8,12},{9,13},{10,... | collective-permute-start | bytes 221192 | tf_op jit(solution)/shard_map/ppermute | solution.py:602
  144.0 0.1 concatenate.35
  144.2 2.3 %collective-permute-start.9 = (bf16[144,256]{1,0:T(8,128)(2,1)S(1)}, bf16[144,256]{1,0:T(8,128)(2,1)S(1)}, u32[]{:S(2)}, u32[]{:S(2)}) collective-permute-start(bf16[144,256]{1,0:T(8,128)(2,1)S(1)} %concatenate.35), channel_id=1, source_target_pairs={{0,6},{1,7},{2,4},{3,5},{4,2},{5,3},{6,0},{7,1},{8,14},{9,15},{10,... | collective-permute-start | bytes 221192 | tf_op jit(solution)/shard_map/ppermute | solution.py:602
  146.5 3.9 %collective-permute-done.8 = bf16[144,256]{1,0:T(8,128)(2,1)S(1)} collective-permute-done((bf16[144,256]{1,0:T(8,128)(2,1)S(1)}, bf16[144,256]{1,0:T(8,128)(2,1)S(1)}, u32[]{:S(2)}, u32[]{:S(2)}) %collective-permute-start.8) | collective-permute-done | bytes 73760 | tf_op jit(solution)/shard_map/ppermute | solution.py:602
  150.5 0.0 slice-start.1
  150.5 0.8 slice-done
  151.3 0.0 slice-done.1
  151.4 0.6 collective-permute-start.10
  151.9 1.5 collective-permute-start.11
  153.5 2.4 %collective-permute-start.12 = (bf16[1,2,64,256]{3,2,1,0:T(8,128)(2,1)S(1)}, bf16[1,2,64,256]{3,2,1,0:T(8,128)(2,1)S(1)}, u32[]{:S(2)}, u32[]{:S(2)}) collective-permute-start(bf16[1,2,64,256]{3,2,1,0:T(8,128)(2,1)S(1)} %bitcast.18), channel_id=1, source_target_pairs={{0,6},{1,7},{2,4},{3,5},{4,2},{5,3},{6,0},{7,1},{8,14},{9,15},{10,... | collective-permute-start | bytes 196616 | tf_op jit(solution)/shard_map/ppermute | solution.py:602
  155.8 1.6 collective-permute-done.10
  157.4 0.9 collective-permute-done.11
  158.3 1.3 collective-permute-done.12
  159.7 1.5 collective-permute-start.13
  161.2 0.5 collective-permute-start.14
  161.6 4.5 %collective-permute-done.13.refs_1_ = bf16[4,2,64,256]{3,2,1,0:T(8,128)(2,1)S(1)} collective-permute-done((bf16[4,2,64,256]{3,2,1,0:T(8,128)(2,1)S(1)}, bf16[4,2,64,256]{3,2,1,0:T(8,128)(2,1)S(1)}, u32[]{:S(2)}, u32[]{:S(2)}) %collective-permute-start.13) | collective-permute-done | bytes 262176 | tf_op jit(solution)/shard_map/ppermute | solution.py:602
  166.1 0.5 collective-permute-start.15
  166.6 1.1 broadcast_maximum_fusion.1
  167.7 0.5 collective-permute-start.17
  168.2 1.5 collective-permute-done.14.refs_2_
  169.7 2.8 %collective-permute-done.15.refs_3_ = bf16[4,2,64,256]{3,2,1,0:T(8,128)(2,1)S(1)} collective-permute-done((bf16[4,2,64,256]{3,2,1,0:T(8,128)(2,1)S(1)}, bf16[4,2,64,256]{3,2,1,0:T(8,128)(2,1)S(1)}, u32[]{:S(2)}, u32[]{:S(2)}) %collective-permute-start.15) | collective-permute-done | bytes 262176 | tf_op jit(solution)/shard_map/ppermute | solution.py:602
  172.5 1.1 broadcast_maximum_fusion
  173.6 0.6 copy.16
  174.2 0.7 copy-done.12
  174.9 0.1 copy-done.13
  175.0 0.1 copy-done.14
  175.1 0.7 copy-done.15
  175.8 3.7 %place.1 = (f32[512,512]{1,0:T(8,128)}, f32[512,512]{1,0:T(8,128)}, f32[512,512]{1,0:T(8,128)}, f32[512,512]{1,0:T(8,128)}) custom-call(bf16[4,2,64,256]{3,2,1,0:T(8,128)(2,1)} %copy-done.6, bf16[4,2,64,256]{3,2,1,0:T(8,128)(2,1)} %copy-done.9, bf16[4,2,64,256]{3,2,1,0:T(8,128)(2,1)} %copy-done.10, bf16[4,2,64,256]{3,2,1,0:T(8,128)(2,1)} %copy-done.11, ...), custom_call_target="tpu_custom_call" | custom-call | bytes 6291456 | tf_op jit(solution)/shard_map/place/pallas_call | solution.py:681
  (59 shorter events, 0.5 us)
Async XLA Ops:
  33.8 29.2 %all-to-all-start.1 = ((bf16[8,128,512]{2,1,0:T(8,128)(2,1)}), bf16[8,128,512]{2,1,0:T(8,128)(2,1)S(1)}, u32[]{:S(2)}, u32[]{:S(2)}) async-start(bf16[8,128,512]{2,1,0:T(8,128)(2,1)} %param.10), calls=%async_computation.1 | async-start | bytes 2097152 | tf_op jit(solution)/shard_map/all_to_all | solution.py:592
  63.0 1.0 copy-start
  63.9 34.0 %all-to-all-start.2 = ((bf16[8,128,512]{2,1,0:T(8,128)(2,1)}), bf16[8,128,512]{2,1,0:T(8,128)(2,1)S(1)}, u32[]{:S(2)}, u32[]{:S(2)}) async-start(bf16[8,128,512]{2,1,0:T(8,128)(2,1)} %bitcast.15), calls=%async_computation.2 | async-start | bytes 2097152 | tf_op jit(solution)/shard_map/all_to_all | solution.py:592
  82.2 15.7 %collective-permute-start = (bf16[1024,256]{1,0:T(8,128)(2,1)}, bf16[1024,256]{1,0:T(8,128)(2,1)S(1)}, u32[]{:S(2)}, u32[]{:S(2)}) collective-permute-start(bf16[1024,256]{1,0:T(8,128)(2,1)} %get-tuple-element.63), channel_id=1, source_target_pairs={{0,1},{1,0},{2,3},{3,2},{4,5},{5,4},{6,7},{7,6},{8,9},{9,8},{10,11... | collective-permute-start | bytes 1572872 | tf_op jit(solution)/shard_map/ppermute | solution.py:602
  97.9 0.8 copy-start.7
  98.7 6.5 %collective-permute-start.1 = (f32[1024,256]{1,0:T(8,128)}, f32[1024,256]{1,0:T(8,128)S(1)}, u32[]{:S(2)}, u32[]{:S(2)}) collective-permute-start(f32[1024,256]{1,0:T(8,128)} %get-tuple-element.73), channel_id=1, source_target_pairs={{0,8},{8,0},{16,24},{24,16},{1,9},{9,1},{17,25},{25,17},{2,10},{10... | collective-permute-start | bytes 3145736 | tf_op jit(solution)/shard_map/ppermute | solution.py:602
  98.7 7.9 %copy-start.4 = (f32[1024,256]{1,0:T(8,128)S(1)}, f32[1024,256]{1,0:T(8,128)}, u32[]{:S(2)}) copy-start(f32[1024,256]{1,0:T(8,128)} %get-tuple-element.79) | copy-start | bytes 3145732
  105.3 4.4 %copy-start.5 = (f32[1024,256]{1,0:T(8,128)}, f32[1024,256]{1,0:T(8,128)S(1)}, u32[]{:S(2)}) copy-start(f32[1024,256]{1,0:T(8,128)S(1)} %collective-permute-done.1) | copy-start | bytes 3145732
  106.1 1.4 collective-permute-start.4
  108.2 8.9 %collective-permute-start.5 = (bf16[528,256]{1,0:T(8,128)(2,1)}, bf16[528,256]{1,0:T(8,128)(2,1)S(1)}, u32[]{:S(2)}, u32[]{:S(2)}) collective-permute-start(bf16[528,256]{1,0:T(8,128)(2,1)} %pad_maximum_fusion), channel_id=1, source_target_pairs={{0,16},{8,24},{16,0},{24,8},{1,17},{9,25},{17,1},{25,9},{2,18},{10... | collective-permute-start | bytes 811016 | tf_op jit(solution)/shard_map/ppermute | solution.py:602
  109.7 31.7 %all-to-all-start.3 = ((bf16[8,128,512]{2,1,0:T(8,128)(2,1)}), bf16[8,128,512]{2,1,0:T(8,128)(2,1)S(1)}, u32[]{:S(2)}, u32[]{:S(2)}) async-start(bf16[8,128,512]{2,1,0:T(8,128)(2,1)} %bitcast.5), calls=%async_computation.3 | async-start | bytes 2097152 | tf_op jit(solution)/shard_map/all_to_all | solution.py:592
  117.2 3.0 %copy-start.3 = (f32[1024,256]{1,0:T(8,128)S(1)}, f32[1024,256]{1,0:T(8,128)}, u32[]{:S(2)}) copy-start(f32[1024,256]{1,0:T(8,128)} %get-tuple-element.77) | copy-start | bytes 3145732
  118.4 1.7 copy-start.8
  118.5 10.3 %collective-permute-start.6 = (bf16[272,256]{1,0:T(8,128)(2,1)S(1)}, bf16[272,256]{1,0:T(8,128)(2,1)S(1)}, u32[]{:S(2)}, u32[]{:S(2)}) collective-permute-start(bf16[272,256]{1,0:T(8,128)(2,1)S(1)} %pad_maximum_fusion.2), channel_id=1, source_target_pairs={{0,1},{1,0},{2,3},{3,2},{4,5},{5,4},{6,7},{7,6},{8,9},{9,8},{10,11... | collective-permute-start | bytes 417800 | tf_op jit(solution)/shard_map/ppermute | solution.py:602
  120.3 8.6 %collective-permute-start.2 = (f32[512,256]{1,0:T(8,128)S(1)}, f32[512,256]{1,0:T(8,128)S(1)}, u32[]{:S(2)}, u32[]{:S(2)}) collective-permute-start(f32[512,256]{1,0:T(8,128)S(1)} %slice.149), channel_id=1, source_target_pairs={{0,8},{8,0},{16,24},{24,16},{1,9},{9,1},{17,25},{25,17},{2,10},{10... | collective-permute-start | bytes 1572872 | tf_op jit(solution)/shard_map/ppermute | solution.py:602
  128.9 17.6 %copy-start.1 = (f32[256,256]{1,0:T(8,128)}, f32[256,256]{1,0:T(8,128)S(1)}, u32[]{:S(2)}) copy-start(f32[256,256]{1,0:T(8,128)S(1)} %slice_add_fusion.2) | copy-start | bytes 786436
  129.0 5.0 %collective-permute-start.3 = (bf16[256,256]{1,0:T(8,128)(2,1)S(1)}, bf16[256,256]{1,0:T(8,128)(2,1)S(1)}, u32[]{:S(2)}, u32[]{:S(2)}) collective-permute-start(bf16[256,256]{1,0:T(8,128)(2,1)S(1)} %slice.225), channel_id=1, source_target_pairs={{0,16},{8,24},{16,0},{24,8},{1,17},{9,25},{17,1},{25,9},{2,18},{10... | collective-permute-start | bytes 393224 | tf_op jit(solution)/shard_map/ppermute | solution.py:602
  134.1 12.4 %copy-start.2 = (f32[256,256]{1,0:T(8,128)}, f32[256,256]{1,0:T(8,128)S(1)}, u32[]{:S(2)}) copy-start(f32[256,256]{1,0:T(8,128)S(1)} %slice_add_fusion.3) | copy-start | bytes 786436
  141.6 4.9 %collective-permute-start.7 = (bf16[144,256]{1,0:T(8,128)(2,1)S(1)}, bf16[144,256]{1,0:T(8,128)(2,1)S(1)}, u32[]{:S(2)}, u32[]{:S(2)}) collective-permute-start(bf16[144,256]{1,0:T(8,128)(2,1)S(1)} %concatenate.33), channel_id=1, source_target_pairs={{0,2},{1,3},{2,0},{3,1},{4,6},{5,7},{6,4},{7,5},{8,10},{9,11},{10,... | collective-permute-start | bytes 221192 | tf_op jit(solution)/shard_map/ppermute | solution.py:602
  141.8 8.6 %collective-permute-start.8 = (bf16[144,256]{1,0:T(8,128)(2,1)S(1)}, bf16[144,256]{1,0:T(8,128)(2,1)S(1)}, u32[]{:S(2)}, u32[]{:S(2)}) collective-permute-start(bf16[144,256]{1,0:T(8,128)(2,1)S(1)} %concatenate.34), channel_id=1, source_target_pairs={{0,4},{1,5},{2,6},{3,7},{4,0},{5,1},{6,2},{7,3},{8,12},{9,13},{10,... | collective-permute-start | bytes 221192 | tf_op jit(solution)/shard_map/ppermute | solution.py:602
  144.2 6.3 %collective-permute-start.9 = (bf16[144,256]{1,0:T(8,128)(2,1)S(1)}, bf16[144,256]{1,0:T(8,128)(2,1)S(1)}, u32[]{:S(2)}, u32[]{:S(2)}) collective-permute-start(bf16[144,256]{1,0:T(8,128)(2,1)S(1)} %concatenate.35), channel_id=1, source_target_pairs={{0,6},{1,7},{2,4},{3,5},{4,2},{5,3},{6,0},{7,1},{8,14},{9,15},{10,... | collective-permute-start | bytes 221192 | tf_op jit(solution)/shard_map/ppermute | solution.py:602
  150.5 0.8 slice-start
  150.5 0.9 slice-start.1
  151.4 6.0 %collective-permute-start.10 = (bf16[1,2,64,256]{3,2,1,0:T(8,128)(2,1)S(1)}, bf16[1,2,64,256]{3,2,1,0:T(8,128)(2,1)S(1)}, u32[]{:S(2)}, u32[]{:S(2)}) collective-permute-start(bf16[1,2,64,256]{3,2,1,0:T(8,128)(2,1)S(1)} %bitcast.16), channel_id=1, source_target_pairs={{0,2},{1,3},{2,0},{3,1},{4,6},{5,7},{6,4},{7,5},{8,10},{9,11},{10,... | collective-permute-start | bytes 196616 | tf_op jit(solution)/shard_map/ppermute | solution.py:602
  151.9 6.4 %collective-permute-start.11 = (bf16[1,2,64,256]{3,2,1,0:T(8,128)(2,1)S(1)}, bf16[1,2,64,256]{3,2,1,0:T(8,128)(2,1)S(1)}, u32[]{:S(2)}, u32[]{:S(2)}) collective-permute-start(bf16[1,2,64,256]{3,2,1,0:T(8,128)(2,1)S(1)} %bitcast.17), channel_id=1, source_target_pairs={{0,4},{1,5},{2,6},{3,7},{4,0},{5,1},{6,2},{7,3},{8,12},{9,13},{10,... | collective-permute-start | bytes 196616 | tf_op jit(solution)/shard_map/ppermute | solution.py:602
  153.5 6.2 %collective-permute-start.12 = (bf16[1,2,64,256]{3,2,1,0:T(8,128)(2,1)S(1)}, bf16[1,2,64,256]{3,2,1,0:T(8,128)(2,1)S(1)}, u32[]{:S(2)}, u32[]{:S(2)}) collective-permute-start(bf16[1,2,64,256]{3,2,1,0:T(8,128)(2,1)S(1)} %bitcast.18), channel_id=1, source_target_pairs={{0,6},{1,7},{2,4},{3,5},{4,2},{5,3},{6,0},{7,1},{8,14},{9,15},{10,... | collective-permute-start | bytes 196616 | tf_op jit(solution)/shard_map/ppermute | solution.py:602
  159.7 8.0 %copy-start.6 = (bf16[4,2,64,256]{3,2,1,0:T(8,128)(2,1)}, bf16[4,2,64,256]{3,2,1,0:T(8,128)(2,1)S(1)}, u32[]{:S(2)}) copy-start(bf16[4,2,64,256]{3,2,1,0:T(8,128)(2,1)S(1)} %pad_maximum_fusion.1.refs_0_) | copy-start | bytes 786436
  159.7 6.4 %collective-permute-start.13 = (bf16[4,2,64,256]{3,2,1,0:T(8,128)(2,1)S(1)}, bf16[4,2,64,256]{3,2,1,0:T(8,128)(2,1)S(1)}, u32[]{:S(2)}, u32[]{:S(2)}) collective-permute-start(bf16[4,2,64,256]{3,2,1,0:T(8,128)(2,1)S(1)} %pad_maximum_fusion.1.refs_0_), channel_id=1, source_target_pairs={{0,1},{1,0},{2,3},{3,2},{4,5},{5,4},{6,7},{7,6},{8,9},{9,8},{10,11... | collective-permute-start | bytes 786440 | tf_op jit(solution)/shard_map/ppermute | solution.py:602
  161.2 8.6 %collective-permute-start.14 = (bf16[4,2,64,256]{3,2,1,0:T(8,128)(2,1)S(1)}, bf16[4,2,64,256]{3,2,1,0:T(8,128)(2,1)S(1)}, u32[]{:S(2)}, u32[]{:S(2)}) collective-permute-start(bf16[4,2,64,256]{3,2,1,0:T(8,128)(2,1)S(1)} %pad_maximum_fusion.1.refs_0_), channel_id=1, source_target_pairs={{0,16},{8,24},{16,0},{24,8},{1,17},{9,25},{17,1},{25,9},{2,18},{10... | collective-permute-start | bytes 786440 | tf_op jit(solution)/shard_map/ppermute | solution.py:602
  166.1 1.6 copy-start.9
  166.1 6.4 %collective-permute-start.15 = (bf16[4,2,64,256]{3,2,1,0:T(8,128)(2,1)S(1)}, bf16[4,2,64,256]{3,2,1,0:T(8,128)(2,1)S(1)}, u32[]{:S(2)}, u32[]{:S(2)}) collective-permute-start(bf16[4,2,64,256]{3,2,1,0:T(8,128)(2,1)S(1)} %collective-permute-done.13.refs_1_), channel_id=1, source_target_pairs={{0,16},{8,24},{16,0},{24,8},{1,17},{9,25},{17,1},{25,9},{2,18},{10... | collective-permute-start | bytes 786440 | tf_op jit(solution)/shard_map/ppermute | solution.py:602
  167.7 6.5 %collective-permute-start.16 = (bf16[4,2,64,256]{3,2,1,0:T(8,128)(2,1)S(1)}, bf16[4,2,64,256]{3,2,1,0:T(8,128)(2,1)S(1)}, u32[]{:S(2)}, u32[]{:S(2)}) collective-permute-start(bf16[4,2,64,256]{3,2,1,0:T(8,128)(2,1)S(1)} %pad_maximum_fusion.1.refs_0_), channel_id=1, source_target_pairs={{0,8},{8,0},{16,24},{24,16},{1,9},{9,1},{17,25},{25,17},{2,10},{10... | collective-permute-start | bytes 786440 | tf_op jit(solution)/shard_map/ppermute | solution.py:602
  167.7 6.5 %collective-permute-start.17 = (bf16[4,2,64,256]{3,2,1,0:T(8,128)(2,1)S(1)}, bf16[4,2,64,256]{3,2,1,0:T(8,128)(2,1)S(1)}, u32[]{:S(2)}, u32[]{:S(2)}) collective-permute-start(bf16[4,2,64,256]{3,2,1,0:T(8,128)(2,1)S(1)} %collective-permute-done.13.refs_1_), channel_id=1, source_target_pairs={{0,8},{8,0},{16,24},{24,16},{1,9},{9,1},{17,25},{25,17},{2,10},{10... | collective-permute-start | bytes 786440 | tf_op jit(solution)/shard_map/ppermute | solution.py:602
  169.7 3.9 %copy-start.10 = (bf16[4,2,64,256]{3,2,1,0:T(8,128)(2,1)}, bf16[4,2,64,256]{3,2,1,0:T(8,128)(2,1)S(1)}, u32[]{:S(2)}) copy-start(bf16[4,2,64,256]{3,2,1,0:T(8,128)(2,1)S(1)} %collective-permute-done.14.refs_2_) | copy-start | bytes 786436
  169.7 4.5 %collective-permute-start.18 = (bf16[4,2,64,256]{3,2,1,0:T(8,128)(2,1)S(1)}, bf16[4,2,64,256]{3,2,1,0:T(8,128)(2,1)S(1)}, u32[]{:S(2)}, u32[]{:S(2)}) collective-permute-start(bf16[4,2,64,256]{3,2,1,0:T(8,128)(2,1)S(1)} %collective-permute-done.14.refs_2_), channel_id=1, source_target_pairs={{0,8},{8,0},{16,24},{24,16},{1,9},{9,1},{17,25},{25,17},{2,10},{10... | collective-permute-start | bytes 786440 | tf_op jit(solution)/shard_map/ppermute | solution.py:602
  172.5 1.1 copy-start.11
  172.5 1.7 collective-permute-start.19
  174.2 0.7 copy-start.12
  174.2 0.8 copy-start.13
  174.2 0.9 copy-start.14
  175.1 0.7 copy-start.15
